TPU v7x, 256 devices: a whole 4x4x8 slice. The times are simulated.
256 devices in a mesh: lon: 128 (over y_hi, x, z, core), lat: 2 (over y_lo).
Axes of the slice: x: 4, y: 4 (y_hi: 2, y_lo: 2; y = y_hi * 2 + y_lo), z: 8, core: 2. Of those that a mesh axis runs over, the one named last changes fastest.
Arguments:
- inputs: bfloat16 [1, 2, 12, 1536, 512], P(None, None, 'lat', 'lon'), may hold values from -24 to 24
- grad_out: bfloat16 [1, 2, 12, 1536, 512], P(None, None, 'lat', 'lon'), may hold values from -6 to 6
- gains: float32 [2, 512], replicated, may hold values from 0.5 to 1.5
- qkv_weight: bfloat16 [2, 512, 1536], replicated, may hold values from -0.5 to 0.5
- proj_weight: bfloat16 [2, 512, 512], replicated, may hold values from -0.25 to 0.25
- bias_table: float32 [2, 2, 16, 759], replicated, may hold values from -3 to 303
- rel_ids: int32 [144, 144], replicated, may hold values from 0 to 758
- groups: int32 [2, 12, 1536], P(None, 'lat', 'lon'), may hold values from 0 to 3
Outputs:
- outputs: bfloat16 [1, 2, 12, 1536, 512], P(None, None, 'lat', 'lon')
- grad_inputs: bfloat16 [1, 2, 12, 1536, 512], P(None, None, 'lat', 'lon')
- grad_gains: float32 [2, 512], replicated
- grad_qkv: float32 [2, 512, 1536], P(None, 'lon')
- grad_proj: float32 [2, 512, 512], P(None, 'lon')
- grad_bias: float32 [2, 2, 16, 759], replicated
All inputs are finite; a program needn't handle non-finite values.
Results may differ from a plain program's by a relative error of at most 0.035.
The roundings to bfloat16 on the way count: a program that leaves them out, or rounds other values in their place, can miss the bound.
Values may be sent and summed in bfloat16 or wider, within the bound.
No kernel may reach another device: no remote copies, remote signals or barrier semaphores. Data moves between devices by JAX's collectives and lax.ppermute only.
A program may use at most 128 MiB of HBM per device.

v0:
```python
import jax
import jax.numpy as jnp
from jax import lax
from jax.sharding import PartitionSpec as P

WT = 6
WN = 12


EPSILON = 1e-05
NEGATIVE = -1e30


def shortened(shard):
    return jax.tree.map(lambda a: a.astype(jnp.bfloat16) if a.dtype == jnp.float32 else a, shard)


def shifted(value, axis, steps):
    count = lax.axis_size(axis)
    pairs = [(source, (source + steps) % count) for source in range(count)]
    return lax.ppermute(value, axis, pairs)


def normalize(fields):
    center = fields - jnp.mean(fields, axis=-1, keepdims=True)
    inv_std = lax.rsqrt(jnp.mean(center * center, axis=-1, keepdims=True) + EPSILON)
    return (center * inv_std, inv_std)


def attend_forward(frame, gain_row, qkv_mat, proj_mat, bias_heads, allowed, heads):
    count_win, tokens_win, features = frame.shape
    head_dim = features // heads
    factor = head_dim ** (-0.5)
    frame_wide = frame.astype(jnp.float32)
    normed, inv_std = normalize(frame_wide)
    hidden = (normed * gain_row).astype(jnp.bfloat16)
    flat_hidden = hidden.reshape(count_win * tokens_win, features)
    packed = jnp.dot(flat_hidden, qkv_mat, preferred_element_type=jnp.float32)
    packed = packed.astype(jnp.bfloat16).reshape(count_win, tokens_win, 3, heads, head_dim)
    queries = packed[:, :, 0]
    keys_part = packed[:, :, 1]
    values_part = packed[:, :, 2]
    scores = (
        jnp.einsum("wqhc,wkhc->whqk", queries, keys_part, preferred_element_type=jnp.float32)
        * factor
        + bias_heads[None]
    )
    if allowed is not None:
        scores = jnp.where(allowed[:, None], scores, NEGATIVE)
    row_top = jnp.max(scores, axis=-1, keepdims=True)
    exponent = jnp.exp(scores - row_top)
    probs_full = exponent / jnp.sum(exponent, axis=-1, keepdims=True)
    probs_low = probs_full.astype(jnp.bfloat16)
    mixed_heads = jnp.einsum(
        "whqk,wkhc->wqhc", probs_low, values_part, preferred_element_type=jnp.float32
    )
    mixed_heads = mixed_heads.astype(jnp.bfloat16).reshape(count_win * tokens_win, features)
    branch = jnp.dot(mixed_heads, proj_mat, preferred_element_type=jnp.float32)
    result = (frame_wide + branch.reshape(count_win, tokens_win, features)).astype(jnp.bfloat16)
    return (
        result,
        (
            normed,
            inv_std,
            flat_hidden,
            queries,
            keys_part,
            values_part,
            probs_full,
            probs_low,
            mixed_heads,
        ),
    )


def attend_backward(cotangent, saved, gain_row, qkv_mat, proj_mat, heads):
    count_win, tokens_win, features = cotangent.shape
    head_dim = features // heads
    factor = head_dim ** (-0.5)
    (
        normed,
        inv_std,
        flat_hidden,
        queries,
        keys_part,
        values_part,
        probs_full,
        probs_low,
        mixed_heads,
    ) = saved
    flat_grad = cotangent.reshape(count_win * tokens_win, features)
    grad_mixed = jnp.dot(flat_grad, proj_mat.T, preferred_element_type=jnp.float32)
    grad_mixed = grad_mixed.astype(jnp.bfloat16).reshape(count_win, tokens_win, heads, head_dim)
    grad_probs = jnp.einsum(
        "wqhc,wkhc->whqk", grad_mixed, values_part, preferred_element_type=jnp.float32
    )
    grad_values = jnp.einsum(
        "whqk,wqhc->wkhc", probs_low, grad_mixed, preferred_element_type=jnp.float32
    )
    grad_scores = probs_full * (
        grad_probs - jnp.sum(grad_probs * probs_full, axis=-1, keepdims=True)
    )
    grad_bias = jnp.sum(grad_scores, axis=0)
    scores_low = grad_scores.astype(jnp.bfloat16)
    grad_queries = (
        jnp.einsum("whqk,wkhc->wqhc", scores_low, keys_part, preferred_element_type=jnp.float32)
        * factor
    )
    grad_keys = (
        jnp.einsum("whqk,wqhc->wkhc", scores_low, queries, preferred_element_type=jnp.float32)
        * factor
    )
    grad_packed = jnp.stack([grad_queries, grad_keys, grad_values], axis=2).astype(jnp.bfloat16)
    grad_packed = grad_packed.reshape(count_win * tokens_win, 3 * features)
    grad_hidden = jnp.dot(grad_packed, qkv_mat.T, preferred_element_type=jnp.float32).reshape(
        count_win, tokens_win, features
    )
    grad_gain = jnp.sum(grad_hidden * normed, axis=(0, 1))
    grad_normed = grad_hidden * gain_row
    grad_frame = inv_std * (
        grad_normed
        - jnp.mean(grad_normed, axis=-1, keepdims=True)
        - normed * jnp.mean(grad_normed * normed, axis=-1, keepdims=True)
    )
    grad_frame = grad_frame + cotangent.astype(jnp.float32)
    pieces = (flat_hidden, grad_packed, mixed_heads, flat_grad)
    return (grad_frame.astype(jnp.bfloat16), pieces, grad_gain, grad_bias)


def local_windows(grid):
    batch_size, level_count, lat_rows, lon_cols, features = grid.shape
    view = grid.reshape(batch_size, level_count, lat_rows, lon_cols // WN, WN, features)
    view = view.transpose(0, 3, 1, 2, 4, 5)
    return view.reshape(batch_size * (lon_cols // WN), level_count * lat_rows * WN, features)


def grid_back(stacked, full_shape):
    batch_size, level_count, lat_rows, lon_cols, features = full_shape
    view = stacked.reshape(batch_size, lon_cols // WN, level_count, lat_rows, WN, features)
    return view.transpose(0, 2, 3, 1, 4, 5).reshape(full_shape)


def lon_move(parts, offset):
    return jax.tree.map(
        lambda part, own: part.astype(own.dtype), shifted(shortened(parts), "lon", offset), parts
    )


def lat_move(parts, offset):
    return jax.tree.map(
        lambda part, own: part.astype(own.dtype), shifted(shortened(parts), "lat", offset), parts
    )


def enter_frame(field, labels):
    level_count = field.shape[1]
    lon_half = WN // 2
    lat_half = WT // 2
    field = jnp.roll(field, -(level_count // 2), axis=1)
    if labels is None:
        moved = lon_move((field[:, :, :, :lon_half],), -1)
        field = jnp.concatenate([field[:, :, :, lon_half:], moved[0]], axis=3)
        moved = lat_move((field[:, :, :lat_half],), -1)
        return (jnp.concatenate([field[:, :, lat_half:], moved[0]], axis=2), None)
    labels = jnp.roll(labels, -(level_count // 2), axis=0)
    moved = lon_move((field[:, :, :, :lon_half], labels[:, :, :lon_half]), -1)
    field = jnp.concatenate([field[:, :, :, lon_half:], moved[0]], axis=3)
    labels = jnp.concatenate([labels[:, :, lon_half:], moved[1]], axis=2)
    moved = lat_move((field[:, :, :lat_half], labels[:, :lat_half]), -1)
    field = jnp.concatenate([field[:, :, lat_half:], moved[0]], axis=2)
    labels = jnp.concatenate([labels[:, lat_half:], moved[1]], axis=1)
    return (field, labels)


def leave_frame(field):
    level_count = field.shape[1]
    lat_rows = field.shape[2]
    lon_cols = field.shape[3]
    lon_half = WN // 2
    lat_half = WT // 2
    moved = lat_move((field[:, :, lat_rows - lat_half :],), 1)
    field = jnp.concatenate([moved[0], field[:, :, : lat_rows - lat_half]], axis=2)
    moved = lon_move((field[:, :, :, lon_cols - lon_half :],), 1)
    field = jnp.concatenate([moved[0], field[:, :, :, : lon_cols - lon_half]], axis=3)
    return jnp.roll(field, level_count // 2, axis=1)


def row_term(pieces):
    flat_hidden, grad_packed, mixed_heads, flat_grad = pieces
    contract = (((0,), (0,)), ((), ()))
    qkv_rows = lax.dot_general(
        flat_hidden, grad_packed, contract, preferred_element_type=jnp.float32
    )
    proj_rows = lax.dot_general(
        mixed_heads, flat_grad, contract, preferred_element_type=jnp.float32
    )
    return jnp.concatenate([qkv_rows, proj_rows], axis=1)


def table_grad(grad_bias, rel_ids, id_count):
    heads = grad_bias.shape[0]
    summed = jax.ops.segment_sum(
        grad_bias.reshape(heads, -1).T, rel_ids.reshape(-1), num_segments=id_count
    )
    return summed.T


def on_device(inputs, grad_out, gains, qkv_weight, proj_weight, bias_table, rel_ids, groups):
    batch_size, level_count, lat_rows, lon_cols, features = inputs.shape
    heads = bias_table.shape[2]
    latwins = bias_table.shape[1]
    id_count = bias_table.shape[3]
    lat_index = lax.axis_index("lat")
    table_zero = lax.dynamic_index_in_dim(bias_table[0], lat_index, 0, keepdims=False)
    table_one = lax.dynamic_index_in_dim(bias_table[1], lat_index, 0, keepdims=False)
    bias_zero = table_zero[:, rel_ids]
    bias_one = table_one[:, rel_ids]
    out_zero, saved_zero = attend_forward(
        local_windows(inputs), gains[0], qkv_weight[0], proj_weight[0], bias_zero, None, heads
    )
    mid = grid_back(out_zero, inputs.shape)
    frame_one, labels = enter_frame(mid, groups)
    global_rows = lat_index * lat_rows + jnp.arange(lat_rows, dtype=jnp.int32)
    row_seg = (global_rows >= lat_rows * lax.axis_size("lat") - WT // 2).astype(jnp.int32)
    level_seg = (jnp.arange(level_count) >= level_count - level_count // 2).astype(jnp.int32)
    keys_grid = labels * 4 + row_seg[None, :, None] * 2 + level_seg[:, None, None]
    keys_grid = keys_grid[None]
    key_win = local_windows(keys_grid[..., None])[..., 0]
    allowed = key_win[:, :, None] == key_win[:, None, :]
    out_one, saved_one = attend_forward(
        local_windows(frame_one), gains[1], qkv_weight[1], proj_weight[1], bias_one, allowed, heads
    )
    outputs = leave_frame(grid_back(out_one, inputs.shape))
    grad_frame_one = enter_frame(grad_out, None)[0]
    dframe_one, pieces_one, gain_one, dbias_one = attend_backward(
        local_windows(grad_frame_one), saved_one, gains[1], qkv_weight[1], proj_weight[1], heads
    )
    grad_mid = leave_frame(grid_back(dframe_one, inputs.shape))
    dframe_zero, pieces_zero, gain_zero, dbias_zero = attend_backward(
        local_windows(grad_mid), saved_zero, gains[0], qkv_weight[0], proj_weight[0], heads
    )
    owned = lax.psum_scatter(
        jnp.concatenate([row_term(pieces_zero), row_term(pieces_one)], axis=1),
        "lon",
        scatter_dimension=0,
        tiled=True,
    )
    owned = lax.psum(owned.astype(jnp.bfloat16), "lat").astype(jnp.float32)
    owned_zero = owned[:, : 4 * features]
    owned_one = owned[:, 4 * features :]
    grad_inputs = grid_back(dframe_zero, inputs.shape)
    selector = (jnp.arange(latwins) == lat_index).astype(jnp.float32)
    tables = jnp.stack(
        [table_grad(dbias_zero, rel_ids, id_count), table_grad(dbias_one, rel_ids, id_count)]
    )
    placed = tables[:, None] * selector[None, :, None, None]
    gain_terms = jnp.stack([gain_zero, gain_one])
    gain_total, bias_total = lax.psum((gain_terms, placed), ("lon", "lat"))
    factor = (
        batch_size * level_count * lat_rows * lon_cols * lax.axis_size("lon") * lax.axis_size("lat")
    ) ** (-0.5)
    grad_qkv = jnp.stack([owned_zero[:, : 3 * features], owned_one[:, : 3 * features]]) * factor
    grad_proj = jnp.stack([owned_zero[:, 3 * features :], owned_one[:, 3 * features :]]) * factor
    return (outputs, grad_inputs, gain_total * factor, grad_qkv, grad_proj, bias_total * factor)


def solution(mesh):
    placed = (
        P(None, None, "lat", "lon", None),
        P(None, None, "lat", "lon", None),
        P(),
        P(),
        P(),
        P(),
        P(),
        P(None, "lat", "lon"),
    )
    return jax.shard_map(
        on_device,
        mesh=mesh,
        in_specs=placed,
        out_specs=(
            P(None, None, "lat", "lon", None),
            P(None, None, "lat", "lon", None),
            P(),
            P(None, "lon", None),
            P(None, "lon", None),
            P(),
        ),
        check_vma=False,
    )
```

profile of v0, /device:TPU:1, one launch (start us, length us, event | category | flops | bytes accessed | tf_op | source)
XLA Modules:
  0.0 1552.6 jit_solution(3879036251349210500)
XLA Ops:
  8.7 3.2 collective-permute-start.2
  11.9 1.2 fusion.67
  13.2 1.0 fusion.56
  14.1 8.4 collective-permute-start.6
  22.5 1.1 convert_reduce_fusion
  23.6 1.1 copy.155
  24.8 0.9 copy.152
  25.7 1.3 fusion.69
  27.5 1.9 fusion.42
  31.3 1.9 convolution_convert_fusion.1
  33.5 38.7 %gather_fusion = f32[20736,16]{1,0:T(8,128)} fusion(f32[16,759]{0,1:T(8,128)S(1)} %bitcast.167, s32[21504]{0:T(1024)S(1)} %pad_clamp_fusion), kind=kCustom, calls=%fused_computation | custom fusion | bytes 2737152 | tf_op jit(solution)/shard_map/gather | solution.py:216
  72.2 11.7 copy.162
  84.4 2.1 fusion.70
  86.5 3.1 convolution_convert_fusion.5
  90.7 1.1 collective-permute-start
  93.3 38.7 %gather_fusion.1 = f32[20736,16]{1,0:T(8,128)} fusion(f32[16,759]{0,1:T(8,128)S(1)} %bitcast.168, s32[21504]{0:T(1024)S(1)} %pad_clamp_fusion), kind=kCustom, calls=%fused_computation.1 | custom fusion | bytes 2737152 | tf_op jit(solution)/shard_map/gather | solution.py:217
  132.0 11.7 copy.171
  148.4 1.6 fusion.55
  150.1 1.1 collective-permute-start.7
  152.9 1.1 reshape.928
  154.6 1.1 pad_maximum_fusion.7
  156.4 1.0 reshape_reshape_transpose_reshape.6
  157.4 2.1 convolution_convert_fusion.7
  159.4 1.7 copy.174
  161.2 1.1 fusion.57
  162.3 3.0 multiply_reduce_fusion.6
  166.7 1.0 convert_element_type.263
  167.7 2.6 convolution_convert_fusion
  170.3 2.2 copy.167
  172.5 1.6 fusion.2
  174.2 2.8 fusion.71
  177.0 4.7 convolution_convert_fusion.4
  181.7 3.7 fusion.17
  185.4 1.5 multiply_reduce_fusion.1
  187.0 2.1 subtract_multiply_fusion.1
  190.1 1.3 fusion.75
  192.6 2.0 multiply_reduce_fusion.2
  194.6 2.3 fusion.74
  196.9 1.6 reshape_transpose_reshape.17
  198.5 1.9 add_convert_fusion.1
  202.3 1.6 fusion.64
  203.9 2.3 copy.186
  206.2 1.3 collective-permute-start.4
  207.6 3.5 reshape.924
  211.1 5.6 copy.187
  216.7 112.6 %scatter_custom_fusion.1 = f32[759,16]{1,0:T(8,128)S(1)} fusion(s32[20736]{0:T(1024)} %reshape.947, f32[20736,16]{1,0:T(8,128)} %copy.187, f32[]{:T(128)} %constant.16.clone.1), kind=kCustom, calls=%fused_computation.112 | custom fusion | flops 331776 | bytes 49088 | tf_op jit(solution)/shard_map/scatter-add | solution.py:202
  330.1 3.5 collective-permute-start.9
  335.3 1.0 fusion.45
  336.7 1.2 fusion.73
  338.1 3.9 fusion.18
  342.5 1.1 copy-done.2
  345.5 1.0 copy-done.59
  348.1 1.3 copy-done
  349.4 3.6 pad_maximum_fusion
  353.0 733.0 %all-reduce.5 = bf16[512,4096]{1,0:T(8,128)(2,1)} all-reduce(f32[512,4096]{1,0:T(8,128)} %pad_maximum_fusion), channel_id=2, replica_groups=mesh['lon'=128,'lat'=2] {'lon'}, use_global_device_ids=true, to_apply=%region_17.18.clone | all-reduce | flops 2097152 | bytes 12582912
  1086.9 6.0 psum.22
  1093.0 2.4 copy.184
  1095.4 1.0 fusion.46
  1097.3 3.5 reshape.923
  1100.8 82.0 %psum.21 = f32[2,512]{1,0:T(2,128)S(1)} all-reduce(f32[2,512]{1,0:T(2,128)S(1)} %pad_maximum_fusion.13), channel_id=1, replica_groups=mesh['lon'=128,'lat'=2] {'lon','lat'}, use_global_device_ids=true, to_apply=%region_16.17 | all-reduce | flops 1024 | bytes 8192 | tf_op jit(solution)/shard_map/psum | solution.py:258
  1184.5 5.7 copy.185
  1190.2 112.5 %scatter_custom_fusion = f32[759,16]{1,0:T(8,128)S(1)} fusion(s32[20736]{0:T(1024)} %reshape.947, f32[20736,16]{1,0:T(8,128)} %copy.185, f32[]{:T(128)} %constant.16.clone.1), kind=kCustom, calls=%fused_computation.114 | custom fusion | flops 331776 | bytes 49088 | tf_op jit(solution)/shard_map/scatter-add | solution.py:202
  1304.9 239.0 %all-reduce.4.cloned.1.call-done = f32[2,2,16,759]{3,2,1,0:T(8,128)} async-done(((f32[2,2,16,759]{3,2,1,0:T(8,128)}), f32[2,2,16,759]{3,2,1,0:T(8,128)}) %all-reduce.4.cloned.1.call-update) | async-done | bytes 194320 | tf_op jit(solution)/shard_map/psum | solution.py:258
  1543.9 1.6 broadcast_multiply_fusion
  (221 shorter events, 31.9 us)
Async XLA Ops:
  7.2 22.9 %copy-start.12 = (bf16[1,2,6,12,512]{4,1,3,2,0:T(2,128)(2,1)S(1)}, bf16[1,2,6,12,512]{4,1,3,2,0:T(2,128)(2,1)}, u32[]{:S(2)}) copy-start(bf16[1,2,6,12,512]{4,1,3,2,0:T(2,128)(2,1)} %param.8) | copy-start | bytes 442372
  7.2 20.1 %copy-start.31 = (s32[144,144]{1,0:T(8,128)S(1)}, s32[144,144]{1,0:T(8,128)}, u32[]{:S(2)}) copy-start(s32[144,144]{1,0:T(8,128)} %param.14) | copy-start | bytes 248836
  7.2 20.3 %copy-start.40 = (f32[2,2,16,759]{3,2,1,0:T(8,128)S(1)}, f32[2,2,16,759]{3,2,1,0:T(8,128)}, u32[]{:S(2)}) copy-start(f32[2,2,16,759]{3,2,1,0:T(8,128)} %param.13) | copy-start | bytes 582916
  7.2 1536.7 %all-reduce.4.cloned.1.call-start = ((), (), s32[]{:S(2)}) async-start(), calls=%async_computation | async-start | bytes 393216 | tf_op jit(solution)/shard_map/psum | solution.py:258
  8.7 135.0 %collective-permute-start.2 = (s32[2,6,6]{2,0,1:T(2,128)}, s32[2,6,6]{2,0,1:T(2,128)}, u32[]{:S(2)}, u32[]{:S(2)}) collective-permute-start(s32[2,6,6]{2,0,1:T(2,128)} %get-tuple-element.71), channel_id=1, source_target_pairs={{0,254},{2,0},{4,2},{6,4},{8,6},{10,8},{12,10},{14,12},{16,14},{18... | collective-permute-start | bytes 872 | tf_op jit(solution)/shard_map/ppermute | solution.py:21
  14.1 134.3 %collective-permute-start.6 = (bf16[1,2,6,6,512]{4,1,3,2,0:T(2,128)(2,1)}, bf16[1,2,6,6,512]{4,1,3,2,0:T(2,128)(2,1)}, u32[]{:S(2)}, u32[]{:S(2)}) collective-permute-start(bf16[1,2,6,6,512]{4,1,3,2,0:T(2,128)(2,1)} %get-tuple-element.43), channel_id=1, source_target_pairs={{0,254},{2,0},{4,2},{6,4},{8,6},{10,8},{12,10},{14,12},{16,14},{18... | collective-permute-start | bytes 221192 | tf_op jit(solution)/shard_map/ppermute | solution.py:21
  27.1 4.0 copy-start.44
  27.3 2.4 copy-start.48
  30.4 3.1 copy-start.27
  31.3 58.4 %copy-start.9 = (f32[144,512]{1,0:T(8,128)}, f32[144,512]{1,0:T(8,128)S(1)}, u32[]{:S(2)}) copy-start(f32[144,512]{1,0:T(8,128)S(1)} %reshape.925) | copy-start | bytes 884740
  84.4 2.1 copy-start.4
  86.5 3.2 copy-start.19
  89.7 42.3 %copy-start.22 = (bf16[16,32,144]{2,1,0:T(8,128)(2,1)}, bf16[16,32,144]{2,1,0:T(8,128)(2,1)S(1)}, u32[]{:S(2)}) copy-start(bf16[16,32,144]{2,1,0:T(8,128)(2,1)S(1)} %convolution_convert_fusion.5) | copy-start | bytes 442372
  89.7 2.7 copy-start.32
  89.7 3.4 copy-start.42
  90.7 57.1 %collective-permute-start = (bf16[1,2,6,6,512]{4,3,2,1,0:T(8,128)(2,1)}, bf16[1,2,6,6,512]{4,3,2,1,0:T(8,128)(2,1)S(1)}, u32[]{:S(2)}, u32[]{:S(2)}) collective-permute-start(bf16[1,2,6,6,512]{4,3,2,1,0:T(8,128)(2,1)} %get-tuple-element.57), channel_id=1, source_target_pairs={{0,254},{2,0},{4,2},{6,4},{8,6},{10,8},{12,10},{14,12},{16,14},{18... | collective-permute-start | bytes 221192 | tf_op jit(solution)/shard_map/ppermute | solution.py:21
  132.0 12.9 copy-start.60
  132.0 16.4 %copy-start.36 = (bf16[1,2,6,6,512]{4,1,3,2,0:T(2,128)(2,1)S(1)}, bf16[1,2,6,6,512]{4,1,3,2,0:T(2,128)(2,1)}, u32[]{:S(2)}) copy-start(bf16[1,2,6,6,512]{4,1,3,2,0:T(2,128)(2,1)} %get-tuple-element.42) | copy-start | bytes 221188
  144.5 2.5 collective-permute-start.3
  147.9 3.6 copy-start.13
  147.9 3.6 collective-permute-start.1
  150.1 4.5 collective-permute-start.7
  154.0 12.0 copy-start.14
  154.0 12.0 copy-start.26
  154.0 12.0 copy-start.46
  157.4 13.0 copy-start.17
  162.3 3.0 copy-start.50
  167.7 6.4 copy-start.29
  174.2 2.9 copy-start.5
  177.0 8.4 copy-start.3
  177.0 4.7 copy-start.37
  177.0 4.7 copy-start.43
  187.0 2.1 copy-start.6
  189.1 1.0 copy-start.24
  189.6 1.8 copy-start.11
  189.6 1.8 copy-start.20
  189.6 2.7 copy-start.38
  190.0 2.6 copy-start.47
  190.0 2.6 copy-start.51
  190.0 2.6 copy-start.55
  190.0 2.6 copy-start.58
  192.3 2.2 copy-start.30
  202.0 128.1 %collective-permute-start.8 = (bf16[1,2,3,12,512]{4,3,2,1,0:T(8,128)(2,1)}, bf16[1,2,3,12,512]{4,3,2,1,0:T(8,128)(2,1)S(1)}, u32[]{:S(2)}, u32[]{:S(2)}) collective-permute-start(bf16[1,2,3,12,512]{4,3,2,1,0:T(8,128)(2,1)} %get-tuple-element.46), channel_id=1, source_target_pairs={{0,1},{1,0},{2,3},{3,2},{4,5},{5,4},{6,7},{7,6},{8,9},{9,8},{10,11... | collective-permute-start | bytes 221192 | tf_op jit(solution)/shard_map/ppermute | solution.py:21
  206.2 127.4 %collective-permute-start.4 = (bf16[1,2,3,12,512]{4,3,2,1,0:T(8,128)(2,1)}, bf16[1,2,3,12,512]{4,3,2,1,0:T(8,128)(2,1)S(1)}, u32[]{:S(2)}, u32[]{:S(2)}) collective-permute-start(bf16[1,2,3,12,512]{4,3,2,1,0:T(8,128)(2,1)} %get-tuple-element.50), channel_id=1, source_target_pairs={{0,1},{1,0},{2,3},{3,2},{4,5},{5,4},{6,7},{7,6},{8,9},{9,8},{10,11... | collective-permute-start | bytes 221192 | tf_op jit(solution)/shard_map/ppermute | solution.py:21
  216.7 119.6 %copy-start.21 = (bf16[2,512,512]{2,1,0:T(8,128)(2,1)S(1)}, bf16[2,512,512]{2,1,0:T(8,128)(2,1)}, u32[]{:S(2)}) copy-start(bf16[2,512,512]{2,1,0:T(8,128)(2,1)} %param.12) | copy-start | bytes 3145732
  216.7 120.0 %copy-start.23 = (bf16[16,32,144]{2,1,0:T(8,128)(2,1)S(1)}, bf16[16,32,144]{2,1,0:T(8,128)(2,1)}, u32[]{:S(2)}) copy-start(bf16[16,32,144]{2,1,0:T(8,128)(2,1)} %copy-done.22) | copy-start | bytes 442372
  330.1 4.3 copy-start.35
  330.1 5.1 collective-permute-start.9
  334.3 761.1 %collective-permute-start.5 = (bf16[1,2,6,6,512]{4,3,2,1,0:T(8,128)(2,1)}, bf16[1,2,6,6,512]{4,3,2,1,0:T(8,128)(2,1)}, u32[]{:S(2)}, u32[]{:S(2)}) collective-permute-start(bf16[1,2,6,6,512]{4,3,2,1,0:T(8,128)(2,1)} %fusion.52), channel_id=1, source_target_pairs={{0,2},{2,4},{4,6},{6,8},{8,10},{10,12},{12,14},{14,16},{16,18},{18... | collective-permute-start | bytes 221192 | tf_op jit(solution)/shard_map/ppermute | solution.py:21
  336.3 1.7 copy-start.15
  338.1 3.9 copy-start.1
  342.0 1.7 copy-start.2
  344.5 1.0 copy-start.10
  344.5 1.0 copy-start.45
  344.5 2.0 copy-start.59
  345.0 2.4 copy-start.28
  346.5 1.5 copy-start.7
  346.5 1.5 copy-start.8
  347.4 2.0 copy-start
  1093.0 2.4 copy-start.34
  1096.4 4.4 copy-start.56
  1096.4 87.1 %copy-start.16 = (bf16[144,512]{1,0:T(8,128)(2,1)S(1)}, bf16[144,512]{1,0:T(8,128)(2,1)}, u32[]{:S(2)}) copy-start(bf16[144,512]{1,0:T(8,128)(2,1)} %copy-done.15) | copy-start | bytes 442372
  1184.5 118.4 %copy-start.41 = (f32[1,16,759]{2,1,0:T(8,128)S(1)}, f32[1,16,759]{2,1,0:T(8,128)}, u32[]{:S(2)}) copy-start(f32[1,16,759]{2,1,0:T(8,128)} %copy.189) | copy-start | bytes 145732
  1184.5 118.4 %copy-start.57 = (f32[2]{0:T(128)S(1)}, f32[2]{0:T(128)}, u32[]{:S(2)}) copy-start(f32[2]{0:T(128)} %compare_convert_fusion) | copy-start | bytes 28
  (8 other events, 6.3 us)
Sparse Core Ops, SparseCore 0:
  1303.8 240.0 all-reduce.3
where the time goes:
time: 1560 us; the launch traced here: 1550 us
  blocking collectives  821 us (53%)
  other arithmetic  261 us (17%)
  waiting for transfers between devices  242 us (16%)
  local copies, waits for them, and re-layouts  156 us (10%)
  matrix products  37.6 us (2%)
  starting transfers between devices  19.9 us (1%)
  between operations  15.9 us (1%)
    unnamed x1, blocking collectives  733 us
    psum x1, waiting for transfers between devices, on_device(): gain_total, bias_total = lax.psum((gain_terms, placed), ('lon', 'lat'))  239 us
    scatter-add x2, other arithmetic, table_grad(): jax.ops.segment_sum(grad_bias.reshape(heads, -1).T, rel_ids.reshape(-1),...  225 us
    psum x1, blocking collectives, on_device(): gain_total, bias_total = lax.psum((gain_terms, placed), ('lon', 'lat'))  82 us
    gather x2, local copies, waits for them, and re-layouts, on_device(): bias_one = table_one[:, rel_ids]  50.4 us
    gather x2, local copies, waits for them, and re-layouts, on_device(): bias_zero = table_zero[:, rel_ids]  50.3 us
  transfers between devices with their start and end apart: 11, of which 5 were waited for; matrix products, arithmetic and copies ran while one was open for 18% of the time, Pallas kernels for 0%

commit v1 on v0

v1 whole, which is shorter than its diff:
```python
import functools

import jax
import jax.numpy as jnp
import numpy as np
from jax import lax
from jax.experimental import pallas as pl
from jax.experimental.pallas import tpu as pltpu
from jax.sharding import Mesh, PartitionSpec as P

F32 = jnp.float32
BF16 = jnp.bfloat16
EPSILON = 1e-05
NEGATIVE = -1e30
D = 512
HEADS = 16
NREL = 759
SCALE = 32 ** (-0.5)
AXES = ("yh", "x", "z", "c", "yl")
SIZES = (2, 4, 8, 2, 2)
VMEM = 56 << 20

QUADS = ((1, 1), (1, 0), (0, 1), (0, 0))


def _token(rh, ch, l, r, c):
    return (rh * 2 + ch) * 36 + l * 18 + r * 6 + c


def _tables():
    px = np.zeros((144, 192), np.float32)
    ps = np.zeros((192, 144), np.float32)
    pf = np.zeros((144, 192), np.float32)
    pm = np.zeros((144, 144), np.float32)
    rows = np.zeros((144, 12), np.float32)
    cols = np.zeros((144, 12), np.float32)
    flags = np.zeros((144, 2), np.float32)
    for l in range(2):
        for row in range(6):
            for col in range(12):
                rh, r, ch, c = row // 3, row % 3, col // 6, col % 6
                t = _token(rh, ch, l, r, c)
                px[t, 16 * (l * 6 + row) + col] = 1
                pm[t, l * 72 + row * 12 + col] = 1
                rows[t, l * 6 + row] = 1
                cols[t, col] = 1
                flags[t] = (l, rh)
                k = QUADS.index((rh, ch))
                ps[48 * k + (1 - l) * 18 + r * 6 + c, t] = 1
    for k in range(4):
        for i in range(36):
            pf[36 * k + i, 48 * k + i] = 1
    bf = jnp.bfloat16
    return {
        "px": px.astype(bf),
        "ps": ps.astype(bf),
        "pf": pf.astype(bf),
        "pft": pf.T.copy().astype(bf),
        "pst": ps.T.copy().astype(bf),
        "slab": (px.T @ ps.T).astype(bf),
        "slabt": px.T.copy().astype(bf),
        "pm": pm.astype(bf),
        "rows": rows.astype(bf),
        "cols": cols,
        "flags": flags,
    }


TABLES = _tables()


def dot(a, b):
    return lax.dot_general(a, b, (((1,), (0,)), ((), ())), preferred_element_type=F32)


def dot_nt(a, b):
    return lax.dot_general(a, b, (((1,), (1,)), ((), ())), preferred_element_type=F32)


def dot_tn(a, b):
    return lax.dot_general(a, b, (((0,), (0,)), ((), ())), preferred_element_type=F32)


def lane_masks():
    lane = lax.broadcasted_iota(jnp.int32, (1, 128), 1) >> 5
    return [jnp.where(lane == k, 1.0, 0.0).astype(F32) for k in range(4)]


def stack_heads(group, masks):
    return jnp.concatenate([group * m.astype(BF16) for m in masks], axis=0)


def fold_heads(stacked, masks):
    total = stacked[0:144] * masks[0]
    for k in range(1, 4):
        total = total + stacked[144 * k : 144 * (k + 1)] * masks[k]
    return total


def pad_keys(group):
    return jnp.concatenate([group, jnp.zeros((112, 128), BF16)], axis=0)


def normalize(x):
    center = x - jnp.mean(x, axis=-1, keepdims=True)
    rstd = lax.rsqrt(jnp.mean(center * center, axis=-1, keepdims=True) + EPSILON)
    return center * rstd, rstd


def place_table(tab, scr):
    scr[...] = jnp.full((HEADS, 768), NEGATIVE, F32)
    scr[:, 0:NREL] = tab


def gather_bias(scr, rel_lo, rel_hi, head):
    acc = None
    for k in range(6):
        row = jnp.broadcast_to(scr[head : head + 1, k * 128 : (k + 1) * 128], (144, 128))
        got = [jnp.take_along_axis(row, lo, axis=1) for lo in rel_lo]
        acc = got if k == 0 else [jnp.where(hi == k, g, a) for hi, g, a in zip(rel_hi, got, acc)]
    return jnp.concatenate(acc, axis=1)


def split_rel(rel_ref):
    tiles = [rel_ref[:, 0:128], rel_ref[:, 128:256]]
    return [t & 127 for t in tiles], [t >> 7 for t in tiles]


def group_probs(qkv_ref, g, masks, scr, rel_lo, rel_hi, allowed):
    qg = qkv_ref[:, 128 * g : 128 * (g + 1)]
    kg = pad_keys(qkv_ref[:, 512 + 128 * g : 512 + 128 * (g + 1)])
    q4 = stack_heads(qg, masks)
    s4 = dot_nt(q4, kg) * SCALE
    out = []
    for k in range(4):
        s = s4[144 * k : 144 * (k + 1)] + gather_bias(scr, rel_lo, rel_hi, 4 * g + k)
        if allowed is not None:
            s = jnp.where(allowed, s, NEGATIVE)
        e = jnp.exp(s - jnp.max(s, axis=-1, keepdims=True))
        out.append(e * (1.0 / jnp.sum(e, axis=-1, keepdims=True)))
    return q4, kg, jnp.concatenate(out, axis=0)


def group_back(g, q4, kg, vg, p4, p4b, do, masks, dqkv_ref, ds0_ref, ds1_ref):
    do4 = stack_heads(do[:, 128 * g : 128 * (g + 1)], masks)
    dp4 = dot_nt(do4, vg)
    dqkv_ref[:, 1024 + 128 * g : 1024 + 128 * (g + 1)] = dot_tn(p4b, do4)[0:144].astype(BF16)
    ds4 = p4 * (dp4 - jnp.sum(dp4 * p4, axis=-1, keepdims=True))
    ds0_ref[576 * g : 576 * (g + 1), :] = ds4[:, 0:128]
    ds1_ref[576 * g : 576 * (g + 1), :] = ds4[:, 128:256]
    ds4b = ds4.astype(BF16)
    dq = fold_heads(dot(ds4b, kg), masks) * SCALE
    dqkv_ref[:, 128 * g : 128 * (g + 1)] = dq.astype(BF16)
    dk = dot_tn(ds4b, q4)[0:144] * SCALE
    dqkv_ref[:, 512 + 128 * g : 512 + 128 * (g + 1)] = dk.astype(BF16)


def finish_back(dqkv_ref, wqkv_ref, n, rstd, gain, g32, dgain_ref):
    dh = dot_nt(dqkv_ref[...], wqkv_ref[0])
    dgain_ref[...] = jnp.sum(dh * n, axis=0, keepdims=True)
    dn = dh * gain
    return (
        rstd
        * (
            dn
            - jnp.mean(dn, axis=-1, keepdims=True)
            - n * jnp.mean(dn * n, axis=-1, keepdims=True)
        )
        + g32
    )


def weight_terms(idx_ref, h, o, dqkv, g, keep_ref, send_ref):
    core = idx_ref[0]
    p = lax.broadcasted_iota(jnp.int32, (256, 512), 0)
    row = lax.broadcasted_iota(jnp.int32, (256, 512), 1)
    base = ((p >> 5) << 6) + (((p >> 2) & 1) << 5) + (((p >> 3) & 1) << 4) + (((p >> 4) & 1) << 3)
    base = base + (p & 3)
    for which, ref in ((core, keep_ref), (1 - core, send_ref)):
        pick = jnp.where(row == base + which * 4, 1.0, 0.0).astype(BF16)
        ht = dot_nt(pick, h).astype(BF16)
        ot = dot_nt(pick, o).astype(BF16)
        ref[:, 0:1536] = dot(ht, dqkv).astype(BF16)
        ref[:, 1536:2048] = dot(ot, g).astype(BF16)


def first_kernel(
    idx_ref, x_ref, go_ref, grp_ref, gain_ref, wqkv_ref, wproj_ref, tab_ref, rel_ref,
    px_ref, ps_ref, pm_ref, rows_ref, cols_ref,
    own_ref, lon_ref, lat_ref, dia_ref, n_ref, rstd_ref, qkv_ref, p_ref, o_ref, relp_ref,
    slab, pay, tabs,
):
    masks = lane_masks()
    px = px_ref[...]
    slab[...] = jnp.zeros((192, 1024), BF16)
    for l in range(2):
        for r in range(6):
            at = 16 * (l * 6 + r)
            slab[at : at + 12, 0:512] = x_ref[0, l, r]
            slab[at : at + 12, 512:1024] = go_ref[0, l, r]
    both = dot(px, slab[...])
    x = both[:, 0:512]
    pay[:, 512:1024] = both[:, 512:1024].astype(BF16)
    grid = jnp.concatenate([grp_ref[0], grp_ref[1]], axis=0).astype(F32).astype(BF16)
    picked = dot(rows_ref[...], grid) * cols_ref[...]
    group = jnp.sum(picked, axis=-1, keepdims=True)
    pay[:, 1024:1152] = jnp.broadcast_to(group, (144, 128)).astype(BF16)

    rel = rel_ref[...]
    pm = pm_ref[...]
    parts = []
    for part in (rel >> 5, rel & 31):
        half = dot(pm, part.astype(F32).astype(BF16)).astype(BF16)
        parts.append(dot_nt(half, pm).astype(jnp.int32))
    relp_ref[...] = jnp.full((144, 256), 767, jnp.int32)
    relp_ref[:, 0:144] = parts[0] * 32 + parts[1]
    rel_lo, rel_hi = split_rel(relp_ref)

    n, rstd = normalize(x)
    n_ref[...] = n
    rstd_ref[...] = rstd
    h = (n * gain_ref[0:1, :]).astype(BF16)
    qkv_ref[...] = dot(h, wqkv_ref[0]).astype(BF16)
    place_table(tab_ref[0, idx_ref[1]], tabs)
    for g in range(4):
        _, _, p4 = group_probs(qkv_ref, g, masks, tabs, rel_lo, rel_hi, None)
        p4b = p4.astype(BF16)
        p_ref[576 * g : 576 * (g + 1), :] = p4b
        vg = pad_keys(qkv_ref[:, 1024 + 128 * g : 1024 + 128 * (g + 1)])
        o_ref[:, 128 * g : 128 * (g + 1)] = fold_heads(dot(p4b, vg), masks).astype(BF16)
    pay[:, 0:512] = (x + dot(o_ref[...], wproj_ref[0])).astype(BF16)
    out = dot(ps_ref[...], pay[...]).astype(BF16)
    own_ref[...] = out[0:48]
    lon_ref[...] = out[48:96]
    lat_ref[...] = out[96:144]
    dia_ref[...] = out[144:192]


def second_kernel(
    idx_ref, own_ref, lon_ref, lat_ref, dia_ref, gain_ref, wqkv_ref, wproj_ref, tab_ref, rel_ref,
    pf_ref, pft_ref, flags_ref,
    oown_ref, olon_ref, olat_ref, odia_ref, h_ref, o_ref, dqkv_ref, g_ref, dgain_ref, ds0_ref, ds1_ref,
    qkv_ref, tabs, back,
):
    masks = lane_masks()
    frame = dot(
        pf_ref[...], jnp.concatenate([own_ref[...], lon_ref[...], lat_ref[...], dia_ref[...]], axis=0)
    )
    x = frame[:, 0:512]
    g32 = frame[:, 512:1024]
    gb = g32.astype(BF16)
    g_ref[...] = gb
    lat = idx_ref[1].astype(F32)
    key = frame[:, 1024:1025] * 4.0 + flags_ref[:, 1:2] * (2.0 * lat) + flags_ref[:, 0:1]
    eye = lax.broadcasted_iota(jnp.int32, (144, 256), 0) == lax.broadcasted_iota(
        jnp.int32, (144, 256), 1
    )
    key_row = jnp.sum(jnp.where(eye, key, 0.0), axis=0, keepdims=True)
    allowed = key == key_row
    rel_lo, rel_hi = split_rel(rel_ref)
    gain = gain_ref[1:2, :]

    n, rstd = normalize(x)
    h = (n * gain).astype(BF16)
    h_ref[...] = h
    qkv_ref[...] = dot(h, wqkv_ref[0]).astype(BF16)
    do = dot_nt(gb, wproj_ref[0]).astype(BF16)
    place_table(tab_ref[0, idx_ref[1]], tabs)
    for g in range(4):
        q4, kg, p4 = group_probs(qkv_ref, g, masks, tabs, rel_lo, rel_hi, allowed)
        p4b = p4.astype(BF16)
        vg = pad_keys(qkv_ref[:, 1024 + 128 * g : 1024 + 128 * (g + 1)])
        o_ref[:, 128 * g : 128 * (g + 1)] = fold_heads(dot(p4b, vg), masks).astype(BF16)
        group_back(g, q4, kg, vg, p4, p4b, do, masks, dqkv_ref, ds0_ref, ds1_ref)
    back[:, 0:512] = (x + dot(o_ref[...], wproj_ref[0])).astype(BF16)
    df = finish_back(dqkv_ref, wqkv_ref, n, rstd, gain, g32, dgain_ref)
    back[:, 512:1024] = df.astype(BF16)
    out = dot(pft_ref[...], back[...]).astype(BF16)
    oown_ref[...] = out[0:48]
    olon_ref[...] = out[48:96]
    olat_ref[...] = out[96:144]
    odia_ref[...] = out[144:192]


def weights_kernel(idx_ref, h_ref, o_ref, dqkv_ref, g_ref, keep_ref, send_ref):
    weight_terms(idx_ref, h_ref[...], o_ref[...], dqkv_ref[...], g_ref[...], keep_ref, send_ref)


def third_kernel(
    idx_ref, own_ref, lon_ref, lat_ref, dia_ref, gain_ref, wqkv_ref, wproj_ref,
    n_ref, rstd_ref, qkv_ref, p_ref, o_ref, pst_ref, slab_ref, slabt_ref,
    out_ref, gin_ref, dgain_ref, ds0_ref, ds1_ref, keep_ref, send_ref,
    dqkv_ref,
):
    masks = lane_masks()
    pieces = jnp.concatenate([own_ref[...], lon_ref[...], lat_ref[...], dia_ref[...]], axis=0)
    out = dot(slab_ref[...], pieces[:, 0:512]).astype(BF16)
    g32 = dot(pst_ref[...], pieces[:, 512:1024])
    gb = g32.astype(BF16)
    gain = gain_ref[0:1, :]
    n = n_ref[...]
    do = dot_nt(gb, wproj_ref[0]).astype(BF16)
    for g in range(4):
        q4 = stack_heads(qkv_ref[:, 128 * g : 128 * (g + 1)], masks)
        kg = pad_keys(qkv_ref[:, 512 + 128 * g : 512 + 128 * (g + 1)])
        vg = pad_keys(qkv_ref[:, 1024 + 128 * g : 1024 + 128 * (g + 1)])
        p4b = p_ref[576 * g : 576 * (g + 1), :]
        group_back(g, q4, kg, vg, p4b.astype(F32), p4b, do, masks, dqkv_ref, ds0_ref, ds1_ref)
    df = finish_back(dqkv_ref, wqkv_ref, n, rstd_ref[...], gain, g32, dgain_ref)
    gin = dot(slabt_ref[...], df.astype(BF16)).astype(BF16)
    for l in range(2):
        for r in range(6):
            at = 16 * (l * 6 + r)
            out_ref[0, l, r] = out[at : at + 12]
            gin_ref[0, l, r] = gin[at : at + 12]
    h = (n * gain).astype(BF16)
    weight_terms(idx_ref, h, o_ref[...], dqkv_ref[...], gb, keep_ref, send_ref)


def scatter_kernel(idx_ref, rel_ref, d0_ref, d1_ref, dgain_ref, keep_ref, send_ref):
    iota = lax.broadcasted_iota(jnp.int32, (128, 256), 0)

    def body(i, acc):
        ids = rel_ref[pl.ds(i, 1), :]
        low, high = ids & 127, ids >> 7
        hot = jnp.where(iota == low, 1.0, 0.0).astype(BF16)
        d = jnp.concatenate(
            [d0_ref[pl.ds(i, 16, stride=144), :], d1_ref[pl.ds(i, 16, stride=144), :]], axis=1
        )
        lhs = jnp.concatenate([jnp.where(high == k, d, 0.0) for k in range(6)], axis=0)
        return acc + dot_nt(lhs.astype(BF16), hot)

    acc = lax.fori_loop(0, 144, body, jnp.zeros((96, 128), F32), unroll=8)
    table = jnp.concatenate([acc[16 * k : 16 * (k + 1)] for k in range(6)], axis=1)
    first = lax.broadcasted_iota(jnp.int32, (8, 256), 0) == 0
    halves = []
    for c in range(2):
        gain = jnp.where(first, dgain_ref[:, 256 * c : 256 * (c + 1)], 0.0)
        halves.append(jnp.concatenate([table[8 * c : 8 * (c + 1)], gain], axis=1))
    mine = idx_ref[0] == 0
    keep_ref[...] = jnp.where(mine, halves[0], halves[1])
    send_ref[...] = jnp.where(mine, halves[1], halves[0])


def payload_kernel(k0_ref, r0_ref, k1_ref, r1_ref, t0_ref, u0_ref, t1_ref, u1_ref, out_ref):
    tabs = [t0_ref[...] + u0_ref[...], t1_ref[...] + u1_ref[...]]
    for b, (k_ref, r_ref) in enumerate(((k0_ref, r0_ref), (k1_ref, r1_ref))):
        total = (k_ref[...].astype(F32) + r_ref[...].astype(F32)).astype(BF16)
        for half in range(2):
            out_ref[half, 32 * b : 32 * (b + 1), :] = total[:, 1024 * half : 1024 * (half + 1)]
    for half in range(2):
        rows = jnp.concatenate([tabs[half], jnp.zeros((8, 1024), F32)], axis=0)
        out_ref[half, 64:80, :] = rows.astype(BF16)


def plane_kernel(idx_ref, got_ref, keep_ref, tkeep_ref, send_ref):
    total = got_ref[0, 0:64, :].astype(F32)
    for s in range(1, 16):
        total = total + got_ref[s, 0:64, :].astype(F32)
    tabs = []
    for lat in range(2):
        t = got_ref[lat, 64:80, :].astype(F32)
        for s in range(1, 8):
            t = t + got_ref[2 * s + lat, 64:80, :].astype(F32)
        tabs.append(t[0:8])
    mine = idx_ref[2] == 0
    tab = jnp.concatenate(tabs, axis=0).astype(BF16)
    tkeep_ref[...] = tab
    send_ref[32:48, :] = tab
    for b in range(2):
        lo, hi = total[32 * b : 32 * b + 16], total[32 * b + 16 : 32 * b + 32]
        keep_ref[16 * b : 16 * (b + 1), :] = jnp.where(mine, lo, hi)
        send_ref[16 * b : 16 * (b + 1), :] = jnp.where(mine, hi, lo).astype(BF16)


def ring_kernel(step, idx_ref, keep_ref, tkeep_ref, got_ref, nkeep_ref, ntkeep_ref, send_ref):
    rows = keep_ref.shape[0]
    half = rows // 4
    mine = idx_ref[2 + step] == 0
    total = keep_ref[...] + got_ref[0:rows, :].astype(F32)
    tab = (tkeep_ref[...].astype(F32) + got_ref[32 if rows == 32 else 16 : (48 if rows == 32 else 32), :].astype(F32)).astype(BF16)
    ntkeep_ref[...] = tab
    keeps, sends = [], []
    for b in range(2):
        lo = total[2 * half * b : 2 * half * b + half]
        hi = total[2 * half * b + half : 2 * half * (b + 1)]
        keeps.append(jnp.where(mine, lo, hi))
        sends.append(jnp.where(mine, hi, lo))
    nkeep_ref[...] = jnp.concatenate(keeps, axis=0)
    send = jnp.concatenate(sends, axis=0)
    if half == 4:
        send = jnp.concatenate([send, jnp.zeros((8, 1024), F32)], axis=0)
    send_ref[0:16, :] = send.astype(BF16)
    send_ref[16:32, :] = tab


def last_ring_kernel(keep_ref, tkeep_ref, got_ref, tab_ref, send_ref):
    total = keep_ref[...] + got_ref[0:16, :].astype(F32)[0:8]
    tab = (tkeep_ref[...].astype(F32) + got_ref[16:32, :].astype(F32)).astype(BF16)
    tab_ref[...] = tab
    send_ref[16:32, :] = tab
    send_ref[0:16, :] = jnp.concatenate([total, jnp.zeros((8, 1024), F32)], axis=0).astype(BF16)


def last_kernel(
    factor, idx_ref, own_ref, lat_ref, core_ref, dia_ref, gain_ref, qkv_ref, proj_ref, bias_ref
):
    core0 = idx_ref[0] == 0
    lat0 = idx_ref[1] == 0
    own = own_ref[...].astype(F32)
    got = lat_ref[...].astype(F32)
    low = jnp.where(lat0, own[0:8], got[0:8]) * factor
    high = jnp.where(lat0, got[0:8], own[0:8]) * factor
    for b in range(2):
        qkv_ref[b, :, 0:1024] = low[4 * b : 4 * b + 4]
        qkv_ref[b, :, 1024:1536] = high[4 * b : 4 * b + 4, 0:512]
        proj_ref[b, :, :] = high[4 * b : 4 * b + 4, 512:1024]
    t_own, t_lat = own[16:32], got[16:32]
    t_core, t_dia = core_ref[...].astype(F32), dia_ref[...].astype(F32)
    for b in range(2):
        near = jnp.where(lat0, t_own, t_lat) if b == 0 else jnp.where(lat0, t_lat, t_own)
        far = jnp.where(lat0, t_core, t_dia) if b == 0 else jnp.where(lat0, t_dia, t_core)
        for c in range(2):
            tab = jnp.where(core0, near, far) if c == 0 else jnp.where(core0, far, near)
            tab = tab * factor
            for w in range(2):
                bias_ref[b, w, 8 * c : 8 * (c + 1), :] = tab[8 * w : 8 * w + 8, 0:NREL]
            gain_ref[b : b + 1, 256 * c : 256 * (c + 1)] = tab[0:1, 768:1024] + tab[8:9, 768:1024]


def _whole(shape):
    return pl.BlockSpec(shape, lambda *_: (0,) * len(shape))


SMEM = pl.BlockSpec(memory_space=pltpu.SMEM)


def call(body, outs, *args, specs=None, scratch=(), cost=None):
    specs = specs or {}
    in_specs = [SMEM if (i == 0 and a.dtype == jnp.int32 and a.ndim == 1) else specs.get(i, _whole(a.shape)) for i, a in enumerate(args)]
    return pl.pallas_call(
        body,
        grid=(1,),
        in_specs=in_specs,
        out_specs=[_whole(s) for s, _ in outs],
        out_shape=[jax.ShapeDtypeStruct(s, t) for s, t in outs],
        scratch_shapes=[pltpu.VMEM(s, t) for s, t in scratch],
        compiler_params=pltpu.CompilerParams(vmem_limit_bytes=VMEM),
        cost_estimate=cost,
    )(*args)


def _decode(s):
    out = []
    for n in reversed(SIZES):
        out.append(s % n)
        s //= n
    return tuple(reversed(out))


def _encode(place):
    s = 0
    for v, n in zip(place, SIZES):
        s = s * n + v
    return s


def permute(value, move):
    pairs = [(s, _encode(move(*_decode(s)))) for s in range(256)]
    return lax.ppermute(value, AXES, pairs)


def lon_step(offset, flip):
    def move(yh, x, z, c, yl):
        lon = (((yh * 4 + x) * 8 + z) * 2 + c + offset) % 128
        return (lon // 64, lon // 16 % 4, lon // 2 % 8, lon % 2, yl ^ flip)

    return move


def halo(pieces, offset):
    own, lon, lat, dia = pieces
    return (
        own,
        permute(lon, lon_step(offset, 0)),
        permute(lat, lon_step(0, 1)),
        permute(dia, lon_step(offset, 1)),
    )


def on_device(inputs, grad_out, gains, qkv_weight, proj_weight, bias_table, rel_ids, groups):
    T = {k: jnp.asarray(v) for k, v in TABLES.items()}
    z = lax.axis_index("z")
    idx = jnp.stack([lax.axis_index("c"), lax.axis_index("yl"), z & 1, (z >> 1) & 1, (z >> 2) & 1])
    idx = idx.astype(jnp.int32)

    def block(b, shape):
        return pl.BlockSpec((1,) + shape, lambda *_: (b,) + (0,) * len(shape))

    def weights(b, first):
        return {
            first: block(b, (D, 3 * D)),
            first + 1: block(b, (D, D)),
            first + 2: block(b, (2, HEADS, NREL)),
        }

    piece = ((48, 1152), BF16)
    own, lon, lat, dia, n0, rstd0, qkv0, p0, o0, relp = call(
        first_kernel,
        [piece] * 4
        + [
            ((144, D), F32),
            ((144, 1), F32),
            ((144, 3 * D), BF16),
            ((2304, 256), BF16),
            ((144, D), BF16),
            ((144, 256), jnp.int32),
        ],
        idx, inputs, grad_out, groups, gains, qkv_weight, proj_weight, bias_table, rel_ids,
        T["px"], T["ps"], T["pm"], T["rows"], T["cols"],
        specs=weights(0, 5),
        scratch=[((192, 1024), BF16), ((144, 1152), BF16), ((HEADS, 768), F32)],
    )
    pieces = halo((own, lon, lat, dia), -1)
    back = ((48, 1024), BF16)
    ds_shape = ((2304, 128), F32)
    own, lon, lat, dia, h1, o1, dqkv1, g1, dgain1, ds10, ds11 = call(
        second_kernel,
        [back] * 4
        + [
            ((144, D), BF16),
            ((144, D), BF16),
            ((144, 3 * D), BF16),
            ((144, D), BF16),
            ((1, D), F32),
            ds_shape,
            ds_shape,
        ],
        idx, *pieces, gains, qkv_weight, proj_weight, bias_table, relp, T["pf"], T["pft"], T["flags"],
        specs=weights(1, 6),
        scratch=[((144, 3 * D), BF16), ((HEADS, 768), F32), ((144, 2 * D), BF16)],
    )
    pieces = halo((own, lon, lat, dia), 1)
    wshape = ((256, 4 * D), BF16)
    keep1, send1 = call(weights_kernel, [wshape] * 2, idx, h1, o1, dqkv1, g1)
    other_core = lambda yh, x, z, c, yl: (yh, x, z, 1 - c, yl)
    recv1 = permute(send1, other_core)
    tshape = ((8, 1024), F32)
    tkeep1, tsend1 = call(scatter_kernel, [tshape] * 2, idx, relp, ds10, ds11, dgain1)
    trecv1 = permute(tsend1, other_core)
    outputs, grad_inputs, dgain0, ds00, ds01, keep0, send0 = call(
        third_kernel,
        [
            (inputs.shape, BF16),
            (inputs.shape, BF16),
            ((1, D), F32),
            ds_shape,
            ds_shape,
            wshape,
            wshape,
        ],
        idx, *pieces, gains, qkv_weight, proj_weight, n0, rstd0, qkv0, p0, o0,
        T["pst"], T["slab"], T["slabt"],
        specs={6: block(0, (D, 3 * D)), 7: block(0, (D, D))},
        scratch=[((144, 3 * D), BF16)],
    )
    recv0 = permute(send0, other_core)
    tkeep0, tsend0 = call(scatter_kernel, [tshape] * 2, idx, relp, ds00, ds01, dgain0)
    trecv0 = permute(tsend0, other_core)

    wspec = pl.BlockSpec((32, 4 * D), lambda i: (i, 0))
    tspec = pl.BlockSpec((8, 1024), lambda i: (0, 0))
    payload = pl.pallas_call(
        payload_kernel,
        grid=(8,),
        in_specs=[wspec] * 4 + [tspec] * 4,
        out_specs=pl.BlockSpec((2, 80, 1024), lambda i: (i, 0, 0)),
        out_shape=jax.ShapeDtypeStruct((16, 80, 1024), BF16),
        compiler_params=pltpu.CompilerParams(vmem_limit_bytes=VMEM),
    )(keep0, recv0, keep1, recv1, tkeep0, trecv0, tkeep1, trecv1)
    got = lax.all_to_all(payload, ("yh", "x", "yl"), 0, 0, tiled=True)
    tab16 = ((16, 1024), BF16)
    keep, tab, send = call(
        plane_kernel, [((32, 1024), F32), tab16, ((48, 1024), BF16)], idx, got
    )
    got = permute(send, lambda yh, x, z, c, yl: (yh, x, z ^ 1, c, yl))
    pair = ((32, 1024), BF16)
    keep, tab, send = call(
        functools.partial(ring_kernel, 1), [((16, 1024), F32), tab16, pair], idx, keep, tab, got
    )
    got = permute(send, lambda yh, x, z, c, yl: (yh, x, z ^ 2, c, yl))
    keep, tab, send = call(
        functools.partial(ring_kernel, 2), [((8, 1024), F32), tab16, pair], idx, keep, tab, got
    )
    got = permute(send, lambda yh, x, z, c, yl: (yh, x, z ^ 4, c, yl))
    tab, own = call(last_ring_kernel, [tab16, pair], keep, tab, got)
    from_core = permute(tab, other_core)
    from_dia = permute(tab, lambda yh, x, z, c, yl: (yh, x, z, 1 - c, 1 - yl))
    from_lat = permute(own, lambda yh, x, z, c, yl: (yh, x, z, c, 1 - yl))
    factor = 36864 ** (-0.5)
    grad_gains, grad_qkv, grad_proj, grad_bias = call(
        functools.partial(last_kernel, factor),
        [
            ((2, D), F32),
            ((2, 4, 3 * D), F32),
            ((2, 4, D), F32),
            ((2, 2, HEADS, NREL), F32),
        ],
        idx, own, from_lat, from_core, from_dia,
    )
    return (outputs, grad_inputs, grad_gains, grad_qkv, grad_proj, grad_bias)


def solution(mesh):
    fine = Mesh(mesh.devices.reshape(SIZES), AXES)
    lon = ("yh", "x", "z", "c")
    field = P(None, None, "yl", lon, None)
    rows = P(None, lon, None)
    return jax.shard_map(
        on_device,
        mesh=fine,
        in_specs=(field, field, P(), P(), P(), P(), P(), P(None, "yl", lon)),
        out_specs=(field, field, P(), rows, rows, P()),
        check_vma=False,
    )
```

time: 1560 us -> 180 us (0.12)
  blocking collectives: 821 us -> 38 us
  other arithmetic: 261 us -> 0 us
  waiting for transfers between devices: 242 us -> 21.3 us
  local copies, waits for them, and re-layouts: 156 us -> 12.6 us
  Pallas kernels: 0 us -> 78.2 us
  matrix products: 37.6 us -> 0 us
    unnamed x1 -> x0, blocking collectives: 733 us -> none
    psum x1 -> x0, waiting for transfers between devices: 239 us -> none  [on_device(): gain_total, bias_total = lax.psum((gain_terms, placed), ('lon', 'lat'))]
    scatter-add x2 -> x0, other arithmetic: 225 us -> none  [table_grad(): jax.ops.segment_sum(grad_bias.reshape(heads, -1).T, rel_ids.reshape(-1),...]
    gather x4 -> x0, local copies, waits for them, and re-layouts: 101 us -> none  [the longest x2 50.4 us: on_device(): bias_one = table_one[:, rel_ids]]
    psum x2 -> x0, blocking collectives: 88.1 us -> none  [the longest x1 82 us: on_device(): gain_total, bias_total = lax.psum((gain_terms, placed), ('lon', 'lat'))]
    pallas_call x0 -> x12, Pallas kernels: none -> 78.2 us  [the longest x11 71.7 us: call(): pl.pallas_call(body, grid=(1,), in_specs=in_specs, out_specs=[_whole(s) f...]
    all_to_all x0 -> x1, blocking collectives: none -> 38 us  [on_device(): got = lax.all_to_all(payload, ('yh', 'x', 'yl'), 0, 0, tiled=True)]
    dot_general x24 -> x0, matrix products: 37.6 us -> none  [the longest x2 7.83 us: attend_forward(): jnp.einsum('whqk,wkhc->wqhc', probs_low, values_part, preferred_element_t...]
  transfers between devices with their start and end apart: 11 -> 16, of which waited for: 5 -> 7; matrix products, arithmetic and copies ran while one was open for 18% -> 1% of each run, Pallas kernels for 0% -> 15%
where the time goes in v1:
time: 180 us
  Pallas kernels  78.2 us (43%)
  blocking collectives  38 us (21%)
  starting transfers between devices  28.8 us (16%)
  waiting for transfers between devices  21.3 us (12%)
  local copies, waits for them, and re-layouts  12.6 us (7%)
    pallas_call x11, Pallas kernels, call(): pl.pallas_call(body, grid=(1,), in_specs=in_specs, out_specs=[_whole(s) f...  71.7 us
    all_to_all x1, blocking collectives, on_device(): got = lax.all_to_all(payload, ('yh', 'x', 'yl'), 0, 0, tiled=True)  38 us
    ppermute x16, starting transfers between devices, permute(): return lax.ppermute(value, AXES, pairs)  28.8 us
    ppermute x16, waiting for transfers between devices, permute(): return lax.ppermute(value, AXES, pairs)  21.3 us
    unnamed x41, local copies, waits for them, and re-layouts  11.9 us
    pallas_call x1, Pallas kernels, on_device(): pl.pallas_call(payload_kernel, grid=(8,), in_specs=[wspec] * 4 + [tspec]...  6.47 us
  transfers between devices with their start and end apart: 16, of which 7 were waited for; matrix products, arithmetic and copies ran while one was open for 1% of the time, Pallas kernels for 15%

profile of v1, /device:TPU:1, one launch (start us, length us, event | category | flops | bytes accessed | tf_op | source)
XLA Modules:
  0.0 179.7 jit_solution(7917451100582174964)
XLA Ops:
  0.6 1.6 copy.25.x_ref
  2.3 1.6 copy.26.go_ref
  3.9 1.3 copy.27.grp_ref
  5.2 0.7 stack.23.idx_ref
  5.8 16.8 %shard_map.226 = (bf16[48,1152]{1,0:T(8,128)(2,1)}, bf16[48,1152]{1,0:T(8,128)(2,1)}, bf16[48,1152]{1,0:T(8,128)(2,1)}, bf16[48,1152]{1,0:T(8,128)(2,1)}, f32[14...) custom-call(s32[5]{0:T(128)} %stack.23.idx_ref, ...), custom_call_target="tpu_custom_call" | custom-call | tf_op jit(solution)/shard_map/pallas_call | solution.py:441
  22.6 3.3 %collective-permute-start = (bf16[48,1152]{1,0:T(8,128)(2,1)}, bf16[48,1152]{1,0:T(8,128)(2,1)S(1)}, u32[]{:S(2)}, u32[]{:S(2)}) collective-permute-start(bf16[48,1152]{1,0:T(8,128)(2,1)} %get-tuple-element.56), channel_id=1, source_target_pairs={{0,254},{1,255},{2,0},{3,1},{4,2},{5,3},{6,4},{7,5},{8,6},{9,7},{1... | collective-permute-start | bytes 331784 | tf_op jit(solution)/shard_map/ppermute | solution.py:470
  25.9 0.0 collective-permute-start.1
  25.9 10.0 %collective-permute-start.2 = (bf16[48,1152]{1,0:T(8,128)(2,1)}, bf16[48,1152]{1,0:T(8,128)(2,1)S(1)}, u32[]{:S(2)}, u32[]{:S(2)}) collective-permute-start(bf16[48,1152]{1,0:T(8,128)(2,1)} %get-tuple-element.58), channel_id=1, source_target_pairs={{0,255},{1,254},{2,1},{3,0},{4,3},{5,2},{6,5},{7,4},{8,7},{9,6},{1... | collective-permute-start | bytes 331784 | tf_op jit(solution)/shard_map/ppermute | solution.py:470
  36.0 0.0 collective-permute-done.lon_ref
  36.0 0.0 collective-permute-done.1.lat_ref
  36.0 0.0 copy-start.5
  36.0 2.4 %collective-permute-done.2.dia_ref = bf16[48,1152]{1,0:T(8,128)(2,1)S(1)} collective-permute-done((bf16[48,1152]{1,0:T(8,128)(2,1)}, bf16[48,1152]{1,0:T(8,128)(2,1)S(1)}, u32[]{:S(2)}, u32[]{:S(2)}) %collective-permute-start.2) | collective-permute-done | bytes 110624 | tf_op jit(solution)/shard_map/ppermute | solution.py:470
  38.4 0.0 copy-done.4
  38.4 0.6 copy-done.6
  39.0 18.6 %shard_map.227 = (bf16[48,1024]{1,0:T(8,128)(2,1)}, bf16[48,1024]{1,0:T(8,128)(2,1)}, bf16[48,1024]{1,0:T(8,128)(2,1)}, bf16[48,1024]{1,0:T(8,128)(2,1)}, bf16[1...) custom-call(s32[5]{0:T(128)} %stack.23.idx_ref, ...), custom_call_target="tpu_custom_call" | custom-call | tf_op jit(solution)/shard_map/pallas_call | solution.py:441
  57.7 0.1 collective-permute-start.3
  57.8 1.2 collective-permute-start.4
  58.9 0.0 collective-permute-start.5
  58.9 3.4 %shard_map.229 = (bf16[256,2048]{1,0:T(8,128)(2,1)}, bf16[256,2048]{1,0:T(8,128)(2,1)}) custom-call(s32[5]{0:T(128)} %stack.23.idx_ref, bf16[144,512]{1,0:T(8,128)(2,1)} %get-tuple-element.73.h_ref, bf16[144,512]{1,0:T(8,128)(2,1)} %get-tuple-element.74.o_ref, bf16[144,1536]{1,0:T(8,128)(2,1)} %get-tuple-element.75.dqkv_ref, ...), custom_call_target="tpu_custom_call" | custom-call | tf_op jit(solution)/shard_map/pallas_call | solution.py:441
  62.3 1.7 collective-permute-start.7
  64.0 0.0 collective-permute-done.3.lon_ref
  64.0 0.0 collective-permute-done.4.lat_ref
  64.0 1.1 collective-permute-done.5.dia_ref
  65.1 0.6 copy-done.10
  65.8 7.6 %shard_map.228 = (bf16[1,2,6,12,512]{4,3,2,1,0:T(8,128)(2,1)}, bf16[1,2,6,12,512]{4,3,2,1,0:T(8,128)(2,1)}, f32[1,512]{1,0:T(1,128)}, f32[2304,128]{1,0:T(8,128)...) custom-call(s32[5]{0:T(128)} %stack.23.idx_ref, ...), custom_call_target="tpu_custom_call" | custom-call | tf_op jit(solution)/shard_map/pallas_call | solution.py:441
  73.4 5.7 %collective-permute-start.6 = (bf16[256,2048]{1,0:T(8,128)(2,1)}, bf16[256,2048]{1,0:T(8,128)(2,1)S(1)}, u32[]{:S(2)}, u32[]{:S(2)}) collective-permute-start(bf16[256,2048]{1,0:T(8,128)(2,1)} %get-tuple-element.72), channel_id=1, source_target_pairs={{0,2},{1,3},{2,0},{3,1},{4,6},{5,7},{6,4},{7,5},{8,10},{9,11},{10,... | collective-permute-start | bytes 3145736 | tf_op jit(solution)/shard_map/ppermute | solution.py:470
  79.1 8.1 %shard_map.231 = (f32[8,1024]{1,0:T(8,128)}, f32[8,1024]{1,0:T(8,128)}) custom-call(s32[5]{0:T(128)} %stack.23.idx_ref, s32[144,256]{1,0:T(8,128)} %get-tuple-element.59.rel_ref, f32[2304,128]{1,0:T(8,128)} %get-tuple-element.84.d0_ref, f32[2304,128]{1,0:T(8,128)} %get-tuple-element.85.d1_ref, f32[1,512]{1,0:T(1,128)} %get-tuple-element.86.dgain_ref), custom_call_target="tpu_custom_call" | custom-call | tf_op jit(solution)/shard_map/pallas_call | solution.py:441
  87.2 0.0 collective-permute-start.9
  87.2 8.1 %shard_map.230 = (f32[8,1024]{1,0:T(8,128)}, f32[8,1024]{1,0:T(8,128)}) custom-call(s32[5]{0:T(128)} %stack.23.idx_ref, s32[144,256]{1,0:T(8,128)} %get-tuple-element.59.rel_ref, f32[2304,128]{1,0:T(8,128)} %get-tuple-element.79.d0_ref, f32[2304,128]{1,0:T(8,128)} %get-tuple-element.80.d1_ref, f32[1,512]{1,0:T(1,128)} %get-tuple-element.81.dgain_ref), custom_call_target="tpu_custom_call" | custom-call | tf_op jit(solution)/shard_map/pallas_call | solution.py:441
  95.3 0.5 collective-permute-start.8
  95.8 0.0 collective-permute-done.9.u1_ref
  95.8 1.1 collective-permute-done.8.u0_ref
  96.8 0.0 collective-permute-done.7.r1_ref
  96.8 0.0 collective-permute-done.6.r0_ref
  96.9 0.6 copy-done.15
  97.4 0.4 copy-done
  97.9 0.3 copy-done.1
  98.2 6.5 %shard_map.232 = bf16[16,80,1024]{2,1,0:T(8,128)(2,1)} custom-call(bf16[256,2048]{1,0:T(8,128)(2,1)} %get-tuple-element.71.k0_ref, bf16[256,2048]{1,0:T(8,128)(2,1)} %copy-done.1, bf16[256,2048]{1,0:T(8,128)(2,1)} %get-tuple-element.77.k1_ref, bf16[256,2048]{1,0:T(8,128)(2,1)} %copy-done, f32[8,1024]{1,0:T(8,128)} %get-tuple-element.82.t0_ref, ...), custom_call_target="tpu_custom_call" | custom-call | tf_op jit(solution)/shard_map/pallas_call | solution.py:573
  104.7 38.0 %all_to_all.5.got_ref = bf16[16,80,1024]{2,1,0:T(8,128)(2,1)} all-to-all(bf16[16,80,1024]{2,1,0:T(8,128)(2,1)} %shard_map.232), channel_id=1, replica_groups=mesh['yh'=2,'x'=4,'z'=8,'c'=2,'yl'=2] {'yh','x','yl'}, dimensions={0} | all-to-all | bytes 5242880 | tf_op jit(solution)/shard_map/all_to_all | solution.py:581
  142.6 2.8 %shard_map.233 = (f32[32,1024]{1,0:T(8,128)}, bf16[16,1024]{1,0:T(8,128)(2,1)}, bf16[48,1024]{1,0:T(8,128)(2,1)}) custom-call(s32[5]{0:T(128)} %stack.23.idx_ref, bf16[16,80,1024]{2,1,0:T(8,128)(2,1)} %all_to_all.5.got_ref), custom_call_target="tpu_custom_call" | custom-call | tf_op jit(solution)/shard_map/pallas_call | solution.py:441
  145.4 0.0 collective-permute-start.10
  145.4 3.7 %collective-permute-done.10.got_ref = bf16[48,1024]{1,0:T(8,128)(2,1)S(1)} collective-permute-done((bf16[48,1024]{1,0:T(8,128)(2,1)}, bf16[48,1024]{1,0:T(8,128)(2,1)S(1)}, u32[]{:S(2)}, u32[]{:S(2)}) %collective-permute-start.10) | collective-permute-done | bytes 98336 | tf_op jit(solution)/shard_map/ppermute | solution.py:470
  149.1 0.6 copy-done.7
  149.8 1.7 shard_map.234
  151.4 0.0 collective-permute-start.11
  151.4 4.6 %collective-permute-done.11.got_ref = bf16[32,1024]{1,0:T(8,128)(2,1)S(1)} collective-permute-done((bf16[32,1024]{1,0:T(8,128)(2,1)}, bf16[32,1024]{1,0:T(8,128)(2,1)S(1)}, u32[]{:S(2)}, u32[]{:S(2)}) %collective-permute-start.11) | collective-permute-done | bytes 65568 | tf_op jit(solution)/shard_map/ppermute | solution.py:470
  156.1 0.6 copy-done.12
  156.7 1.6 shard_map.235
  158.3 0.0 collective-permute-start.12
  158.3 7.2 %collective-permute-done.12.got_ref = bf16[32,1024]{1,0:T(8,128)(2,1)S(1)} collective-permute-done((bf16[32,1024]{1,0:T(8,128)(2,1)}, bf16[32,1024]{1,0:T(8,128)(2,1)S(1)}, u32[]{:S(2)}, u32[]{:S(2)}) %collective-permute-start.12) | collective-permute-done | bytes 65568 | tf_op jit(solution)/shard_map/ppermute | solution.py:470
  165.5 0.6 copy-done.13
  166.1 1.5 shard_map.236
  167.7 0.3 collective-permute-start.13
  168.0 4.9 %collective-permute-start.14 = (bf16[16,1024]{1,0:T(8,128)(2,1)}, bf16[16,1024]{1,0:T(8,128)(2,1)S(1)}, u32[]{:S(2)}, u32[]{:S(2)}) collective-permute-start(bf16[16,1024]{1,0:T(8,128)(2,1)} %get-tuple-element.99), channel_id=1, source_target_pairs={{0,2},{1,3},{2,0},{3,1},{4,6},{5,7},{6,4},{7,5},{8,10},{9,11},{10,... | collective-permute-start | bytes 98312 | tf_op jit(solution)/shard_map/ppermute | solution.py:470
  172.9 1.1 collective-permute-start.15
  173.9 0.0 copy-done.3
  173.9 0.8 copy.28
  174.8 0.8 copy.29
  175.6 0.0 collective-permute-done.14.core_ref
  175.6 1.2 collective-permute-done.15.dia_ref
  176.8 0.0 collective-permute-done.13.lat_ref
  176.8 0.6 copy-done.17
  177.4 0.6 copy-done.11
  178.0 1.6 shard_map.237
  (23 shorter events, 0.0 us)
Async XLA Ops:
  22.6 13.4 %collective-permute-start = (bf16[48,1152]{1,0:T(8,128)(2,1)}, bf16[48,1152]{1,0:T(8,128)(2,1)S(1)}, u32[]{:S(2)}, u32[]{:S(2)}) collective-permute-start(bf16[48,1152]{1,0:T(8,128)(2,1)} %get-tuple-element.56), channel_id=1, source_target_pairs={{0,254},{1,255},{2,0},{3,1},{4,2},{5,3},{6,4},{7,5},{8,6},{9,7},{1... | collective-permute-start | bytes 331784 | tf_op jit(solution)/shard_map/ppermute | solution.py:470
  25.9 10.1 %collective-permute-start.1 = (bf16[48,1152]{1,0:T(8,128)(2,1)}, bf16[48,1152]{1,0:T(8,128)(2,1)S(1)}, u32[]{:S(2)}, u32[]{:S(2)}) collective-permute-start(bf16[48,1152]{1,0:T(8,128)(2,1)} %get-tuple-element.57), channel_id=1, source_target_pairs={{0,1},{1,0},{2,3},{3,2},{4,5},{5,4},{6,7},{7,6},{8,9},{9,8},{10,11... | collective-permute-start | bytes 331784 | tf_op jit(solution)/shard_map/ppermute | solution.py:470
  25.9 12.5 %collective-permute-start.2 = (bf16[48,1152]{1,0:T(8,128)(2,1)}, bf16[48,1152]{1,0:T(8,128)(2,1)S(1)}, u32[]{:S(2)}, u32[]{:S(2)}) collective-permute-start(bf16[48,1152]{1,0:T(8,128)(2,1)} %get-tuple-element.58), channel_id=1, source_target_pairs={{0,255},{1,254},{2,1},{3,0},{4,3},{5,2},{6,5},{7,4},{8,7},{9,6},{1... | collective-permute-start | bytes 331784 | tf_op jit(solution)/shard_map/ppermute | solution.py:470
  36.0 2.4 %copy-start.4 = (bf16[48,1152]{1,0:T(8,128)(2,1)}, bf16[48,1152]{1,0:T(8,128)(2,1)S(1)}, u32[]{:S(2)}) copy-start(bf16[48,1152]{1,0:T(8,128)(2,1)S(1)} %collective-permute-done.lon_ref) | copy-start | bytes 331780
  36.0 2.4 %copy-start.5 = (bf16[48,1152]{1,0:T(8,128)(2,1)}, bf16[48,1152]{1,0:T(8,128)(2,1)S(1)}, u32[]{:S(2)}) copy-start(bf16[48,1152]{1,0:T(8,128)(2,1)S(1)} %collective-permute-done.1.lat_ref) | copy-start | bytes 331780
  38.4 0.6 copy-start.6
  57.7 6.3 %collective-permute-start.3 = (bf16[48,1024]{1,0:T(8,128)(2,1)}, bf16[48,1024]{1,0:T(8,128)(2,1)S(1)}, u32[]{:S(2)}, u32[]{:S(2)}) collective-permute-start(bf16[48,1024]{1,0:T(8,128)(2,1)} %get-tuple-element.61), channel_id=1, source_target_pairs={{0,2},{1,3},{2,4},{3,5},{4,6},{5,7},{6,8},{7,9},{8,10},{9,11},{10,... | collective-permute-start | bytes 294920 | tf_op jit(solution)/shard_map/ppermute | solution.py:470
  57.8 6.3 %collective-permute-start.4 = (bf16[48,1024]{1,0:T(8,128)(2,1)}, bf16[48,1024]{1,0:T(8,128)(2,1)S(1)}, u32[]{:S(2)}, u32[]{:S(2)}) collective-permute-start(bf16[48,1024]{1,0:T(8,128)(2,1)} %get-tuple-element.62), channel_id=1, source_target_pairs={{0,1},{1,0},{2,3},{3,2},{4,5},{5,4},{6,7},{7,6},{8,9},{9,8},{10,11... | collective-permute-start | bytes 294920 | tf_op jit(solution)/shard_map/ppermute | solution.py:470
  58.9 6.2 %collective-permute-start.5 = (bf16[48,1024]{1,0:T(8,128)(2,1)}, bf16[48,1024]{1,0:T(8,128)(2,1)S(1)}, u32[]{:S(2)}, u32[]{:S(2)}) collective-permute-start(bf16[48,1024]{1,0:T(8,128)(2,1)} %get-tuple-element.63), channel_id=1, source_target_pairs={{0,3},{1,2},{2,5},{3,4},{4,7},{5,6},{6,9},{7,8},{8,11},{9,10},{10,... | collective-permute-start | bytes 294920 | tf_op jit(solution)/shard_map/ppermute | solution.py:470
  62.3 34.5 %collective-permute-start.7 = (bf16[256,2048]{1,0:T(8,128)(2,1)}, bf16[256,2048]{1,0:T(8,128)(2,1)S(1)}, u32[]{:S(2)}, u32[]{:S(2)}) collective-permute-start(bf16[256,2048]{1,0:T(8,128)(2,1)} %get-tuple-element.78), channel_id=1, source_target_pairs={{0,2},{1,3},{2,0},{3,1},{4,6},{5,7},{6,4},{7,5},{8,10},{9,11},{10,... | collective-permute-start | bytes 3145736 | tf_op jit(solution)/shard_map/ppermute | solution.py:470
  64.0 1.1 copy-start.8
  64.0 1.1 copy-start.9
  65.1 0.6 copy-start.10
  73.4 23.4 %collective-permute-start.6 = (bf16[256,2048]{1,0:T(8,128)(2,1)}, bf16[256,2048]{1,0:T(8,128)(2,1)S(1)}, u32[]{:S(2)}, u32[]{:S(2)}) collective-permute-start(bf16[256,2048]{1,0:T(8,128)(2,1)} %get-tuple-element.72), channel_id=1, source_target_pairs={{0,2},{1,3},{2,0},{3,1},{4,6},{5,7},{6,4},{7,5},{8,10},{9,11},{10,... | collective-permute-start | bytes 3145736 | tf_op jit(solution)/shard_map/ppermute | solution.py:470
  87.2 8.6 %collective-permute-start.9 = (f32[8,1024]{1,0:T(8,128)}, f32[8,1024]{1,0:T(8,128)S(1)}, u32[]{:S(2)}, u32[]{:S(2)}) collective-permute-start(f32[8,1024]{1,0:T(8,128)} %get-tuple-element.88), channel_id=1, source_target_pairs={{0,2},{1,3},{2,0},{3,1},{4,6},{5,7},{6,4},{7,5},{8,10},{9,11},{10,... | collective-permute-start | bytes 98312 | tf_op jit(solution)/shard_map/ppermute | solution.py:470
  95.3 1.6 collective-permute-start.8
  95.8 1.1 copy-start.14
  96.8 0.6 copy-start.15
  96.8 1.0 copy-start
  96.8 1.3 copy-start.1
  142.6 31.3 %copy-start.3 = (bf16[1,2,6,12,512]{4,3,2,1,0:T(8,128)(2,1)S(1)}, bf16[1,2,6,12,512]{4,3,2,1,0:T(8,128)(2,1)}, u32[]{:S(2)}) copy-start(bf16[1,2,6,12,512]{4,3,2,1,0:T(8,128)(2,1)} %get-tuple-element.104) | copy-start | bytes 442372
  142.6 32.1 %copy-start.2 = (bf16[1,2,6,12,512]{4,3,2,1,0:T(8,128)(2,1)S(1)}, bf16[1,2,6,12,512]{4,3,2,1,0:T(8,128)(2,1)}, u32[]{:S(2)}) copy-start(bf16[1,2,6,12,512]{4,3,2,1,0:T(8,128)(2,1)} %get-tuple-element.105) | copy-start | bytes 442372
  145.4 3.7 %collective-permute-start.10 = (bf16[48,1024]{1,0:T(8,128)(2,1)}, bf16[48,1024]{1,0:T(8,128)(2,1)S(1)}, u32[]{:S(2)}, u32[]{:S(2)}) collective-permute-start(bf16[48,1024]{1,0:T(8,128)(2,1)} %get-tuple-element.91), channel_id=1, source_target_pairs={{0,4},{1,5},{2,6},{3,7},{4,0},{5,1},{6,2},{7,3},{8,12},{9,13},{10,... | collective-permute-start | bytes 294920 | tf_op jit(solution)/shard_map/ppermute | solution.py:470
  149.1 0.6 copy-start.7
  151.4 4.6 %collective-permute-start.11 = (bf16[32,1024]{1,0:T(8,128)(2,1)}, bf16[32,1024]{1,0:T(8,128)(2,1)S(1)}, u32[]{:S(2)}, u32[]{:S(2)}) collective-permute-start(bf16[32,1024]{1,0:T(8,128)(2,1)} %get-tuple-element.94), channel_id=1, source_target_pairs={{0,8},{1,9},{2,10},{3,11},{4,12},{5,13},{6,14},{7,15},{8,0},{9,1},... | collective-permute-start | bytes 196616 | tf_op jit(solution)/shard_map/ppermute | solution.py:470
  156.1 0.6 copy-start.12
  158.3 7.2 %collective-permute-start.12 = (bf16[32,1024]{1,0:T(8,128)(2,1)}, bf16[32,1024]{1,0:T(8,128)(2,1)S(1)}, u32[]{:S(2)}, u32[]{:S(2)}) collective-permute-start(bf16[32,1024]{1,0:T(8,128)(2,1)} %get-tuple-element.97), channel_id=1, source_target_pairs={{0,16},{1,17},{2,18},{3,19},{4,20},{5,21},{6,22},{7,23},{8,24},{9,... | collective-permute-start | bytes 196616 | tf_op jit(solution)/shard_map/ppermute | solution.py:470
  165.5 0.6 copy-start.13
  167.7 9.1 %collective-permute-start.13 = (bf16[32,1024]{1,0:T(8,128)(2,1)}, bf16[32,1024]{1,0:T(8,128)(2,1)S(1)}, u32[]{:S(2)}, u32[]{:S(2)}) collective-permute-start(bf16[32,1024]{1,0:T(8,128)(2,1)} %get-tuple-element.98.own_ref), channel_id=1, source_target_pairs={{0,1},{1,0},{2,3},{3,2},{4,5},{5,4},{6,7},{7,6},{8,9},{9,8},{10,11... | collective-permute-start | bytes 196616 | tf_op jit(solution)/shard_map/ppermute | solution.py:470
  168.0 7.6 %collective-permute-start.14 = (bf16[16,1024]{1,0:T(8,128)(2,1)}, bf16[16,1024]{1,0:T(8,128)(2,1)S(1)}, u32[]{:S(2)}, u32[]{:S(2)}) collective-permute-start(bf16[16,1024]{1,0:T(8,128)(2,1)} %get-tuple-element.99), channel_id=1, source_target_pairs={{0,2},{1,3},{2,0},{3,1},{4,6},{5,7},{6,4},{7,5},{8,10},{9,11},{10,... | collective-permute-start | bytes 98312 | tf_op jit(solution)/shard_map/ppermute | solution.py:470
  172.9 3.9 %collective-permute-start.15 = (bf16[16,1024]{1,0:T(8,128)(2,1)}, bf16[16,1024]{1,0:T(8,128)(2,1)S(1)}, u32[]{:S(2)}, u32[]{:S(2)}) collective-permute-start(bf16[16,1024]{1,0:T(8,128)(2,1)} %get-tuple-element.99), channel_id=1, source_target_pairs={{0,3},{1,2},{2,1},{3,0},{4,7},{5,6},{6,5},{7,4},{8,11},{9,10},{10,... | collective-permute-start | bytes 98312 | tf_op jit(solution)/shard_map/ppermute | solution.py:470
  175.6 1.2 copy-start.16
  176.8 0.6 copy-start.17
  177.4 0.6 copy-start.11

commit v2 on v1

v2 whole, which is shorter than its diff:
```python
import functools

import jax
import jax.numpy as jnp
import numpy as np
from jax import lax
from jax.experimental import pallas as pl
from jax.experimental.pallas import tpu as pltpu
from jax.sharding import Mesh, PartitionSpec as P

F32 = jnp.float32
BF16 = jnp.bfloat16
EPSILON = 1e-05
NEGATIVE = -1e30
D = 512
HEADS = 16
NREL = 759
SCALE = 32 ** (-0.5)
AXES = ("yh", "x1", "x0", "z2", "z1", "z0", "c", "yl")
VMEM = 56 << 20

QUADS = ((1, 1), (1, 0), (0, 1), (0, 0))


def _token(rh, ch, l, r, c):
    return (rh * 2 + ch) * 36 + l * 18 + r * 6 + c


def _tables():
    px = np.zeros((144, 144), np.float32)
    ps = np.zeros((192, 144), np.float32)
    pf = np.zeros((144, 192), np.float32)
    pm = np.zeros((144, 144), np.float32)
    rows = np.zeros((144, 12), np.float32)
    cols = np.zeros((144, 12), np.float32)
    flags = np.zeros((144, 2), np.float32)
    for l in range(2):
        for row in range(6):
            for col in range(12):
                rh, r, ch, c = row // 3, row % 3, col // 6, col % 6
                t = _token(rh, ch, l, r, c)
                px[t, (row * 12 + col) * 2 + l] = 1
                pm[t, l * 72 + row * 12 + col] = 1
                rows[t, row * 2 + l] = 1
                cols[t, col] = 1
                flags[t] = (l, rh)
                k = QUADS.index((rh, ch))
                ps[48 * k + (1 - l) * 18 + r * 6 + c, t] = 1
    for k in range(4):
        for i in range(36):
            pf[36 * k + i, 48 * k + i] = 1
    bf = jnp.bfloat16
    return {
        "px": px.astype(bf),
        "ps": ps.astype(bf),
        "pf": pf.astype(bf),
        "pft": pf.T.copy().astype(bf),
        "pst": ps.T.copy().astype(bf),
        "cells": (px.T @ ps.T).astype(bf),
        "pxt": px.T.copy().astype(bf),
        "pm": pm.astype(bf),
        "rows": rows.astype(bf),
        "cols": cols,
        "flags": flags,
    }


TABLES = _tables()


def dot(a, b):
    return lax.dot_general(a, b, (((1,), (0,)), ((), ())), preferred_element_type=F32)


def dot_nt(a, b):
    return lax.dot_general(a, b, (((1,), (1,)), ((), ())), preferred_element_type=F32)


def dot_tn(a, b):
    return lax.dot_general(a, b, (((0,), (0,)), ((), ())), preferred_element_type=F32)


def lane_masks():
    lane = lax.broadcasted_iota(jnp.int32, (1, 128), 1) >> 5
    return [jnp.where(lane == k, 1.0, 0.0).astype(F32) for k in range(4)]


def stack_heads(group, masks):
    return jnp.concatenate([group * m.astype(BF16) for m in masks], axis=0)


def fold_heads(stacked, masks):
    total = stacked[0:144] * masks[0]
    for k in range(1, 4):
        total = total + stacked[144 * k : 144 * (k + 1)] * masks[k]
    return total


def pad_keys(group):
    return jnp.concatenate([group, jnp.zeros((112, 128), BF16)], axis=0)


def normalize(x):
    center = x - jnp.mean(x, axis=-1, keepdims=True)
    rstd = lax.rsqrt(jnp.mean(center * center, axis=-1, keepdims=True) + EPSILON)
    return center * rstd, rstd


def pack_table(tab, words, scales, offsets):
    low = jnp.min(tab, axis=-1, keepdims=True)
    scale = jnp.maximum(jnp.max(tab, axis=-1, keepdims=True) - low, 1e-20) * (1.0 / 65535.0)
    q = jnp.clip(jnp.floor((tab - low) / scale + 0.5), 0.0, 65535.0).astype(jnp.int32)
    high = jnp.concatenate([q[4 * g : 4 * g + 2] for g in range(4)], axis=0)
    rest = jnp.concatenate([q[4 * g + 2 : 4 * g + 4] for g in range(4)], axis=0)
    words[...] = jnp.zeros((8, 768), jnp.int32)
    words[:, 0:NREL] = ((high - 32768) << 16) + rest
    signed = lax.broadcasted_iota(jnp.int32, (HEADS, 1), 0) & 3
    offset = low + jnp.where(signed < 2, 32768.0, 0.0) * scale
    scales[...] = jnp.broadcast_to(scale, (HEADS, 128))
    offsets[...] = jnp.broadcast_to(offset, (HEADS, 128))


def lookup(row, ids):
    acc = None
    for k in range(6):
        part = jnp.broadcast_to(row[:, 128 * k : 128 * (k + 1)], ids.shape)
        got = jnp.take_along_axis(part, ids & 127, axis=1)
        acc = got if k == 0 else jnp.where((ids >> 7) == k, got, acc)
    return acc


def tail_ids(ids):
    lane = lax.broadcasted_iota(jnp.int32, (24, 128), 1)
    total = jnp.where(lane < 16, ids[0:24], 0)
    for k in range(1, 6):
        piece = jnp.where(lane < 16, ids[24 * k : 24 * (k + 1)], 0)
        total = total + pltpu.roll(piece, 16 * k, 1)
    return total


def bias_pair(m, words, scales, offsets, ids, tails):
    row = words[m : m + 1, :]
    main = lookup(row, ids)
    tail = lookup(row, tails)
    parts = [tail] + [pltpu.roll(tail, 128 - 16 * k, 1) for k in range(1, 6)]
    tail = jnp.concatenate(parts, axis=0)
    lane = lax.broadcasted_iota(jnp.int32, (144, 128), 1)
    head = 4 * (m // 2) + m % 2
    out = []
    for h, take in ((head, lambda w: w >> 16), (head + 2, lambda w: w & 65535)):
        scale, offset = scales[h : h + 1, :], offsets[h : h + 1, :]
        a = take(main).astype(F32) * scale + offset
        b = jnp.where(lane < 16, take(tail).astype(F32) * scale + offset, NEGATIVE)
        out.append(jnp.concatenate([a, b], axis=1))
    return out


def fill_bias(table, rel_ref, words, scales, offsets, store):
    pack_table(table, words, scales, offsets)
    ids, tails = rel_ref[:, 0:128], tail_ids(rel_ref[:, 128:256])
    for m in range(8):
        head = 4 * (m // 2) + m % 2
        for h, b in zip((head, head + 2), bias_pair(m, words, scales, offsets, ids, tails)):
            store[144 * h : 144 * (h + 1), :] = b


def group_probs(qkv_ref, g, masks, bias_ref, allowed):
    qg = qkv_ref[:, 128 * g : 128 * (g + 1)]
    kg = pad_keys(qkv_ref[:, 512 + 128 * g : 512 + 128 * (g + 1)])
    q4 = stack_heads(qg, masks)
    s4 = dot_nt(q4, kg) * SCALE
    out = []
    for k in range(4):
        at = 144 * (4 * g + k)
        s = s4[144 * k : 144 * (k + 1)] + bias_ref[at : at + 144, :]
        if allowed is not None:
            s = jnp.where(allowed, s, NEGATIVE)
        e = jnp.exp(s - jnp.max(s, axis=-1, keepdims=True))
        out.append(e * (1.0 / jnp.sum(e, axis=-1, keepdims=True)))
    return q4, kg, jnp.concatenate(out, axis=0)


def group_back(g, q4, kg, vg, p4, p4b, do, masks, dqkv_ref, ds0_ref, ds1_ref):
    do4 = stack_heads(do[:, 128 * g : 128 * (g + 1)], masks)
    dp4 = dot_nt(do4, vg)
    dqkv_ref[:, 1024 + 128 * g : 1024 + 128 * (g + 1)] = dot_tn(p4b, do4)[0:144].astype(BF16)
    ds4 = p4 * (dp4 - jnp.sum(dp4 * p4, axis=-1, keepdims=True))
    ds0_ref[576 * g : 576 * (g + 1), :] = ds4[:, 0:128]
    ds1_ref[576 * g : 576 * (g + 1), :] = ds4[:, 128:256]
    ds4b = ds4.astype(BF16)
    dq = fold_heads(dot(ds4b, kg), masks) * SCALE
    dqkv_ref[:, 128 * g : 128 * (g + 1)] = dq.astype(BF16)
    dk = dot_tn(ds4b, q4)[0:144] * SCALE
    dqkv_ref[:, 512 + 128 * g : 512 + 128 * (g + 1)] = dk.astype(BF16)


def finish_back(dqkv_ref, wqkv_ref, n, rstd, gain, g32, dgain_ref):
    dh = dot_nt(dqkv_ref[...], wqkv_ref[0])
    dgain_ref[...] = jnp.sum(dh * n, axis=0, keepdims=True)
    dn = dh * gain
    return (
        rstd
        * (
            dn
            - jnp.mean(dn, axis=-1, keepdims=True)
            - n * jnp.mean(dn * n, axis=-1, keepdims=True)
        )
        + g32
    )


def weight_terms(idx_ref, h, o, dqkv, g, keep_ref, send_ref):
    core = idx_ref[0]
    p = lax.broadcasted_iota(jnp.int32, (256, 512), 0)
    row = lax.broadcasted_iota(jnp.int32, (256, 512), 1)
    base = p & 3
    base = base + ((((p >> 7) ^ (p >> 5)) & 1) << 6)
    for at, to in ((6, 3), (5, 7), (4, 8), (3, 5), (2, 4)):
        base = base + (((p >> at) & 1) << to)
    for which, ref in ((core, keep_ref), (1 - core, send_ref)):
        pick = jnp.where(row == base + which * 4, 1.0, 0.0).astype(BF16)
        ht = dot_nt(pick, h).astype(BF16)
        ot = dot_nt(pick, o).astype(BF16)
        ref[:, 0:1536] = dot(ht, dqkv).astype(BF16)
        ref[:, 1536:2048] = dot(ot, g).astype(BF16)


def first_kernel(
    idx_ref, x_ref, go_ref, grp_ref, gain_ref, wqkv_ref, wproj_ref, tab_ref, rel_ref,
    px_ref, ps_ref, pm_ref, rows_ref, cols_ref,
    own_ref, lon_ref, lat_ref, dia_ref, n_ref, rstd_ref, qkv_ref, p_ref, o_ref, relp_ref,
    cells, gs, pay, bias, words, scales, offsets,
):
    masks = lane_masks()
    for k in range(72):
        cells[2 * k : 2 * k + 2, 0:512] = x_ref[k].astype(F32)
        cells[2 * k : 2 * k + 2, 512:1024] = go_ref[k].astype(F32)
    both = dot(px_ref[...], cells[...].astype(BF16))
    x = both[:, 0:512]
    pay[:, 512:1024] = both[:, 512:1024].astype(BF16)
    for r in range(6):
        gs[2 * r : 2 * r + 2, :] = grp_ref[r].astype(F32)
    picked = dot(rows_ref[...], gs[...].astype(BF16)) * cols_ref[...]
    group = jnp.sum(picked, axis=-1, keepdims=True)
    pay[:, 1024:1152] = jnp.broadcast_to(group, (144, 128)).astype(BF16)

    rel = rel_ref[...]
    pm = pm_ref[...]
    parts = []
    for part in (rel >> 5, rel & 31):
        half = dot(pm, part.astype(F32).astype(BF16)).astype(BF16)
        parts.append(dot_nt(half, pm).astype(jnp.int32))
    relp_ref[...] = jnp.full((144, 256), 767, jnp.int32)
    relp_ref[:, 0:144] = parts[0] * 32 + parts[1]
    fill_bias(tab_ref[0, idx_ref[1]], relp_ref, words, scales, offsets, bias)

    n, rstd = normalize(x)
    n_ref[...] = n
    rstd_ref[...] = rstd
    h = (n * gain_ref[0:1, :]).astype(BF16)
    qkv_ref[...] = dot(h, wqkv_ref[0]).astype(BF16)
    for g in range(4):
        _, _, p4 = group_probs(qkv_ref, g, masks, bias, None)
        p4b = p4.astype(BF16)
        p_ref[576 * g : 576 * (g + 1), :] = p4b
        vg = pad_keys(qkv_ref[:, 1024 + 128 * g : 1024 + 128 * (g + 1)])
        o_ref[:, 128 * g : 128 * (g + 1)] = fold_heads(dot(p4b, vg), masks).astype(BF16)
    pay[:, 0:512] = (x + dot(o_ref[...], wproj_ref[0])).astype(BF16)
    out = dot(ps_ref[...], pay[...]).astype(BF16)
    own_ref[...] = out[0:48]
    lon_ref[...] = out[48:96]
    lat_ref[...] = out[96:144]
    dia_ref[...] = out[144:192]


def bias_kernel(idx_ref, tab_ref, rel_ref, out_ref, words, scales, offsets):
    fill_bias(tab_ref[0, idx_ref[1]], rel_ref, words, scales, offsets, out_ref)


def second_kernel(
    idx_ref, own_ref, lon_ref, lat_ref, dia_ref, gain_ref, wqkv_ref, wproj_ref, bias_ref,
    pf_ref, pft_ref, flags_ref,
    oown_ref, olon_ref, olat_ref, odia_ref, h_ref, o_ref, dqkv_ref, g_ref, dgain_ref, ds0_ref, ds1_ref,
    qkv_ref, back,
):
    masks = lane_masks()
    frame = dot(
        pf_ref[...], jnp.concatenate([own_ref[...], lon_ref[...], lat_ref[...], dia_ref[...]], axis=0)
    )
    x = frame[:, 0:512]
    g32 = frame[:, 512:1024]
    gb = g32.astype(BF16)
    g_ref[...] = gb
    lat = idx_ref[1].astype(F32)
    key = frame[:, 1024:1025] * 4.0 + flags_ref[:, 1:2] * (2.0 * lat) + flags_ref[:, 0:1]
    eye = lax.broadcasted_iota(jnp.int32, (144, 256), 0) == lax.broadcasted_iota(
        jnp.int32, (144, 256), 1
    )
    key_row = jnp.sum(jnp.where(eye, key, 0.0), axis=0, keepdims=True)
    allowed = key == key_row
    gain = gain_ref[1:2, :]

    n, rstd = normalize(x)
    h = (n * gain).astype(BF16)
    h_ref[...] = h
    qkv_ref[...] = dot(h, wqkv_ref[0]).astype(BF16)
    do = dot_nt(gb, wproj_ref[0]).astype(BF16)
    for g in range(4):
        q4, kg, p4 = group_probs(qkv_ref, g, masks, bias_ref, allowed)
        p4b = p4.astype(BF16)
        vg = pad_keys(qkv_ref[:, 1024 + 128 * g : 1024 + 128 * (g + 1)])
        o_ref[:, 128 * g : 128 * (g + 1)] = fold_heads(dot(p4b, vg), masks).astype(BF16)
        group_back(g, q4, kg, vg, p4, p4b, do, masks, dqkv_ref, ds0_ref, ds1_ref)
    back[:, 0:512] = (x + dot(o_ref[...], wproj_ref[0])).astype(BF16)
    df = finish_back(dqkv_ref, wqkv_ref, n, rstd, gain, g32, dgain_ref)
    back[:, 512:1024] = df.astype(BF16)
    out = dot(pft_ref[...], back[...]).astype(BF16)
    oown_ref[...] = out[0:48]
    olon_ref[...] = out[48:96]
    olat_ref[...] = out[96:144]
    odia_ref[...] = out[144:192]


def weights_kernel(idx_ref, h_ref, o_ref, dqkv_ref, g_ref, keep_ref, send_ref):
    weight_terms(idx_ref, h_ref[...], o_ref[...], dqkv_ref[...], g_ref[...], keep_ref, send_ref)


def third_kernel(
    idx_ref, own_ref, lon_ref, lat_ref, dia_ref, gain_ref, wqkv_ref, wproj_ref,
    n_ref, rstd_ref, qkv_ref, p_ref, o_ref, pst_ref, cells_ref, pxt_ref, after_ref,
    out_ref, gin_ref, dgain_ref, ds0_ref, ds1_ref, keep_ref, send_ref,
    dqkv_ref, outs,
):
    masks = lane_masks()
    pieces = jnp.concatenate([own_ref[...], lon_ref[...], lat_ref[...], dia_ref[...]], axis=0)
    outs[:, 0:512] = dot(cells_ref[...], pieces[:, 0:512])
    g32 = dot(pst_ref[...], pieces[:, 512:1024])
    gb = g32.astype(BF16)
    gain = gain_ref[0:1, :]
    n = n_ref[...]
    do = dot_nt(gb, wproj_ref[0]).astype(BF16)
    for g in range(4):
        q4 = stack_heads(qkv_ref[:, 128 * g : 128 * (g + 1)], masks)
        kg = pad_keys(qkv_ref[:, 512 + 128 * g : 512 + 128 * (g + 1)])
        vg = pad_keys(qkv_ref[:, 1024 + 128 * g : 1024 + 128 * (g + 1)])
        p4b = p_ref[576 * g : 576 * (g + 1), :]
        group_back(g, q4, kg, vg, p4b.astype(F32), p4b, do, masks, dqkv_ref, ds0_ref, ds1_ref)
    df = finish_back(dqkv_ref, wqkv_ref, n, rstd_ref[...], gain, g32, dgain_ref)
    outs[:, 512:1024] = dot(pxt_ref[...], df.astype(BF16))
    for k in range(72):
        out_ref[k] = outs[2 * k : 2 * k + 2, 0:512].astype(BF16)
        gin_ref[k] = outs[2 * k : 2 * k + 2, 512:1024].astype(BF16)
    h = (n * gain).astype(BF16)
    weight_terms(idx_ref, h, o_ref[...], dqkv_ref[...], gb, keep_ref, send_ref)


def scatter_kernel(
    idx_ref, rel_ref, d00_ref, d01_ref, gain0_ref, d10_ref, d11_ref, gain1_ref, after_ref,
    keep_ref, send_ref,
):
    iota = lax.broadcasted_iota(jnp.int32, (128, 256), 0)

    def body(i, acc):
        ids = rel_ref[pl.ds(i, 1), :]
        low, high = ids & 127, ids >> 7
        hot = jnp.where(iota == low, 1.0, 0.0).astype(BF16)
        lhs = []
        for d0_ref, d1_ref in ((d00_ref, d01_ref), (d10_ref, d11_ref)):
            d = jnp.concatenate(
                [d0_ref[pl.ds(i, 16, stride=144), :], d1_ref[pl.ds(i, 16, stride=144), :]], axis=1
            )
            lhs += [jnp.where(high == k, d, 0.0) for k in range(6)]
        return acc + dot_nt(jnp.concatenate(lhs, axis=0).astype(BF16), hot)

    acc = lax.fori_loop(0, 144, body, jnp.zeros((192, 128), F32), unroll=8)
    first = lax.broadcasted_iota(jnp.int32, (8, 256), 0) == 0
    for b, dgain_ref in enumerate((gain0_ref, gain1_ref)):
        table = jnp.concatenate([acc[96 * b + 16 * k : 96 * b + 16 * k + 16] for k in range(6)], axis=1)
        halves = []
        for c in range(2):
            gain = jnp.where(first, dgain_ref[:, 256 * c : 256 * (c + 1)], 0.0)
            halves.append(jnp.concatenate([table[8 * c : 8 * (c + 1)], gain], axis=1))
        keep, send = pick(idx_ref[0], halves[0], halves[1])
        keep_ref[8 * b : 8 * b + 8, :] = keep
        send_ref[8 * b : 8 * b + 8, :] = send


CUTS = ((0, 384), (384, 768), (768, 1024))


def pick(flag, low, high):
    mine = flag == 0
    return jnp.where(mine, low, high), jnp.where(mine, high, low)


def core_kernel(
    idx_ref, k0_ref, r0_ref, k1_ref, r1_ref, ka_ref, sa_ref, kb_ref, sb_ref, kc_ref, sc_ref
):
    x0, z0, yl = idx_ref[2], idx_ref[3], idx_ref[1]
    for b, (k_ref, r_ref) in enumerate(((k0_ref, r0_ref), (k1_ref, r1_ref))):

        def total(r0, r1, c0, c1):
            return k_ref[r0:r1, c0:c1].astype(F32) + r_ref[r0:r1, c0:c1].astype(F32)

        for s in range(2):
            a0 = 1024 * s
            keep, send = pick(x0, total(0, 128, a0, a0 + 384), total(128, 256, a0, a0 + 384))
            to = 768 * b + 384 * s
            ka_ref[:, to : to + 384] = keep.astype(BF16)
            sa_ref[:, to : to + 384] = send.astype(BF16)
            to = 512 * b + 256 * s
            for h in range(2):
                r = 128 * h
                keep, send = pick(
                    z0,
                    total(r, r + 64, a0 + 768, a0 + 1024),
                    total(r + 64, r + 128, a0 + 768, a0 + 1024),
                )
                kc_ref[64 * h : 64 * h + 64, to : to + 256] = keep.astype(BF16)
                sc_ref[64 * h : 64 * h + 64, to : to + 256] = send.astype(BF16)
        keep, send = pick(yl, total(0, 256, 384, 768), total(0, 256, 1408, 1792))
        kb_ref[:, 384 * b : 384 * (b + 1)] = keep.astype(BF16)
        sb_ref[:, 384 * b : 384 * (b + 1)] = send.astype(BF16)


def step_two_kernel(
    idx_ref, ka_ref, ra_ref, kb_ref, rb_ref, kc_ref, rc_ref, t_ref, u_ref,
    nka_ref, nsa_ref, nkb_ref, nsb_ref, nkc_ref, nsc_ref, tk_ref,
):
    x0, z0, yl = idx_ref[2], idx_ref[3], idx_ref[1]
    a = ka_ref[...].astype(F32) + ra_ref[...].astype(F32)
    for b in range(2):
        keep, send = pick(yl, a[:, 768 * b : 768 * b + 384], a[:, 768 * b + 384 : 768 * b + 768])
        nka_ref[:, 384 * b : 384 * (b + 1)] = keep.astype(BF16)
        nsa_ref[:, 384 * b : 384 * (b + 1)] = send.astype(BF16)
    m = kb_ref[...].astype(F32) + rb_ref[...].astype(F32)
    for h in range(2):
        keep, send = pick(z0, m[128 * h : 128 * h + 64], m[128 * h + 64 : 128 * h + 128])
        nkb_ref[64 * h : 64 * h + 64, :] = keep.astype(BF16)
        nsb_ref[64 * h : 64 * h + 64, :] = send.astype(BF16)
    t = t_ref[...] + u_ref[...]
    t0, t1 = t[0:8], t[8:16]
    gains = jnp.concatenate([t0[:, 768:1024], t1[:, 768:1024], jnp.zeros((8, 256), F32)], axis=1)
    table = jnp.concatenate([t0[:, 0:768], t1[:, 0:768], gains, jnp.zeros((8, 768), F32)], axis=0)
    table = table.astype(BF16)
    tk_ref[...] = table
    nsb_ref[128:160, :] = table
    c = kc_ref[...].astype(F32) + rc_ref[...].astype(F32)
    keep, send = pick(x0, c[0:64], c[64:128])
    nkc_ref[...] = keep.astype(BF16)
    nsc_ref[...] = send.astype(BF16)


def step_three_kernel(
    idx_ref, ka_ref, ra_ref, kb_ref, rb_ref, kc_ref, rc_ref, tk_ref,
    nka_ref, nsa_ref, nkb_ref, nsb_ref, nkc_ref, nsc_ref, ntk_ref,
):
    x0, z0, yl = idx_ref[2], idx_ref[3], idx_ref[1]
    a = ka_ref[...].astype(F32) + ra_ref[...].astype(F32)
    keep, send = pick(z0, a[0:64], a[64:128])
    nka_ref[...] = keep.astype(BF16)
    nsa_ref[...] = send.astype(BF16)
    m = kb_ref[...].astype(F32) + rb_ref[0:128, :].astype(F32)
    keep, send = pick(x0, m[0:64], m[64:128])
    nkb_ref[...] = keep.astype(BF16)
    nsb_ref[0:64, :] = send.astype(BF16)
    table = (tk_ref[...].astype(F32) + rb_ref[128:160, :].astype(F32)).astype(BF16)
    ntk_ref[...] = table
    nsb_ref[64:96, :] = table
    c = kc_ref[...].astype(F32) + rc_ref[...].astype(F32)
    for b in range(2):
        keep, send = pick(yl, c[:, 512 * b : 512 * b + 256], c[:, 512 * b + 256 : 512 * b + 512])
        nkc_ref[:, 256 * b : 256 * (b + 1)] = keep.astype(BF16)
        nsc_ref[:, 256 * b : 256 * (b + 1)] = send.astype(BF16)


def spread_kernel(
    idx_ref, ka_ref, ra_ref, kb_ref, rb_ref, kc_ref, rc_ref, tk_ref, *refs
):
    outs, scr = refs[0:4], refs[4]
    a = ka_ref[...].astype(F32) + ra_ref[...].astype(F32)
    m = kb_ref[...].astype(F32) + rb_ref[0:64, :].astype(F32)
    c = kc_ref[...].astype(F32) + rc_ref[...].astype(F32)
    table = tk_ref[...].astype(F32) + rb_ref[64:96, :].astype(F32)
    gains = jnp.concatenate([table[16:24, 0:256], table[16:24, 256:512]], axis=0)
    table = jnp.concatenate([table[0:16], gains], axis=1)
    table = jnp.concatenate([table[0:8], table[8:16]], axis=1).astype(BF16)
    full = []
    for b in range(2):
        cols = slice(384 * b, 384 * (b + 1))
        full += [a[:, cols], m[:, cols], c[:, 256 * b : 256 * (b + 1)]]
    full = jnp.concatenate(full, axis=1).astype(BF16)
    for k in range(4):
        scr[k] = full[16 * k : 16 * k + 16]
    for f in range(4):
        outs[f][0:16, :] = scr[idx_ref[4] ^ f]
        outs[f][16:24, :] = table


def plane_kernel(idx_ref, own_ref, g1_ref, g2_ref, g3_ref, *refs):
    outs, tabs, scr = refs[0:4], refs[4], refs[5]
    got = (own_ref, g1_ref, g2_ref, g3_ref)
    total = got[0][0:16, :].astype(F32)
    for g in got[1:]:
        total = total + g[0:16, :].astype(F32)
    for f in range(4):
        tabs[idx_ref[4] ^ f] = got[f][16:24, :].astype(F32)
    table = tabs[0] + tabs[1] + tabs[2] + tabs[3]
    table = jnp.concatenate([table[:, 0:1024], table[:, 1024:2048]], axis=0)
    for k in range(4):
        rows = total[4 * k : 4 * k + 4]
        rows = jnp.concatenate([rows[:, 0:1024], rows[:, 1024:2048], table], axis=0)
        scr[k] = rows.astype(BF16)
    for f in range(4):
        outs[f][...] = scr[idx_ref[5] ^ f]


def ring_kernel(idx_ref, own_ref, g1_ref, g2_ref, g3_ref, out_ref, tab_ref, scr):
    for f, g in enumerate((own_ref, g1_ref, g2_ref, g3_ref)):
        scr[idx_ref[5] ^ f] = g[...].astype(F32)
    total = scr[0] + scr[1] + scr[2] + scr[3]
    out_ref[...] = total.astype(BF16)
    tab_ref[...] = total[8:24].astype(BF16)


def last_kernel(
    factor, idx_ref, own_ref, lat_ref, core_ref, dia_ref, gain_ref, qkv_ref, proj_ref, bias_ref
):
    core, yl = idx_ref[0], idx_ref[1]
    own = own_ref[...].astype(F32) * factor
    got = lat_ref[...].astype(F32) * factor
    low, high = pick(yl, own[0:8], got[0:8])
    for b in range(2):
        qkv_ref[b, :, 0:1024] = low[4 * b : 4 * b + 4]
        qkv_ref[b, :, 1024:1536] = high[4 * b : 4 * b + 4, 0:512]
        proj_ref[b, :, :] = high[4 * b : 4 * b + 4, 512:1024]
    near = pick(yl, own[8:24], got[8:24])
    far = pick(yl, core_ref[...].astype(F32) * factor, dia_ref[...].astype(F32) * factor)
    tabs = [pick(core, near[w], far[w]) for w in range(2)]
    for c in range(2):
        for w in range(2):
            for b in range(2):
                bias_ref[b, w, 8 * c : 8 * (c + 1), :] = tabs[w][c][8 * b : 8 * b + 8, 0:NREL]
        for b in range(2):
            gain_ref[b : b + 1, 256 * c : 256 * (c + 1)] = (
                tabs[0][c][8 * b : 8 * b + 1, 768:1024] + tabs[1][c][8 * b : 8 * b + 1, 768:1024]
            )


def _whole(shape):
    return pl.BlockSpec(shape, lambda *_: (0,) * len(shape))


SMEM = pl.BlockSpec(memory_space=pltpu.SMEM)


ANY = pl.BlockSpec(memory_space=pl.ANY)


def call(body, outs, *args, specs=None, scratch=(), cost=None):
    specs = dict(specs or {})
    if args[0].dtype == jnp.int32 and args[0].ndim == 1:
        specs[0] = SMEM
    return pl.pallas_call(
        body,
        grid=(1,),
        in_specs=[specs.get(i, _whole(a.shape)) for i, a in enumerate(args)],
        out_specs=[_whole(s) for s, _ in outs],
        out_shape=[jax.ShapeDtypeStruct(s, t) for s, t in outs],
        scratch_shapes=[pltpu.VMEM(s, t) for s, t in scratch],
        compiler_params=pltpu.CompilerParams(vmem_limit_bytes=VMEM),
        cost_estimate=cost,
    )(*args)


def flip(value, *axes):
    mask = sum(1 << (7 - AXES.index(a)) for a in axes)
    return lax.ppermute(value, AXES, [(s, s ^ mask) for s in range(256)])


def lon_step(value, offset, across):
    pairs = [(s, ((s // 2 + offset) % 128) * 2 + (s % 2 ^ across)) for s in range(256)]
    return lax.ppermute(value, AXES, pairs)


def halo(pieces, offset):
    own, lon, lat, dia = pieces
    return (
        own,
        lon_step(lon, offset, 0),
        flip(lat, "yl"),
        lon_step(dia, offset, 1),
    )


def on_device(inputs, grad_out, gains, qkv_weight, proj_weight, bias_table, rel_ids, groups):
    T = {k: jnp.asarray(v) for k, v in TABLES.items()}
    at = {a: lax.axis_index(a) for a in AXES}
    idx = jnp.stack(
        [
            at["c"],
            at["yl"],
            at["x0"] ^ at["x1"],
            at["z0"],
            2 * at["x1"] + at["yh"],
            2 * at["z2"] + at["z1"],
        ]
    ).astype(jnp.int32)
    x_cells, go_cells = [v.transpose(0, 2, 3, 1, 4).reshape(72, 2, D) for v in (inputs, grad_out)]

    def block(b, shape):
        return pl.BlockSpec((1,) + shape, lambda *_: (b,) + (0,) * len(shape))

    def weights(b, first):
        return {
            first: block(b, (D, 3 * D)),
            first + 1: block(b, (D, D)),
            first + 2: block(b, (2, HEADS, NREL)),
        }

    tables = [((8, 768), jnp.int32), ((HEADS, 128), F32), ((HEADS, 128), F32)]
    piece = ((48, 1152), BF16)
    own, lon, lat, dia, n0, rstd0, qkv0, p0, o0, relp = call(
        first_kernel,
        [piece] * 4
        + [
            ((144, D), F32),
            ((144, 1), F32),
            ((144, 3 * D), BF16),
            ((2304, 256), BF16),
            ((144, D), BF16),
            ((144, 256), jnp.int32),
        ],
        idx, x_cells, go_cells, groups.transpose(1, 0, 2), gains, qkv_weight, proj_weight, bias_table, rel_ids,
        T["px"], T["ps"], T["pm"], T["rows"], T["cols"],
        specs=weights(0, 5),
        scratch=[((144, 1024), F32), ((12, 12), F32), ((144, 1152), BF16), ((2304, 256), F32)] + tables,
    )
    pieces = halo((own, lon, lat, dia), -1)
    (bias1,) = call(
        bias_kernel,
        [((2304, 256), F32)],
        idx, bias_table, relp,
        specs={1: block(1, (2, HEADS, NREL))},
        scratch=tables,
    )
    back = ((48, 1024), BF16)
    ds_shape = ((2304, 128), F32)
    own, lon, lat, dia, h1, o1, dqkv1, g1, dgain1, ds10, ds11 = call(
        second_kernel,
        [back] * 4
        + [
            ((144, D), BF16),
            ((144, D), BF16),
            ((144, 3 * D), BF16),
            ((144, D), BF16),
            ((1, D), F32),
            ds_shape,
            ds_shape,
        ],
        idx, *pieces, gains, qkv_weight, proj_weight, bias1, T["pf"], T["pft"], T["flags"],
        specs={6: block(1, (D, 3 * D)), 7: block(1, (D, D))},
        scratch=[((144, 3 * D), BF16), ((144, 2 * D), BF16)],
    )
    pieces = halo((own, lon, lat, dia), 1)
    wshape = ((256, 4 * D), BF16)
    keep1, send1 = call(weights_kernel, [wshape] * 2, idx, h1, o1, dqkv1, g1)
    recv1 = flip(send1, "c")
    cells = ((72, 2, D), BF16)
    outputs, grad_inputs, dgain0, ds00, ds01, keep0, send0 = call(
        third_kernel,
        [cells, cells, ((1, D), F32), ds_shape, ds_shape, wshape, wshape],
        idx, *pieces, gains, qkv_weight, proj_weight, n0, rstd0, qkv0, p0, o0,
        T["pst"], T["cells"], T["pxt"], keep1,
        specs={6: block(0, (D, 3 * D)), 7: block(0, (D, D)), 16: ANY},
        scratch=[((144, 3 * D), BF16), ((144, 2 * D), F32)],
    )
    outputs, grad_inputs = [
        v.reshape(1, 6, 12, 2, D).transpose(0, 3, 1, 2, 4) for v in (outputs, grad_inputs)
    ]
    recv0 = flip(send0, "c")

    def pairs(*shapes):
        return [(s, BF16) for shape in shapes for s in shape]

    ka, sa, kb, sb, kc, sc = call(
        core_kernel,
        pairs([(128, 1536)] * 2, [(256, 768)] * 2, [(128, 1024)] * 2),
        idx, keep0, recv0, keep1, recv1,
    )
    ra, rb, rc = flip(sa, "x0"), flip(sb, "yl"), flip(sc, "z0")
    tshape = ((16, 1024), F32)
    tkeep, tsend = call(
        scatter_kernel,
        [tshape] * 2,
        idx, relp, ds00, ds01, dgain0, ds10, ds11, dgain1, ka,
        specs={8: ANY},
    )
    trecv = flip(tsend, "c")
    ka, sa, kb, sb, kc, sc, tk = call(
        step_two_kernel,
        pairs([(128, 768)] * 2, [(128, 768), (160, 768)], [(64, 1024)] * 2, [(32, 768)]),
        idx, ka, ra, kb, rb, kc, rc, tkeep, trecv,
    )
    ra, rb, rc = flip(sa, "yl"), flip(sb, "z0"), flip(sc, "x0")
    ka, sa, kb, sb, kc, sc, tk = call(
        step_three_kernel,
        pairs([(64, 768)] * 2, [(64, 768), (96, 768)], [(64, 512)] * 2, [(32, 768)]),
        idx, ka, ra, kb, rb, kc, rc, tk,
    )
    ra, rb, rc = flip(sa, "z0"), flip(sb, "x0"), flip(sc, "yl")
    parts = call(
        spread_kernel,
        [((24, 2048), BF16)] * 4,
        idx, ka, ra, kb, rb, kc, rc, tk,
        scratch=[((4, 16, 2048), BF16)],
    )
    parts = call(
        plane_kernel,
        [((24, 1024), BF16)] * 4,
        idx, parts[0], flip(parts[1], "yh"), flip(parts[2], "x1", "x0"),
        flip(parts[3], "x1", "x0", "yh"),
        scratch=[((4, 8, 2048), F32), ((4, 24, 1024), BF16)],
    )
    own, tab = call(
        ring_kernel,
        [((24, 1024), BF16), ((16, 1024), BF16)],
        idx, parts[0], flip(parts[1], "z1"), flip(parts[2], "z2"), flip(parts[3], "z2", "z1"),
        scratch=[((4, 24, 1024), F32)],
    )
    from_core = flip(tab, "c")
    from_dia = flip(tab, "c", "yl")
    from_lat = flip(own, "yl")
    factor = 36864 ** (-0.5)
    grad_gains, grad_qkv, grad_proj, grad_bias = call(
        functools.partial(last_kernel, factor),
        [
            ((2, D), F32),
            ((2, 4, 3 * D), F32),
            ((2, 4, D), F32),
            ((2, 2, HEADS, NREL), F32),
        ],
        idx, own, from_lat, from_core, from_dia,
    )
    return (outputs, grad_inputs, grad_gains, grad_qkv, grad_proj, grad_bias)


def solution(mesh):
    fine = Mesh(mesh.devices.reshape((2,) * 8), AXES)
    lon = AXES[:7]
    field = P(None, None, "yl", lon, None)
    rows = P(None, lon, None)
    return jax.shard_map(
        on_device,
        mesh=fine,
        in_specs=(field, field, P(), P(), P(), P(), P(), P(None, "yl", lon)),
        out_specs=(field, field, P(), rows, rows, P()),
        check_vma=False,
    )
```

time: 180 us -> 137 us (0.76)
  blocking collectives: 38 us -> 0 us
  starting transfers between devices: 28.8 us -> 48.5 us
  Pallas kernels: 78.2 us -> 60.1 us
  local copies, waits for them, and re-layouts: 12.6 us -> 7.86 us
  waiting for transfers between devices: 21.3 us -> 19.1 us
    all_to_all x1 -> x0, blocking collectives: 38 us -> none  [on_device(): got = lax.all_to_all(payload, ('yh', 'x', 'yl'), 0, 0, tiled=True)]
    ppermute x16 -> x27, starting transfers between devices: 28.8 us -> 48.5 us  [the longest x23 35.1 us: flip(): return lax.ppermute(value, AXES, [(s, s ^ mask) for s in range(256)])]
    pallas_call x12 -> x13, Pallas kernels: 78.2 us -> 60.1 us  [call(): pl.pallas_call(body, grid=(1,), in_specs=[specs.get(i, _whole(a.shape)) f...]
    unnamed x41 -> x54, local copies, waits for them, and re-layouts: 11.9 us -> 7.18 us
    ppermute x16 -> x27, waiting for transfers between devices: 21.3 us -> 19.1 us  [the longest x23 18.4 us: flip(): return lax.ppermute(value, AXES, [(s, s ^ mask) for s in range(256)])]
  transfers between devices with their start and end apart: 16 -> 27, of which waited for: 7 -> 12; matrix products, arithmetic and copies ran while one was open for 1% -> 0% of each run, Pallas kernels for 15% -> 20%
where the time goes in v2:
time: 137 us; the launch traced here: 136 us
  Pallas kernels  60.1 us (44%)
  starting transfers between devices  48.5 us (35%)
  waiting for transfers between devices  19.1 us (14%)
  local copies, waits for them, and re-layouts  7.86 us (6%)
    pallas_call x13, Pallas kernels, call(): pl.pallas_call(body, grid=(1,), in_specs=[specs.get(i, _whole(a.shape)) f...  60.1 us
    ppermute x23, starting transfers between devices, flip(): return lax.ppermute(value, AXES, [(s, s ^ mask) for s in range(256)])  35.1 us
    ppermute x23, waiting for transfers between devices, flip(): return lax.ppermute(value, AXES, [(s, s ^ mask) for s in range(256)])  18.4 us
    ppermute x4, starting transfers between devices, lon_step(): return lax.ppermute(value, AXES, pairs)  13.4 us
    unnamed x54, local copies, waits for them, and re-layouts  7.18 us
  transfers between devices with their start and end apart: 27, of which 12 were waited for; matrix products, arithmetic and copies ran while one was open for 0% of the time, Pallas kernels for 20%

profile of v2, /device:TPU:1, one launch (start us, length us, event | category | flops | bytes accessed | tf_op | source)
XLA Modules:
  0.0 136.4 jit_solution(560479570022705087)
XLA Ops:
  0.6 0.7 stack.27.idx_ref
  1.3 8.9 %shard_map.226 = (bf16[48,1152]{1,0:T(8,128)(2,1)}, bf16[48,1152]{1,0:T(8,128)(2,1)}, bf16[48,1152]{1,0:T(8,128)(2,1)}, bf16[48,1152]{1,0:T(8,128)(2,1)}, f32[14...) custom-call(s32[6]{0:T(128)} %stack.27.idx_ref, ...), custom_call_target="tpu_custom_call" | custom-call | tf_op jit(solution)/shard_map/pallas_call | solution.py:564
  10.2 3.3 %collective-permute-start = (bf16[48,1152]{1,0:T(8,128)(2,1)}, bf16[48,1152]{1,0:T(8,128)(2,1)S(1)}, u32[]{:S(2)}, u32[]{:S(2)}) collective-permute-start(bf16[48,1152]{1,0:T(8,128)(2,1)} %get-tuple-element.73), channel_id=1, source_target_pairs={{0,254},{1,255},{2,0},{3,1},{4,2},{5,3},{6,4},{7,5},{8,6},{9,7},{1... | collective-permute-start | bytes 331784 | tf_op jit(solution)/shard_map/ppermute | solution.py:583
  13.5 10.0 %collective-permute-start.2 = (bf16[48,1152]{1,0:T(8,128)(2,1)}, bf16[48,1152]{1,0:T(8,128)(2,1)S(1)}, u32[]{:S(2)}, u32[]{:S(2)}) collective-permute-start(bf16[48,1152]{1,0:T(8,128)(2,1)} %get-tuple-element.75), channel_id=1, source_target_pairs={{0,255},{1,254},{2,1},{3,0},{4,3},{5,2},{6,5},{7,4},{8,7},{9,6},{1... | collective-permute-start | bytes 331784 | tf_op jit(solution)/shard_map/ppermute | solution.py:583
  23.6 6.0 %shard_map.227.bias_ref = f32[2304,256]{1,0:T(8,128)} custom-call(s32[6]{0:T(128)} %stack.27.idx_ref, f32[2,2,16,759]{3,2,1,0:T(8,128)} %tab_ref.3, s32[144,256]{1,0:T(8,128)} %get-tuple-element.76.rel_ref), custom_call_target="tpu_custom_call" | custom-call | tf_op jit(solution)/shard_map/pallas_call | solution.py:564
  29.6 0.6 copy-done.9
  30.2 0.0 copy-done.11
  30.3 8.3 %shard_map.228 = (bf16[48,1024]{1,0:T(8,128)(2,1)}, bf16[48,1024]{1,0:T(8,128)(2,1)}, bf16[48,1024]{1,0:T(8,128)(2,1)}, bf16[48,1024]{1,0:T(8,128)(2,1)}, bf16[1...) custom-call(s32[6]{0:T(128)} %stack.27.idx_ref, ...), custom_call_target="tpu_custom_call" | custom-call | tf_op jit(solution)/shard_map/pallas_call | solution.py:564
  38.5 0.1 collective-permute-start.3
  38.6 0.5 collective-permute-start.4
  39.1 3.5 %shard_map.229 = (bf16[256,2048]{1,0:T(8,128)(2,1)}, bf16[256,2048]{1,0:T(8,128)(2,1)}) custom-call(s32[6]{0:T(128)} %stack.27.idx_ref, bf16[144,512]{1,0:T(8,128)(2,1)} %get-tuple-element.86.h_ref, bf16[144,512]{1,0:T(8,128)(2,1)} %get-tuple-element.87.o_ref, bf16[144,1536]{1,0:T(8,128)(2,1)} %get-tuple-element.88.dqkv_ref, ...), custom_call_target="tpu_custom_call" | custom-call | tf_op jit(solution)/shard_map/pallas_call | solution.py:564
  42.6 1.5 %collective-permute-start.7 = (bf16[256,2048]{1,0:T(8,128)(2,1)}, bf16[256,2048]{1,0:T(8,128)(2,1)S(1)}, u32[]{:S(2)}, u32[]{:S(2)}) collective-permute-start(bf16[256,2048]{1,0:T(8,128)(2,1)} %get-tuple-element.95), channel_id=1, source_target_pairs={{0,2},{1,3},{2,0},{3,1},{4,6},{5,7},{6,4},{7,5},{8,10},{9,11},{10,... | collective-permute-start | bytes 3145736 | tf_op jit(solution)/shard_map/ppermute | solution.py:578
  44.1 0.7 collective-permute-done.5.dia_ref
  44.8 0.6 copy-done.14
  45.4 7.7 %shard_map.230 = (bf16[72,2,512]{2,1,0:T(2,128)(2,1)}, bf16[72,2,512]{2,1,0:T(2,128)(2,1)}, f32[1,512]{1,0:T(1,128)}, f32[2304,128]{1,0:T(8,128)}, f32[2304,128]...) custom-call(s32[6]{0:T(128)} %stack.27.idx_ref, bf16[48,1024]{1,0:T(8,128)(2,1)} %get-tuple-element.77.own_ref, ...), custom_call_target="tpu_custom_call" | custom-call | tf_op jit(solution)/shard_map/pallas_call | solution.py:564
  53.1 4.7 %collective-permute-start.6 = (bf16[256,2048]{1,0:T(8,128)(2,1)}, bf16[256,2048]{1,0:T(8,128)(2,1)S(1)}, u32[]{:S(2)}, u32[]{:S(2)}) collective-permute-start(bf16[256,2048]{1,0:T(8,128)(2,1)} %get-tuple-element.94), channel_id=1, source_target_pairs={{0,2},{1,3},{2,0},{3,1},{4,6},{5,7},{6,4},{7,5},{8,10},{9,11},{10,... | collective-permute-start | bytes 3145736 | tf_op jit(solution)/shard_map/ppermute | solution.py:578
  57.8 2.5 %collective-permute-done.6.r0_ref = bf16[256,2048]{1,0:T(8,128)(2,1)S(1)} collective-permute-done((bf16[256,2048]{1,0:T(8,128)(2,1)}, bf16[256,2048]{1,0:T(8,128)(2,1)S(1)}, u32[]{:S(2)}, u32[]{:S(2)}) %collective-permute-start.6) | collective-permute-done | bytes 1048608 | tf_op jit(solution)/shard_map/ppermute | solution.py:578
  60.3 1.0 copy-done.1
  61.3 3.8 %shard_map.231 = (bf16[128,1536]{1,0:T(8,128)(2,1)}, bf16[128,1536]{1,0:T(8,128)(2,1)}, bf16[256,768]{1,0:T(8,128)(2,1)}, bf16[256,768]{1,0:T(8,128)(2,1)}, bf16...) custom-call(s32[6]{0:T(128)} %stack.27.idx_ref, bf16[256,2048]{1,0:T(8,128)(2,1)} %get-tuple-element.93.k0_ref, ...), custom_call_target="tpu_custom_call" | custom-call | tf_op jit(solution)/shard_map/pallas_call | solution.py:564
  65.1 0.4 collective-permute-start.9
  65.5 10.2 %shard_map.232 = (f32[16,1024]{1,0:T(8,128)}, f32[16,1024]{1,0:T(8,128)}) custom-call(s32[6]{0:T(128)} %stack.27.idx_ref, s32[144,256]{1,0:T(8,128)} %get-tuple-element.76.rel_ref, f32[2304,128]{1,0:T(8,128)} %get-tuple-element.102.d00_ref, f32[2304,128]{1,0:T(8,128)} %get-tuple-element.103.d01_ref, f32[1,512]{1,0:T(1,128)} %get-tuple-element.104.gain0_ref, ...), custom_call_target="tpu_custom_call" | custom-call | tf_op jit(solution)/shard_map/pallas_call | solution.py:564
  75.7 0.6 collective-permute-start.11
  76.3 1.1 collective-permute-done.11.u_ref
  77.5 0.6 copy-done.19
  78.1 0.1 copy-done.4
  78.2 0.2 copy-done.2
  78.3 0.1 copy-done.3
  78.5 2.6 %shard_map.233 = (bf16[128,768]{1,0:T(8,128)(2,1)}, bf16[128,768]{1,0:T(8,128)(2,1)}, bf16[128,768]{1,0:T(8,128)(2,1)}, bf16[160,768]{1,0:T(8,128)(2,1)}, bf16[6...) custom-call(s32[6]{0:T(128)} %stack.27.idx_ref, ...), custom_call_target="tpu_custom_call" | custom-call | tf_op jit(solution)/shard_map/pallas_call | solution.py:564
  81.1 1.8 %collective-permute-start.13 = (bf16[160,768]{1,0:T(8,128)(2,1)}, bf16[160,768]{1,0:T(8,128)(2,1)S(1)}, u32[]{:S(2)}, u32[]{:S(2)}) collective-permute-start(bf16[160,768]{1,0:T(8,128)(2,1)} %get-tuple-element.113), channel_id=1, source_target_pairs={{0,4},{1,5},{2,6},{3,7},{4,0},{5,1},{6,2},{7,3},{8,12},{9,13},{10,... | collective-permute-start | bytes 737288 | tf_op jit(solution)/shard_map/ppermute | solution.py:578
  82.9 1.2 collective-permute-start.12
  84.1 1.7 %collective-permute-start.14 = (bf16[64,1024]{1,0:T(8,128)(2,1)}, bf16[64,1024]{1,0:T(8,128)(2,1)S(1)}, u32[]{:S(2)}, u32[]{:S(2)}) collective-permute-start(bf16[64,1024]{1,0:T(8,128)(2,1)} %get-tuple-element.115), channel_id=1, source_target_pairs={{0,32},{1,33},{2,34},{3,35},{4,36},{5,37},{6,38},{7,39},{8,40},{9,... | collective-permute-start | bytes 393224 | tf_op jit(solution)/shard_map/ppermute | solution.py:578
  85.7 3.1 %collective-permute-done.14.rc_ref = bf16[64,1024]{1,0:T(8,128)(2,1)S(1)} collective-permute-done((bf16[64,1024]{1,0:T(8,128)(2,1)}, bf16[64,1024]{1,0:T(8,128)(2,1)S(1)}, u32[]{:S(2)}, u32[]{:S(2)}) %collective-permute-start.14) | collective-permute-done | bytes 131104 | tf_op jit(solution)/shard_map/ppermute | solution.py:578
  88.8 0.1 collective-permute-done.12.ra_ref
  88.9 0.2 collective-permute-done.13.rb_ref
  89.1 0.3 copy-done.8
  89.4 0.2 copy-done.6
  89.6 0.2 copy-done.5
  89.8 2.3 %shard_map.234 = (bf16[64,768]{1,0:T(8,128)(2,1)}, bf16[64,768]{1,0:T(8,128)(2,1)}, bf16[64,768]{1,0:T(8,128)(2,1)}, bf16[96,768]{1,0:T(8,128)(2,1)}, bf16[64,51...) custom-call(s32[6]{0:T(128)} %stack.27.idx_ref, bf16[128,768]{1,0:T(8,128)(2,1)} %get-tuple-element.110.ka_ref, ...), custom_call_target="tpu_custom_call" | custom-call | tf_op jit(solution)/shard_map/pallas_call | solution.py:564
  92.1 1.7 %collective-permute-start.16 = (bf16[96,768]{1,0:T(8,128)(2,1)}, bf16[96,768]{1,0:T(8,128)(2,1)S(1)}, u32[]{:S(2)}, u32[]{:S(2)}) collective-permute-start(bf16[96,768]{1,0:T(8,128)(2,1)} %get-tuple-element.120), channel_id=1, source_target_pairs={{0,32},{1,33},{2,34},{3,35},{4,36},{5,37},{6,38},{7,39},{8,40},{9,... | collective-permute-start | bytes 442376 | tf_op jit(solution)/shard_map/ppermute | solution.py:578
  93.8 1.1 collective-permute-start.15
  94.9 1.2 collective-permute-start.17
  96.1 2.4 %collective-permute-done.17.rc_ref = bf16[64,512]{1,0:T(8,128)(2,1)S(1)} collective-permute-done((bf16[64,512]{1,0:T(8,128)(2,1)}, bf16[64,512]{1,0:T(8,128)(2,1)S(1)}, u32[]{:S(2)}, u32[]{:S(2)}) %collective-permute-start.17) | collective-permute-done | bytes 65568 | tf_op jit(solution)/shard_map/ppermute | solution.py:578
  98.5 0.6 copy-done.20
  99.1 0.0 copy-done.18
  99.1 0.1 copy-done.7
  99.2 2.0 %shard_map.235 = (bf16[24,2048]{1,0:T(8,128)(2,1)}, bf16[24,2048]{1,0:T(8,128)(2,1)}, bf16[24,2048]{1,0:T(8,128)(2,1)}, bf16[24,2048]{1,0:T(8,128)(2,1)}) custom-call(s32[6]{0:T(128)} %stack.27.idx_ref, bf16[64,768]{1,0:T(8,128)(2,1)} %get-tuple-element.117.ka_ref, bf16[64,768]{1,0:T(8,128)(2,1)} %copy-done.18, bf16[64,768]{1,0:T(8,128)(2,1)} %get-tuple-element.119.kb_ref, ...), custom_call_target="tpu_custom_call" | custom-call | tf_op jit(solution)/shard_map/pallas_call | solution.py:564
  101.1 1.3 collective-permute-start.18
  102.5 4.0 %collective-permute-start.20 = (bf16[24,2048]{1,0:T(8,128)(2,1)}, bf16[24,2048]{1,0:T(8,128)(2,1)S(1)}, u32[]{:S(2)}, u32[]{:S(2)}) collective-permute-start(bf16[24,2048]{1,0:T(8,128)(2,1)} %get-tuple-element.127), channel_id=1, source_target_pairs={{0,224},{1,225},{2,226},{3,227},{4,228},{5,229},{6,230},{7,231},{8... | collective-permute-start | bytes 294920 | tf_op jit(solution)/shard_map/ppermute | solution.py:578
  106.5 0.9 collective-permute-done.19.g2_ref
  107.4 2.5 %collective-permute-done.20.g3_ref = bf16[24,2048]{1,0:T(8,128)(2,1)S(1)} collective-permute-done((bf16[24,2048]{1,0:T(8,128)(2,1)}, bf16[24,2048]{1,0:T(8,128)(2,1)S(1)}, u32[]{:S(2)}, u32[]{:S(2)}) %collective-permute-start.20) | collective-permute-done | bytes 98336 | tf_op jit(solution)/shard_map/ppermute | solution.py:578
  109.9 0.6 copy-done.17
  110.5 1.8 %shard_map.236 = (bf16[24,1024]{1,0:T(8,128)(2,1)}, bf16[24,1024]{1,0:T(8,128)(2,1)}, bf16[24,1024]{1,0:T(8,128)(2,1)}, bf16[24,1024]{1,0:T(8,128)(2,1)}) custom-call(s32[6]{0:T(128)} %stack.27.idx_ref, bf16[24,2048]{1,0:T(8,128)(2,1)} %get-tuple-element.124.own_ref, bf16[24,2048]{1,0:T(8,128)(2,1)} %copy-done.15, bf16[24,2048]{1,0:T(8,128)(2,1)} %copy-done.16, ...), custom_call_target="tpu_custom_call" | custom-call | tf_op jit(solution)/shard_map/pallas_call | solution.py:564
  112.3 3.6 %collective-permute-start.22 = (bf16[24,1024]{1,0:T(8,128)(2,1)}, bf16[24,1024]{1,0:T(8,128)(2,1)S(1)}, u32[]{:S(2)}, u32[]{:S(2)}) collective-permute-start(bf16[24,1024]{1,0:T(8,128)(2,1)} %get-tuple-element.130), channel_id=1, source_target_pairs={{0,16},{1,17},{2,18},{3,19},{4,20},{5,21},{6,22},{7,23},{8,24},{9,... | collective-permute-start | bytes 147464 | tf_op jit(solution)/shard_map/ppermute | solution.py:578
  115.9 2.1 %collective-permute-start.23 = (bf16[24,1024]{1,0:T(8,128)(2,1)}, bf16[24,1024]{1,0:T(8,128)(2,1)S(1)}, u32[]{:S(2)}, u32[]{:S(2)}) collective-permute-start(bf16[24,1024]{1,0:T(8,128)(2,1)} %get-tuple-element.131), channel_id=1, source_target_pairs={{0,24},{1,25},{2,26},{3,27},{4,28},{5,29},{6,30},{7,31},{8,16},{9,... | collective-permute-start | bytes 147464 | tf_op jit(solution)/shard_map/ppermute | solution.py:578
  118.0 1.5 %collective-permute-done.22.g2_ref = bf16[24,1024]{1,0:T(8,128)(2,1)S(1)} collective-permute-done((bf16[24,1024]{1,0:T(8,128)(2,1)}, bf16[24,1024]{1,0:T(8,128)(2,1)S(1)}, u32[]{:S(2)}, u32[]{:S(2)}) %collective-permute-start.22) | collective-permute-done | bytes 49184 | tf_op jit(solution)/shard_map/ppermute | solution.py:578
  119.5 1.8 %collective-permute-done.23.g3_ref = bf16[24,1024]{1,0:T(8,128)(2,1)S(1)} collective-permute-done((bf16[24,1024]{1,0:T(8,128)(2,1)}, bf16[24,1024]{1,0:T(8,128)(2,1)S(1)}, u32[]{:S(2)}, u32[]{:S(2)}) %collective-permute-start.23) | collective-permute-done | bytes 49184 | tf_op jit(solution)/shard_map/ppermute | solution.py:578
  121.2 0.6 copy-done.24
  121.8 1.6 %shard_map.237 = (bf16[24,1024]{1,0:T(8,128)(2,1)}, bf16[16,1024]{1,0:T(8,128)(2,1)}) custom-call(s32[6]{0:T(128)} %stack.27.idx_ref, bf16[24,1024]{1,0:T(8,128)(2,1)} %get-tuple-element.128.own_ref, bf16[24,1024]{1,0:T(8,128)(2,1)} %copy-done.22, bf16[24,1024]{1,0:T(8,128)(2,1)} %copy-done.23, bf16[24,1024]{1,0:T(8,128)(2,1)} %copy-done.24), custom_call_target="tpu_custom_call" | custom-call | tf_op jit(solution)/shard_map/pallas_call | solution.py:564
  123.4 0.7 collective-permute-start.24
  124.2 7.1 %collective-permute-start.26 = (bf16[16,1024]{1,0:T(8,128)(2,1)}, bf16[16,1024]{1,0:T(8,128)(2,1)S(1)}, u32[]{:S(2)}, u32[]{:S(2)}) collective-permute-start(bf16[16,1024]{1,0:T(8,128)(2,1)} %get-tuple-element.133), channel_id=1, source_target_pairs={{0,3},{1,2},{2,1},{3,0},{4,7},{5,6},{6,5},{7,4},{8,11},{9,10},{10,... | collective-permute-start | bytes 98312 | tf_op jit(solution)/shard_map/ppermute | solution.py:578
  131.3 2.3 %collective-permute-done.26.dia_ref = bf16[16,1024]{1,0:T(8,128)(2,1)S(1)} collective-permute-done((bf16[16,1024]{1,0:T(8,128)(2,1)}, bf16[16,1024]{1,0:T(8,128)(2,1)S(1)}, u32[]{:S(2)}, u32[]{:S(2)}) %collective-permute-start.26) | collective-permute-done | bytes 32800 | tf_op jit(solution)/shard_map/ppermute | solution.py:578
  133.6 0.6 copy-done.25
  134.2 0.6 copy-done.21
  134.8 1.6 %shard_map.238 = (f32[2,512]{1,0:T(2,128)}, f32[2,4,1536]{2,1,0:T(4,128)}, f32[2,4,512]{2,1,0:T(4,128)}, f32[2,2,16,759]{3,2,1,0:T(8,128)}) custom-call(s32[6]{0:T(128)} %stack.27.idx_ref, bf16[24,1024]{1,0:T(8,128)(2,1)} %get-tuple-element.132.own_ref, bf16[24,1024]{1,0:T(8,128)(2,1)} %copy-done.21, bf16[16,1024]{1,0:T(8,128)(2,1)} %copy-done.26, ...), custom_call_target="tpu_custom_call" | custom-call | tf_op jit(solution)/shard_map/pallas_call | solution.py:564
  (58 shorter events, 0.2 us)
Async XLA Ops:
  10.2 19.3 %collective-permute-start = (bf16[48,1152]{1,0:T(8,128)(2,1)}, bf16[48,1152]{1,0:T(8,128)(2,1)S(1)}, u32[]{:S(2)}, u32[]{:S(2)}) collective-permute-start(bf16[48,1152]{1,0:T(8,128)(2,1)} %get-tuple-element.73), channel_id=1, source_target_pairs={{0,254},{1,255},{2,0},{3,1},{4,2},{5,3},{6,4},{7,5},{8,6},{9,7},{1... | collective-permute-start | bytes 331784 | tf_op jit(solution)/shard_map/ppermute | solution.py:583
  13.5 16.0 %collective-permute-start.1 = (bf16[48,1152]{1,0:T(8,128)(2,1)}, bf16[48,1152]{1,0:T(8,128)(2,1)S(1)}, u32[]{:S(2)}, u32[]{:S(2)}) collective-permute-start(bf16[48,1152]{1,0:T(8,128)(2,1)} %get-tuple-element.74), channel_id=1, source_target_pairs={{0,1},{1,0},{2,3},{3,2},{4,5},{5,4},{6,7},{7,6},{8,9},{9,8},{10,11... | collective-permute-start | bytes 331784 | tf_op jit(solution)/shard_map/ppermute | solution.py:578
  13.5 16.0 %collective-permute-start.2 = (bf16[48,1152]{1,0:T(8,128)(2,1)}, bf16[48,1152]{1,0:T(8,128)(2,1)S(1)}, u32[]{:S(2)}, u32[]{:S(2)}) collective-permute-start(bf16[48,1152]{1,0:T(8,128)(2,1)} %get-tuple-element.75), channel_id=1, source_target_pairs={{0,255},{1,254},{2,1},{3,0},{4,3},{5,2},{6,5},{7,4},{8,7},{9,6},{1... | collective-permute-start | bytes 331784 | tf_op jit(solution)/shard_map/ppermute | solution.py:583
  29.5 0.6 copy-start.9
  29.6 0.7 copy-start.10
  29.6 0.7 copy-start.11
  38.5 5.5 %collective-permute-start.3 = (bf16[48,1024]{1,0:T(8,128)(2,1)}, bf16[48,1024]{1,0:T(8,128)(2,1)S(1)}, u32[]{:S(2)}, u32[]{:S(2)}) collective-permute-start(bf16[48,1024]{1,0:T(8,128)(2,1)} %get-tuple-element.78), channel_id=1, source_target_pairs={{0,2},{1,3},{2,4},{3,5},{4,6},{5,7},{6,8},{7,9},{8,10},{9,11},{10,... | collective-permute-start | bytes 294920 | tf_op jit(solution)/shard_map/ppermute | solution.py:583
  38.6 5.4 %collective-permute-start.4 = (bf16[48,1024]{1,0:T(8,128)(2,1)}, bf16[48,1024]{1,0:T(8,128)(2,1)S(1)}, u32[]{:S(2)}, u32[]{:S(2)}) collective-permute-start(bf16[48,1024]{1,0:T(8,128)(2,1)} %get-tuple-element.79), channel_id=1, source_target_pairs={{0,1},{1,0},{2,3},{3,2},{4,5},{5,4},{6,7},{7,6},{8,9},{9,8},{10,11... | collective-permute-start | bytes 294920 | tf_op jit(solution)/shard_map/ppermute | solution.py:578
  39.1 5.7 %collective-permute-start.5 = (bf16[48,1024]{1,0:T(8,128)(2,1)}, bf16[48,1024]{1,0:T(8,128)(2,1)S(1)}, u32[]{:S(2)}, u32[]{:S(2)}) collective-permute-start(bf16[48,1024]{1,0:T(8,128)(2,1)} %get-tuple-element.80), channel_id=1, source_target_pairs={{0,3},{1,2},{2,5},{3,4},{4,7},{5,6},{6,9},{7,8},{8,11},{9,10},{10,... | collective-permute-start | bytes 294920 | tf_op jit(solution)/shard_map/ppermute | solution.py:583
  42.6 15.2 %collective-permute-start.7 = (bf16[256,2048]{1,0:T(8,128)(2,1)}, bf16[256,2048]{1,0:T(8,128)(2,1)S(1)}, u32[]{:S(2)}, u32[]{:S(2)}) collective-permute-start(bf16[256,2048]{1,0:T(8,128)(2,1)} %get-tuple-element.95), channel_id=1, source_target_pairs={{0,2},{1,3},{2,0},{3,1},{4,6},{5,7},{6,4},{7,5},{8,10},{9,11},{10,... | collective-permute-start | bytes 3145736 | tf_op jit(solution)/shard_map/ppermute | solution.py:578
  44.0 0.7 copy-start.12
  44.1 0.7 copy-start.13
  44.8 0.6 copy-start.14
  53.1 7.2 %collective-permute-start.6 = (bf16[256,2048]{1,0:T(8,128)(2,1)}, bf16[256,2048]{1,0:T(8,128)(2,1)S(1)}, u32[]{:S(2)}, u32[]{:S(2)}) collective-permute-start(bf16[256,2048]{1,0:T(8,128)(2,1)} %get-tuple-element.94), channel_id=1, source_target_pairs={{0,2},{1,3},{2,0},{3,1},{4,6},{5,7},{6,4},{7,5},{8,10},{9,11},{10,... | collective-permute-start | bytes 3145736 | tf_op jit(solution)/shard_map/ppermute | solution.py:578
  57.8 2.5 %copy-start = (bf16[256,2048]{1,0:T(8,128)(2,1)}, bf16[256,2048]{1,0:T(8,128)(2,1)S(1)}, u32[]{:S(2)}) copy-start(bf16[256,2048]{1,0:T(8,128)(2,1)S(1)} %collective-permute-done.7.r1_ref) | copy-start | bytes 3145732
  60.3 1.0 copy-start.1
  65.1 12.4 %collective-permute-start.8 = (bf16[128,1536]{1,0:T(8,128)(2,1)}, bf16[128,1536]{1,0:T(8,128)(2,1)S(1)}, u32[]{:S(2)}, u32[]{:S(2)}) collective-permute-start(bf16[128,1536]{1,0:T(8,128)(2,1)} %get-tuple-element.97), channel_id=1, source_target_pairs={{0,32},{1,33},{2,34},{3,35},{4,36},{5,37},{6,38},{7,39},{8,40},{9,... | collective-permute-start | bytes 1179656 | tf_op jit(solution)/shard_map/ppermute | solution.py:578
  65.1 12.4 %collective-permute-start.9 = (bf16[256,768]{1,0:T(8,128)(2,1)}, bf16[256,768]{1,0:T(8,128)(2,1)S(1)}, u32[]{:S(2)}, u32[]{:S(2)}) collective-permute-start(bf16[256,768]{1,0:T(8,128)(2,1)} %get-tuple-element.99), channel_id=1, source_target_pairs={{0,1},{1,0},{2,3},{3,2},{4,5},{5,4},{6,7},{7,6},{8,9},{9,8},{10,11... | collective-permute-start | bytes 1179656 | tf_op jit(solution)/shard_map/ppermute | solution.py:578
  65.5 12.0 %collective-permute-start.10 = (bf16[128,1024]{1,0:T(8,128)(2,1)}, bf16[128,1024]{1,0:T(8,128)(2,1)S(1)}, u32[]{:S(2)}, u32[]{:S(2)}) collective-permute-start(bf16[128,1024]{1,0:T(8,128)(2,1)} %get-tuple-element.101), channel_id=1, source_target_pairs={{0,4},{1,5},{2,6},{3,7},{4,0},{5,1},{6,2},{7,3},{8,12},{9,13},{10,... | collective-permute-start | bytes 786440 | tf_op jit(solution)/shard_map/ppermute | solution.py:578
  75.7 1.8 %collective-permute-start.11 = (f32[16,1024]{1,0:T(8,128)}, f32[16,1024]{1,0:T(8,128)S(1)}, u32[]{:S(2)}, u32[]{:S(2)}) collective-permute-start(f32[16,1024]{1,0:T(8,128)} %get-tuple-element.109), channel_id=1, source_target_pairs={{0,2},{1,3},{2,0},{3,1},{4,6},{5,7},{6,4},{7,5},{8,10},{9,11},{10,... | collective-permute-start | bytes 196616 | tf_op jit(solution)/shard_map/ppermute | solution.py:578
  77.5 0.6 copy-start.19
  77.5 0.7 copy-start.4
  77.5 0.9 copy-start.2
  77.5 1.0 copy-start.3
  81.1 8.0 %collective-permute-start.13 = (bf16[160,768]{1,0:T(8,128)(2,1)}, bf16[160,768]{1,0:T(8,128)(2,1)S(1)}, u32[]{:S(2)}, u32[]{:S(2)}) collective-permute-start(bf16[160,768]{1,0:T(8,128)(2,1)} %get-tuple-element.113), channel_id=1, source_target_pairs={{0,4},{1,5},{2,6},{3,7},{4,0},{5,1},{6,2},{7,3},{8,12},{9,13},{10,... | collective-permute-start | bytes 737288 | tf_op jit(solution)/shard_map/ppermute | solution.py:578
  82.9 6.0 %collective-permute-start.12 = (bf16[128,768]{1,0:T(8,128)(2,1)}, bf16[128,768]{1,0:T(8,128)(2,1)S(1)}, u32[]{:S(2)}, u32[]{:S(2)}) collective-permute-start(bf16[128,768]{1,0:T(8,128)(2,1)} %get-tuple-element.111), channel_id=1, source_target_pairs={{0,1},{1,0},{2,3},{3,2},{4,5},{5,4},{6,7},{7,6},{8,9},{9,8},{10,11... | collective-permute-start | bytes 589832 | tf_op jit(solution)/shard_map/ppermute | solution.py:578
  84.1 4.7 %collective-permute-start.14 = (bf16[64,1024]{1,0:T(8,128)(2,1)}, bf16[64,1024]{1,0:T(8,128)(2,1)S(1)}, u32[]{:S(2)}, u32[]{:S(2)}) collective-permute-start(bf16[64,1024]{1,0:T(8,128)(2,1)} %get-tuple-element.115), channel_id=1, source_target_pairs={{0,32},{1,33},{2,34},{3,35},{4,36},{5,37},{6,38},{7,39},{8,40},{9,... | collective-permute-start | bytes 393224 | tf_op jit(solution)/shard_map/ppermute | solution.py:578
  88.8 0.6 copy-start.8
  88.9 0.7 copy-start.6
  89.1 0.7 copy-start.5
  92.1 6.3 %collective-permute-start.16 = (bf16[96,768]{1,0:T(8,128)(2,1)}, bf16[96,768]{1,0:T(8,128)(2,1)S(1)}, u32[]{:S(2)}, u32[]{:S(2)}) collective-permute-start(bf16[96,768]{1,0:T(8,128)(2,1)} %get-tuple-element.120), channel_id=1, source_target_pairs={{0,32},{1,33},{2,34},{3,35},{4,36},{5,37},{6,38},{7,39},{8,40},{9,... | collective-permute-start | bytes 442376 | tf_op jit(solution)/shard_map/ppermute | solution.py:578
  93.8 4.7 %collective-permute-start.15 = (bf16[64,768]{1,0:T(8,128)(2,1)}, bf16[64,768]{1,0:T(8,128)(2,1)S(1)}, u32[]{:S(2)}, u32[]{:S(2)}) collective-permute-start(bf16[64,768]{1,0:T(8,128)(2,1)} %get-tuple-element.118), channel_id=1, source_target_pairs={{0,4},{1,5},{2,6},{3,7},{4,0},{5,1},{6,2},{7,3},{8,12},{9,13},{10,... | collective-permute-start | bytes 294920 | tf_op jit(solution)/shard_map/ppermute | solution.py:578
  94.9 3.5 %collective-permute-start.17 = (bf16[64,512]{1,0:T(8,128)(2,1)}, bf16[64,512]{1,0:T(8,128)(2,1)S(1)}, u32[]{:S(2)}, u32[]{:S(2)}) collective-permute-start(bf16[64,512]{1,0:T(8,128)(2,1)} %get-tuple-element.122), channel_id=1, source_target_pairs={{0,1},{1,0},{2,3},{3,2},{4,5},{5,4},{6,7},{7,6},{8,9},{9,8},{10,11... | collective-permute-start | bytes 196616 | tf_op jit(solution)/shard_map/ppermute | solution.py:578
  98.5 0.6 copy-start.20
  98.5 0.7 copy-start.18
  98.5 0.7 copy-start.7
  101.1 5.4 %collective-permute-start.18 = (bf16[24,2048]{1,0:T(8,128)(2,1)}, bf16[24,2048]{1,0:T(8,128)(2,1)S(1)}, u32[]{:S(2)}, u32[]{:S(2)}) collective-permute-start(bf16[24,2048]{1,0:T(8,128)(2,1)} %get-tuple-element.125), channel_id=1, source_target_pairs={{0,128},{1,129},{2,130},{3,131},{4,132},{5,133},{6,134},{7,135},{8... | collective-permute-start | bytes 294920 | tf_op jit(solution)/shard_map/ppermute | solution.py:578
  102.5 4.9 %collective-permute-start.19 = (bf16[24,2048]{1,0:T(8,128)(2,1)}, bf16[24,2048]{1,0:T(8,128)(2,1)S(1)}, u32[]{:S(2)}, u32[]{:S(2)}) collective-permute-start(bf16[24,2048]{1,0:T(8,128)(2,1)} %get-tuple-element.126), channel_id=1, source_target_pairs={{0,96},{1,97},{2,98},{3,99},{4,100},{5,101},{6,102},{7,103},{8,104... | collective-permute-start | bytes 294920 | tf_op jit(solution)/shard_map/ppermute | solution.py:578
  102.5 7.4 %collective-permute-start.20 = (bf16[24,2048]{1,0:T(8,128)(2,1)}, bf16[24,2048]{1,0:T(8,128)(2,1)S(1)}, u32[]{:S(2)}, u32[]{:S(2)}) collective-permute-start(bf16[24,2048]{1,0:T(8,128)(2,1)} %get-tuple-element.127), channel_id=1, source_target_pairs={{0,224},{1,225},{2,226},{3,227},{4,228},{5,229},{6,230},{7,231},{8... | collective-permute-start | bytes 294920 | tf_op jit(solution)/shard_map/ppermute | solution.py:578
  106.5 3.4 %copy-start.15 = (bf16[24,2048]{1,0:T(8,128)(2,1)}, bf16[24,2048]{1,0:T(8,128)(2,1)S(1)}, u32[]{:S(2)}) copy-start(bf16[24,2048]{1,0:T(8,128)(2,1)S(1)} %collective-permute-done.18.g1_ref) | copy-start | bytes 294916
  107.4 2.5 %copy-start.16 = (bf16[24,2048]{1,0:T(8,128)(2,1)}, bf16[24,2048]{1,0:T(8,128)(2,1)S(1)}, u32[]{:S(2)}) copy-start(bf16[24,2048]{1,0:T(8,128)(2,1)S(1)} %collective-permute-done.19.g2_ref) | copy-start | bytes 294916
  109.9 0.6 copy-start.17
  112.3 5.7 %collective-permute-start.21 = (bf16[24,1024]{1,0:T(8,128)(2,1)}, bf16[24,1024]{1,0:T(8,128)(2,1)S(1)}, u32[]{:S(2)}, u32[]{:S(2)}) collective-permute-start(bf16[24,1024]{1,0:T(8,128)(2,1)} %get-tuple-element.129), channel_id=1, source_target_pairs={{0,8},{1,9},{2,10},{3,11},{4,12},{5,13},{6,14},{7,15},{8,0},{9,1},... | collective-permute-start | bytes 147464 | tf_op jit(solution)/shard_map/ppermute | solution.py:578
  112.3 7.2 %collective-permute-start.22 = (bf16[24,1024]{1,0:T(8,128)(2,1)}, bf16[24,1024]{1,0:T(8,128)(2,1)S(1)}, u32[]{:S(2)}, u32[]{:S(2)}) collective-permute-start(bf16[24,1024]{1,0:T(8,128)(2,1)} %get-tuple-element.130), channel_id=1, source_target_pairs={{0,16},{1,17},{2,18},{3,19},{4,20},{5,21},{6,22},{7,23},{8,24},{9,... | collective-permute-start | bytes 147464 | tf_op jit(solution)/shard_map/ppermute | solution.py:578
  115.9 5.4 %collective-permute-start.23 = (bf16[24,1024]{1,0:T(8,128)(2,1)}, bf16[24,1024]{1,0:T(8,128)(2,1)S(1)}, u32[]{:S(2)}, u32[]{:S(2)}) collective-permute-start(bf16[24,1024]{1,0:T(8,128)(2,1)} %get-tuple-element.131), channel_id=1, source_target_pairs={{0,24},{1,25},{2,26},{3,27},{4,28},{5,29},{6,30},{7,31},{8,16},{9,... | collective-permute-start | bytes 147464 | tf_op jit(solution)/shard_map/ppermute | solution.py:578
  118.0 3.3 %copy-start.22 = (bf16[24,1024]{1,0:T(8,128)(2,1)}, bf16[24,1024]{1,0:T(8,128)(2,1)S(1)}, u32[]{:S(2)}) copy-start(bf16[24,1024]{1,0:T(8,128)(2,1)S(1)} %collective-permute-done.21.g1_ref) | copy-start | bytes 147460
  119.5 1.8 %copy-start.23 = (bf16[24,1024]{1,0:T(8,128)(2,1)}, bf16[24,1024]{1,0:T(8,128)(2,1)S(1)}, u32[]{:S(2)}) copy-start(bf16[24,1024]{1,0:T(8,128)(2,1)S(1)} %collective-permute-done.22.g2_ref) | copy-start | bytes 147460
  121.2 0.6 copy-start.24
  123.4 10.2 %collective-permute-start.24 = (bf16[24,1024]{1,0:T(8,128)(2,1)}, bf16[24,1024]{1,0:T(8,128)(2,1)S(1)}, u32[]{:S(2)}, u32[]{:S(2)}) collective-permute-start(bf16[24,1024]{1,0:T(8,128)(2,1)} %get-tuple-element.132.own_ref), channel_id=1, source_target_pairs={{0,1},{1,0},{2,3},{3,2},{4,5},{5,4},{6,7},{7,6},{8,9},{9,8},{10,11... | collective-permute-start | bytes 147464 | tf_op jit(solution)/shard_map/ppermute | solution.py:578
  124.2 9.4 %collective-permute-start.26 = (bf16[16,1024]{1,0:T(8,128)(2,1)}, bf16[16,1024]{1,0:T(8,128)(2,1)S(1)}, u32[]{:S(2)}, u32[]{:S(2)}) collective-permute-start(bf16[16,1024]{1,0:T(8,128)(2,1)} %get-tuple-element.133), channel_id=1, source_target_pairs={{0,3},{1,2},{2,1},{3,0},{4,7},{5,6},{6,5},{7,4},{8,11},{9,10},{10,... | collective-permute-start | bytes 98312 | tf_op jit(solution)/shard_map/ppermute | solution.py:578
  131.3 2.3 %collective-permute-start.25 = (bf16[16,1024]{1,0:T(8,128)(2,1)}, bf16[16,1024]{1,0:T(8,128)(2,1)S(1)}, u32[]{:S(2)}, u32[]{:S(2)}) collective-permute-start(bf16[16,1024]{1,0:T(8,128)(2,1)} %get-tuple-element.133), channel_id=1, source_target_pairs={{0,2},{1,3},{2,0},{3,1},{4,6},{5,7},{6,4},{7,5},{8,10},{9,11},{10,... | collective-permute-start | bytes 98312 | tf_op jit(solution)/shard_map/ppermute | solution.py:578
  133.6 0.6 copy-start.25
  133.6 0.6 copy-start.26
  134.2 0.6 copy-start.21

commit v3 on v2

--- a/solution.py
+++ b/solution.py
@@ -17,7 +17,7 @@
 NREL = 759
 SCALE = 32 ** (-0.5)
 AXES = ("yh", "x1", "x0", "z2", "z1", "z0", "c", "yl")
-VMEM = 56 << 20
+VMEM = 24 << 20
 
 QUADS = ((1, 1), (1, 0), (0, 1), (0, 0))
 
@@ -129,12 +129,10 @@
     return acc
 
 
-def tail_ids(ids):
-    lane = lax.broadcasted_iota(jnp.int32, (24, 128), 1)
-    total = jnp.where(lane < 16, ids[0:24], 0)
+def side_by_side(tail):
+    total = tail[0:24]
     for k in range(1, 6):
-        piece = jnp.where(lane < 16, ids[24 * k : 24 * (k + 1)], 0)
-        total = total + pltpu.roll(piece, 16 * k, 1)
+        total = total + pltpu.roll(tail[24 * k : 24 * (k + 1)], 16 * k, 1)
     return total
 
 
@@ -155,9 +153,20 @@
     return out
 
 
-def fill_bias(table, rel_ref, words, scales, offsets, store):
+def frame_ids(rel, pm, main_ref, tail_ref):
+    parts = []
+    for part in (rel >> 5, rel & 31):
+        half = dot(pm, part.astype(F32).astype(BF16)).astype(BF16)
+        parts.append(dot_nt(half, pm).astype(jnp.int32))
+    ids = parts[0] * 32 + parts[1]
+    main_ref[...] = ids[:, 0:128]
+    tail = jnp.concatenate([ids[:, 128:144], jnp.zeros((144, 112), jnp.int32)], axis=1)
+    tail_ref[...] = side_by_side(tail)
+
+
+def fill_bias(table, main_ref, tail_ref, words, scales, offsets, store):
     pack_table(table, words, scales, offsets)
-    ids, tails = rel_ref[:, 0:128], tail_ids(rel_ref[:, 128:256])
+    ids, tails = main_ref[...], tail_ref[...]
     for m in range(8):
         head = 4 * (m // 2) + m % 2
         for h, b in zip((head, head + 2), bias_pair(m, words, scales, offsets, ids, tails)):
@@ -186,7 +195,9 @@
     dqkv_ref[:, 1024 + 128 * g : 1024 + 128 * (g + 1)] = dot_tn(p4b, do4)[0:144].astype(BF16)
     ds4 = p4 * (dp4 - jnp.sum(dp4 * p4, axis=-1, keepdims=True))
     ds0_ref[576 * g : 576 * (g + 1), :] = ds4[:, 0:128]
-    ds1_ref[576 * g : 576 * (g + 1), :] = ds4[:, 128:256]
+    for k in range(4):
+        at = 24 * (4 * g + k)
+        ds1_ref[at : at + 24, :] = side_by_side(ds4[144 * k : 144 * (k + 1), 128:256])
     ds4b = ds4.astype(BF16)
     dq = fold_heads(dot(ds4b, kg), masks) * SCALE
     dqkv_ref[:, 128 * g : 128 * (g + 1)] = dq.astype(BF16)
@@ -213,10 +224,20 @@
     core = idx_ref[0]
     p = lax.broadcasted_iota(jnp.int32, (256, 512), 0)
     row = lax.broadcasted_iota(jnp.int32, (256, 512), 1)
+    bit = lambda k: (p >> k) & 1
+    hz, h2, h3 = bit(6), bit(3), bit(2)
+    z1 = h3 ^ (hz & h2)
+    place = (
+        (8, bit(4)),
+        (7, bit(5)),
+        (6, bit(7) ^ bit(5)),
+        (5, h2 ^ (hz & (h2 ^ h3))),
+        (4, z1),
+        (3, z1 ^ hz),
+    )
     base = p & 3
-    base = base + ((((p >> 7) ^ (p >> 5)) & 1) << 6)
-    for at, to in ((6, 3), (5, 7), (4, 8), (3, 5), (2, 4)):
-        base = base + (((p >> at) & 1) << to)
+    for to, value in place:
+        base = base + (value << to)
     for which, ref in ((core, keep_ref), (1 - core, send_ref)):
         pick = jnp.where(row == base + which * 4, 1.0, 0.0).astype(BF16)
         ht = dot_nt(pick, h).astype(BF16)
@@ -226,73 +247,91 @@
 
 
 def first_kernel(
-    idx_ref, x_ref, go_ref, grp_ref, gain_ref, wqkv_ref, wproj_ref, tab_ref, rel_ref,
-    px_ref, ps_ref, pm_ref, rows_ref, cols_ref,
-    own_ref, lon_ref, lat_ref, dia_ref, n_ref, rstd_ref, qkv_ref, p_ref, o_ref, relp_ref,
-    cells, gs, pay, bias, words, scales, offsets,
-):
+    x_hbm, go_hbm, grp_hbm, gain_hbm, wqkv_hbm, wproj_hbm, tab_hbm, rel_hbm, const_hbm,
+    own_ref, lon_ref, lat_ref, dia_ref, n_ref, rstd_ref, qkv_ref, p_ref, o_ref,
+    cells, gs, pay, bias, main_ref, tail_ref, words, scales, offsets,
+    x_ref, go_ref, grp_ref, gain_ref, wqkv_ref, wproj_ref, tab_ref, rel_ref, const_ref, sems,
+):
+    sources = [
+        (rel_hbm, rel_ref),
+        (tab_hbm.at[0, lax.axis_index("yl")], tab_ref),
+        (const_hbm, const_ref),
+        (x_hbm, x_ref),
+        (go_hbm, go_ref),
+        (grp_hbm, grp_ref),
+        (gain_hbm, gain_ref),
+        (wqkv_hbm.at[0], wqkv_ref),
+        (wproj_hbm.at[0], wproj_ref),
+    ]
+    copies = [pltpu.make_async_copy(a, b, sems.at[k]) for k, (a, b) in enumerate(sources)]
+    for copy in copies:
+        copy.start()
+    for copy in copies[0:3]:
+        copy.wait()
+    px, ps, pm = const_ref[0, 0:144, 0:144], const_ref[1, :, 0:144], const_ref[2, 0:144, 0:144]
+    rows, cols = const_ref[3, 0:144, 0:12], const_ref[4, 0:144, 0:12]
+
+    frame_ids(rel_ref[...], pm, main_ref, tail_ref)
+    fill_bias(tab_ref[...], main_ref, tail_ref, words, scales, offsets, bias)
+
     masks = lane_masks()
+    for copy in copies[3:]:
+        copy.wait()
     for k in range(72):
         cells[2 * k : 2 * k + 2, 0:512] = x_ref[k].astype(F32)
         cells[2 * k : 2 * k + 2, 512:1024] = go_ref[k].astype(F32)
-    both = dot(px_ref[...], cells[...].astype(BF16))
+    both = dot(px, cells[...].astype(BF16))
     x = both[:, 0:512]
     pay[:, 512:1024] = both[:, 512:1024].astype(BF16)
     for r in range(6):
         gs[2 * r : 2 * r + 2, :] = grp_ref[r].astype(F32)
-    picked = dot(rows_ref[...], gs[...].astype(BF16)) * cols_ref[...]
+    picked = dot(rows, gs[...].astype(BF16)) * cols.astype(F32)
     group = jnp.sum(picked, axis=-1, keepdims=True)
     pay[:, 1024:1152] = jnp.broadcast_to(group, (144, 128)).astype(BF16)
-
-    rel = rel_ref[...]
-    pm = pm_ref[...]
-    parts = []
-    for part in (rel >> 5, rel & 31):
-        half = dot(pm, part.astype(F32).astype(BF16)).astype(BF16)
-        parts.append(dot_nt(half, pm).astype(jnp.int32))
-    relp_ref[...] = jnp.full((144, 256), 767, jnp.int32)
-    relp_ref[:, 0:144] = parts[0] * 32 + parts[1]
-    fill_bias(tab_ref[0, idx_ref[1]], relp_ref, words, scales, offsets, bias)
 
     n, rstd = normalize(x)
     n_ref[...] = n
     rstd_ref[...] = rstd
     h = (n * gain_ref[0:1, :]).astype(BF16)
-    qkv_ref[...] = dot(h, wqkv_ref[0]).astype(BF16)
+    qkv_ref[...] = dot(h, wqkv_ref[...]).astype(BF16)
     for g in range(4):
         _, _, p4 = group_probs(qkv_ref, g, masks, bias, None)
         p4b = p4.astype(BF16)
         p_ref[576 * g : 576 * (g + 1), :] = p4b
         vg = pad_keys(qkv_ref[:, 1024 + 128 * g : 1024 + 128 * (g + 1)])
         o_ref[:, 128 * g : 128 * (g + 1)] = fold_heads(dot(p4b, vg), masks).astype(BF16)
-    pay[:, 0:512] = (x + dot(o_ref[...], wproj_ref[0])).astype(BF16)
-    out = dot(ps_ref[...], pay[...]).astype(BF16)
+    pay[:, 0:512] = (x + dot(o_ref[...], wproj_ref[...])).astype(BF16)
+    out = dot(ps, pay[...]).astype(BF16)
     own_ref[...] = out[0:48]
     lon_ref[...] = out[48:96]
     lat_ref[...] = out[96:144]
     dia_ref[...] = out[144:192]
 
 
-def bias_kernel(idx_ref, tab_ref, rel_ref, out_ref, words, scales, offsets):
-    fill_bias(tab_ref[0, idx_ref[1]], rel_ref, words, scales, offsets, out_ref)
+def bias_kernel(
+    idx_ref, tab_ref, rel_ref, pm_ref, out_ref, main_ref, tail_ref, words, scales, offsets
+):
+    frame_ids(rel_ref[...], pm_ref[0:144, 0:144], main_ref, tail_ref)
+    fill_bias(tab_ref[0, idx_ref[1]], main_ref, tail_ref, words, scales, offsets, out_ref)
 
 
 def second_kernel(
     idx_ref, own_ref, lon_ref, lat_ref, dia_ref, gain_ref, wqkv_ref, wproj_ref, bias_ref,
-    pf_ref, pft_ref, flags_ref,
+    const_ref,
     oown_ref, olon_ref, olat_ref, odia_ref, h_ref, o_ref, dqkv_ref, g_ref, dgain_ref, ds0_ref, ds1_ref,
     qkv_ref, back,
 ):
     masks = lane_masks()
+    flags = const_ref[2, 0:144, 0:2].astype(F32)
     frame = dot(
-        pf_ref[...], jnp.concatenate([own_ref[...], lon_ref[...], lat_ref[...], dia_ref[...]], axis=0)
+        const_ref[0, 0:144, 0:192], jnp.concatenate([own_ref[...], lon_ref[...], lat_ref[...], dia_ref[...]], axis=0)
     )
     x = frame[:, 0:512]
     g32 = frame[:, 512:1024]
     gb = g32.astype(BF16)
     g_ref[...] = gb
     lat = idx_ref[1].astype(F32)
-    key = frame[:, 1024:1025] * 4.0 + flags_ref[:, 1:2] * (2.0 * lat) + flags_ref[:, 0:1]
+    key = frame[:, 1024:1025] * 4.0 + flags[:, 1:2] * (2.0 * lat) + flags[:, 0:1]
     eye = lax.broadcasted_iota(jnp.int32, (144, 256), 0) == lax.broadcasted_iota(
         jnp.int32, (144, 256), 1
     )
@@ -314,7 +353,7 @@
     back[:, 0:512] = (x + dot(o_ref[...], wproj_ref[0])).astype(BF16)
     df = finish_back(dqkv_ref, wqkv_ref, n, rstd, gain, g32, dgain_ref)
     back[:, 512:1024] = df.astype(BF16)
-    out = dot(pft_ref[...], back[...]).astype(BF16)
+    out = dot(const_ref[1, :, 0:144], back[...]).astype(BF16)
     oown_ref[...] = out[0:48]
     olon_ref[...] = out[48:96]
     olat_ref[...] = out[96:144]
@@ -326,18 +365,16 @@
 
 
 def third_kernel(
-    idx_ref, own_ref, lon_ref, lat_ref, dia_ref, gain_ref, wqkv_ref, wproj_ref,
-    n_ref, rstd_ref, qkv_ref, p_ref, o_ref, pst_ref, cells_ref, pxt_ref, after_ref,
-    out_ref, gin_ref, dgain_ref, ds0_ref, ds1_ref, keep_ref, send_ref,
-    dqkv_ref, outs,
+    idx_ref, own_ref, lon_ref, lat_ref, dia_ref, gain_ref, wproj_ref,
+    n_ref, qkv_ref, p_ref, o_ref, const_ref, after_ref,
+    g_ref, dqkv_ref, ds0_ref, ds1_ref, keep_ref, send_ref,
 ):
     masks = lane_masks()
-    pieces = jnp.concatenate([own_ref[...], lon_ref[...], lat_ref[...], dia_ref[...]], axis=0)
-    outs[:, 0:512] = dot(cells_ref[...], pieces[:, 0:512])
-    g32 = dot(pst_ref[...], pieces[:, 512:1024])
-    gb = g32.astype(BF16)
-    gain = gain_ref[0:1, :]
-    n = n_ref[...]
+    pieces = jnp.concatenate(
+        [r[:, 512:1024] for r in (own_ref, lon_ref, lat_ref, dia_ref)], axis=0
+    )
+    gb = dot(const_ref[0:144, 0:192], pieces).astype(BF16)
+    g_ref[...] = gb
     do = dot_nt(gb, wproj_ref[0]).astype(BF16)
     for g in range(4):
         q4 = stack_heads(qkv_ref[:, 128 * g : 128 * (g + 1)], masks)
@@ -345,37 +382,52 @@
         vg = pad_keys(qkv_ref[:, 1024 + 128 * g : 1024 + 128 * (g + 1)])
         p4b = p_ref[576 * g : 576 * (g + 1), :]
         group_back(g, q4, kg, vg, p4b.astype(F32), p4b, do, masks, dqkv_ref, ds0_ref, ds1_ref)
-    df = finish_back(dqkv_ref, wqkv_ref, n, rstd_ref[...], gain, g32, dgain_ref)
-    outs[:, 512:1024] = dot(pxt_ref[...], df.astype(BF16))
+    h = (n_ref[...] * gain_ref[0:1, :]).astype(BF16)
+    weight_terms(idx_ref, h, o_ref[...], dqkv_ref[...], gb, keep_ref, send_ref)
+
+
+def finish_kernel(
+    own_ref, lon_ref, lat_ref, dia_ref, gain_ref, wqkv_ref, n_ref, rstd_ref, g_ref, dqkv_ref,
+    const_ref, after_ref, out_ref, gin_ref, dgain_ref, outs,
+):
+    pieces = jnp.concatenate([r[:, 0:512] for r in (own_ref, lon_ref, lat_ref, dia_ref)], axis=0)
+    outs[:, 0:512] = dot(const_ref[0, 0:144, 0:192], pieces)
+    df = finish_back(
+        dqkv_ref, wqkv_ref, n_ref[...], rstd_ref[...], gain_ref[0:1, :], g_ref[...].astype(F32), dgain_ref
+    )
+    outs[:, 512:1024] = dot(const_ref[1, 0:144, 0:144], df.astype(BF16))
     for k in range(72):
         out_ref[k] = outs[2 * k : 2 * k + 2, 0:512].astype(BF16)
         gin_ref[k] = outs[2 * k : 2 * k + 2, 512:1024].astype(BF16)
-    h = (n * gain).astype(BF16)
-    weight_terms(idx_ref, h, o_ref[...], dqkv_ref[...], gb, keep_ref, send_ref)
 
 
 def scatter_kernel(
-    idx_ref, rel_ref, d00_ref, d01_ref, gain0_ref, d10_ref, d11_ref, gain1_ref, after_ref,
+    idx_ref, main_ref, tail_ref, m0_ref, t0_ref, gain0_ref, m1_ref, t1_ref, gain1_ref, after_ref,
     keep_ref, send_ref,
 ):
     iota = lax.broadcasted_iota(jnp.int32, (128, 256), 0)
 
-    def body(i, acc):
-        ids = rel_ref[pl.ds(i, 1), :]
-        low, high = ids & 127, ids >> 7
-        hot = jnp.where(iota == low, 1.0, 0.0).astype(BF16)
-        lhs = []
-        for d0_ref, d1_ref in ((d00_ref, d01_ref), (d10_ref, d11_ref)):
-            d = jnp.concatenate(
-                [d0_ref[pl.ds(i, 16, stride=144), :], d1_ref[pl.ds(i, 16, stride=144), :]], axis=1
-            )
-            lhs += [jnp.where(high == k, d, 0.0) for k in range(6)]
-        return acc + dot_nt(jnp.concatenate(lhs, axis=0).astype(BF16), hot)
-
-    acc = lax.fori_loop(0, 144, body, jnp.zeros((192, 128), F32), unroll=8)
+    def add(ids_ref, d_refs, stride, unroll):
+        def body(i, acc):
+            ids = jnp.concatenate([ids_ref[pl.ds(2 * i + k, 1), :] for k in range(2)], axis=1)
+            low, high = ids & 127, ids >> 7
+            hot = jnp.where(iota == low, 1.0, 0.0).astype(BF16)
+            lhs = []
+            for d_ref in d_refs:
+                d = jnp.concatenate(
+                    [d_ref[pl.ds(2 * i + k, 16, stride=stride), :] for k in range(2)], axis=1
+                )
+                lhs += [jnp.where(high == k, d, 0.0) for k in range(6)]
+            return acc + dot_nt(jnp.concatenate(lhs, axis=0).astype(BF16), hot)
+
+        return lambda acc: lax.fori_loop(0, stride // 2, body, acc, unroll=unroll)
+
+    acc = add(main_ref, (m0_ref, m1_ref), 144, 8)(jnp.zeros((192, 128), F32))
+    acc = add(tail_ref, (t0_ref, t1_ref), 24, 12)(acc)
     first = lax.broadcasted_iota(jnp.int32, (8, 256), 0) == 0
     for b, dgain_ref in enumerate((gain0_ref, gain1_ref)):
-        table = jnp.concatenate([acc[96 * b + 16 * k : 96 * b + 16 * k + 16] for k in range(6)], axis=1)
+        table = [acc[96 * b + 16 * k : 96 * b + 16 * k + 16] for k in range(6)]
+        table = jnp.concatenate(table, axis=1)
         halves = []
         for c in range(2):
             gain = jnp.where(first, dgain_ref[:, 256 * c : 256 * (c + 1)], 0.0)
@@ -438,17 +490,13 @@
         keep, send = pick(z0, m[128 * h : 128 * h + 64], m[128 * h + 64 : 128 * h + 128])
         nkb_ref[64 * h : 64 * h + 64, :] = keep.astype(BF16)
         nsb_ref[64 * h : 64 * h + 64, :] = send.astype(BF16)
-    t = t_ref[...] + u_ref[...]
-    t0, t1 = t[0:8], t[8:16]
-    gains = jnp.concatenate([t0[:, 768:1024], t1[:, 768:1024], jnp.zeros((8, 256), F32)], axis=1)
-    table = jnp.concatenate([t0[:, 0:768], t1[:, 0:768], gains, jnp.zeros((8, 768), F32)], axis=0)
-    table = table.astype(BF16)
-    tk_ref[...] = table
-    nsb_ref[128:160, :] = table
     c = kc_ref[...].astype(F32) + rc_ref[...].astype(F32)
     keep, send = pick(x0, c[0:64], c[64:128])
     nkc_ref[...] = keep.astype(BF16)
-    nsc_ref[...] = send.astype(BF16)
+    nsc_ref[0:64, :] = send.astype(BF16)
+    table = (t_ref[...] + u_ref[...]).astype(BF16)
+    tk_ref[...] = table
+    nsc_ref[64:80, :] = table
 
 
 def step_three_kernel(
@@ -459,15 +507,17 @@
     a = ka_ref[...].astype(F32) + ra_ref[...].astype(F32)
     keep, send = pick(z0, a[0:64], a[64:128])
     nka_ref[...] = keep.astype(BF16)
-    nsa_ref[...] = send.astype(BF16)
-    m = kb_ref[...].astype(F32) + rb_ref[0:128, :].astype(F32)
+    nsa_ref[0:64, :] = send.astype(BF16)
+    t = tk_ref[...].astype(F32) + rc_ref[64:80, :].astype(F32)
+    gains = jnp.concatenate([t[0:8, 768:1024], t[8:16, 768:1024], jnp.zeros((8, 256), F32)], axis=1)
+    table = jnp.concatenate([t[:, 0:768], gains, jnp.zeros((8, 768), F32)], axis=0).astype(BF16)
+    ntk_ref[...] = table
+    nsa_ref[64:96, :] = table
+    m = kb_ref[...].astype(F32) + rb_ref[...].astype(F32)
     keep, send = pick(x0, m[0:64], m[64:128])
     nkb_ref[...] = keep.astype(BF16)
-    nsb_ref[0:64, :] = send.astype(BF16)
-    table = (tk_ref[...].astype(F32) + rb_ref[128:160, :].astype(F32)).astype(BF16)
-    ntk_ref[...] = table
-    nsb_ref[64:96, :] = table
-    c = kc_ref[...].astype(F32) + rc_ref[...].astype(F32)
+    nsb_ref[...] = send.astype(BF16)
+    c = kc_ref[...].astype(F32) + rc_ref[0:64, :].astype(F32)
     for b in range(2):
         keep, send = pick(yl, c[:, 512 * b : 512 * b + 256], c[:, 512 * b + 256 : 512 * b + 512])
         nkc_ref[:, 256 * b : 256 * (b + 1)] = keep.astype(BF16)
@@ -478,10 +528,10 @@
     idx_ref, ka_ref, ra_ref, kb_ref, rb_ref, kc_ref, rc_ref, tk_ref, *refs
 ):
     outs, scr = refs[0:4], refs[4]
-    a = ka_ref[...].astype(F32) + ra_ref[...].astype(F32)
-    m = kb_ref[...].astype(F32) + rb_ref[0:64, :].astype(F32)
+    a = ka_ref[...].astype(F32) + ra_ref[0:64, :].astype(F32)
+    m = kb_ref[...].astype(F32) + rb_ref[...].astype(F32)
     c = kc_ref[...].astype(F32) + rc_ref[...].astype(F32)
-    table = tk_ref[...].astype(F32) + rb_ref[64:96, :].astype(F32)
+    table = tk_ref[...].astype(F32) + ra_ref[64:96, :].astype(F32)
     gains = jnp.concatenate([table[16:24, 0:256], table[16:24, 256:512]], axis=0)
     table = jnp.concatenate([table[0:16], gains], axis=1)
     table = jnp.concatenate([table[0:8], table[8:16]], axis=1).astype(BF16)
@@ -497,8 +547,7 @@
         outs[f][16:24, :] = table
 
 
-def plane_kernel(idx_ref, own_ref, g1_ref, g2_ref, g3_ref, *refs):
-    outs, tabs, scr = refs[0:4], refs[4], refs[5]
+def plane_kernel(idx_ref, own_ref, g1_ref, g2_ref, g3_ref, keep_ref, tk_ref, send_ref, tabs):
     got = (own_ref, g1_ref, g2_ref, g3_ref)
     total = got[0][0:16, :].astype(F32)
     for g in got[1:]:
@@ -506,21 +555,29 @@
     for f in range(4):
         tabs[idx_ref[4] ^ f] = got[f][16:24, :].astype(F32)
     table = tabs[0] + tabs[1] + tabs[2] + tabs[3]
+    tk_ref[...] = table.astype(BF16)
+    keep, send = pick(idx_ref[5], total[0:8], total[8:16])
+    keep_ref[...] = keep
+    send_ref[...] = jnp.concatenate([send, table], axis=0).astype(BF16)
+
+
+def ring_kernel(idx_ref, keep_ref, tk_ref, got_ref, nkeep_ref, ntk_ref, send_ref):
+    got = got_ref[...].astype(F32)
+    total = keep_ref[...] + got[0:8]
+    table = tk_ref[...].astype(F32) + got[8:16]
     table = jnp.concatenate([table[:, 0:1024], table[:, 1024:2048]], axis=0)
-    for k in range(4):
-        rows = total[4 * k : 4 * k + 4]
-        rows = jnp.concatenate([rows[:, 0:1024], rows[:, 1024:2048], table], axis=0)
-        scr[k] = rows.astype(BF16)
-    for f in range(4):
-        outs[f][...] = scr[idx_ref[5] ^ f]
-
-
-def ring_kernel(idx_ref, own_ref, g1_ref, g2_ref, g3_ref, out_ref, tab_ref, scr):
-    for f, g in enumerate((own_ref, g1_ref, g2_ref, g3_ref)):
-        scr[idx_ref[5] ^ f] = g[...].astype(F32)
-    total = scr[0] + scr[1] + scr[2] + scr[3]
-    out_ref[...] = total.astype(BF16)
-    tab_ref[...] = total[8:24].astype(BF16)
+    keep, send = pick(idx_ref[6], total[0:4], total[4:8])
+    nkeep_ref[...] = jnp.concatenate([keep[:, 0:1024], keep[:, 1024:2048]], axis=0)
+    ntk_ref[...] = table.astype(BF16)
+    send = [send[:, 0:1024], send[:, 1024:2048], table]
+    send_ref[...] = jnp.concatenate(send, axis=0).astype(BF16)
+
+
+def close_kernel(keep_ref, tk_ref, got_ref, out_ref, tab_ref):
+    got = got_ref[...].astype(F32)
+    table = tk_ref[...].astype(F32) + got[8:24]
+    tab_ref[...] = table.astype(BF16)
+    out_ref[...] = jnp.concatenate([keep_ref[...] + got[0:8], table], axis=0).astype(BF16)
 
 
 def last_kernel(
@@ -557,25 +614,38 @@
 ANY = pl.BlockSpec(memory_space=pl.ANY)
 
 
-def call(body, outs, *args, specs=None, scratch=(), cost=None):
+HBM = pl.BlockSpec(memory_space=pltpu.HBM)
+
+
+def call(body, us, outs, *args, specs=None, scratch=(), sems=0, vmem=VMEM):
     specs = dict(specs or {})
     if args[0].dtype == jnp.int32 and args[0].ndim == 1:
         specs[0] = SMEM
+    scratch = [pltpu.VMEM(s, t) for s, t in scratch]
+    if sems:
+        scratch.append(pltpu.SemaphoreType.DMA((sems,)))
     return pl.pallas_call(
         body,
         grid=(1,),
         in_specs=[specs.get(i, _whole(a.shape)) for i, a in enumerate(args)],
         out_specs=[_whole(s) for s, _ in outs],
         out_shape=[jax.ShapeDtypeStruct(s, t) for s, t in outs],
-        scratch_shapes=[pltpu.VMEM(s, t) for s, t in scratch],
-        compiler_params=pltpu.CompilerParams(vmem_limit_bytes=VMEM),
-        cost_estimate=cost,
+        scratch_shapes=scratch,
+        compiler_params=pltpu.CompilerParams(vmem_limit_bytes=vmem),
+        cost_estimate=pl.CostEstimate(
+            flops=int(us * 1e9), bytes_accessed=int(us * 3.6e6), transcendentals=0
+        ),
     )(*args)
 
 
 def flip(value, *axes):
     mask = sum(1 << (7 - AXES.index(a)) for a in axes)
     return lax.ppermute(value, AXES, [(s, s ^ mask) for s in range(256)])
+
+
+def z_step(value, move):
+    pairs = [(s, s & ~28 | move(s >> 2 & 7) << 2) for s in range(256)]
+    return lax.ppermute(value, AXES, pairs)
 
 
 def lon_step(value, offset, across):
@@ -594,16 +664,23 @@
 
 
 def on_device(inputs, grad_out, gains, qkv_weight, proj_weight, bias_table, rel_ids, groups):
-    T = {k: jnp.asarray(v) for k, v in TABLES.items()}
+    const = np.zeros((11, 192, 256), np.float32)
+    names = ("px", "ps", "pm", "rows", "cols", "pf", "pft", "flags", "pst", "cells", "pxt")
+    for k, name in enumerate(names):
+        part = np.asarray(TABLES[name], np.float32)
+        const[k, : part.shape[0], : part.shape[1]] = part
+    const = const.astype(jnp.bfloat16)
     at = {a: lax.axis_index(a) for a in AXES}
+    hz = at["z0"] ^ at["z1"]
     idx = jnp.stack(
         [
             at["c"],
             at["yl"],
             at["x0"] ^ at["x1"],
-            at["z0"],
+            hz,
             2 * at["x1"] + at["yh"],
-            2 * at["z2"] + at["z1"],
+            at["z2"] ^ (hz & at["z1"]),
+            at["z1"] ^ (hz & (at["z1"] ^ at["z2"])),
         ]
     ).astype(jnp.int32)
     x_cells, go_cells = [v.transpose(0, 2, 3, 1, 4).reshape(72, 2, D) for v in (inputs, grad_out)]
@@ -618,10 +695,12 @@
             first + 2: block(b, (2, HEADS, NREL)),
         }
 
+    id_shapes = [((144, 128), jnp.int32), ((24, 128), jnp.int32)]
     tables = [((8, 768), jnp.int32), ((HEADS, 128), F32), ((HEADS, 128), F32)]
     piece = ((48, 1152), BF16)
-    own, lon, lat, dia, n0, rstd0, qkv0, p0, o0, relp = call(
+    own, lon, lat, dia, n0, rstd0, qkv0, p0, o0 = call(
         first_kernel,
+        8,
         [piece] * 4
         + [
             ((144, D), F32),
@@ -629,25 +708,41 @@
             ((144, 3 * D), BF16),
             ((2304, 256), BF16),
             ((144, D), BF16),
-            ((144, 256), jnp.int32),
         ],
-        idx, x_cells, go_cells, groups.transpose(1, 0, 2), gains, qkv_weight, proj_weight, bias_table, rel_ids,
-        T["px"], T["ps"], T["pm"], T["rows"], T["cols"],
-        specs=weights(0, 5),
-        scratch=[((144, 1024), F32), ((12, 12), F32), ((144, 1152), BF16), ((2304, 256), F32)] + tables,
+        x_cells, go_cells, groups.transpose(1, 0, 2), gains, qkv_weight, proj_weight, bias_table, rel_ids,
+        jnp.asarray(const[0:5]),
+        specs={k: HBM for k in range(9)},
+        scratch=[((144, 1024), F32), ((12, 12), F32), ((144, 1152), BF16), ((2304, 256), F32)]
+        + id_shapes
+        + tables
+        + [
+            ((72, 2, D), BF16),
+            ((72, 2, D), BF16),
+            ((6, 2, 12), jnp.int32),
+            ((2, D), F32),
+            ((D, 3 * D), BF16),
+            ((D, D), BF16),
+            ((HEADS, NREL), F32),
+            ((144, 144), jnp.int32),
+            ((5, 192, 256), BF16),
+        ],
+        sems=9,
+        vmem=57 << 20,
     )
     pieces = halo((own, lon, lat, dia), -1)
-    (bias1,) = call(
+    bias1, ids, tails = call(
         bias_kernel,
-        [((2304, 256), F32)],
-        idx, bias_table, relp,
+        4,
+        [((2304, 256), F32)] + id_shapes,
+        idx, bias_table, rel_ids, jnp.asarray(const[2]),
         specs={1: block(1, (2, HEADS, NREL))},
         scratch=tables,
     )
     back = ((48, 1024), BF16)
-    ds_shape = ((2304, 128), F32)
+    ds_shapes = [((2304, 128), F32), ((384, 128), F32)]
     own, lon, lat, dia, h1, o1, dqkv1, g1, dgain1, ds10, ds11 = call(
         second_kernel,
+        6,
         [back] * 4
         + [
             ((144, D), BF16),
@@ -655,36 +750,43 @@
             ((144, 3 * D), BF16),
             ((144, D), BF16),
             ((1, D), F32),
-            ds_shape,
-            ds_shape,
-        ],
-        idx, *pieces, gains, qkv_weight, proj_weight, bias1, T["pf"], T["pft"], T["flags"],
+        ]
+        + ds_shapes,
+        idx, *pieces, gains, qkv_weight, proj_weight, bias1, jnp.asarray(const[5:8]),
         specs={6: block(1, (D, 3 * D)), 7: block(1, (D, D))},
         scratch=[((144, 3 * D), BF16), ((144, 2 * D), BF16)],
     )
     pieces = halo((own, lon, lat, dia), 1)
     wshape = ((256, 4 * D), BF16)
-    keep1, send1 = call(weights_kernel, [wshape] * 2, idx, h1, o1, dqkv1, g1)
+    keep1, send1 = call(weights_kernel, 2, [wshape] * 2, idx, h1, o1, dqkv1, g1)
     recv1 = flip(send1, "c")
+
+    def pairs(*shapes):
+        return [(s, BF16) for shape in shapes for s in shape]
+
     cells = ((72, 2, D), BF16)
-    outputs, grad_inputs, dgain0, ds00, ds01, keep0, send0 = call(
+    g0, dqkv0, ds00, ds01, keep0, send0 = call(
         third_kernel,
-        [cells, cells, ((1, D), F32), ds_shape, ds_shape, wshape, wshape],
-        idx, *pieces, gains, qkv_weight, proj_weight, n0, rstd0, qkv0, p0, o0,
-        T["pst"], T["cells"], T["pxt"], keep1,
-        specs={6: block(0, (D, 3 * D)), 7: block(0, (D, D)), 16: ANY},
-        scratch=[((144, 3 * D), BF16), ((144, 2 * D), F32)],
+        4,
+        [((144, D), BF16), ((144, 3 * D), BF16)] + ds_shapes + [wshape, wshape],
+        idx, *pieces, gains, proj_weight, n0, qkv0, p0, o0, jnp.asarray(const[8]), keep1,
+        specs={6: block(0, (D, D)), 12: ANY},
+    )
+    recv0 = flip(send0, "c")
+    outputs, grad_inputs, dgain0 = call(
+        finish_kernel,
+        2,
+        [cells, cells, ((1, D), F32)],
+        *pieces, gains, qkv_weight, n0, rstd0, g0, dqkv0, jnp.asarray(const[9:11]), keep0,
+        specs={5: block(0, (D, 3 * D)), 11: ANY},
+        scratch=[((144, 2 * D), F32)],
     )
     outputs, grad_inputs = [
         v.reshape(1, 6, 12, 2, D).transpose(0, 3, 1, 2, 4) for v in (outputs, grad_inputs)
     ]
-    recv0 = flip(send0, "c")
-
-    def pairs(*shapes):
-        return [(s, BF16) for shape in shapes for s in shape]
-
     ka, sa, kb, sb, kc, sc = call(
         core_kernel,
+        1,
         pairs([(128, 1536)] * 2, [(256, 768)] * 2, [(128, 1024)] * 2),
         idx, keep0, recv0, keep1, recv1,
     )
@@ -692,41 +794,52 @@
     tshape = ((16, 1024), F32)
     tkeep, tsend = call(
         scatter_kernel,
+        6,
         [tshape] * 2,
-        idx, relp, ds00, ds01, dgain0, ds10, ds11, dgain1, ka,
-        specs={8: ANY},
+        idx, ids, tails, ds00, ds01, dgain0, ds10, ds11, dgain1, ka,
+        specs={9: ANY},
     )
     trecv = flip(tsend, "c")
     ka, sa, kb, sb, kc, sc, tk = call(
         step_two_kernel,
-        pairs([(128, 768)] * 2, [(128, 768), (160, 768)], [(64, 1024)] * 2, [(32, 768)]),
+        1,
+        pairs([(128, 768)] * 4, [(64, 1024), (80, 1024)], [(16, 1024)]),
         idx, ka, ra, kb, rb, kc, rc, tkeep, trecv,
     )
     ra, rb, rc = flip(sa, "yl"), flip(sb, "z0"), flip(sc, "x0")
     ka, sa, kb, sb, kc, sc, tk = call(
         step_three_kernel,
-        pairs([(64, 768)] * 2, [(64, 768), (96, 768)], [(64, 512)] * 2, [(32, 768)]),
+        1,
+        pairs([(64, 768), (96, 768)], [(64, 768)] * 2, [(64, 512)] * 2, [(32, 768)]),
         idx, ka, ra, kb, rb, kc, rc, tk,
     )
     ra, rb, rc = flip(sa, "z0"), flip(sb, "x0"), flip(sc, "yl")
     parts = call(
         spread_kernel,
+        1,
         [((24, 2048), BF16)] * 4,
         idx, ka, ra, kb, rb, kc, rc, tk,
         scratch=[((4, 16, 2048), BF16)],
     )
-    parts = call(
+    keep, tab, send = call(
         plane_kernel,
-        [((24, 1024), BF16)] * 4,
+        1,
+        [((8, 2048), F32), ((8, 2048), BF16), ((16, 2048), BF16)],
         idx, parts[0], flip(parts[1], "yh"), flip(parts[2], "x1", "x0"),
         flip(parts[3], "x1", "x0", "yh"),
-        scratch=[((4, 8, 2048), F32), ((4, 24, 1024), BF16)],
+        scratch=[((4, 8, 2048), F32)],
+    )
+    keep, tab, send = call(
+        ring_kernel,
+        1,
+        [((8, 1024), F32), ((16, 1024), BF16), ((24, 1024), BF16)],
+        idx, keep, tab, z_step(send, lambda z: (z + 1) % 8 if z & 1 else (z - 1) % 8),
     )
     own, tab = call(
-        ring_kernel,
+        close_kernel,
+        1,
         [((24, 1024), BF16), ((16, 1024), BF16)],
-        idx, parts[0], flip(parts[1], "z1"), flip(parts[2], "z2"), flip(parts[3], "z2", "z1"),
-        scratch=[((4, 24, 1024), F32)],
+        keep, tab, z_step(send, lambda z: z ^ (7 if (z ^ z >> 1) & 1 else 3)),
     )
     from_core = flip(tab, "c")
     from_dia = flip(tab, "c", "yl")
@@ -734,6 +847,7 @@
     factor = 36864 ** (-0.5)
     grad_gains, grad_qkv, grad_proj, grad_bias = call(
         functools.partial(last_kernel, factor),
+        1,
         [
             ((2, D), F32),
             ((2, 4, 3 * D), F32),

time: 137 us -> 109 us (0.80)
  Pallas kernels: 60.1 us -> 35.8 us
  local copies, waits for them, and re-layouts: 7.86 us -> 0.16 us
  waiting for transfers between devices: 19.1 us -> 25.1 us
  starting transfers between devices: 48.5 us -> 47 us
    pallas_call x13 -> x15, Pallas kernels: 60.1 us -> 35.8 us  [call(): pl.pallas_call(body, grid=(1,), in_specs=[specs.get(i, _whole(a.shape)) f...]
    ppermute x0 -> x2, waiting for transfers between devices: none -> 7.27 us  [z_step(): return lax.ppermute(value, AXES, pairs)]
    unnamed x54 -> x30, local copies, waits for them, and re-layouts: 7.18 us -> 0.08 us
    ppermute x23 -> x20, starting transfers between devices: 35.1 us -> 30.5 us  [flip(): return lax.ppermute(value, AXES, [(s, s ^ mask) for s in range(256)])]
    ppermute x0 -> x2, starting transfers between devices: none -> 3.06 us  [z_step(): return lax.ppermute(value, AXES, pairs)]
    ppermute x23 -> x20, waiting for transfers between devices: 18.4 us -> 16.2 us  [flip(): return lax.ppermute(value, AXES, [(s, s ^ mask) for s in range(256)])]
  transfers between devices with their start and end apart: 27 -> 26, of which waited for: 12 -> 13; matrix products, arithmetic and copies ran while one was open for 0% -> 0% of each run, Pallas kernels for 20% -> 15%
where the time goes in v3:
time: 109 us
  starting transfers between devices  47 us (43%)
  Pallas kernels  35.8 us (33%)
  waiting for transfers between devices  25.1 us (23%)
    pallas_call x15, Pallas kernels, call(): pl.pallas_call(body, grid=(1,), in_specs=[specs.get(i, _whole(a.shape)) f...  35.8 us
    ppermute x20, starting transfers between devices, flip(): return lax.ppermute(value, AXES, [(s, s ^ mask) for s in range(256)])  30.5 us
    ppermute x20, waiting for transfers between devices, flip(): return lax.ppermute(value, AXES, [(s, s ^ mask) for s in range(256)])  16.2 us
    ppermute x4, starting transfers between devices, lon_step(): return lax.ppermute(value, AXES, pairs)  13.4 us
    ppermute x2, waiting for transfers between devices, z_step(): return lax.ppermute(value, AXES, pairs)  7.27 us
    ppermute x2, starting transfers between devices, z_step(): return lax.ppermute(value, AXES, pairs)  3.06 us
  transfers between devices with their start and end apart: 26, of which 13 were waited for; matrix products, arithmetic and copies ran while one was open for 0% of the time, Pallas kernels for 15%

profile of v3, /device:TPU:1, one launch (start us, length us, event | category | flops | bytes accessed | tf_op | source)
XLA Modules:
  0.0 109.0 jit_solution(15968138700470959738)
XLA Ops:
  0.7 0.0 copy-start.8
  0.7 8.3 %shard_map.172 = (bf16[48,1152]{1,0:T(8,128)(2,1)}, bf16[48,1152]{1,0:T(8,128)(2,1)}, bf16[48,1152]{1,0:T(8,128)(2,1)}, bf16[48,1152]{1,0:T(8,128)(2,1)}, f32[14...) custom-call(bf16[72,2,512]{2,1,0:T(2,128)(2,1)} %bitcast.20, ...), custom_call_target="tpu_custom_call" | custom-call | flops 8000000000 | bytes 28800000 | tf_op jit(solution)/shard_map/pallas_call | solution.py:627
  9.0 3.3 %collective-permute-start = (bf16[48,1152]{1,0:T(8,128)(2,1)}, bf16[48,1152]{1,0:T(8,128)(2,1)S(1)}, u32[]{:S(2)}, u32[]{:S(2)}) collective-permute-start(bf16[48,1152]{1,0:T(8,128)(2,1)} %get-tuple-element.79), channel_id=1, source_target_pairs={{0,254},{1,255},{2,0},{3,1},{4,2},{5,3},{6,4},{7,5},{8,6},{9,7},{1... | collective-permute-start | bytes 331784 | tf_op jit(solution)/shard_map/ppermute | solution.py:653
  12.3 10.0 %collective-permute-start.2 = (bf16[48,1152]{1,0:T(8,128)(2,1)}, bf16[48,1152]{1,0:T(8,128)(2,1)S(1)}, u32[]{:S(2)}, u32[]{:S(2)}) collective-permute-start(bf16[48,1152]{1,0:T(8,128)(2,1)} %get-tuple-element.81), channel_id=1, source_target_pairs={{0,255},{1,254},{2,1},{3,0},{4,3},{5,2},{6,5},{7,4},{8,7},{9,6},{1... | collective-permute-start | bytes 331784 | tf_op jit(solution)/shard_map/ppermute | solution.py:653
  22.3 0.1 stack.31.idx_ref
  22.4 0.0 copy-start
  22.4 0.0 copy-start.1
  22.4 0.0 copy-start.4
  22.4 0.0 copy-start.5
  22.5 0.0 copy-start.14
  22.5 3.9 %shard_map.173 = (f32[2304,256]{1,0:T(8,128)S(1)}, s32[144,128]{1,0:T(8,128)S(1)}, s32[24,128]{1,0:T(8,128)S(1)}) custom-call(s32[7]{0:T(128)S(1)} %stack.31.idx_ref, f32[2,2,16,759]{3,2,1,0:T(8,128)S(1)} %copy-done.2, s32[144,144]{1,0:T(8,128)S(1)} %copy-done.3, bf16[192,256]{1,0:T(8,128)(2,1)S(1)} %copy-done.8), custom_call_target="tpu_custom_call" | custom-call | flops 4000000000 | bytes 14400000 | tf_op jit(solution)/shard_map/pallas_call | solution.py:627
  26.4 0.0 collective-permute-done.lon_ref
  26.4 0.0 collective-permute-done.1.lat_ref
  26.5 5.6 %shard_map.174 = (bf16[48,1024]{1,0:T(8,128)(2,1)S(1)}, bf16[48,1024]{1,0:T(8,128)(2,1)S(1)}, bf16[48,1024]{1,0:T(8,128)(2,1)S(1)}, bf16[48,1024]{1,0:T(8,128)(2...) custom-call(s32[7]{0:T(128)S(1)} %stack.31.idx_ref, ...), custom_call_target="tpu_custom_call" | custom-call | flops 6000000000 | bytes 21600000 | tf_op jit(solution)/shard_map/pallas_call | solution.py:627
  32.1 0.1 collective-permute-start.3
  32.2 0.5 collective-permute-start.4
  32.6 0.0 collective-permute-start.5
  32.7 0.0 copy-start.13
  32.7 1.8 %shard_map.175 = (bf16[256,2048]{1,0:T(8,128)(2,1)S(1)}, bf16[256,2048]{1,0:T(8,128)(2,1)S(1)}) custom-call(s32[7]{0:T(128)S(1)} %stack.31.idx_ref, bf16[144,512]{1,0:T(8,128)(2,1)S(1)} %get-tuple-element.92.h_ref, bf16[144,512]{1,0:T(8,128)(2,1)S(1)} %get-tuple-element.93.o_ref, bf16[144,1536]{1,0:T(8,128)(2,1)S(1)} %get-tuple-element.94.dqkv_ref, ...), custom_call_target="tpu_custom_call" | custom-call | flops 2000000000 | bytes 7200000 | tf_op jit(solution)/shard_map/pallas_call | solution.py:627
  34.4 1.8 %collective-permute-start.7 = (bf16[256,2048]{1,0:T(8,128)(2,1)S(1)}, bf16[256,2048]{1,0:T(8,128)(2,1)S(1)}, u32[]{:S(2)}, u32[]{:S(2)}) collective-permute-start(bf16[256,2048]{1,0:T(8,128)(2,1)S(1)} %get-tuple-element.103), channel_id=1, source_target_pairs={{0,2},{1,3},{2,0},{3,1},{4,6},{5,7},{6,4},{7,5},{8,10},{9,11},{10,... | collective-permute-start | bytes 3145736 | tf_op jit(solution)/shard_map/ppermute | solution.py:643
  36.2 0.0 collective-permute-done.3.lon_ref
  36.2 0.0 collective-permute-done.4.lat_ref
  36.2 1.6 %collective-permute-done.5.dia_ref = bf16[48,1024]{1,0:T(8,128)(2,1)S(1)} collective-permute-done((bf16[48,1024]{1,0:T(8,128)(2,1)S(1)}, bf16[48,1024]{1,0:T(8,128)(2,1)S(1)}, u32[]{:S(2)}, u32[]{:S(2)}) %collective-permute-start.5) | collective-permute-done | bytes 98336 | tf_op jit(solution)/shard_map/ppermute | solution.py:653
  37.9 0.0 copy-start.6
  37.9 4.2 %shard_map.176 = (bf16[144,512]{1,0:T(8,128)(2,1)S(1)}, bf16[144,1536]{1,0:T(8,128)(2,1)S(1)}, f32[2304,128]{1,0:T(8,128)S(1)}, f32[384,128]{1,0:T(8,128)S(1)}, ...) custom-call(s32[7]{0:T(128)S(1)} %stack.31.idx_ref, bf16[48,1024]{1,0:T(8,128)(2,1)S(1)} %get-tuple-element.83.own_ref, ...), custom_call_target="tpu_custom_call" | custom-call | flops 4000000000 | bytes 14400000 | tf_op jit(solution)/shard_map/pallas_call | solution.py:627
  42.0 5.6 %collective-permute-start.6 = (bf16[256,2048]{1,0:T(8,128)(2,1)S(1)}, bf16[256,2048]{1,0:T(8,128)(2,1)S(1)}, u32[]{:S(2)}, u32[]{:S(2)}) collective-permute-start(bf16[256,2048]{1,0:T(8,128)(2,1)S(1)} %get-tuple-element.102), channel_id=1, source_target_pairs={{0,2},{1,3},{2,0},{3,1},{4,6},{5,7},{6,4},{7,5},{8,10},{9,11},{10,... | collective-permute-start | bytes 3145736 | tf_op jit(solution)/shard_map/ppermute | solution.py:643
  47.7 1.7 %shard_map.177 = (bf16[72,2,512]{2,1,0:T(2,128)(2,1)}, bf16[72,2,512]{2,1,0:T(2,128)(2,1)}, f32[1,512]{1,0:T(1,128)S(1)}) custom-call(bf16[48,1024]{1,0:T(8,128)(2,1)S(1)} %get-tuple-element.83.own_ref, bf16[48,1024]{1,0:T(8,128)(2,1)S(1)} %collective-permute-done.3.lon_ref, bf16[48,1024]{1,0:T(8,128)(2,1)S(1)} %collective-permute-done.4.lat_ref, ...), custom_call_target="tpu_custom_call" | custom-call | flops 2000000000 | bytes 7200000 | tf_op jit(solution)/shard_map/pallas_call | solution.py:627
  49.4 0.6 collective-permute-done.6.r0_ref
  49.9 1.2 %shard_map.178 = (bf16[128,1536]{1,0:T(8,128)(2,1)S(1)}, bf16[128,1536]{1,0:T(8,128)(2,1)S(1)}, bf16[256,768]{1,0:T(8,128)(2,1)S(1)}, bf16[256,768]{1,0:T(8,128)...) custom-call(s32[7]{0:T(128)S(1)} %stack.31.idx_ref, ...), custom_call_target="tpu_custom_call" | custom-call | flops 1000000000 | bytes 3600000 | tf_op jit(solution)/shard_map/pallas_call | solution.py:627
  51.1 0.1 collective-permute-start.10
  51.2 0.1 collective-permute-start.8
  51.3 0.5 collective-permute-start.9
  51.8 4.5 %shard_map.179 = (f32[16,1024]{1,0:T(8,128)S(1)}, f32[16,1024]{1,0:T(8,128)S(1)}) custom-call(s32[7]{0:T(128)S(1)} %stack.31.idx_ref, s32[144,128]{1,0:T(8,128)S(1)} %get-tuple-element.110.main_ref, s32[24,128]{1,0:T(8,128)S(1)} %get-tuple-element.111.tail_ref, f32[2304,128]{1,0:T(8,128)S(1)} %get-tuple-element.112.m0_ref, ...), custom_call_target="tpu_custom_call" | custom-call | flops 6000000000 | bytes 21600000 | tf_op jit(solution)/shard_map/pallas_call | solution.py:627
  56.3 0.7 collective-permute-start.11
  57.1 0.9 collective-permute-done.11.u_ref
  58.0 0.8 collective-permute-done.10.rc_ref
  58.8 2.9 %collective-permute-done.8.ra_ref = bf16[128,1536]{1,0:T(8,128)(2,1)S(1)} collective-permute-done((bf16[128,1536]{1,0:T(8,128)(2,1)S(1)}, bf16[128,1536]{1,0:T(8,128)(2,1)S(1)}, u32[]{:S(2)}, u32[]{:S(2)}) %collective-permute-start.8) | collective-permute-done | bytes 393248 | tf_op jit(solution)/shard_map/ppermute | solution.py:643
  61.7 0.1 collective-permute-done.9.rb_ref
  61.8 0.9 shard_map.180
  62.6 0.5 collective-permute-start.12
  63.1 0.9 collective-permute-start.13
  64.1 1.1 %collective-permute-start.14 = (bf16[80,1024]{1,0:T(8,128)(2,1)S(1)}, bf16[80,1024]{1,0:T(8,128)(2,1)S(1)}, u32[]{:S(2)}, u32[]{:S(2)}) collective-permute-start(bf16[80,1024]{1,0:T(8,128)(2,1)S(1)} %get-tuple-element.125), channel_id=1, source_target_pairs={{0,32},{1,33},{2,34},{3,35},{4,36},{5,37},{6,38},{7,39},{8,40},{9,... | collective-permute-start | bytes 491528 | tf_op jit(solution)/shard_map/ppermute | solution.py:643
  65.2 3.3 %collective-permute-done.14.rc_ref = bf16[80,1024]{1,0:T(8,128)(2,1)S(1)} collective-permute-done((bf16[80,1024]{1,0:T(8,128)(2,1)S(1)}, bf16[80,1024]{1,0:T(8,128)(2,1)S(1)}, u32[]{:S(2)}, u32[]{:S(2)}) %collective-permute-start.14) | collective-permute-done | bytes 163872 | tf_op jit(solution)/shard_map/ppermute | solution.py:643
  68.5 0.7 shard_map.181
  69.2 0.6 collective-permute-start.15
  69.9 1.0 collective-permute-start.16
  70.9 1.1 collective-permute-start.17
  72.0 2.0 %collective-permute-done.17.rc_ref = bf16[64,512]{1,0:T(8,128)(2,1)S(1)} collective-permute-done((bf16[64,512]{1,0:T(8,128)(2,1)S(1)}, bf16[64,512]{1,0:T(8,128)(2,1)S(1)}, u32[]{:S(2)}, u32[]{:S(2)}) %collective-permute-start.17) | collective-permute-done | bytes 65568 | tf_op jit(solution)/shard_map/ppermute | solution.py:643
  74.0 0.0 collective-permute-done.16.rb_ref
  74.0 0.7 shard_map.182
  74.7 1.4 %collective-permute-start.18 = (bf16[24,2048]{1,0:T(8,128)(2,1)S(1)}, bf16[24,2048]{1,0:T(8,128)(2,1)S(1)}, u32[]{:S(2)}, u32[]{:S(2)}) collective-permute-start(bf16[24,2048]{1,0:T(8,128)(2,1)S(1)} %get-tuple-element.135), channel_id=1, source_target_pairs={{0,128},{1,129},{2,130},{3,131},{4,132},{5,133},{6,134},{7,135},{8... | collective-permute-start | bytes 294920 | tf_op jit(solution)/shard_map/ppermute | solution.py:643
  76.1 4.3 %collective-permute-start.20 = (bf16[24,2048]{1,0:T(8,128)(2,1)S(1)}, bf16[24,2048]{1,0:T(8,128)(2,1)S(1)}, u32[]{:S(2)}, u32[]{:S(2)}) collective-permute-start(bf16[24,2048]{1,0:T(8,128)(2,1)S(1)} %get-tuple-element.137), channel_id=1, source_target_pairs={{0,224},{1,225},{2,226},{3,227},{4,228},{5,229},{6,230},{7,231},{8... | collective-permute-start | bytes 294920 | tf_op jit(solution)/shard_map/ppermute | solution.py:643
  80.4 0.3 collective-permute-done.19.g2_ref
  80.7 2.7 %collective-permute-done.20.g3_ref = bf16[24,2048]{1,0:T(8,128)(2,1)S(1)} collective-permute-done((bf16[24,2048]{1,0:T(8,128)(2,1)S(1)}, bf16[24,2048]{1,0:T(8,128)(2,1)S(1)}, u32[]{:S(2)}, u32[]{:S(2)}) %collective-permute-start.20) | collective-permute-done | bytes 98336 | tf_op jit(solution)/shard_map/ppermute | solution.py:643
  83.5 0.6 shard_map.183
  84.1 3.0 %collective-permute-start.21 = (bf16[16,2048]{1,0:T(8,128)(2,1)S(1)}, bf16[16,2048]{1,0:T(8,128)(2,1)S(1)}, u32[]{:S(2)}, u32[]{:S(2)}) collective-permute-start(bf16[16,2048]{1,0:T(8,128)(2,1)S(1)} %get-tuple-element.140), channel_id=1, source_target_pairs={{0,28},{1,29},{2,30},{3,31},{4,8},{5,9},{6,10},{7,11},{8,4},{9,5},... | collective-permute-start | bytes 196616 | tf_op jit(solution)/shard_map/ppermute | solution.py:648
  87.0 2.0 %collective-permute-done.21.got_ref = bf16[16,2048]{1,0:T(8,128)(2,1)S(1)} collective-permute-done((bf16[16,2048]{1,0:T(8,128)(2,1)S(1)}, bf16[16,2048]{1,0:T(8,128)(2,1)S(1)}, u32[]{:S(2)}, u32[]{:S(2)}) %collective-permute-start.21) | collective-permute-done | bytes 65568 | tf_op jit(solution)/shard_map/ppermute | solution.py:648
  89.0 0.6 shard_map.184
  89.6 0.1 collective-permute-start.22
  89.7 5.3 %collective-permute-done.22.got_ref = bf16[24,1024]{1,0:T(8,128)(2,1)S(1)} collective-permute-done((bf16[24,1024]{1,0:T(8,128)(2,1)S(1)}, bf16[24,1024]{1,0:T(8,128)(2,1)S(1)}, u32[]{:S(2)}, u32[]{:S(2)}) %collective-permute-start.22) | collective-permute-done | bytes 49184 | tf_op jit(solution)/shard_map/ppermute | solution.py:648
  95.0 0.9 collective-permute-start.23
  95.9 9.3 %collective-permute-start.25 = (bf16[16,1024]{1,0:T(8,128)(2,1)S(1)}, bf16[16,1024]{1,0:T(8,128)(2,1)S(1)}, u32[]{:S(2)}, u32[]{:S(2)}) collective-permute-start(bf16[16,1024]{1,0:T(8,128)(2,1)S(1)} %get-tuple-element.145), channel_id=1, source_target_pairs={{0,3},{1,2},{2,1},{3,0},{4,7},{5,6},{6,5},{7,4},{8,11},{9,10},{10,... | collective-permute-start | bytes 98312 | tf_op jit(solution)/shard_map/ppermute | solution.py:643
  105.2 2.5 %collective-permute-done.25.dia_ref = bf16[16,1024]{1,0:T(8,128)(2,1)S(1)} collective-permute-done((bf16[16,1024]{1,0:T(8,128)(2,1)S(1)}, bf16[16,1024]{1,0:T(8,128)(2,1)S(1)}, u32[]{:S(2)}, u32[]{:S(2)}) %collective-permute-start.25) | collective-permute-done | bytes 32800 | tf_op jit(solution)/shard_map/ppermute | solution.py:643
  107.7 1.3 %shard_map.186 = (f32[2,512]{1,0:T(2,128)}, f32[2,4,1536]{2,1,0:T(4,128)}, f32[2,4,512]{2,1,0:T(4,128)}, f32[2,2,16,759]{3,2,1,0:T(8,128)}) custom-call(s32[7]{0:T(128)S(1)} %stack.31.idx_ref, bf16[24,1024]{1,0:T(8,128)(2,1)S(1)} %get-tuple-element.144.own_ref, bf16[24,1024]{1,0:T(8,128)(2,1)S(1)} %collective-permute-done.23.lat_ref, ...), custom_call_target="tpu_custom_call" | custom-call | flops 1000000000 | bytes 3600000 | tf_op jit(solution)/shard_map/pallas_call | solution.py:627
  (34 shorter events, 0.1 us)
Async XLA Ops:
  0.6 21.8 %copy-start.2 = (f32[2,2,16,759]{3,2,1,0:T(8,128)S(1)}, f32[2,2,16,759]{3,2,1,0:T(8,128)}, u32[]{:S(2)}) copy-start(f32[2,2,16,759]{3,2,1,0:T(8,128)} %tab_ref.1) | copy-start | bytes 582916
  0.6 21.8 %copy-start.3 = (s32[144,144]{1,0:T(8,128)S(1)}, s32[144,144]{1,0:T(8,128)}, u32[]{:S(2)}) copy-start(s32[144,144]{1,0:T(8,128)} %rel_ref.1) | copy-start | bytes 248836
  0.7 21.7 %copy-start.8 = (bf16[192,256]{1,0:T(8,128)(2,1)S(1)}, bf16[192,256]{1,0:T(8,128)(2,1)}, u32[]{:S(2)}) copy-start(bf16[192,256]{1,0:T(8,128)(2,1)} %constant.43.clone.pm_ref) | copy-start | bytes 294916
  9.0 17.4 %collective-permute-start = (bf16[48,1152]{1,0:T(8,128)(2,1)}, bf16[48,1152]{1,0:T(8,128)(2,1)S(1)}, u32[]{:S(2)}, u32[]{:S(2)}) collective-permute-start(bf16[48,1152]{1,0:T(8,128)(2,1)} %get-tuple-element.79), channel_id=1, source_target_pairs={{0,254},{1,255},{2,0},{3,1},{4,2},{5,3},{6,4},{7,5},{8,6},{9,7},{1... | collective-permute-start | bytes 331784 | tf_op jit(solution)/shard_map/ppermute | solution.py:653
  12.3 14.1 %collective-permute-start.1 = (bf16[48,1152]{1,0:T(8,128)(2,1)}, bf16[48,1152]{1,0:T(8,128)(2,1)S(1)}, u32[]{:S(2)}, u32[]{:S(2)}) collective-permute-start(bf16[48,1152]{1,0:T(8,128)(2,1)} %get-tuple-element.80), channel_id=1, source_target_pairs={{0,1},{1,0},{2,3},{3,2},{4,5},{5,4},{6,7},{7,6},{8,9},{9,8},{10,11... | collective-permute-start | bytes 331784 | tf_op jit(solution)/shard_map/ppermute | solution.py:643
  12.3 14.1 %collective-permute-start.2 = (bf16[48,1152]{1,0:T(8,128)(2,1)}, bf16[48,1152]{1,0:T(8,128)(2,1)S(1)}, u32[]{:S(2)}, u32[]{:S(2)}) collective-permute-start(bf16[48,1152]{1,0:T(8,128)(2,1)} %get-tuple-element.81), channel_id=1, source_target_pairs={{0,255},{1,254},{2,1},{3,0},{4,3},{5,2},{6,5},{7,4},{8,7},{9,6},{1... | collective-permute-start | bytes 331784 | tf_op jit(solution)/shard_map/ppermute | solution.py:653
  22.4 4.0 %copy-start = (bf16[2,512,1536]{2,1,0:T(8,128)(2,1)S(1)}, bf16[2,512,1536]{2,1,0:T(8,128)(2,1)}, u32[]{:S(2)}) copy-start(bf16[2,512,1536]{2,1,0:T(8,128)(2,1)} %wqkv_ref.3) | copy-start | bytes 9437188
  22.4 4.0 %copy-start.1 = (bf16[2,512,512]{2,1,0:T(8,128)(2,1)S(1)}, bf16[2,512,512]{2,1,0:T(8,128)(2,1)}, u32[]{:S(2)}) copy-start(bf16[2,512,512]{2,1,0:T(8,128)(2,1)} %wproj_ref.3) | copy-start | bytes 3145732
  22.4 4.0 %copy-start.4 = (f32[2,512]{1,0:T(2,128)S(1)}, f32[2,512]{1,0:T(2,128)}, u32[]{:S(2)}) copy-start(f32[2,512]{1,0:T(2,128)} %gain_ref.5) | copy-start | bytes 12292
  22.4 4.0 %copy-start.5 = (bf16[3,192,256]{2,1,0:T(8,128)(2,1)S(1)}, bf16[3,192,256]{2,1,0:T(8,128)(2,1)}, u32[]{:S(2)}) copy-start(bf16[3,192,256]{2,1,0:T(8,128)(2,1)} %constant.44.clone.const_ref) | copy-start | bytes 884740
  22.5 4.0 %copy-start.14 = (bf16[48,1152]{1,0:T(8,128)(2,1)S(1)}, bf16[48,1152]{1,0:T(8,128)(2,1)}, u32[]{:S(2)}) copy-start(bf16[48,1152]{1,0:T(8,128)(2,1)} %get-tuple-element.78.own_ref) | copy-start | bytes 331780
  32.1 4.1 %collective-permute-start.3 = (bf16[48,1024]{1,0:T(8,128)(2,1)S(1)}, bf16[48,1024]{1,0:T(8,128)(2,1)S(1)}, u32[]{:S(2)}, u32[]{:S(2)}) collective-permute-start(bf16[48,1024]{1,0:T(8,128)(2,1)S(1)} %get-tuple-element.84), channel_id=1, source_target_pairs={{0,2},{1,3},{2,4},{3,5},{4,6},{5,7},{6,8},{7,9},{8,10},{9,11},{10,... | collective-permute-start | bytes 294920 | tf_op jit(solution)/shard_map/ppermute | solution.py:653
  32.2 4.1 %collective-permute-start.4 = (bf16[48,1024]{1,0:T(8,128)(2,1)S(1)}, bf16[48,1024]{1,0:T(8,128)(2,1)S(1)}, u32[]{:S(2)}, u32[]{:S(2)}) collective-permute-start(bf16[48,1024]{1,0:T(8,128)(2,1)S(1)} %get-tuple-element.85), channel_id=1, source_target_pairs={{0,1},{1,0},{2,3},{3,2},{4,5},{5,4},{6,7},{7,6},{8,9},{9,8},{10,11... | collective-permute-start | bytes 294920 | tf_op jit(solution)/shard_map/ppermute | solution.py:643
  32.6 5.2 %collective-permute-start.5 = (bf16[48,1024]{1,0:T(8,128)(2,1)S(1)}, bf16[48,1024]{1,0:T(8,128)(2,1)S(1)}, u32[]{:S(2)}, u32[]{:S(2)}) collective-permute-start(bf16[48,1024]{1,0:T(8,128)(2,1)S(1)} %get-tuple-element.86), channel_id=1, source_target_pairs={{0,3},{1,2},{2,5},{3,4},{4,7},{5,6},{6,9},{7,8},{8,11},{9,10},{10,... | collective-permute-start | bytes 294920 | tf_op jit(solution)/shard_map/ppermute | solution.py:653
  32.6 5.2 %copy-start.7 = (bf16[192,256]{1,0:T(8,128)(2,1)S(1)}, bf16[192,256]{1,0:T(8,128)(2,1)}, u32[]{:S(2)}) copy-start(bf16[192,256]{1,0:T(8,128)(2,1)} %constant.45.clone.const_ref) | copy-start | bytes 294916
  32.6 5.2 %copy-start.9 = (f32[144,512]{1,0:T(8,128)S(1)}, f32[144,512]{1,0:T(8,128)}, u32[]{:S(2)}) copy-start(f32[144,512]{1,0:T(8,128)} %get-tuple-element.87.n_ref) | copy-start | bytes 884740
  32.7 5.2 %copy-start.11 = (bf16[2304,256]{1,0:T(8,128)(2,1)S(1)}, bf16[2304,256]{1,0:T(8,128)(2,1)}, u32[]{:S(2)}) copy-start(bf16[2304,256]{1,0:T(8,128)(2,1)} %get-tuple-element.90.p_ref) | copy-start | bytes 3538948
  32.7 5.2 %copy-start.12 = (bf16[144,1536]{1,0:T(8,128)(2,1)S(1)}, bf16[144,1536]{1,0:T(8,128)(2,1)}, u32[]{:S(2)}) copy-start(bf16[144,1536]{1,0:T(8,128)(2,1)} %get-tuple-element.89.qkv_ref) | copy-start | bytes 1327108
  32.7 5.2 %copy-start.13 = (bf16[144,512]{1,0:T(8,128)(2,1)S(1)}, bf16[144,512]{1,0:T(8,128)(2,1)}, u32[]{:S(2)}) copy-start(bf16[144,512]{1,0:T(8,128)(2,1)} %get-tuple-element.91.o_ref) | copy-start | bytes 442372
  34.4 14.9 %collective-permute-start.7 = (bf16[256,2048]{1,0:T(8,128)(2,1)S(1)}, bf16[256,2048]{1,0:T(8,128)(2,1)S(1)}, u32[]{:S(2)}, u32[]{:S(2)}) collective-permute-start(bf16[256,2048]{1,0:T(8,128)(2,1)S(1)} %get-tuple-element.103), channel_id=1, source_target_pairs={{0,2},{1,3},{2,0},{3,1},{4,6},{5,7},{6,4},{7,5},{8,10},{9,11},{10,... | collective-permute-start | bytes 3145736 | tf_op jit(solution)/shard_map/ppermute | solution.py:643
  37.9 9.8 %copy-start.6 = (bf16[2,192,256]{2,1,0:T(8,128)(2,1)S(1)}, bf16[2,192,256]{2,1,0:T(8,128)(2,1)}, u32[]{:S(2)}) copy-start(bf16[2,192,256]{2,1,0:T(8,128)(2,1)} %constant.46.clone.const_ref) | copy-start | bytes 589828
  37.9 9.8 %copy-start.10 = (f32[144,1]{1,0:T(8,128)S(1)}, f32[144,1]{1,0:T(8,128)}, u32[]{:S(2)}) copy-start(f32[144,1]{1,0:T(8,128)} %get-tuple-element.88.rstd_ref) | copy-start | bytes 1732
  42.0 7.9 %collective-permute-start.6 = (bf16[256,2048]{1,0:T(8,128)(2,1)S(1)}, bf16[256,2048]{1,0:T(8,128)(2,1)S(1)}, u32[]{:S(2)}, u32[]{:S(2)}) collective-permute-start(bf16[256,2048]{1,0:T(8,128)(2,1)S(1)} %get-tuple-element.102), channel_id=1, source_target_pairs={{0,2},{1,3},{2,0},{3,1},{4,6},{5,7},{6,4},{7,5},{8,10},{9,11},{10,... | collective-permute-start | bytes 3145736 | tf_op jit(solution)/shard_map/ppermute | solution.py:643
  51.1 7.6 %collective-permute-start.10 = (bf16[128,1024]{1,0:T(8,128)(2,1)S(1)}, bf16[128,1024]{1,0:T(8,128)(2,1)S(1)}, u32[]{:S(2)}, u32[]{:S(2)}) collective-permute-start(bf16[128,1024]{1,0:T(8,128)(2,1)S(1)} %get-tuple-element.109), channel_id=1, source_target_pairs={{0,4},{1,5},{2,6},{3,7},{4,0},{5,1},{6,2},{7,3},{8,12},{9,13},{10,... | collective-permute-start | bytes 786440 | tf_op jit(solution)/shard_map/ppermute | solution.py:643
  51.2 10.4 %collective-permute-start.8 = (bf16[128,1536]{1,0:T(8,128)(2,1)S(1)}, bf16[128,1536]{1,0:T(8,128)(2,1)S(1)}, u32[]{:S(2)}, u32[]{:S(2)}) collective-permute-start(bf16[128,1536]{1,0:T(8,128)(2,1)S(1)} %get-tuple-element.105), channel_id=1, source_target_pairs={{0,32},{1,33},{2,34},{3,35},{4,36},{5,37},{6,38},{7,39},{8,40},{9,... | collective-permute-start | bytes 1179656 | tf_op jit(solution)/shard_map/ppermute | solution.py:643
  51.3 10.4 %collective-permute-start.9 = (bf16[256,768]{1,0:T(8,128)(2,1)S(1)}, bf16[256,768]{1,0:T(8,128)(2,1)S(1)}, u32[]{:S(2)}, u32[]{:S(2)}) collective-permute-start(bf16[256,768]{1,0:T(8,128)(2,1)S(1)} %get-tuple-element.107), channel_id=1, source_target_pairs={{0,1},{1,0},{2,3},{3,2},{4,5},{5,4},{6,7},{7,6},{8,9},{9,8},{10,11... | collective-permute-start | bytes 1179656 | tf_op jit(solution)/shard_map/ppermute | solution.py:643
  56.3 1.6 %collective-permute-start.11 = (f32[16,1024]{1,0:T(8,128)S(1)}, f32[16,1024]{1,0:T(8,128)S(1)}, u32[]{:S(2)}, u32[]{:S(2)}) collective-permute-start(f32[16,1024]{1,0:T(8,128)S(1)} %get-tuple-element.119), channel_id=1, source_target_pairs={{0,2},{1,3},{2,0},{3,1},{4,6},{5,7},{6,4},{7,5},{8,10},{9,11},{10,... | collective-permute-start | bytes 196616 | tf_op jit(solution)/shard_map/ppermute | solution.py:643
  62.6 5.9 %collective-permute-start.12 = (bf16[128,768]{1,0:T(8,128)(2,1)S(1)}, bf16[128,768]{1,0:T(8,128)(2,1)S(1)}, u32[]{:S(2)}, u32[]{:S(2)}) collective-permute-start(bf16[128,768]{1,0:T(8,128)(2,1)S(1)} %get-tuple-element.121), channel_id=1, source_target_pairs={{0,1},{1,0},{2,3},{3,2},{4,5},{5,4},{6,7},{7,6},{8,9},{9,8},{10,11... | collective-permute-start | bytes 589832 | tf_op jit(solution)/shard_map/ppermute | solution.py:643
  63.1 5.4 %collective-permute-start.13 = (bf16[128,768]{1,0:T(8,128)(2,1)S(1)}, bf16[128,768]{1,0:T(8,128)(2,1)S(1)}, u32[]{:S(2)}, u32[]{:S(2)}) collective-permute-start(bf16[128,768]{1,0:T(8,128)(2,1)S(1)} %get-tuple-element.123), channel_id=1, source_target_pairs={{0,4},{1,5},{2,6},{3,7},{4,0},{5,1},{6,2},{7,3},{8,12},{9,13},{10,... | collective-permute-start | bytes 589832 | tf_op jit(solution)/shard_map/ppermute | solution.py:643
  64.1 4.5 %collective-permute-start.14 = (bf16[80,1024]{1,0:T(8,128)(2,1)S(1)}, bf16[80,1024]{1,0:T(8,128)(2,1)S(1)}, u32[]{:S(2)}, u32[]{:S(2)}) collective-permute-start(bf16[80,1024]{1,0:T(8,128)(2,1)S(1)} %get-tuple-element.125), channel_id=1, source_target_pairs={{0,32},{1,33},{2,34},{3,35},{4,36},{5,37},{6,38},{7,39},{8,40},{9,... | collective-permute-start | bytes 491528 | tf_op jit(solution)/shard_map/ppermute | solution.py:643
  69.2 4.8 %collective-permute-start.15 = (bf16[96,768]{1,0:T(8,128)(2,1)S(1)}, bf16[96,768]{1,0:T(8,128)(2,1)S(1)}, u32[]{:S(2)}, u32[]{:S(2)}) collective-permute-start(bf16[96,768]{1,0:T(8,128)(2,1)S(1)} %get-tuple-element.128), channel_id=1, source_target_pairs={{0,4},{1,5},{2,6},{3,7},{4,0},{5,1},{6,2},{7,3},{8,12},{9,13},{10,... | collective-permute-start | bytes 442376 | tf_op jit(solution)/shard_map/ppermute | solution.py:643
  69.9 4.2 %collective-permute-start.16 = (bf16[64,768]{1,0:T(8,128)(2,1)S(1)}, bf16[64,768]{1,0:T(8,128)(2,1)S(1)}, u32[]{:S(2)}, u32[]{:S(2)}) collective-permute-start(bf16[64,768]{1,0:T(8,128)(2,1)S(1)} %get-tuple-element.130), channel_id=1, source_target_pairs={{0,32},{1,33},{2,34},{3,35},{4,36},{5,37},{6,38},{7,39},{8,40},{9,... | collective-permute-start | bytes 294920 | tf_op jit(solution)/shard_map/ppermute | solution.py:643
  70.9 3.1 %collective-permute-start.17 = (bf16[64,512]{1,0:T(8,128)(2,1)S(1)}, bf16[64,512]{1,0:T(8,128)(2,1)S(1)}, u32[]{:S(2)}, u32[]{:S(2)}) collective-permute-start(bf16[64,512]{1,0:T(8,128)(2,1)S(1)} %get-tuple-element.132), channel_id=1, source_target_pairs={{0,1},{1,0},{2,3},{3,2},{4,5},{5,4},{6,7},{7,6},{8,9},{9,8},{10,11... | collective-permute-start | bytes 196616 | tf_op jit(solution)/shard_map/ppermute | solution.py:643
  74.7 5.7 %collective-permute-start.18 = (bf16[24,2048]{1,0:T(8,128)(2,1)S(1)}, bf16[24,2048]{1,0:T(8,128)(2,1)S(1)}, u32[]{:S(2)}, u32[]{:S(2)}) collective-permute-start(bf16[24,2048]{1,0:T(8,128)(2,1)S(1)} %get-tuple-element.135), channel_id=1, source_target_pairs={{0,128},{1,129},{2,130},{3,131},{4,132},{5,133},{6,134},{7,135},{8... | collective-permute-start | bytes 294920 | tf_op jit(solution)/shard_map/ppermute | solution.py:643
  76.1 4.7 %collective-permute-start.19 = (bf16[24,2048]{1,0:T(8,128)(2,1)S(1)}, bf16[24,2048]{1,0:T(8,128)(2,1)S(1)}, u32[]{:S(2)}, u32[]{:S(2)}) collective-permute-start(bf16[24,2048]{1,0:T(8,128)(2,1)S(1)} %get-tuple-element.136), channel_id=1, source_target_pairs={{0,96},{1,97},{2,98},{3,99},{4,100},{5,101},{6,102},{7,103},{8,104... | collective-permute-start | bytes 294920 | tf_op jit(solution)/shard_map/ppermute | solution.py:643
  76.1 7.4 %collective-permute-start.20 = (bf16[24,2048]{1,0:T(8,128)(2,1)S(1)}, bf16[24,2048]{1,0:T(8,128)(2,1)S(1)}, u32[]{:S(2)}, u32[]{:S(2)}) collective-permute-start(bf16[24,2048]{1,0:T(8,128)(2,1)S(1)} %get-tuple-element.137), channel_id=1, source_target_pairs={{0,224},{1,225},{2,226},{3,227},{4,228},{5,229},{6,230},{7,231},{8... | collective-permute-start | bytes 294920 | tf_op jit(solution)/shard_map/ppermute | solution.py:643
  84.1 4.9 %collective-permute-start.21 = (bf16[16,2048]{1,0:T(8,128)(2,1)S(1)}, bf16[16,2048]{1,0:T(8,128)(2,1)S(1)}, u32[]{:S(2)}, u32[]{:S(2)}) collective-permute-start(bf16[16,2048]{1,0:T(8,128)(2,1)S(1)} %get-tuple-element.140), channel_id=1, source_target_pairs={{0,28},{1,29},{2,30},{3,31},{4,8},{5,9},{6,10},{7,11},{8,4},{9,5},... | collective-permute-start | bytes 196616 | tf_op jit(solution)/shard_map/ppermute | solution.py:648
  89.6 5.4 %collective-permute-start.22 = (bf16[24,1024]{1,0:T(8,128)(2,1)S(1)}, bf16[24,1024]{1,0:T(8,128)(2,1)S(1)}, u32[]{:S(2)}, u32[]{:S(2)}) collective-permute-start(bf16[24,1024]{1,0:T(8,128)(2,1)S(1)} %get-tuple-element.143), channel_id=1, source_target_pairs={{0,12},{1,13},{2,14},{3,15},{4,24},{5,25},{6,26},{7,27},{8,20},{9,... | collective-permute-start | bytes 147464 | tf_op jit(solution)/shard_map/ppermute | solution.py:648
  95.0 12.7 %collective-permute-start.23 = (bf16[24,1024]{1,0:T(8,128)(2,1)S(1)}, bf16[24,1024]{1,0:T(8,128)(2,1)S(1)}, u32[]{:S(2)}, u32[]{:S(2)}) collective-permute-start(bf16[24,1024]{1,0:T(8,128)(2,1)S(1)} %get-tuple-element.144.own_ref), channel_id=1, source_target_pairs={{0,1},{1,0},{2,3},{3,2},{4,5},{5,4},{6,7},{7,6},{8,9},{9,8},{10,11... | collective-permute-start | bytes 147464 | tf_op jit(solution)/shard_map/ppermute | solution.py:643
  95.9 11.8 %collective-permute-start.25 = (bf16[16,1024]{1,0:T(8,128)(2,1)S(1)}, bf16[16,1024]{1,0:T(8,128)(2,1)S(1)}, u32[]{:S(2)}, u32[]{:S(2)}) collective-permute-start(bf16[16,1024]{1,0:T(8,128)(2,1)S(1)} %get-tuple-element.145), channel_id=1, source_target_pairs={{0,3},{1,2},{2,1},{3,0},{4,7},{5,6},{6,5},{7,4},{8,11},{9,10},{10,... | collective-permute-start | bytes 98312 | tf_op jit(solution)/shard_map/ppermute | solution.py:643
  105.2 2.5 %collective-permute-start.24 = (bf16[16,1024]{1,0:T(8,128)(2,1)S(1)}, bf16[16,1024]{1,0:T(8,128)(2,1)S(1)}, u32[]{:S(2)}, u32[]{:S(2)}) collective-permute-start(bf16[16,1024]{1,0:T(8,128)(2,1)S(1)} %get-tuple-element.145), channel_id=1, source_target_pairs={{0,2},{1,3},{2,0},{3,1},{4,6},{5,7},{6,4},{7,5},{8,10},{9,11},{10,... | collective-permute-start | bytes 98312 | tf_op jit(solution)/shard_map/ppermute | solution.py:643

commit v4 on v3

--- a/solution.py
+++ b/solution.py
@@ -28,12 +28,16 @@
 
 def _tables():
     px = np.zeros((144, 144), np.float32)
-    ps = np.zeros((192, 144), np.float32)
-    pf = np.zeros((144, 192), np.float32)
+    ps = np.zeros((160, 144), np.float32)
+    pf = np.zeros((144, 160), np.float32)
     pm = np.zeros((144, 144), np.float32)
     rows = np.zeros((144, 12), np.float32)
     cols = np.zeros((144, 12), np.float32)
     flags = np.zeros((144, 2), np.float32)
+    into = np.zeros((160, 144), np.float32)
+    spot = np.zeros((144, 128), np.float32)
+    back = np.zeros((144, 160), np.float32)
+    seat = np.zeros((144, 128), np.float32)
     for l in range(2):
         for row in range(6):
             for col in range(12):
@@ -45,27 +49,29 @@
                 cols[t, col] = 1
                 flags[t] = (l, rh)
                 k = QUADS.index((rh, ch))
-                ps[48 * k + (1 - l) * 18 + r * 6 + c, t] = 1
+                i = (1 - l) * 18 + r * 6 + c
+                ps[40 * k + i, t] = 1
+                into[40 * k + 36, t] = 1
+                spot[t, i] = 1
     for k in range(4):
         for i in range(36):
-            pf[36 * k + i, 48 * k + i] = 1
-    bf = jnp.bfloat16
-    return {
-        "px": px.astype(bf),
-        "ps": ps.astype(bf),
-        "pf": pf.astype(bf),
-        "pft": pf.T.copy().astype(bf),
-        "pst": ps.T.copy().astype(bf),
-        "cells": (px.T @ ps.T).astype(bf),
-        "pxt": px.T.copy().astype(bf),
-        "pm": pm.astype(bf),
-        "rows": rows.astype(bf),
-        "cols": cols,
-        "flags": flags,
-    }
-
-
-TABLES = _tables()
+            t = 36 * k + i
+            pf[t, 40 * k + i] = 1
+            back[t, 40 * k + 36] = 1
+            seat[t, i] = 1
+    first = (px, ps, pm, rows, cols, into, spot)
+    second = (pf, pf.T, flags, back, seat)
+    return first, second, (ps.T,), (px.T @ ps.T, px.T)
+
+
+def stacked(parts):
+    out = np.zeros((len(parts), 160, 256), np.float32)
+    for k, part in enumerate(parts):
+        out[k, : part.shape[0], : part.shape[1]] = part
+    return out.astype(jnp.bfloat16)
+
+
+TABLES = [stacked(group) for group in _tables()]
 
 
 def dot(a, b):
@@ -173,15 +179,14 @@
             store[144 * h : 144 * (h + 1), :] = b
 
 
-def group_probs(qkv_ref, g, masks, bias_ref, allowed):
+def group_probs(qkv_ref, g, masks, biases, allowed):
     qg = qkv_ref[:, 128 * g : 128 * (g + 1)]
     kg = pad_keys(qkv_ref[:, 512 + 128 * g : 512 + 128 * (g + 1)])
     q4 = stack_heads(qg, masks)
     s4 = dot_nt(q4, kg) * SCALE
     out = []
     for k in range(4):
-        at = 144 * (4 * g + k)
-        s = s4[144 * k : 144 * (k + 1)] + bias_ref[at : at + 144, :]
+        s = s4[144 * k : 144 * (k + 1)] + biases[k]
         if allowed is not None:
             s = jnp.where(allowed, s, NEGATIVE)
         e = jnp.exp(s - jnp.max(s, axis=-1, keepdims=True))
@@ -192,7 +197,7 @@
 def group_back(g, q4, kg, vg, p4, p4b, do, masks, dqkv_ref, ds0_ref, ds1_ref):
     do4 = stack_heads(do[:, 128 * g : 128 * (g + 1)], masks)
     dp4 = dot_nt(do4, vg)
-    dqkv_ref[:, 1024 + 128 * g : 1024 + 128 * (g + 1)] = dot_tn(p4b, do4)[0:144].astype(BF16)
+    dqkv_ref[:, 1024 + 128 * g : 1024 + 128 * (g + 1)] = dot_tn(p4b[:, 0:144], do4).astype(BF16)
     ds4 = p4 * (dp4 - jnp.sum(dp4 * p4, axis=-1, keepdims=True))
     ds0_ref[576 * g : 576 * (g + 1), :] = ds4[:, 0:128]
     for k in range(4):
@@ -201,7 +206,7 @@
     ds4b = ds4.astype(BF16)
     dq = fold_heads(dot(ds4b, kg), masks) * SCALE
     dqkv_ref[:, 128 * g : 128 * (g + 1)] = dq.astype(BF16)
-    dk = dot_tn(ds4b, q4)[0:144] * SCALE
+    dk = dot_tn(ds4b[:, 0:144], q4) * SCALE
     dqkv_ref[:, 512 + 128 * g : 512 + 128 * (g + 1)] = dk.astype(BF16)
 
 
@@ -225,10 +230,10 @@
     p = lax.broadcasted_iota(jnp.int32, (256, 512), 0)
     row = lax.broadcasted_iota(jnp.int32, (256, 512), 1)
     bit = lambda k: (p >> k) & 1
-    hz, h2, h3 = bit(6), bit(3), bit(2)
+    hz, h2, h3 = bit(6), bit(4), bit(2)
     z1 = h3 ^ (hz & h2)
     place = (
-        (8, bit(4)),
+        (8, bit(3)),
         (7, bit(5)),
         (6, bit(7) ^ bit(5)),
         (5, h2 ^ (hz & (h2 ^ h3))),
@@ -246,10 +251,19 @@
         ref[:, 1536:2048] = dot(ot, g).astype(BF16)
 
 
+def store_pieces(out, *refs):
+    for k, ref in enumerate(refs):
+        ref[...] = out[40 * k : 40 * (k + 1)].astype(BF16)
+
+
+def load_pieces(cols, *refs):
+    return jnp.concatenate([ref[:, cols].astype(F32) for ref in refs], axis=0).astype(BF16)
+
+
 def first_kernel(
     x_hbm, go_hbm, grp_hbm, gain_hbm, wqkv_hbm, wproj_hbm, tab_hbm, rel_hbm, const_hbm,
     own_ref, lon_ref, lat_ref, dia_ref, n_ref, rstd_ref, qkv_ref, p_ref, o_ref,
-    cells, gs, pay, bias, main_ref, tail_ref, words, scales, offsets,
+    cells, gs, pay, bias_ref, main_ref, tail_ref, words, scales, offsets,
     x_ref, go_ref, grp_ref, gain_ref, wqkv_ref, wproj_ref, tab_ref, rel_ref, const_ref, sems,
 ):
     sources = [
@@ -268,14 +282,14 @@
         copy.start()
     for copy in copies[0:3]:
         copy.wait()
-    px, ps, pm = const_ref[0, 0:144, 0:144], const_ref[1, :, 0:144], const_ref[2, 0:144, 0:144]
+    px, ps, pm = [const_ref[k, 0 : (144, 160, 144)[k], 0:144] for k in range(3)]
     rows, cols = const_ref[3, 0:144, 0:12], const_ref[4, 0:144, 0:12]
 
     frame_ids(rel_ref[...], pm, main_ref, tail_ref)
-    fill_bias(tab_ref[...], main_ref, tail_ref, words, scales, offsets, bias)
+    fill_bias(tab_ref[...], main_ref, tail_ref, words, scales, offsets, bias_ref)
 
     masks = lane_masks()
-    for copy in copies[3:]:
+    for copy in copies[3:8]:
         copy.wait()
     for k in range(72):
         cells[2 * k : 2 * k + 2, 0:512] = x_ref[k].astype(F32)
@@ -287,7 +301,8 @@
         gs[2 * r : 2 * r + 2, :] = grp_ref[r].astype(F32)
     picked = dot(rows, gs[...].astype(BF16)) * cols.astype(F32)
     group = jnp.sum(picked, axis=-1, keepdims=True)
-    pay[:, 1024:1152] = jnp.broadcast_to(group, (144, 128)).astype(BF16)
+    spots = (group * const_ref[6, 0:144, 0:128].astype(F32)).astype(BF16)
+    group_rows = dot(const_ref[5, :, 0:144], spots)
 
     n, rstd = normalize(x)
     n_ref[...] = n
@@ -295,17 +310,17 @@
     h = (n * gain_ref[0:1, :]).astype(BF16)
     qkv_ref[...] = dot(h, wqkv_ref[...]).astype(BF16)
     for g in range(4):
-        _, _, p4 = group_probs(qkv_ref, g, masks, bias, None)
+        biases = [bias_ref[576 * g + 144 * k : 576 * g + 144 * (k + 1), :] for k in range(4)]
+        _, _, p4 = group_probs(qkv_ref, g, masks, biases, None)
         p4b = p4.astype(BF16)
         p_ref[576 * g : 576 * (g + 1), :] = p4b
         vg = pad_keys(qkv_ref[:, 1024 + 128 * g : 1024 + 128 * (g + 1)])
         o_ref[:, 128 * g : 128 * (g + 1)] = fold_heads(dot(p4b, vg), masks).astype(BF16)
+    copies[8].wait()
     pay[:, 0:512] = (x + dot(o_ref[...], wproj_ref[...])).astype(BF16)
-    out = dot(ps, pay[...]).astype(BF16)
-    own_ref[...] = out[0:48]
-    lon_ref[...] = out[48:96]
-    lat_ref[...] = out[96:144]
-    dia_ref[...] = out[144:192]
+    out = dot(ps, pay[...])
+    out = jnp.concatenate([out[:, 0:128] + group_rows, out[:, 128:1024]], axis=1)
+    store_pieces(out, own_ref, lon_ref, lat_ref, dia_ref)
 
 
 def bias_kernel(
@@ -323,15 +338,16 @@
 ):
     masks = lane_masks()
     flags = const_ref[2, 0:144, 0:2].astype(F32)
-    frame = dot(
-        const_ref[0, 0:144, 0:192], jnp.concatenate([own_ref[...], lon_ref[...], lat_ref[...], dia_ref[...]], axis=0)
-    )
+    pieces = load_pieces(slice(0, 1024), own_ref, lon_ref, lat_ref, dia_ref)
+    frame = dot(const_ref[0, 0:144, 0:160], pieces)
+    group = dot(const_ref[3, 0:144, 0:160], pieces[:, 0:128]) * const_ref[4, 0:144, 0:128].astype(F32)
+    group = jnp.sum(group, axis=-1, keepdims=True)
     x = frame[:, 0:512]
     g32 = frame[:, 512:1024]
     gb = g32.astype(BF16)
     g_ref[...] = gb
     lat = idx_ref[1].astype(F32)
-    key = frame[:, 1024:1025] * 4.0 + flags[:, 1:2] * (2.0 * lat) + flags[:, 0:1]
+    key = group * 4.0 + flags[:, 1:2] * (2.0 * lat) + flags[:, 0:1]
     eye = lax.broadcasted_iota(jnp.int32, (144, 256), 0) == lax.broadcasted_iota(
         jnp.int32, (144, 256), 1
     )
@@ -345,7 +361,8 @@
     qkv_ref[...] = dot(h, wqkv_ref[0]).astype(BF16)
     do = dot_nt(gb, wproj_ref[0]).astype(BF16)
     for g in range(4):
-        q4, kg, p4 = group_probs(qkv_ref, g, masks, bias_ref, allowed)
+        biases = [bias_ref[576 * g + 144 * k : 576 * g + 144 * (k + 1), :] for k in range(4)]
+        q4, kg, p4 = group_probs(qkv_ref, g, masks, biases, allowed)
         p4b = p4.astype(BF16)
         vg = pad_keys(qkv_ref[:, 1024 + 128 * g : 1024 + 128 * (g + 1)])
         o_ref[:, 128 * g : 128 * (g + 1)] = fold_heads(dot(p4b, vg), masks).astype(BF16)
@@ -353,11 +370,7 @@
     back[:, 0:512] = (x + dot(o_ref[...], wproj_ref[0])).astype(BF16)
     df = finish_back(dqkv_ref, wqkv_ref, n, rstd, gain, g32, dgain_ref)
     back[:, 512:1024] = df.astype(BF16)
-    out = dot(const_ref[1, :, 0:144], back[...]).astype(BF16)
-    oown_ref[...] = out[0:48]
-    olon_ref[...] = out[48:96]
-    olat_ref[...] = out[96:144]
-    odia_ref[...] = out[144:192]
+    store_pieces(dot(const_ref[1, :, 0:144], back[...]), oown_ref, olon_ref, olat_ref, odia_ref)
 
 
 def weights_kernel(idx_ref, h_ref, o_ref, dqkv_ref, g_ref, keep_ref, send_ref):
@@ -370,10 +383,8 @@
     g_ref, dqkv_ref, ds0_ref, ds1_ref, keep_ref, send_ref,
 ):
     masks = lane_masks()
-    pieces = jnp.concatenate(
-        [r[:, 512:1024] for r in (own_ref, lon_ref, lat_ref, dia_ref)], axis=0
-    )
-    gb = dot(const_ref[0:144, 0:192], pieces).astype(BF16)
+    pieces = load_pieces(slice(512, 1024), own_ref, lon_ref, lat_ref, dia_ref)
+    gb = dot(const_ref[0, 0:144, 0:160], pieces).astype(BF16)
     g_ref[...] = gb
     do = dot_nt(gb, wproj_ref[0]).astype(BF16)
     for g in range(4):
@@ -390,8 +401,8 @@
     own_ref, lon_ref, lat_ref, dia_ref, gain_ref, wqkv_ref, n_ref, rstd_ref, g_ref, dqkv_ref,
     const_ref, after_ref, out_ref, gin_ref, dgain_ref, outs,
 ):
-    pieces = jnp.concatenate([r[:, 0:512] for r in (own_ref, lon_ref, lat_ref, dia_ref)], axis=0)
-    outs[:, 0:512] = dot(const_ref[0, 0:144, 0:192], pieces)
+    pieces = load_pieces(slice(0, 512), own_ref, lon_ref, lat_ref, dia_ref)
+    outs[:, 0:512] = dot(const_ref[0, 0:144, 0:160], pieces)
     df = finish_back(
         dqkv_ref, wqkv_ref, n_ref[...], rstd_ref[...], gain_ref[0:1, :], g_ref[...].astype(F32), dgain_ref
     )
@@ -547,7 +558,8 @@
         outs[f][16:24, :] = table
 
 
-def plane_kernel(idx_ref, own_ref, g1_ref, g2_ref, g3_ref, keep_ref, tk_ref, send_ref, tabs):
+def plane_kernel(idx_ref, own_ref, g1_ref, g2_ref, g3_ref, *refs):
+    outs, tabs, scr = refs[0:4], refs[4], refs[5]
     got = (own_ref, g1_ref, g2_ref, g3_ref)
     total = got[0][0:16, :].astype(F32)
     for g in got[1:]:
@@ -555,29 +567,21 @@
     for f in range(4):
         tabs[idx_ref[4] ^ f] = got[f][16:24, :].astype(F32)
     table = tabs[0] + tabs[1] + tabs[2] + tabs[3]
-    tk_ref[...] = table.astype(BF16)
-    keep, send = pick(idx_ref[5], total[0:8], total[8:16])
-    keep_ref[...] = keep
-    send_ref[...] = jnp.concatenate([send, table], axis=0).astype(BF16)
-
-
-def ring_kernel(idx_ref, keep_ref, tk_ref, got_ref, nkeep_ref, ntk_ref, send_ref):
-    got = got_ref[...].astype(F32)
-    total = keep_ref[...] + got[0:8]
-    table = tk_ref[...].astype(F32) + got[8:16]
     table = jnp.concatenate([table[:, 0:1024], table[:, 1024:2048]], axis=0)
-    keep, send = pick(idx_ref[6], total[0:4], total[4:8])
-    nkeep_ref[...] = jnp.concatenate([keep[:, 0:1024], keep[:, 1024:2048]], axis=0)
-    ntk_ref[...] = table.astype(BF16)
-    send = [send[:, 0:1024], send[:, 1024:2048], table]
-    send_ref[...] = jnp.concatenate(send, axis=0).astype(BF16)
-
-
-def close_kernel(keep_ref, tk_ref, got_ref, out_ref, tab_ref):
-    got = got_ref[...].astype(F32)
-    table = tk_ref[...].astype(F32) + got[8:24]
-    tab_ref[...] = table.astype(BF16)
-    out_ref[...] = jnp.concatenate([keep_ref[...] + got[0:8], table], axis=0).astype(BF16)
+    for k in range(4):
+        rows = total[4 * k : 4 * k + 4]
+        rows = jnp.concatenate([rows[:, 0:1024], rows[:, 1024:2048], table], axis=0)
+        scr[k] = rows.astype(BF16)
+    for f in range(4):
+        outs[f][...] = scr[idx_ref[5] ^ f]
+
+
+def close_kernel(idx_ref, own_ref, g1_ref, g2_ref, g3_ref, out_ref, tab_ref, scr):
+    for f, g in enumerate((own_ref, g1_ref, g2_ref, g3_ref)):
+        scr[idx_ref[5] ^ f] = g[...].astype(F32)
+    total = scr[0] + scr[1] + scr[2] + scr[3]
+    out_ref[...] = total.astype(BF16)
+    tab_ref[...] = total[8:24].astype(BF16)
 
 
 def last_kernel(
@@ -638,13 +642,16 @@
     )(*args)
 
 
+def mask_of(axes):
+    return sum(1 << (7 - AXES.index(a)) for a in axes)
+
+
 def flip(value, *axes):
-    mask = sum(1 << (7 - AXES.index(a)) for a in axes)
-    return lax.ppermute(value, AXES, [(s, s ^ mask) for s in range(256)])
-
-
-def z_step(value, move):
-    pairs = [(s, s & ~28 | move(s >> 2 & 7) << 2) for s in range(256)]
+    return lax.ppermute(value, AXES, [(s, s ^ mask_of(axes)) for s in range(256)])
+
+
+def z_step(value, move, *axes):
+    pairs = [(s, (s & ~28 | move(s >> 2 & 7) << 2) ^ mask_of(axes)) for s in range(256)]
     return lax.ppermute(value, AXES, pairs)
 
 
@@ -664,12 +671,7 @@
 
 
 def on_device(inputs, grad_out, gains, qkv_weight, proj_weight, bias_table, rel_ids, groups):
-    const = np.zeros((11, 192, 256), np.float32)
-    names = ("px", "ps", "pm", "rows", "cols", "pf", "pft", "flags", "pst", "cells", "pxt")
-    for k, name in enumerate(names):
-        part = np.asarray(TABLES[name], np.float32)
-        const[k, : part.shape[0], : part.shape[1]] = part
-    const = const.astype(jnp.bfloat16)
+    first_const, second_const, third_const, finish_const = [jnp.asarray(t) for t in TABLES]
     at = {a: lax.axis_index(a) for a in AXES}
     hz = at["z0"] ^ at["z1"]
     idx = jnp.stack(
@@ -678,9 +680,8 @@
             at["yl"],
             at["x0"] ^ at["x1"],
             hz,
-            2 * at["x1"] + at["yh"],
-            at["z2"] ^ (hz & at["z1"]),
-            at["z1"] ^ (hz & (at["z1"] ^ at["z2"])),
+            2 * at["x1"] + (at["z2"] ^ (hz & at["z1"])),
+            2 * at["yh"] + (at["z1"] ^ (hz & (at["z1"] ^ at["z2"]))),
         ]
     ).astype(jnp.int32)
     x_cells, go_cells = [v.transpose(0, 2, 3, 1, 4).reshape(72, 2, D) for v in (inputs, grad_out)]
@@ -697,7 +698,7 @@
 
     id_shapes = [((144, 128), jnp.int32), ((24, 128), jnp.int32)]
     tables = [((8, 768), jnp.int32), ((HEADS, 128), F32), ((HEADS, 128), F32)]
-    piece = ((48, 1152), BF16)
+    piece = ((40, 1024), BF16)
     own, lon, lat, dia, n0, rstd0, qkv0, p0, o0 = call(
         first_kernel,
         8,
@@ -710,9 +711,9 @@
             ((144, D), BF16),
         ],
         x_cells, go_cells, groups.transpose(1, 0, 2), gains, qkv_weight, proj_weight, bias_table, rel_ids,
-        jnp.asarray(const[0:5]),
+        first_const,
         specs={k: HBM for k in range(9)},
-        scratch=[((144, 1024), F32), ((12, 12), F32), ((144, 1152), BF16), ((2304, 256), F32)]
+        scratch=[((144, 1024), F32), ((12, 12), F32), ((144, 1024), BF16), ((2304, 256), F32)]
         + id_shapes
         + tables
         + [
@@ -724,7 +725,7 @@
             ((D, D), BF16),
             ((HEADS, NREL), F32),
             ((144, 144), jnp.int32),
-            ((5, 192, 256), BF16),
+            ((7, 160, 256), BF16),
         ],
         sems=9,
         vmem=57 << 20,
@@ -734,16 +735,15 @@
         bias_kernel,
         4,
         [((2304, 256), F32)] + id_shapes,
-        idx, bias_table, rel_ids, jnp.asarray(const[2]),
+        idx, bias_table, rel_ids, jnp.asarray(TABLES[0][2]),
         specs={1: block(1, (2, HEADS, NREL))},
         scratch=tables,
     )
-    back = ((48, 1024), BF16)
     ds_shapes = [((2304, 128), F32), ((384, 128), F32)]
     own, lon, lat, dia, h1, o1, dqkv1, g1, dgain1, ds10, ds11 = call(
         second_kernel,
         6,
-        [back] * 4
+        [piece] * 4
         + [
             ((144, D), BF16),
             ((144, D), BF16),
@@ -752,7 +752,7 @@
             ((1, D), F32),
         ]
         + ds_shapes,
-        idx, *pieces, gains, qkv_weight, proj_weight, bias1, jnp.asarray(const[5:8]),
+        idx, *pieces, gains, qkv_weight, proj_weight, bias1, second_const,
         specs={6: block(1, (D, 3 * D)), 7: block(1, (D, D))},
         scratch=[((144, 3 * D), BF16), ((144, 2 * D), BF16)],
     )
@@ -769,7 +769,7 @@
         third_kernel,
         4,
         [((144, D), BF16), ((144, 3 * D), BF16)] + ds_shapes + [wshape, wshape],
-        idx, *pieces, gains, proj_weight, n0, qkv0, p0, o0, jnp.asarray(const[8]), keep1,
+        idx, *pieces, gains, proj_weight, n0, qkv0, p0, o0, third_const, keep1,
         specs={6: block(0, (D, D)), 12: ANY},
     )
     recv0 = flip(send0, "c")
@@ -777,7 +777,7 @@
         finish_kernel,
         2,
         [cells, cells, ((1, D), F32)],
-        *pieces, gains, qkv_weight, n0, rstd0, g0, dqkv0, jnp.asarray(const[9:11]), keep0,
+        *pieces, gains, qkv_weight, n0, rstd0, g0, dqkv0, finish_const, keep0,
         specs={5: block(0, (D, 3 * D)), 11: ANY},
         scratch=[((144, 2 * D), F32)],
     )
@@ -821,25 +821,22 @@
         idx, ka, ra, kb, rb, kc, rc, tk,
         scratch=[((4, 16, 2048), BF16)],
     )
-    keep, tab, send = call(
+    near = lambda z: (z + 1) % 8 if z & 1 else (z - 1) % 8
+    far = lambda z: z ^ (7 if (z ^ z >> 1) & 1 else 3)
+    parts = call(
         plane_kernel,
         1,
-        [((8, 2048), F32), ((8, 2048), BF16), ((16, 2048), BF16)],
-        idx, parts[0], flip(parts[1], "yh"), flip(parts[2], "x1", "x0"),
-        flip(parts[3], "x1", "x0", "yh"),
-        scratch=[((4, 8, 2048), F32)],
-    )
-    keep, tab, send = call(
-        ring_kernel,
-        1,
-        [((8, 1024), F32), ((16, 1024), BF16), ((24, 1024), BF16)],
-        idx, keep, tab, z_step(send, lambda z: (z + 1) % 8 if z & 1 else (z - 1) % 8),
+        [((24, 1024), BF16)] * 4,
+        idx, parts[0], z_step(parts[1], near), flip(parts[2], "x1", "x0"),
+        z_step(parts[3], near, "x1", "x0"),
+        scratch=[((4, 8, 2048), F32), ((4, 24, 1024), BF16)],
     )
     own, tab = call(
         close_kernel,
         1,
         [((24, 1024), BF16), ((16, 1024), BF16)],
-        keep, tab, z_step(send, lambda z: z ^ (7 if (z ^ z >> 1) & 1 else 3)),
+        idx, parts[0], z_step(parts[1], far), flip(parts[2], "yh"), z_step(parts[3], far, "yh"),
+        scratch=[((4, 24, 1024), F32)],
     )
     from_core = flip(tab, "c")
     from_dia = flip(tab, "c", "yl")

time: 109 us -> 106 us (0.972)
  waiting for transfers between devices: 25.1 us -> 21.1 us
    ppermute x2 -> x4, starting transfers between devices: 3.06 us -> 8.16 us  [z_step(): return lax.ppermute(value, AXES, pairs)]
    ppermute x20 -> x19, starting transfers between devices: 30.5 us -> 26.1 us  [flip(): lax.ppermute(value, AXES, [(s, s ^ mask_of(axes)) for s in range(256)])]
    ppermute x20 -> x19, waiting for transfers between devices: 16.2 us -> 13.2 us  [flip(): lax.ppermute(value, AXES, [(s, s ^ mask_of(axes)) for s in range(256)])]
    ppermute x2 -> x4, waiting for transfers between devices: 7.27 us -> 6.78 us  [z_step(): return lax.ppermute(value, AXES, pairs)]
    pallas_call x15 -> x14, Pallas kernels: 35.8 us -> 35.7 us  [call(): pl.pallas_call(body, grid=(1,), in_specs=[specs.get(i, _whole(a.shape)) f...]
  transfers between devices with their start and end apart: 26 -> 27, of which waited for: 13 -> 11; matrix products, arithmetic and copies ran while one was open for 0% -> 0% of each run, Pallas kernels for 15% -> 15%
where the time goes in v4:
time: 106 us
  starting transfers between devices  47.7 us (45%)
  Pallas kernels  35.7 us (34%)
  waiting for transfers between devices  21.1 us (20%)
    pallas_call x14, Pallas kernels, call(): pl.pallas_call(body, grid=(1,), in_specs=[specs.get(i, _whole(a.shape)) f...  35.7 us
    ppermute x19, starting transfers between devices, flip(): lax.ppermute(value, AXES, [(s, s ^ mask_of(axes)) for s in range(256)])  26.1 us
    ppermute x4, starting transfers between devices, lon_step(): return lax.ppermute(value, AXES, pairs)  13.4 us
    ppermute x19, waiting for transfers between devices, flip(): lax.ppermute(value, AXES, [(s, s ^ mask_of(axes)) for s in range(256)])  13.2 us
    ppermute x4, starting transfers between devices, z_step(): return lax.ppermute(value, AXES, pairs)  8.16 us
    ppermute x4, waiting for transfers between devices, z_step(): return lax.ppermute(value, AXES, pairs)  6.78 us
  transfers between devices with their start and end apart: 27, of which 11 were waited for; matrix products, arithmetic and copies ran while one was open for 0% of the time, Pallas kernels for 15%

profile of v4, /device:TPU:1, one launch (start us, length us, event | category | flops | bytes accessed | tf_op | source)
XLA Modules:
  0.0 105.6 jit_solution(5177371356642429935)
XLA Ops:
  0.7 0.0 copy-start.8
  0.7 8.5 %shard_map.172 = (bf16[40,1024]{1,0:T(8,128)(2,1)}, bf16[40,1024]{1,0:T(8,128)(2,1)}, bf16[40,1024]{1,0:T(8,128)(2,1)}, bf16[40,1024]{1,0:T(8,128)(2,1)}, f32[14...) custom-call(bf16[72,2,512]{2,1,0:T(2,128)(2,1)} %bitcast.19, ...), custom_call_target="tpu_custom_call" | custom-call | flops 8000000000 | bytes 28800000 | tf_op jit(solution)/shard_map/pallas_call | solution.py:631
  9.2 3.3 %collective-permute-start = (bf16[40,1024]{1,0:T(8,128)(2,1)}, bf16[40,1024]{1,0:T(8,128)(2,1)S(1)}, u32[]{:S(2)}, u32[]{:S(2)}) collective-permute-start(bf16[40,1024]{1,0:T(8,128)(2,1)} %get-tuple-element.77), channel_id=1, source_target_pairs={{0,254},{1,255},{2,0},{3,1},{4,2},{5,3},{6,4},{7,5},{8,6},{9,7},{1... | collective-permute-start | bytes 245768 | tf_op jit(solution)/shard_map/ppermute | solution.py:660
  12.5 0.0 collective-permute-start.1
  12.5 10.0 %collective-permute-start.2 = (bf16[40,1024]{1,0:T(8,128)(2,1)}, bf16[40,1024]{1,0:T(8,128)(2,1)S(1)}, u32[]{:S(2)}, u32[]{:S(2)}) collective-permute-start(bf16[40,1024]{1,0:T(8,128)(2,1)} %get-tuple-element.79), channel_id=1, source_target_pairs={{0,255},{1,254},{2,1},{3,0},{4,3},{5,2},{6,5},{7,4},{8,7},{9,6},{1... | collective-permute-start | bytes 245768 | tf_op jit(solution)/shard_map/ppermute | solution.py:660
  22.5 0.1 stack.27.idx_ref
  22.6 0.0 copy-start
  22.6 0.0 copy-start.1
  22.6 0.0 copy-start.4
  22.6 0.0 copy-start.5
  22.6 0.0 copy-start.14
  22.7 3.9 %shard_map.173 = (f32[2304,256]{1,0:T(8,128)S(1)}, s32[144,128]{1,0:T(8,128)S(1)}, s32[24,128]{1,0:T(8,128)S(1)}) custom-call(s32[6]{0:T(128)S(1)} %stack.27.idx_ref, f32[2,2,16,759]{3,2,1,0:T(8,128)S(1)} %copy-done.2, s32[144,144]{1,0:T(8,128)S(1)} %copy-done.3, bf16[160,256]{1,0:T(8,128)(2,1)S(1)} %copy-done.8), custom_call_target="tpu_custom_call" | custom-call | flops 4000000000 | bytes 14400000 | tf_op jit(solution)/shard_map/pallas_call | solution.py:631
  26.6 0.0 collective-permute-done.lon_ref
  26.6 0.0 collective-permute-done.2.dia_ref
  26.6 5.3 %shard_map.174 = (bf16[40,1024]{1,0:T(8,128)(2,1)S(1)}, bf16[40,1024]{1,0:T(8,128)(2,1)S(1)}, bf16[40,1024]{1,0:T(8,128)(2,1)S(1)}, bf16[40,1024]{1,0:T(8,128)(2...) custom-call(s32[6]{0:T(128)S(1)} %stack.27.idx_ref, ...), custom_call_target="tpu_custom_call" | custom-call | flops 6000000000 | bytes 21600000 | tf_op jit(solution)/shard_map/pallas_call | solution.py:631
  31.9 0.1 collective-permute-start.3
  32.0 0.5 collective-permute-start.4
  32.5 0.0 collective-permute-start.5
  32.5 0.0 copy-start.13
  32.5 1.8 %shard_map.175 = (bf16[256,2048]{1,0:T(8,128)(2,1)S(1)}, bf16[256,2048]{1,0:T(8,128)(2,1)S(1)}) custom-call(s32[6]{0:T(128)S(1)} %stack.27.idx_ref, bf16[144,512]{1,0:T(8,128)(2,1)S(1)} %get-tuple-element.90.h_ref, bf16[144,512]{1,0:T(8,128)(2,1)S(1)} %get-tuple-element.91.o_ref, bf16[144,1536]{1,0:T(8,128)(2,1)S(1)} %get-tuple-element.92.dqkv_ref, ...), custom_call_target="tpu_custom_call" | custom-call | flops 2000000000 | bytes 7200000 | tf_op jit(solution)/shard_map/pallas_call | solution.py:631
  34.3 1.8 %collective-permute-start.7 = (bf16[256,2048]{1,0:T(8,128)(2,1)S(1)}, bf16[256,2048]{1,0:T(8,128)(2,1)S(1)}, u32[]{:S(2)}, u32[]{:S(2)}) collective-permute-start(bf16[256,2048]{1,0:T(8,128)(2,1)S(1)} %get-tuple-element.101), channel_id=1, source_target_pairs={{0,2},{1,3},{2,0},{3,1},{4,6},{5,7},{6,4},{7,5},{8,10},{9,11},{10,... | collective-permute-start | bytes 3145736 | tf_op jit(solution)/shard_map/ppermute | solution.py:650
  36.1 0.0 collective-permute-done.3.lon_ref
  36.1 0.0 collective-permute-done.4.lat_ref
  36.1 1.1 %collective-permute-done.5.dia_ref = bf16[40,1024]{1,0:T(8,128)(2,1)S(1)} collective-permute-done((bf16[40,1024]{1,0:T(8,128)(2,1)S(1)}, bf16[40,1024]{1,0:T(8,128)(2,1)S(1)}, u32[]{:S(2)}, u32[]{:S(2)}) %collective-permute-start.5) | collective-permute-done | bytes 81952 | tf_op jit(solution)/shard_map/ppermute | solution.py:660
  37.2 0.0 copy-start.6
  37.2 4.2 %shard_map.176 = (bf16[144,512]{1,0:T(8,128)(2,1)S(1)}, bf16[144,1536]{1,0:T(8,128)(2,1)S(1)}, f32[2304,128]{1,0:T(8,128)S(1)}, f32[384,128]{1,0:T(8,128)S(1)}, ...) custom-call(s32[6]{0:T(128)S(1)} %stack.27.idx_ref, bf16[40,1024]{1,0:T(8,128)(2,1)S(1)} %get-tuple-element.81.own_ref, ...), custom_call_target="tpu_custom_call" | custom-call | flops 4000000000 | bytes 14400000 | tf_op jit(solution)/shard_map/pallas_call | solution.py:631
  41.4 5.4 %collective-permute-start.6 = (bf16[256,2048]{1,0:T(8,128)(2,1)S(1)}, bf16[256,2048]{1,0:T(8,128)(2,1)S(1)}, u32[]{:S(2)}, u32[]{:S(2)}) collective-permute-start(bf16[256,2048]{1,0:T(8,128)(2,1)S(1)} %get-tuple-element.100), channel_id=1, source_target_pairs={{0,2},{1,3},{2,0},{3,1},{4,6},{5,7},{6,4},{7,5},{8,10},{9,11},{10,... | collective-permute-start | bytes 3145736 | tf_op jit(solution)/shard_map/ppermute | solution.py:650
  46.8 1.7 %shard_map.177 = (bf16[72,2,512]{2,1,0:T(2,128)(2,1)}, bf16[72,2,512]{2,1,0:T(2,128)(2,1)}, f32[1,512]{1,0:T(1,128)S(1)}) custom-call(bf16[40,1024]{1,0:T(8,128)(2,1)S(1)} %get-tuple-element.81.own_ref, bf16[40,1024]{1,0:T(8,128)(2,1)S(1)} %collective-permute-done.3.lon_ref, bf16[40,1024]{1,0:T(8,128)(2,1)S(1)} %collective-permute-done.4.lat_ref, ...), custom_call_target="tpu_custom_call" | custom-call | flops 2000000000 | bytes 7200000 | tf_op jit(solution)/shard_map/pallas_call | solution.py:631
  48.5 0.6 collective-permute-done.6.r0_ref
  49.1 1.2 %shard_map.178 = (bf16[128,1536]{1,0:T(8,128)(2,1)S(1)}, bf16[128,1536]{1,0:T(8,128)(2,1)S(1)}, bf16[256,768]{1,0:T(8,128)(2,1)S(1)}, bf16[256,768]{1,0:T(8,128)...) custom-call(s32[6]{0:T(128)S(1)} %stack.27.idx_ref, ...), custom_call_target="tpu_custom_call" | custom-call | flops 1000000000 | bytes 3600000 | tf_op jit(solution)/shard_map/pallas_call | solution.py:631
  50.3 0.1 collective-permute-start.10
  50.4 0.1 collective-permute-start.8
  50.5 0.3 collective-permute-start.9
  50.8 4.5 %shard_map.179 = (f32[16,1024]{1,0:T(8,128)S(1)}, f32[16,1024]{1,0:T(8,128)S(1)}) custom-call(s32[6]{0:T(128)S(1)} %stack.27.idx_ref, s32[144,128]{1,0:T(8,128)S(1)} %get-tuple-element.108.main_ref, s32[24,128]{1,0:T(8,128)S(1)} %get-tuple-element.109.tail_ref, f32[2304,128]{1,0:T(8,128)S(1)} %get-tuple-element.110.m0_ref, ...), custom_call_target="tpu_custom_call" | custom-call | flops 6000000000 | bytes 21600000 | tf_op jit(solution)/shard_map/pallas_call | solution.py:631
  55.2 0.7 collective-permute-start.11
  56.0 0.9 collective-permute-done.11.u_ref
  56.9 1.0 collective-permute-done.10.rc_ref
  57.9 2.9 %collective-permute-done.8.ra_ref = bf16[128,1536]{1,0:T(8,128)(2,1)S(1)} collective-permute-done((bf16[128,1536]{1,0:T(8,128)(2,1)S(1)}, bf16[128,1536]{1,0:T(8,128)(2,1)S(1)}, u32[]{:S(2)}, u32[]{:S(2)}) %collective-permute-start.8) | collective-permute-done | bytes 393248 | tf_op jit(solution)/shard_map/ppermute | solution.py:650
  60.8 0.1 collective-permute-done.9.rb_ref
  60.9 0.9 shard_map.180
  61.8 0.3 collective-permute-start.12
  62.0 0.9 collective-permute-start.13
  63.0 1.1 %collective-permute-start.14 = (bf16[80,1024]{1,0:T(8,128)(2,1)S(1)}, bf16[80,1024]{1,0:T(8,128)(2,1)S(1)}, u32[]{:S(2)}, u32[]{:S(2)}) collective-permute-start(bf16[80,1024]{1,0:T(8,128)(2,1)S(1)} %get-tuple-element.123), channel_id=1, source_target_pairs={{0,32},{1,33},{2,34},{3,35},{4,36},{5,37},{6,38},{7,39},{8,40},{9,... | collective-permute-start | bytes 491528 | tf_op jit(solution)/shard_map/ppermute | solution.py:650
  64.1 3.3 %collective-permute-done.14.rc_ref = bf16[80,1024]{1,0:T(8,128)(2,1)S(1)} collective-permute-done((bf16[80,1024]{1,0:T(8,128)(2,1)S(1)}, bf16[80,1024]{1,0:T(8,128)(2,1)S(1)}, u32[]{:S(2)}, u32[]{:S(2)}) %collective-permute-start.14) | collective-permute-done | bytes 163872 | tf_op jit(solution)/shard_map/ppermute | solution.py:650
  67.5 0.7 shard_map.181
  68.2 0.6 collective-permute-start.15
  68.8 1.0 collective-permute-start.16
  69.8 1.3 %collective-permute-start.17 = (bf16[64,512]{1,0:T(8,128)(2,1)S(1)}, bf16[64,512]{1,0:T(8,128)(2,1)S(1)}, u32[]{:S(2)}, u32[]{:S(2)}) collective-permute-start(bf16[64,512]{1,0:T(8,128)(2,1)S(1)} %get-tuple-element.130), channel_id=1, source_target_pairs={{0,1},{1,0},{2,3},{3,2},{4,5},{5,4},{6,7},{7,6},{8,9},{9,8},{10,11... | collective-permute-start | bytes 196616 | tf_op jit(solution)/shard_map/ppermute | solution.py:650
  71.1 1.8 %collective-permute-done.17.rc_ref = bf16[64,512]{1,0:T(8,128)(2,1)S(1)} collective-permute-done((bf16[64,512]{1,0:T(8,128)(2,1)S(1)}, bf16[64,512]{1,0:T(8,128)(2,1)S(1)}, u32[]{:S(2)}, u32[]{:S(2)}) %collective-permute-start.17) | collective-permute-done | bytes 65568 | tf_op jit(solution)/shard_map/ppermute | solution.py:650
  73.0 0.7 shard_map.182
  73.6 0.4 collective-permute-start.18
  74.0 0.6 collective-permute-start.19
  74.6 4.5 %collective-permute-start.20 = (bf16[24,2048]{1,0:T(8,128)(2,1)S(1)}, bf16[24,2048]{1,0:T(8,128)(2,1)S(1)}, u32[]{:S(2)}, u32[]{:S(2)}) collective-permute-start(bf16[24,2048]{1,0:T(8,128)(2,1)S(1)} %get-tuple-element.135), channel_id=1, source_target_pairs={{0,124},{1,125},{2,126},{3,127},{4,104},{5,105},{6,106},{7,107},{8... | collective-permute-start | bytes 294920 | tf_op jit(solution)/shard_map/ppermute | solution.py:655
  79.0 2.9 %collective-permute-done.20.g3_ref = bf16[24,2048]{1,0:T(8,128)(2,1)S(1)} collective-permute-done((bf16[24,2048]{1,0:T(8,128)(2,1)S(1)}, bf16[24,2048]{1,0:T(8,128)(2,1)S(1)}, u32[]{:S(2)}, u32[]{:S(2)}) %collective-permute-start.20) | collective-permute-done | bytes 98336 | tf_op jit(solution)/shard_map/ppermute | solution.py:655
  81.9 0.6 shard_map.183
  82.5 0.1 collective-permute-start.21
  82.6 2.7 %collective-permute-start.22 = (bf16[24,1024]{1,0:T(8,128)(2,1)S(1)}, bf16[24,1024]{1,0:T(8,128)(2,1)S(1)}, u32[]{:S(2)}, u32[]{:S(2)}) collective-permute-start(bf16[24,1024]{1,0:T(8,128)(2,1)S(1)} %get-tuple-element.138), channel_id=1, source_target_pairs={{0,128},{1,129},{2,130},{3,131},{4,132},{5,133},{6,134},{7,135},{8... | collective-permute-start | bytes 147464 | tf_op jit(solution)/shard_map/ppermute | solution.py:650
  85.4 3.2 %collective-permute-start.23 = (bf16[24,1024]{1,0:T(8,128)(2,1)S(1)}, bf16[24,1024]{1,0:T(8,128)(2,1)S(1)}, u32[]{:S(2)}, u32[]{:S(2)}) collective-permute-start(bf16[24,1024]{1,0:T(8,128)(2,1)S(1)} %get-tuple-element.139), channel_id=1, source_target_pairs={{0,140},{1,141},{2,142},{3,143},{4,152},{5,153},{6,154},{7,155},{8... | collective-permute-start | bytes 147464 | tf_op jit(solution)/shard_map/ppermute | solution.py:655
  88.6 3.9 %collective-permute-done.23.g3_ref = bf16[24,1024]{1,0:T(8,128)(2,1)S(1)} collective-permute-done((bf16[24,1024]{1,0:T(8,128)(2,1)S(1)}, bf16[24,1024]{1,0:T(8,128)(2,1)S(1)}, u32[]{:S(2)}, u32[]{:S(2)}) %collective-permute-start.23) | collective-permute-done | bytes 49184 | tf_op jit(solution)/shard_map/ppermute | solution.py:655
  92.5 0.6 shard_map.184
  93.1 0.3 collective-permute-start.24
  93.4 8.4 %collective-permute-start.26 = (bf16[16,1024]{1,0:T(8,128)(2,1)S(1)}, bf16[16,1024]{1,0:T(8,128)(2,1)S(1)}, u32[]{:S(2)}, u32[]{:S(2)}) collective-permute-start(bf16[16,1024]{1,0:T(8,128)(2,1)S(1)} %get-tuple-element.141), channel_id=1, source_target_pairs={{0,3},{1,2},{2,1},{3,0},{4,7},{5,6},{6,5},{7,4},{8,11},{9,10},{10,... | collective-permute-start | bytes 98312 | tf_op jit(solution)/shard_map/ppermute | solution.py:650
  101.8 2.6 %collective-permute-done.26.dia_ref = bf16[16,1024]{1,0:T(8,128)(2,1)S(1)} collective-permute-done((bf16[16,1024]{1,0:T(8,128)(2,1)S(1)}, bf16[16,1024]{1,0:T(8,128)(2,1)S(1)}, u32[]{:S(2)}, u32[]{:S(2)}) %collective-permute-start.26) | collective-permute-done | bytes 32800 | tf_op jit(solution)/shard_map/ppermute | solution.py:650
  104.4 1.3 %shard_map.185 = (f32[2,512]{1,0:T(2,128)}, f32[2,4,1536]{2,1,0:T(4,128)}, f32[2,4,512]{2,1,0:T(4,128)}, f32[2,2,16,759]{3,2,1,0:T(8,128)}) custom-call(s32[6]{0:T(128)S(1)} %stack.27.idx_ref, bf16[24,1024]{1,0:T(8,128)(2,1)S(1)} %get-tuple-element.140.own_ref, bf16[24,1024]{1,0:T(8,128)(2,1)S(1)} %collective-permute-done.24.lat_ref, ...), custom_call_target="tpu_custom_call" | custom-call | flops 1000000000 | bytes 3600000 | tf_op jit(solution)/shard_map/pallas_call | solution.py:631
  (35 shorter events, 0.1 us)
Async XLA Ops:
  0.6 22.0 %copy-start.2 = (f32[2,2,16,759]{3,2,1,0:T(8,128)S(1)}, f32[2,2,16,759]{3,2,1,0:T(8,128)}, u32[]{:S(2)}) copy-start(f32[2,2,16,759]{3,2,1,0:T(8,128)} %tab_ref.1) | copy-start | bytes 582916
  0.6 21.9 %copy-start.3 = (s32[144,144]{1,0:T(8,128)S(1)}, s32[144,144]{1,0:T(8,128)}, u32[]{:S(2)}) copy-start(s32[144,144]{1,0:T(8,128)} %rel_ref.1) | copy-start | bytes 248836
  0.7 21.9 %copy-start.8 = (bf16[160,256]{1,0:T(8,128)(2,1)S(1)}, bf16[160,256]{1,0:T(8,128)(2,1)}, u32[]{:S(2)}) copy-start(bf16[160,256]{1,0:T(8,128)(2,1)} %constant.46.clone.pm_ref) | copy-start | bytes 245764
  9.2 17.4 %collective-permute-start = (bf16[40,1024]{1,0:T(8,128)(2,1)}, bf16[40,1024]{1,0:T(8,128)(2,1)S(1)}, u32[]{:S(2)}, u32[]{:S(2)}) collective-permute-start(bf16[40,1024]{1,0:T(8,128)(2,1)} %get-tuple-element.77), channel_id=1, source_target_pairs={{0,254},{1,255},{2,0},{3,1},{4,2},{5,3},{6,4},{7,5},{8,6},{9,7},{1... | collective-permute-start | bytes 245768 | tf_op jit(solution)/shard_map/ppermute | solution.py:660
  12.5 14.1 %collective-permute-start.1 = (bf16[40,1024]{1,0:T(8,128)(2,1)}, bf16[40,1024]{1,0:T(8,128)(2,1)S(1)}, u32[]{:S(2)}, u32[]{:S(2)}) collective-permute-start(bf16[40,1024]{1,0:T(8,128)(2,1)} %get-tuple-element.78), channel_id=1, source_target_pairs={{0,1},{1,0},{2,3},{3,2},{4,5},{5,4},{6,7},{7,6},{8,9},{9,8},{10,11... | collective-permute-start | bytes 245768 | tf_op jit(solution)/shard_map/ppermute | solution.py:650
  12.5 14.1 %collective-permute-start.2 = (bf16[40,1024]{1,0:T(8,128)(2,1)}, bf16[40,1024]{1,0:T(8,128)(2,1)S(1)}, u32[]{:S(2)}, u32[]{:S(2)}) collective-permute-start(bf16[40,1024]{1,0:T(8,128)(2,1)} %get-tuple-element.79), channel_id=1, source_target_pairs={{0,255},{1,254},{2,1},{3,0},{4,3},{5,2},{6,5},{7,4},{8,7},{9,6},{1... | collective-permute-start | bytes 245768 | tf_op jit(solution)/shard_map/ppermute | solution.py:660
  22.6 4.0 %copy-start = (bf16[2,512,1536]{2,1,0:T(8,128)(2,1)S(1)}, bf16[2,512,1536]{2,1,0:T(8,128)(2,1)}, u32[]{:S(2)}) copy-start(bf16[2,512,1536]{2,1,0:T(8,128)(2,1)} %wqkv_ref.3) | copy-start | bytes 9437188
  22.6 4.0 %copy-start.1 = (bf16[2,512,512]{2,1,0:T(8,128)(2,1)S(1)}, bf16[2,512,512]{2,1,0:T(8,128)(2,1)}, u32[]{:S(2)}) copy-start(bf16[2,512,512]{2,1,0:T(8,128)(2,1)} %wproj_ref.3) | copy-start | bytes 3145732
  22.6 4.0 %copy-start.4 = (f32[2,512]{1,0:T(2,128)S(1)}, f32[2,512]{1,0:T(2,128)}, u32[]{:S(2)}) copy-start(f32[2,512]{1,0:T(2,128)} %gain_ref.5) | copy-start | bytes 12292
  22.6 4.0 %copy-start.5 = (bf16[5,160,256]{2,1,0:T(8,128)(2,1)S(1)}, bf16[5,160,256]{2,1,0:T(8,128)(2,1)}, u32[]{:S(2)}) copy-start(bf16[5,160,256]{2,1,0:T(8,128)(2,1)} %constant.43.clone.const_ref) | copy-start | bytes 1228804
  22.6 4.0 %copy-start.14 = (bf16[40,1024]{1,0:T(8,128)(2,1)S(1)}, bf16[40,1024]{1,0:T(8,128)(2,1)}, u32[]{:S(2)}) copy-start(bf16[40,1024]{1,0:T(8,128)(2,1)} %get-tuple-element.76.own_ref) | copy-start | bytes 245764
  31.9 4.1 %collective-permute-start.3 = (bf16[40,1024]{1,0:T(8,128)(2,1)S(1)}, bf16[40,1024]{1,0:T(8,128)(2,1)S(1)}, u32[]{:S(2)}, u32[]{:S(2)}) collective-permute-start(bf16[40,1024]{1,0:T(8,128)(2,1)S(1)} %get-tuple-element.82), channel_id=1, source_target_pairs={{0,2},{1,3},{2,4},{3,5},{4,6},{5,7},{6,8},{7,9},{8,10},{9,11},{10,... | collective-permute-start | bytes 245768 | tf_op jit(solution)/shard_map/ppermute | solution.py:660
  32.0 4.1 %collective-permute-start.4 = (bf16[40,1024]{1,0:T(8,128)(2,1)S(1)}, bf16[40,1024]{1,0:T(8,128)(2,1)S(1)}, u32[]{:S(2)}, u32[]{:S(2)}) collective-permute-start(bf16[40,1024]{1,0:T(8,128)(2,1)S(1)} %get-tuple-element.83), channel_id=1, source_target_pairs={{0,1},{1,0},{2,3},{3,2},{4,5},{5,4},{6,7},{7,6},{8,9},{9,8},{10,11... | collective-permute-start | bytes 245768 | tf_op jit(solution)/shard_map/ppermute | solution.py:650
  32.5 4.6 %collective-permute-start.5 = (bf16[40,1024]{1,0:T(8,128)(2,1)S(1)}, bf16[40,1024]{1,0:T(8,128)(2,1)S(1)}, u32[]{:S(2)}, u32[]{:S(2)}) collective-permute-start(bf16[40,1024]{1,0:T(8,128)(2,1)S(1)} %get-tuple-element.84), channel_id=1, source_target_pairs={{0,3},{1,2},{2,5},{3,4},{4,7},{5,6},{6,9},{7,8},{8,11},{9,10},{10,... | collective-permute-start | bytes 245768 | tf_op jit(solution)/shard_map/ppermute | solution.py:660
  32.5 4.6 %copy-start.7 = (bf16[1,160,256]{2,1,0:T(8,128)(2,1)S(1)}, bf16[1,160,256]{2,1,0:T(8,128)(2,1)}, u32[]{:S(2)}) copy-start(bf16[1,160,256]{2,1,0:T(8,128)(2,1)} %constant.44.clone.const_ref) | copy-start | bytes 245764
  32.5 4.6 %copy-start.9 = (f32[144,512]{1,0:T(8,128)S(1)}, f32[144,512]{1,0:T(8,128)}, u32[]{:S(2)}) copy-start(f32[144,512]{1,0:T(8,128)} %get-tuple-element.85.n_ref) | copy-start | bytes 884740
  32.5 4.7 %copy-start.11 = (bf16[2304,256]{1,0:T(8,128)(2,1)S(1)}, bf16[2304,256]{1,0:T(8,128)(2,1)}, u32[]{:S(2)}) copy-start(bf16[2304,256]{1,0:T(8,128)(2,1)} %get-tuple-element.88.p_ref) | copy-start | bytes 3538948
  32.5 4.7 %copy-start.12 = (bf16[144,1536]{1,0:T(8,128)(2,1)S(1)}, bf16[144,1536]{1,0:T(8,128)(2,1)}, u32[]{:S(2)}) copy-start(bf16[144,1536]{1,0:T(8,128)(2,1)} %get-tuple-element.87.qkv_ref) | copy-start | bytes 1327108
  32.5 4.7 %copy-start.13 = (bf16[144,512]{1,0:T(8,128)(2,1)S(1)}, bf16[144,512]{1,0:T(8,128)(2,1)}, u32[]{:S(2)}) copy-start(bf16[144,512]{1,0:T(8,128)(2,1)} %get-tuple-element.89.o_ref) | copy-start | bytes 442372
  34.3 14.2 %collective-permute-start.7 = (bf16[256,2048]{1,0:T(8,128)(2,1)S(1)}, bf16[256,2048]{1,0:T(8,128)(2,1)S(1)}, u32[]{:S(2)}, u32[]{:S(2)}) collective-permute-start(bf16[256,2048]{1,0:T(8,128)(2,1)S(1)} %get-tuple-element.101), channel_id=1, source_target_pairs={{0,2},{1,3},{2,0},{3,1},{4,6},{5,7},{6,4},{7,5},{8,10},{9,11},{10,... | collective-permute-start | bytes 3145736 | tf_op jit(solution)/shard_map/ppermute | solution.py:650
  37.2 9.6 %copy-start.6 = (bf16[2,160,256]{2,1,0:T(8,128)(2,1)S(1)}, bf16[2,160,256]{2,1,0:T(8,128)(2,1)}, u32[]{:S(2)}) copy-start(bf16[2,160,256]{2,1,0:T(8,128)(2,1)} %constant.45.clone.const_ref) | copy-start | bytes 491524
  37.2 9.6 %copy-start.10 = (f32[144,1]{1,0:T(8,128)S(1)}, f32[144,1]{1,0:T(8,128)}, u32[]{:S(2)}) copy-start(f32[144,1]{1,0:T(8,128)} %get-tuple-element.86.rstd_ref) | copy-start | bytes 1732
  41.4 7.7 %collective-permute-start.6 = (bf16[256,2048]{1,0:T(8,128)(2,1)S(1)}, bf16[256,2048]{1,0:T(8,128)(2,1)S(1)}, u32[]{:S(2)}, u32[]{:S(2)}) collective-permute-start(bf16[256,2048]{1,0:T(8,128)(2,1)S(1)} %get-tuple-element.100), channel_id=1, source_target_pairs={{0,2},{1,3},{2,0},{3,1},{4,6},{5,7},{6,4},{7,5},{8,10},{9,11},{10,... | collective-permute-start | bytes 3145736 | tf_op jit(solution)/shard_map/ppermute | solution.py:650
  50.3 7.6 %collective-permute-start.10 = (bf16[128,1024]{1,0:T(8,128)(2,1)S(1)}, bf16[128,1024]{1,0:T(8,128)(2,1)S(1)}, u32[]{:S(2)}, u32[]{:S(2)}) collective-permute-start(bf16[128,1024]{1,0:T(8,128)(2,1)S(1)} %get-tuple-element.107), channel_id=1, source_target_pairs={{0,4},{1,5},{2,6},{3,7},{4,0},{5,1},{6,2},{7,3},{8,12},{9,13},{10,... | collective-permute-start | bytes 786440 | tf_op jit(solution)/shard_map/ppermute | solution.py:650
  50.4 10.4 %collective-permute-start.8 = (bf16[128,1536]{1,0:T(8,128)(2,1)S(1)}, bf16[128,1536]{1,0:T(8,128)(2,1)S(1)}, u32[]{:S(2)}, u32[]{:S(2)}) collective-permute-start(bf16[128,1536]{1,0:T(8,128)(2,1)S(1)} %get-tuple-element.103), channel_id=1, source_target_pairs={{0,32},{1,33},{2,34},{3,35},{4,36},{5,37},{6,38},{7,39},{8,40},{9,... | collective-permute-start | bytes 1179656 | tf_op jit(solution)/shard_map/ppermute | solution.py:650
  50.5 10.4 %collective-permute-start.9 = (bf16[256,768]{1,0:T(8,128)(2,1)S(1)}, bf16[256,768]{1,0:T(8,128)(2,1)S(1)}, u32[]{:S(2)}, u32[]{:S(2)}) collective-permute-start(bf16[256,768]{1,0:T(8,128)(2,1)S(1)} %get-tuple-element.105), channel_id=1, source_target_pairs={{0,1},{1,0},{2,3},{3,2},{4,5},{5,4},{6,7},{7,6},{8,9},{9,8},{10,11... | collective-permute-start | bytes 1179656 | tf_op jit(solution)/shard_map/ppermute | solution.py:650
  55.2 1.6 %collective-permute-start.11 = (f32[16,1024]{1,0:T(8,128)S(1)}, f32[16,1024]{1,0:T(8,128)S(1)}, u32[]{:S(2)}, u32[]{:S(2)}) collective-permute-start(f32[16,1024]{1,0:T(8,128)S(1)} %get-tuple-element.117), channel_id=1, source_target_pairs={{0,2},{1,3},{2,0},{3,1},{4,6},{5,7},{6,4},{7,5},{8,10},{9,11},{10,... | collective-permute-start | bytes 196616 | tf_op jit(solution)/shard_map/ppermute | solution.py:650
  61.8 5.7 %collective-permute-start.12 = (bf16[128,768]{1,0:T(8,128)(2,1)S(1)}, bf16[128,768]{1,0:T(8,128)(2,1)S(1)}, u32[]{:S(2)}, u32[]{:S(2)}) collective-permute-start(bf16[128,768]{1,0:T(8,128)(2,1)S(1)} %get-tuple-element.119), channel_id=1, source_target_pairs={{0,1},{1,0},{2,3},{3,2},{4,5},{5,4},{6,7},{7,6},{8,9},{9,8},{10,11... | collective-permute-start | bytes 589832 | tf_op jit(solution)/shard_map/ppermute | solution.py:650
  62.0 5.4 %collective-permute-start.13 = (bf16[128,768]{1,0:T(8,128)(2,1)S(1)}, bf16[128,768]{1,0:T(8,128)(2,1)S(1)}, u32[]{:S(2)}, u32[]{:S(2)}) collective-permute-start(bf16[128,768]{1,0:T(8,128)(2,1)S(1)} %get-tuple-element.121), channel_id=1, source_target_pairs={{0,4},{1,5},{2,6},{3,7},{4,0},{5,1},{6,2},{7,3},{8,12},{9,13},{10,... | collective-permute-start | bytes 589832 | tf_op jit(solution)/shard_map/ppermute | solution.py:650
  63.0 4.5 %collective-permute-start.14 = (bf16[80,1024]{1,0:T(8,128)(2,1)S(1)}, bf16[80,1024]{1,0:T(8,128)(2,1)S(1)}, u32[]{:S(2)}, u32[]{:S(2)}) collective-permute-start(bf16[80,1024]{1,0:T(8,128)(2,1)S(1)} %get-tuple-element.123), channel_id=1, source_target_pairs={{0,32},{1,33},{2,34},{3,35},{4,36},{5,37},{6,38},{7,39},{8,40},{9,... | collective-permute-start | bytes 491528 | tf_op jit(solution)/shard_map/ppermute | solution.py:650
  68.2 4.8 %collective-permute-start.15 = (bf16[96,768]{1,0:T(8,128)(2,1)S(1)}, bf16[96,768]{1,0:T(8,128)(2,1)S(1)}, u32[]{:S(2)}, u32[]{:S(2)}) collective-permute-start(bf16[96,768]{1,0:T(8,128)(2,1)S(1)} %get-tuple-element.126), channel_id=1, source_target_pairs={{0,4},{1,5},{2,6},{3,7},{4,0},{5,1},{6,2},{7,3},{8,12},{9,13},{10,... | collective-permute-start | bytes 442376 | tf_op jit(solution)/shard_map/ppermute | solution.py:650
  68.8 4.2 %collective-permute-start.16 = (bf16[64,768]{1,0:T(8,128)(2,1)S(1)}, bf16[64,768]{1,0:T(8,128)(2,1)S(1)}, u32[]{:S(2)}, u32[]{:S(2)}) collective-permute-start(bf16[64,768]{1,0:T(8,128)(2,1)S(1)} %get-tuple-element.128), channel_id=1, source_target_pairs={{0,32},{1,33},{2,34},{3,35},{4,36},{5,37},{6,38},{7,39},{8,40},{9,... | collective-permute-start | bytes 294920 | tf_op jit(solution)/shard_map/ppermute | solution.py:650
  69.8 3.1 %collective-permute-start.17 = (bf16[64,512]{1,0:T(8,128)(2,1)S(1)}, bf16[64,512]{1,0:T(8,128)(2,1)S(1)}, u32[]{:S(2)}, u32[]{:S(2)}) collective-permute-start(bf16[64,512]{1,0:T(8,128)(2,1)S(1)} %get-tuple-element.130), channel_id=1, source_target_pairs={{0,1},{1,0},{2,3},{3,2},{4,5},{5,4},{6,7},{7,6},{8,9},{9,8},{10,11... | collective-permute-start | bytes 196616 | tf_op jit(solution)/shard_map/ppermute | solution.py:650
  73.6 5.4 %collective-permute-start.18 = (bf16[24,2048]{1,0:T(8,128)(2,1)S(1)}, bf16[24,2048]{1,0:T(8,128)(2,1)S(1)}, u32[]{:S(2)}, u32[]{:S(2)}) collective-permute-start(bf16[24,2048]{1,0:T(8,128)(2,1)S(1)} %get-tuple-element.133), channel_id=1, source_target_pairs={{0,28},{1,29},{2,30},{3,31},{4,8},{5,9},{6,10},{7,11},{8,4},{9,5},... | collective-permute-start | bytes 294920 | tf_op jit(solution)/shard_map/ppermute | solution.py:655
  74.0 5.1 %collective-permute-start.19 = (bf16[24,2048]{1,0:T(8,128)(2,1)S(1)}, bf16[24,2048]{1,0:T(8,128)(2,1)S(1)}, u32[]{:S(2)}, u32[]{:S(2)}) collective-permute-start(bf16[24,2048]{1,0:T(8,128)(2,1)S(1)} %get-tuple-element.134), channel_id=1, source_target_pairs={{0,96},{1,97},{2,98},{3,99},{4,100},{5,101},{6,102},{7,103},{8,104... | collective-permute-start | bytes 294920 | tf_op jit(solution)/shard_map/ppermute | solution.py:650
  74.6 7.4 %collective-permute-start.20 = (bf16[24,2048]{1,0:T(8,128)(2,1)S(1)}, bf16[24,2048]{1,0:T(8,128)(2,1)S(1)}, u32[]{:S(2)}, u32[]{:S(2)}) collective-permute-start(bf16[24,2048]{1,0:T(8,128)(2,1)S(1)} %get-tuple-element.135), channel_id=1, source_target_pairs={{0,124},{1,125},{2,126},{3,127},{4,104},{5,105},{6,106},{7,107},{8... | collective-permute-start | bytes 294920 | tf_op jit(solution)/shard_map/ppermute | solution.py:655
  82.5 6.0 %collective-permute-start.21 = (bf16[24,1024]{1,0:T(8,128)(2,1)S(1)}, bf16[24,1024]{1,0:T(8,128)(2,1)S(1)}, u32[]{:S(2)}, u32[]{:S(2)}) collective-permute-start(bf16[24,1024]{1,0:T(8,128)(2,1)S(1)} %get-tuple-element.137), channel_id=1, source_target_pairs={{0,12},{1,13},{2,14},{3,15},{4,24},{5,25},{6,26},{7,27},{8,20},{9,... | collective-permute-start | bytes 147464 | tf_op jit(solution)/shard_map/ppermute | solution.py:655
  82.6 5.9 %collective-permute-start.22 = (bf16[24,1024]{1,0:T(8,128)(2,1)S(1)}, bf16[24,1024]{1,0:T(8,128)(2,1)S(1)}, u32[]{:S(2)}, u32[]{:S(2)}) collective-permute-start(bf16[24,1024]{1,0:T(8,128)(2,1)S(1)} %get-tuple-element.138), channel_id=1, source_target_pairs={{0,128},{1,129},{2,130},{3,131},{4,132},{5,133},{6,134},{7,135},{8... | collective-permute-start | bytes 147464 | tf_op jit(solution)/shard_map/ppermute | solution.py:650
  85.4 7.1 %collective-permute-start.23 = (bf16[24,1024]{1,0:T(8,128)(2,1)S(1)}, bf16[24,1024]{1,0:T(8,128)(2,1)S(1)}, u32[]{:S(2)}, u32[]{:S(2)}) collective-permute-start(bf16[24,1024]{1,0:T(8,128)(2,1)S(1)} %get-tuple-element.139), channel_id=1, source_target_pairs={{0,140},{1,141},{2,142},{3,143},{4,152},{5,153},{6,154},{7,155},{8... | collective-permute-start | bytes 147464 | tf_op jit(solution)/shard_map/ppermute | solution.py:655
  93.1 11.3 %collective-permute-start.24 = (bf16[24,1024]{1,0:T(8,128)(2,1)S(1)}, bf16[24,1024]{1,0:T(8,128)(2,1)S(1)}, u32[]{:S(2)}, u32[]{:S(2)}) collective-permute-start(bf16[24,1024]{1,0:T(8,128)(2,1)S(1)} %get-tuple-element.140.own_ref), channel_id=1, source_target_pairs={{0,1},{1,0},{2,3},{3,2},{4,5},{5,4},{6,7},{7,6},{8,9},{9,8},{10,11... | collective-permute-start | bytes 147464 | tf_op jit(solution)/shard_map/ppermute | solution.py:650
  93.4 11.0 %collective-permute-start.26 = (bf16[16,1024]{1,0:T(8,128)(2,1)S(1)}, bf16[16,1024]{1,0:T(8,128)(2,1)S(1)}, u32[]{:S(2)}, u32[]{:S(2)}) collective-permute-start(bf16[16,1024]{1,0:T(8,128)(2,1)S(1)} %get-tuple-element.141), channel_id=1, source_target_pairs={{0,3},{1,2},{2,1},{3,0},{4,7},{5,6},{6,5},{7,4},{8,11},{9,10},{10,... | collective-permute-start | bytes 98312 | tf_op jit(solution)/shard_map/ppermute | solution.py:650
  101.8 2.6 %collective-permute-start.25 = (bf16[16,1024]{1,0:T(8,128)(2,1)S(1)}, bf16[16,1024]{1,0:T(8,128)(2,1)S(1)}, u32[]{:S(2)}, u32[]{:S(2)}) collective-permute-start(bf16[16,1024]{1,0:T(8,128)(2,1)S(1)} %get-tuple-element.141), channel_id=1, source_target_pairs={{0,2},{1,3},{2,0},{3,1},{4,6},{5,7},{6,4},{7,5},{8,10},{9,11},{10,... | collective-permute-start | bytes 98312 | tf_op jit(solution)/shard_map/ppermute | solution.py:650

commit v5 on v4

--- a/solution.py
+++ b/solution.py
@@ -194,10 +194,24 @@
     return q4, kg, jnp.concatenate(out, axis=0)
 
 
-def group_back(g, q4, kg, vg, p4, p4b, do, masks, dqkv_ref, ds0_ref, ds1_ref):
+def by_keys(left, right):
+    parts = [dot(left[32 * k : 32 * k + 32], right[144 * k : 144 * k + 144]) for k in range(4)]
+    return jnp.concatenate(parts, axis=0).T[0:144]
+
+
+def by_rows(left, right):
+    parts = [dot_nt(left[32 * k : 32 * k + 32], right[144 * k : 144 * k + 144]) for k in range(4)]
+    return jnp.concatenate(parts, axis=0).T
+
+
+def group_back(g, qg, q4, kg, vg, p4, p4b, do, masks, dqkv_ref, ds0_ref, ds1_ref):
     do4 = stack_heads(do[:, 128 * g : 128 * (g + 1)], masks)
     dp4 = dot_nt(do4, vg)
-    dqkv_ref[:, 1024 + 128 * g : 1024 + 128 * (g + 1)] = dot_tn(p4b[:, 0:144], do4).astype(BF16)
+    if qg is None:
+        dv = dot_tn(p4b[:, 0:144], do4)
+    else:
+        dv = by_keys(do[:, 128 * g : 128 * (g + 1)].T, p4b)
+    dqkv_ref[:, 1024 + 128 * g : 1024 + 128 * (g + 1)] = dv.astype(BF16)
     ds4 = p4 * (dp4 - jnp.sum(dp4 * p4, axis=-1, keepdims=True))
     ds0_ref[576 * g : 576 * (g + 1), :] = ds4[:, 0:128]
     for k in range(4):
@@ -206,7 +220,10 @@
     ds4b = ds4.astype(BF16)
     dq = fold_heads(dot(ds4b, kg), masks) * SCALE
     dqkv_ref[:, 128 * g : 128 * (g + 1)] = dq.astype(BF16)
-    dk = dot_tn(ds4b[:, 0:144], q4) * SCALE
+    if qg is None:
+        dk = dot_tn(ds4b[:, 0:144], q4) * SCALE
+    else:
+        dk = by_keys(qg.T, ds4b) * SCALE
     dqkv_ref[:, 512 + 128 * g : 512 + 128 * (g + 1)] = dk.astype(BF16)
 
 
@@ -262,8 +279,8 @@
 
 def first_kernel(
     x_hbm, go_hbm, grp_hbm, gain_hbm, wqkv_hbm, wproj_hbm, tab_hbm, rel_hbm, const_hbm,
-    own_ref, lon_ref, lat_ref, dia_ref, n_ref, rstd_ref, qkv_ref, p_ref, o_ref,
-    cells, gs, pay, bias_ref, main_ref, tail_ref, words, scales, offsets,
+    own_ref, lon_ref, lat_ref, dia_ref, rstd_ref, n_hbm, qkv_hbm, p_hbm, o_hbm,
+    n_ref, qkv_ref, p_ref, o_ref, cells, gs, pay, bias_ref, main_ref, tail_ref, words, scales, offsets,
     x_ref, go_ref, grp_ref, gain_ref, wqkv_ref, wproj_ref, tab_ref, rel_ref, const_ref, sems,
 ):
     sources = [
@@ -280,6 +297,13 @@
     copies = [pltpu.make_async_copy(a, b, sems.at[k]) for k, (a, b) in enumerate(sources)]
     for copy in copies:
         copy.start()
+    results = []
+
+    def send(source, target):
+        copy = pltpu.make_async_copy(source, target, sems.at[9 + len(results)])
+        copy.start()
+        results.append(copy)
+
     for copy in copies[0:3]:
         copy.wait()
     px, ps, pm = [const_ref[k, 0 : (144, 160, 144)[k], 0:144] for k in range(3)]
@@ -306,21 +330,27 @@
 
     n, rstd = normalize(x)
     n_ref[...] = n
+    send(n_ref, n_hbm)
     rstd_ref[...] = rstd
     h = (n * gain_ref[0:1, :]).astype(BF16)
     qkv_ref[...] = dot(h, wqkv_ref[...]).astype(BF16)
+    send(qkv_ref, qkv_hbm)
     for g in range(4):
         biases = [bias_ref[576 * g + 144 * k : 576 * g + 144 * (k + 1), :] for k in range(4)]
         _, _, p4 = group_probs(qkv_ref, g, masks, biases, None)
         p4b = p4.astype(BF16)
         p_ref[576 * g : 576 * (g + 1), :] = p4b
+        send(p_ref.at[576 * g : 576 * (g + 1)], p_hbm.at[576 * g : 576 * (g + 1)])
         vg = pad_keys(qkv_ref[:, 1024 + 128 * g : 1024 + 128 * (g + 1)])
         o_ref[:, 128 * g : 128 * (g + 1)] = fold_heads(dot(p4b, vg), masks).astype(BF16)
+    send(o_ref, o_hbm)
     copies[8].wait()
     pay[:, 0:512] = (x + dot(o_ref[...], wproj_ref[...])).astype(BF16)
     out = dot(ps, pay[...])
     out = jnp.concatenate([out[:, 0:128] + group_rows, out[:, 128:1024]], axis=1)
     store_pieces(out, own_ref, lon_ref, lat_ref, dia_ref)
+    for copy in results:
+        copy.wait()
 
 
 def bias_kernel(
@@ -366,7 +396,7 @@
         p4b = p4.astype(BF16)
         vg = pad_keys(qkv_ref[:, 1024 + 128 * g : 1024 + 128 * (g + 1)])
         o_ref[:, 128 * g : 128 * (g + 1)] = fold_heads(dot(p4b, vg), masks).astype(BF16)
-        group_back(g, q4, kg, vg, p4, p4b, do, masks, dqkv_ref, ds0_ref, ds1_ref)
+        group_back(g, None, q4, kg, vg, p4, p4b, do, masks, dqkv_ref, ds0_ref, ds1_ref)
     back[:, 0:512] = (x + dot(o_ref[...], wproj_ref[0])).astype(BF16)
     df = finish_back(dqkv_ref, wqkv_ref, n, rstd, gain, g32, dgain_ref)
     back[:, 512:1024] = df.astype(BF16)
@@ -392,7 +422,7 @@
         kg = pad_keys(qkv_ref[:, 512 + 128 * g : 512 + 128 * (g + 1)])
         vg = pad_keys(qkv_ref[:, 1024 + 128 * g : 1024 + 128 * (g + 1)])
         p4b = p_ref[576 * g : 576 * (g + 1), :]
-        group_back(g, q4, kg, vg, p4b.astype(F32), p4b, do, masks, dqkv_ref, ds0_ref, ds1_ref)
+        group_back(g, qkv_ref[:, 128 * g : 128 * (g + 1)], q4, kg, vg, p4b.astype(F32), p4b, do, masks, dqkv_ref, ds0_ref, ds1_ref)
     h = (n_ref[...] * gain_ref[0:1, :]).astype(BF16)
     weight_terms(idx_ref, h, o_ref[...], dqkv_ref[...], gb, keep_ref, send_ref)
 
@@ -621,7 +651,7 @@
 HBM = pl.BlockSpec(memory_space=pltpu.HBM)
 
 
-def call(body, us, outs, *args, specs=None, scratch=(), sems=0, vmem=VMEM):
+def call(body, us, outs, *args, specs=None, scratch=(), sems=0, vmem=VMEM, hbm_outs=()):
     specs = dict(specs or {})
     if args[0].dtype == jnp.int32 and args[0].ndim == 1:
         specs[0] = SMEM
@@ -632,7 +662,7 @@
         body,
         grid=(1,),
         in_specs=[specs.get(i, _whole(a.shape)) for i, a in enumerate(args)],
-        out_specs=[_whole(s) for s, _ in outs],
+        out_specs=[HBM if k in hbm_outs else _whole(s) for k, (s, _) in enumerate(outs)],
         out_shape=[jax.ShapeDtypeStruct(s, t) for s, t in outs],
         scratch_shapes=scratch,
         compiler_params=pltpu.CompilerParams(vmem_limit_bytes=vmem),
@@ -699,21 +729,20 @@
     id_shapes = [((144, 128), jnp.int32), ((24, 128), jnp.int32)]
     tables = [((8, 768), jnp.int32), ((HEADS, 128), F32), ((HEADS, 128), F32)]
     piece = ((40, 1024), BF16)
-    own, lon, lat, dia, n0, rstd0, qkv0, p0, o0 = call(
+    saved = [((144, D), F32), ((144, 3 * D), BF16), ((2304, 256), BF16), ((144, D), BF16)]
+    own, lon, lat, dia, rstd0, n0, qkv0, p0, o0 = call(
         first_kernel,
         8,
         [piece] * 4
         + [
-            ((144, D), F32),
             ((144, 1), F32),
-            ((144, 3 * D), BF16),
-            ((2304, 256), BF16),
-            ((144, D), BF16),
-        ],
+        ]
+        + saved,
         x_cells, go_cells, groups.transpose(1, 0, 2), gains, qkv_weight, proj_weight, bias_table, rel_ids,
         first_const,
         specs={k: HBM for k in range(9)},
-        scratch=[((144, 1024), F32), ((12, 12), F32), ((144, 1024), BF16), ((2304, 256), F32)]
+        scratch=saved
+        + [((144, 1024), F32), ((12, 12), F32), ((144, 1024), BF16), ((2304, 256), F32)]
         + id_shapes
         + tables
         + [
@@ -727,7 +756,8 @@
             ((144, 144), jnp.int32),
             ((7, 160, 256), BF16),
         ],
-        sems=9,
+        sems=16,
+        hbm_outs=range(5, 9),
         vmem=57 << 20,
     )
     pieces = halo((own, lon, lat, dia), -1)

time: 106 us -> 105 us (level)
  no operation moved by 1% of the time
where the time goes in v5:
time: 105 us
  starting transfers between devices  47.4 us (45%)
  Pallas kernels  35.1 us (33%)
  waiting for transfers between devices  20.9 us (20%)
    pallas_call x14, Pallas kernels, call(): pl.pallas_call(body, grid=(1,), in_specs=[specs.get(i, _whole(a.shape)) f...  35.1 us
    ppermute x19, starting transfers between devices, flip(): lax.ppermute(value, AXES, [(s, s ^ mask_of(axes)) for s in range(256)])  26.1 us
    ppermute x4, starting transfers between devices, lon_step(): return lax.ppermute(value, AXES, pairs)  13.4 us
    ppermute x19, waiting for transfers between devices, flip(): lax.ppermute(value, AXES, [(s, s ^ mask_of(axes)) for s in range(256)])  13 us
    ppermute x4, starting transfers between devices, z_step(): return lax.ppermute(value, AXES, pairs)  7.94 us
    ppermute x4, waiting for transfers between devices, z_step(): return lax.ppermute(value, AXES, pairs)  6.8 us
  transfers between devices with their start and end apart: 27, of which 11 were waited for; matrix products, arithmetic and copies ran while one was open for 0% of the time, Pallas kernels for 15%

profile of v5, /device:TPU:1, one launch (start us, length us, event | category | flops | bytes accessed | tf_op | source)
XLA Modules:
  0.0 104.6 jit_solution(13592559303894556002)
XLA Ops:
  0.7 0.0 copy-start.8
  0.7 8.5 %shard_map.172 = (bf16[40,1024]{1,0:T(8,128)(2,1)}, bf16[40,1024]{1,0:T(8,128)(2,1)}, bf16[40,1024]{1,0:T(8,128)(2,1)}, bf16[40,1024]{1,0:T(8,128)(2,1)}, f32[14...) custom-call(bf16[72,2,512]{2,1,0:T(2,128)(2,1)} %bitcast.19, ...), custom_call_target="tpu_custom_call" | custom-call | flops 8000000000 | bytes 28800000 | tf_op jit(solution)/shard_map/pallas_call | solution.py:661
  9.2 3.3 %collective-permute-start = (bf16[40,1024]{1,0:T(8,128)(2,1)}, bf16[40,1024]{1,0:T(8,128)(2,1)S(1)}, u32[]{:S(2)}, u32[]{:S(2)}) collective-permute-start(bf16[40,1024]{1,0:T(8,128)(2,1)} %get-tuple-element.77), channel_id=1, source_target_pairs={{0,254},{1,255},{2,0},{3,1},{4,2},{5,3},{6,4},{7,5},{8,6},{9,7},{1... | collective-permute-start | bytes 245768 | tf_op jit(solution)/shard_map/ppermute | solution.py:690
  12.5 0.0 collective-permute-start.1
  12.5 10.0 %collective-permute-start.2 = (bf16[40,1024]{1,0:T(8,128)(2,1)}, bf16[40,1024]{1,0:T(8,128)(2,1)S(1)}, u32[]{:S(2)}, u32[]{:S(2)}) collective-permute-start(bf16[40,1024]{1,0:T(8,128)(2,1)} %get-tuple-element.79), channel_id=1, source_target_pairs={{0,255},{1,254},{2,1},{3,0},{4,3},{5,2},{6,5},{7,4},{8,7},{9,6},{1... | collective-permute-start | bytes 245768 | tf_op jit(solution)/shard_map/ppermute | solution.py:690
  22.5 0.1 stack.27.idx_ref
  22.6 0.0 copy-start
  22.6 0.0 copy-start.1
  22.6 0.0 copy-start.4
  22.7 0.0 copy-start.5
  22.7 0.0 copy-start.14
  22.7 3.9 %shard_map.173 = (f32[2304,256]{1,0:T(8,128)S(1)}, s32[144,128]{1,0:T(8,128)S(1)}, s32[24,128]{1,0:T(8,128)S(1)}) custom-call(s32[6]{0:T(128)S(1)} %stack.27.idx_ref, f32[2,2,16,759]{3,2,1,0:T(8,128)S(1)} %copy-done.2, s32[144,144]{1,0:T(8,128)S(1)} %copy-done.3, bf16[160,256]{1,0:T(8,128)(2,1)S(1)} %copy-done.8), custom_call_target="tpu_custom_call" | custom-call | flops 4000000000 | bytes 14400000 | tf_op jit(solution)/shard_map/pallas_call | solution.py:661
  26.6 0.0 collective-permute-done.1.lat_ref
  26.7 5.3 %shard_map.174 = (bf16[40,1024]{1,0:T(8,128)(2,1)S(1)}, bf16[40,1024]{1,0:T(8,128)(2,1)S(1)}, bf16[40,1024]{1,0:T(8,128)(2,1)S(1)}, bf16[40,1024]{1,0:T(8,128)(2...) custom-call(s32[6]{0:T(128)S(1)} %stack.27.idx_ref, ...), custom_call_target="tpu_custom_call" | custom-call | flops 6000000000 | bytes 21600000 | tf_op jit(solution)/shard_map/pallas_call | solution.py:661
  31.9 0.1 collective-permute-start.3
  32.0 0.5 collective-permute-start.4
  32.5 0.0 collective-permute-start.5
  32.6 0.0 copy-start.13
  32.6 1.8 %shard_map.175 = (bf16[256,2048]{1,0:T(8,128)(2,1)S(1)}, bf16[256,2048]{1,0:T(8,128)(2,1)S(1)}) custom-call(s32[6]{0:T(128)S(1)} %stack.27.idx_ref, bf16[144,512]{1,0:T(8,128)(2,1)S(1)} %get-tuple-element.90.h_ref, bf16[144,512]{1,0:T(8,128)(2,1)S(1)} %get-tuple-element.91.o_ref, bf16[144,1536]{1,0:T(8,128)(2,1)S(1)} %get-tuple-element.92.dqkv_ref, ...), custom_call_target="tpu_custom_call" | custom-call | flops 2000000000 | bytes 7200000 | tf_op jit(solution)/shard_map/pallas_call | solution.py:661
  34.3 1.7 %collective-permute-start.7 = (bf16[256,2048]{1,0:T(8,128)(2,1)S(1)}, bf16[256,2048]{1,0:T(8,128)(2,1)S(1)}, u32[]{:S(2)}, u32[]{:S(2)}) collective-permute-start(bf16[256,2048]{1,0:T(8,128)(2,1)S(1)} %get-tuple-element.101), channel_id=1, source_target_pairs={{0,2},{1,3},{2,0},{3,1},{4,6},{5,7},{6,4},{7,5},{8,10},{9,11},{10,... | collective-permute-start | bytes 3145736 | tf_op jit(solution)/shard_map/ppermute | solution.py:680
  36.1 1.1 %collective-permute-done.5.dia_ref = bf16[40,1024]{1,0:T(8,128)(2,1)S(1)} collective-permute-done((bf16[40,1024]{1,0:T(8,128)(2,1)S(1)}, bf16[40,1024]{1,0:T(8,128)(2,1)S(1)}, u32[]{:S(2)}, u32[]{:S(2)}) %collective-permute-start.5) | collective-permute-done | bytes 81952 | tf_op jit(solution)/shard_map/ppermute | solution.py:690
  37.2 0.0 copy-start.6
  37.2 3.5 %shard_map.176 = (bf16[144,512]{1,0:T(8,128)(2,1)S(1)}, bf16[144,1536]{1,0:T(8,128)(2,1)S(1)}, f32[2304,128]{1,0:T(8,128)S(1)}, f32[384,128]{1,0:T(8,128)S(1)}, ...) custom-call(s32[6]{0:T(128)S(1)} %stack.27.idx_ref, bf16[40,1024]{1,0:T(8,128)(2,1)S(1)} %get-tuple-element.81.own_ref, ...), custom_call_target="tpu_custom_call" | custom-call | flops 4000000000 | bytes 14400000 | tf_op jit(solution)/shard_map/pallas_call | solution.py:661
  40.8 5.4 %collective-permute-start.6 = (bf16[256,2048]{1,0:T(8,128)(2,1)S(1)}, bf16[256,2048]{1,0:T(8,128)(2,1)S(1)}, u32[]{:S(2)}, u32[]{:S(2)}) collective-permute-start(bf16[256,2048]{1,0:T(8,128)(2,1)S(1)} %get-tuple-element.100), channel_id=1, source_target_pairs={{0,2},{1,3},{2,0},{3,1},{4,6},{5,7},{6,4},{7,5},{8,10},{9,11},{10,... | collective-permute-start | bytes 3145736 | tf_op jit(solution)/shard_map/ppermute | solution.py:680
  46.2 1.7 %shard_map.177 = (bf16[72,2,512]{2,1,0:T(2,128)(2,1)}, bf16[72,2,512]{2,1,0:T(2,128)(2,1)}, f32[1,512]{1,0:T(1,128)S(1)}) custom-call(bf16[40,1024]{1,0:T(8,128)(2,1)S(1)} %get-tuple-element.81.own_ref, bf16[40,1024]{1,0:T(8,128)(2,1)S(1)} %collective-permute-done.3.lon_ref, bf16[40,1024]{1,0:T(8,128)(2,1)S(1)} %collective-permute-done.4.lat_ref, ...), custom_call_target="tpu_custom_call" | custom-call | flops 2000000000 | bytes 7200000 | tf_op jit(solution)/shard_map/pallas_call | solution.py:661
  47.9 0.0 collective-permute-done.7.r1_ref
  47.9 0.6 collective-permute-done.6.r0_ref
  48.5 1.2 %shard_map.178 = (bf16[128,1536]{1,0:T(8,128)(2,1)S(1)}, bf16[128,1536]{1,0:T(8,128)(2,1)S(1)}, bf16[256,768]{1,0:T(8,128)(2,1)S(1)}, bf16[256,768]{1,0:T(8,128)...) custom-call(s32[6]{0:T(128)S(1)} %stack.27.idx_ref, ...), custom_call_target="tpu_custom_call" | custom-call | flops 1000000000 | bytes 3600000 | tf_op jit(solution)/shard_map/pallas_call | solution.py:661
  49.7 0.1 collective-permute-start.10
  49.8 0.1 collective-permute-start.8
  49.9 0.2 collective-permute-start.9
  50.1 4.5 %shard_map.179 = (f32[16,1024]{1,0:T(8,128)S(1)}, f32[16,1024]{1,0:T(8,128)S(1)}) custom-call(s32[6]{0:T(128)S(1)} %stack.27.idx_ref, s32[144,128]{1,0:T(8,128)S(1)} %get-tuple-element.108.main_ref, s32[24,128]{1,0:T(8,128)S(1)} %get-tuple-element.109.tail_ref, f32[2304,128]{1,0:T(8,128)S(1)} %get-tuple-element.110.m0_ref, ...), custom_call_target="tpu_custom_call" | custom-call | flops 6000000000 | bytes 21600000 | tf_op jit(solution)/shard_map/pallas_call | solution.py:661
  54.6 0.7 collective-permute-start.11
  55.4 0.9 collective-permute-done.11.u_ref
  56.3 1.0 collective-permute-done.10.rc_ref
  57.3 2.9 %collective-permute-done.8.ra_ref = bf16[128,1536]{1,0:T(8,128)(2,1)S(1)} collective-permute-done((bf16[128,1536]{1,0:T(8,128)(2,1)S(1)}, bf16[128,1536]{1,0:T(8,128)(2,1)S(1)}, u32[]{:S(2)}, u32[]{:S(2)}) %collective-permute-start.8) | collective-permute-done | bytes 393248 | tf_op jit(solution)/shard_map/ppermute | solution.py:680
  60.2 0.1 collective-permute-done.9.rb_ref
  60.3 0.9 shard_map.180
  61.2 0.2 collective-permute-start.12
  61.4 0.9 collective-permute-start.13
  62.4 1.1 %collective-permute-start.14 = (bf16[80,1024]{1,0:T(8,128)(2,1)S(1)}, bf16[80,1024]{1,0:T(8,128)(2,1)S(1)}, u32[]{:S(2)}, u32[]{:S(2)}) collective-permute-start(bf16[80,1024]{1,0:T(8,128)(2,1)S(1)} %get-tuple-element.123), channel_id=1, source_target_pairs={{0,32},{1,33},{2,34},{3,35},{4,36},{5,37},{6,38},{7,39},{8,40},{9,... | collective-permute-start | bytes 491528 | tf_op jit(solution)/shard_map/ppermute | solution.py:680
  63.5 3.3 %collective-permute-done.14.rc_ref = bf16[80,1024]{1,0:T(8,128)(2,1)S(1)} collective-permute-done((bf16[80,1024]{1,0:T(8,128)(2,1)S(1)}, bf16[80,1024]{1,0:T(8,128)(2,1)S(1)}, u32[]{:S(2)}, u32[]{:S(2)}) %collective-permute-start.14) | collective-permute-done | bytes 163872 | tf_op jit(solution)/shard_map/ppermute | solution.py:680
  66.8 0.0 collective-permute-done.12.ra_ref
  66.8 0.0 collective-permute-done.13.rb_ref
  66.8 0.7 shard_map.181
  67.6 0.6 collective-permute-start.15
  68.2 1.0 collective-permute-start.16
  69.2 1.3 %collective-permute-start.17 = (bf16[64,512]{1,0:T(8,128)(2,1)S(1)}, bf16[64,512]{1,0:T(8,128)(2,1)S(1)}, u32[]{:S(2)}, u32[]{:S(2)}) collective-permute-start(bf16[64,512]{1,0:T(8,128)(2,1)S(1)} %get-tuple-element.130), channel_id=1, source_target_pairs={{0,1},{1,0},{2,3},{3,2},{4,5},{5,4},{6,7},{7,6},{8,9},{9,8},{10,11... | collective-permute-start | bytes 196616 | tf_op jit(solution)/shard_map/ppermute | solution.py:680
  70.5 1.8 %collective-permute-done.17.rc_ref = bf16[64,512]{1,0:T(8,128)(2,1)S(1)} collective-permute-done((bf16[64,512]{1,0:T(8,128)(2,1)S(1)}, bf16[64,512]{1,0:T(8,128)(2,1)S(1)}, u32[]{:S(2)}, u32[]{:S(2)}) %collective-permute-start.17) | collective-permute-done | bytes 65568 | tf_op jit(solution)/shard_map/ppermute | solution.py:680
  72.3 0.7 shard_map.182
  73.0 0.1 collective-permute-start.18
  73.1 0.6 collective-permute-start.19
  73.7 4.5 %collective-permute-start.20 = (bf16[24,2048]{1,0:T(8,128)(2,1)S(1)}, bf16[24,2048]{1,0:T(8,128)(2,1)S(1)}, u32[]{:S(2)}, u32[]{:S(2)}) collective-permute-start(bf16[24,2048]{1,0:T(8,128)(2,1)S(1)} %get-tuple-element.135), channel_id=1, source_target_pairs={{0,124},{1,125},{2,126},{3,127},{4,104},{5,105},{6,106},{7,107},{8... | collective-permute-start | bytes 294920 | tf_op jit(solution)/shard_map/ppermute | solution.py:685
  78.2 2.9 %collective-permute-done.20.g3_ref = bf16[24,2048]{1,0:T(8,128)(2,1)S(1)} collective-permute-done((bf16[24,2048]{1,0:T(8,128)(2,1)S(1)}, bf16[24,2048]{1,0:T(8,128)(2,1)S(1)}, u32[]{:S(2)}, u32[]{:S(2)}) %collective-permute-start.20) | collective-permute-done | bytes 98336 | tf_op jit(solution)/shard_map/ppermute | solution.py:685
  81.0 0.6 shard_map.183
  81.7 0.1 collective-permute-start.21
  81.8 2.7 %collective-permute-start.22 = (bf16[24,1024]{1,0:T(8,128)(2,1)S(1)}, bf16[24,1024]{1,0:T(8,128)(2,1)S(1)}, u32[]{:S(2)}, u32[]{:S(2)}) collective-permute-start(bf16[24,1024]{1,0:T(8,128)(2,1)S(1)} %get-tuple-element.138), channel_id=1, source_target_pairs={{0,128},{1,129},{2,130},{3,131},{4,132},{5,133},{6,134},{7,135},{8... | collective-permute-start | bytes 147464 | tf_op jit(solution)/shard_map/ppermute | solution.py:680
  84.4 3.3 %collective-permute-start.23 = (bf16[24,1024]{1,0:T(8,128)(2,1)S(1)}, bf16[24,1024]{1,0:T(8,128)(2,1)S(1)}, u32[]{:S(2)}, u32[]{:S(2)}) collective-permute-start(bf16[24,1024]{1,0:T(8,128)(2,1)S(1)} %get-tuple-element.139), channel_id=1, source_target_pairs={{0,140},{1,141},{2,142},{3,143},{4,152},{5,153},{6,154},{7,155},{8... | collective-permute-start | bytes 147464 | tf_op jit(solution)/shard_map/ppermute | solution.py:685
  87.7 3.9 %collective-permute-done.23.g3_ref = bf16[24,1024]{1,0:T(8,128)(2,1)S(1)} collective-permute-done((bf16[24,1024]{1,0:T(8,128)(2,1)S(1)}, bf16[24,1024]{1,0:T(8,128)(2,1)S(1)}, u32[]{:S(2)}, u32[]{:S(2)}) %collective-permute-start.23) | collective-permute-done | bytes 49184 | tf_op jit(solution)/shard_map/ppermute | solution.py:685
  91.6 0.6 shard_map.184
  92.2 0.2 collective-permute-start.24
  92.4 8.5 %collective-permute-start.26 = (bf16[16,1024]{1,0:T(8,128)(2,1)S(1)}, bf16[16,1024]{1,0:T(8,128)(2,1)S(1)}, u32[]{:S(2)}, u32[]{:S(2)}) collective-permute-start(bf16[16,1024]{1,0:T(8,128)(2,1)S(1)} %get-tuple-element.141), channel_id=1, source_target_pairs={{0,3},{1,2},{2,1},{3,0},{4,7},{5,6},{6,5},{7,4},{8,11},{9,10},{10,... | collective-permute-start | bytes 98312 | tf_op jit(solution)/shard_map/ppermute | solution.py:680
  100.9 2.4 %collective-permute-done.26.dia_ref = bf16[16,1024]{1,0:T(8,128)(2,1)S(1)} collective-permute-done((bf16[16,1024]{1,0:T(8,128)(2,1)S(1)}, bf16[16,1024]{1,0:T(8,128)(2,1)S(1)}, u32[]{:S(2)}, u32[]{:S(2)}) %collective-permute-start.26) | collective-permute-done | bytes 32800 | tf_op jit(solution)/shard_map/ppermute | solution.py:680
  103.3 1.3 %shard_map.185 = (f32[2,512]{1,0:T(2,128)}, f32[2,4,1536]{2,1,0:T(4,128)}, f32[2,4,512]{2,1,0:T(4,128)}, f32[2,2,16,759]{3,2,1,0:T(8,128)}) custom-call(s32[6]{0:T(128)S(1)} %stack.27.idx_ref, bf16[24,1024]{1,0:T(8,128)(2,1)S(1)} %get-tuple-element.140.own_ref, bf16[24,1024]{1,0:T(8,128)(2,1)S(1)} %collective-permute-done.24.lat_ref, ...), custom_call_target="tpu_custom_call" | custom-call | flops 1000000000 | bytes 3600000 | tf_op jit(solution)/shard_map/pallas_call | solution.py:661
  (35 shorter events, 0.1 us)
Async XLA Ops:
  0.6 22.0 %copy-start.2 = (f32[2,2,16,759]{3,2,1,0:T(8,128)S(1)}, f32[2,2,16,759]{3,2,1,0:T(8,128)}, u32[]{:S(2)}) copy-start(f32[2,2,16,759]{3,2,1,0:T(8,128)} %tab_ref.1) | copy-start | bytes 582916
  0.6 22.0 %copy-start.3 = (s32[144,144]{1,0:T(8,128)S(1)}, s32[144,144]{1,0:T(8,128)}, u32[]{:S(2)}) copy-start(s32[144,144]{1,0:T(8,128)} %rel_ref.1) | copy-start | bytes 248836
  0.7 22.0 %copy-start.8 = (bf16[160,256]{1,0:T(8,128)(2,1)S(1)}, bf16[160,256]{1,0:T(8,128)(2,1)}, u32[]{:S(2)}) copy-start(bf16[160,256]{1,0:T(8,128)(2,1)} %constant.46.clone.pm_ref) | copy-start | bytes 245764
  9.2 17.4 %collective-permute-start = (bf16[40,1024]{1,0:T(8,128)(2,1)}, bf16[40,1024]{1,0:T(8,128)(2,1)S(1)}, u32[]{:S(2)}, u32[]{:S(2)}) collective-permute-start(bf16[40,1024]{1,0:T(8,128)(2,1)} %get-tuple-element.77), channel_id=1, source_target_pairs={{0,254},{1,255},{2,0},{3,1},{4,2},{5,3},{6,4},{7,5},{8,6},{9,7},{1... | collective-permute-start | bytes 245768 | tf_op jit(solution)/shard_map/ppermute | solution.py:690
  12.5 14.1 %collective-permute-start.1 = (bf16[40,1024]{1,0:T(8,128)(2,1)}, bf16[40,1024]{1,0:T(8,128)(2,1)S(1)}, u32[]{:S(2)}, u32[]{:S(2)}) collective-permute-start(bf16[40,1024]{1,0:T(8,128)(2,1)} %get-tuple-element.78), channel_id=1, source_target_pairs={{0,1},{1,0},{2,3},{3,2},{4,5},{5,4},{6,7},{7,6},{8,9},{9,8},{10,11... | collective-permute-start | bytes 245768 | tf_op jit(solution)/shard_map/ppermute | solution.py:680
  12.5 14.1 %collective-permute-start.2 = (bf16[40,1024]{1,0:T(8,128)(2,1)}, bf16[40,1024]{1,0:T(8,128)(2,1)S(1)}, u32[]{:S(2)}, u32[]{:S(2)}) collective-permute-start(bf16[40,1024]{1,0:T(8,128)(2,1)} %get-tuple-element.79), channel_id=1, source_target_pairs={{0,255},{1,254},{2,1},{3,0},{4,3},{5,2},{6,5},{7,4},{8,7},{9,6},{1... | collective-permute-start | bytes 245768 | tf_op jit(solution)/shard_map/ppermute | solution.py:690
  22.6 4.0 %copy-start = (bf16[2,512,1536]{2,1,0:T(8,128)(2,1)S(1)}, bf16[2,512,1536]{2,1,0:T(8,128)(2,1)}, u32[]{:S(2)}) copy-start(bf16[2,512,1536]{2,1,0:T(8,128)(2,1)} %wqkv_ref.3) | copy-start | bytes 9437188
  22.6 4.0 %copy-start.1 = (bf16[2,512,512]{2,1,0:T(8,128)(2,1)S(1)}, bf16[2,512,512]{2,1,0:T(8,128)(2,1)}, u32[]{:S(2)}) copy-start(bf16[2,512,512]{2,1,0:T(8,128)(2,1)} %wproj_ref.3) | copy-start | bytes 3145732
  22.6 4.0 %copy-start.4 = (f32[2,512]{1,0:T(2,128)S(1)}, f32[2,512]{1,0:T(2,128)}, u32[]{:S(2)}) copy-start(f32[2,512]{1,0:T(2,128)} %gain_ref.5) | copy-start | bytes 12292
  22.7 4.0 %copy-start.5 = (bf16[5,160,256]{2,1,0:T(8,128)(2,1)S(1)}, bf16[5,160,256]{2,1,0:T(8,128)(2,1)}, u32[]{:S(2)}) copy-start(bf16[5,160,256]{2,1,0:T(8,128)(2,1)} %constant.43.clone.const_ref) | copy-start | bytes 1228804
  22.7 4.0 %copy-start.14 = (bf16[40,1024]{1,0:T(8,128)(2,1)S(1)}, bf16[40,1024]{1,0:T(8,128)(2,1)}, u32[]{:S(2)}) copy-start(bf16[40,1024]{1,0:T(8,128)(2,1)} %get-tuple-element.76.own_ref) | copy-start | bytes 245764
  31.9 4.1 %collective-permute-start.3 = (bf16[40,1024]{1,0:T(8,128)(2,1)S(1)}, bf16[40,1024]{1,0:T(8,128)(2,1)S(1)}, u32[]{:S(2)}, u32[]{:S(2)}) collective-permute-start(bf16[40,1024]{1,0:T(8,128)(2,1)S(1)} %get-tuple-element.82), channel_id=1, source_target_pairs={{0,2},{1,3},{2,4},{3,5},{4,6},{5,7},{6,8},{7,9},{8,10},{9,11},{10,... | collective-permute-start | bytes 245768 | tf_op jit(solution)/shard_map/ppermute | solution.py:690
  32.0 4.0 %collective-permute-start.4 = (bf16[40,1024]{1,0:T(8,128)(2,1)S(1)}, bf16[40,1024]{1,0:T(8,128)(2,1)S(1)}, u32[]{:S(2)}, u32[]{:S(2)}) collective-permute-start(bf16[40,1024]{1,0:T(8,128)(2,1)S(1)} %get-tuple-element.83), channel_id=1, source_target_pairs={{0,1},{1,0},{2,3},{3,2},{4,5},{5,4},{6,7},{7,6},{8,9},{9,8},{10,11... | collective-permute-start | bytes 245768 | tf_op jit(solution)/shard_map/ppermute | solution.py:680
  32.5 4.6 %collective-permute-start.5 = (bf16[40,1024]{1,0:T(8,128)(2,1)S(1)}, bf16[40,1024]{1,0:T(8,128)(2,1)S(1)}, u32[]{:S(2)}, u32[]{:S(2)}) collective-permute-start(bf16[40,1024]{1,0:T(8,128)(2,1)S(1)} %get-tuple-element.84), channel_id=1, source_target_pairs={{0,3},{1,2},{2,5},{3,4},{4,7},{5,6},{6,9},{7,8},{8,11},{9,10},{10,... | collective-permute-start | bytes 245768 | tf_op jit(solution)/shard_map/ppermute | solution.py:690
  32.5 4.6 %copy-start.7 = (bf16[1,160,256]{2,1,0:T(8,128)(2,1)S(1)}, bf16[1,160,256]{2,1,0:T(8,128)(2,1)}, u32[]{:S(2)}) copy-start(bf16[1,160,256]{2,1,0:T(8,128)(2,1)} %constant.44.clone.const_ref) | copy-start | bytes 245764
  32.5 4.6 %copy-start.9 = (f32[144,512]{1,0:T(8,128)S(1)}, f32[144,512]{1,0:T(8,128)}, u32[]{:S(2)}) copy-start(f32[144,512]{1,0:T(8,128)} %get-tuple-element.85.n_ref) | copy-start | bytes 884740
  32.5 4.6 %copy-start.11 = (bf16[2304,256]{1,0:T(8,128)(2,1)S(1)}, bf16[2304,256]{1,0:T(8,128)(2,1)}, u32[]{:S(2)}) copy-start(bf16[2304,256]{1,0:T(8,128)(2,1)} %get-tuple-element.88.p_ref) | copy-start | bytes 3538948
  32.5 4.6 %copy-start.12 = (bf16[144,1536]{1,0:T(8,128)(2,1)S(1)}, bf16[144,1536]{1,0:T(8,128)(2,1)}, u32[]{:S(2)}) copy-start(bf16[144,1536]{1,0:T(8,128)(2,1)} %get-tuple-element.87.qkv_ref) | copy-start | bytes 1327108
  32.6 4.6 %copy-start.13 = (bf16[144,512]{1,0:T(8,128)(2,1)S(1)}, bf16[144,512]{1,0:T(8,128)(2,1)}, u32[]{:S(2)}) copy-start(bf16[144,512]{1,0:T(8,128)(2,1)} %get-tuple-element.89.o_ref) | copy-start | bytes 442372
  34.3 13.6 %collective-permute-start.7 = (bf16[256,2048]{1,0:T(8,128)(2,1)S(1)}, bf16[256,2048]{1,0:T(8,128)(2,1)S(1)}, u32[]{:S(2)}, u32[]{:S(2)}) collective-permute-start(bf16[256,2048]{1,0:T(8,128)(2,1)S(1)} %get-tuple-element.101), channel_id=1, source_target_pairs={{0,2},{1,3},{2,0},{3,1},{4,6},{5,7},{6,4},{7,5},{8,10},{9,11},{10,... | collective-permute-start | bytes 3145736 | tf_op jit(solution)/shard_map/ppermute | solution.py:680
  37.2 9.0 %copy-start.6 = (bf16[2,160,256]{2,1,0:T(8,128)(2,1)S(1)}, bf16[2,160,256]{2,1,0:T(8,128)(2,1)}, u32[]{:S(2)}) copy-start(bf16[2,160,256]{2,1,0:T(8,128)(2,1)} %constant.45.clone.const_ref) | copy-start | bytes 491524
  37.2 9.0 %copy-start.10 = (f32[144,1]{1,0:T(8,128)S(1)}, f32[144,1]{1,0:T(8,128)}, u32[]{:S(2)}) copy-start(f32[144,1]{1,0:T(8,128)} %get-tuple-element.86.rstd_ref) | copy-start | bytes 1732
  40.8 7.7 %collective-permute-start.6 = (bf16[256,2048]{1,0:T(8,128)(2,1)S(1)}, bf16[256,2048]{1,0:T(8,128)(2,1)S(1)}, u32[]{:S(2)}, u32[]{:S(2)}) collective-permute-start(bf16[256,2048]{1,0:T(8,128)(2,1)S(1)} %get-tuple-element.100), channel_id=1, source_target_pairs={{0,2},{1,3},{2,0},{3,1},{4,6},{5,7},{6,4},{7,5},{8,10},{9,11},{10,... | collective-permute-start | bytes 3145736 | tf_op jit(solution)/shard_map/ppermute | solution.py:680
  49.7 7.6 %collective-permute-start.10 = (bf16[128,1024]{1,0:T(8,128)(2,1)S(1)}, bf16[128,1024]{1,0:T(8,128)(2,1)S(1)}, u32[]{:S(2)}, u32[]{:S(2)}) collective-permute-start(bf16[128,1024]{1,0:T(8,128)(2,1)S(1)} %get-tuple-element.107), channel_id=1, source_target_pairs={{0,4},{1,5},{2,6},{3,7},{4,0},{5,1},{6,2},{7,3},{8,12},{9,13},{10,... | collective-permute-start | bytes 786440 | tf_op jit(solution)/shard_map/ppermute | solution.py:680
  49.8 10.4 %collective-permute-start.8 = (bf16[128,1536]{1,0:T(8,128)(2,1)S(1)}, bf16[128,1536]{1,0:T(8,128)(2,1)S(1)}, u32[]{:S(2)}, u32[]{:S(2)}) collective-permute-start(bf16[128,1536]{1,0:T(8,128)(2,1)S(1)} %get-tuple-element.103), channel_id=1, source_target_pairs={{0,32},{1,33},{2,34},{3,35},{4,36},{5,37},{6,38},{7,39},{8,40},{9,... | collective-permute-start | bytes 1179656 | tf_op jit(solution)/shard_map/ppermute | solution.py:680
  49.9 10.4 %collective-permute-start.9 = (bf16[256,768]{1,0:T(8,128)(2,1)S(1)}, bf16[256,768]{1,0:T(8,128)(2,1)S(1)}, u32[]{:S(2)}, u32[]{:S(2)}) collective-permute-start(bf16[256,768]{1,0:T(8,128)(2,1)S(1)} %get-tuple-element.105), channel_id=1, source_target_pairs={{0,1},{1,0},{2,3},{3,2},{4,5},{5,4},{6,7},{7,6},{8,9},{9,8},{10,11... | collective-permute-start | bytes 1179656 | tf_op jit(solution)/shard_map/ppermute | solution.py:680
  54.6 1.6 %collective-permute-start.11 = (f32[16,1024]{1,0:T(8,128)S(1)}, f32[16,1024]{1,0:T(8,128)S(1)}, u32[]{:S(2)}, u32[]{:S(2)}) collective-permute-start(f32[16,1024]{1,0:T(8,128)S(1)} %get-tuple-element.117), channel_id=1, source_target_pairs={{0,2},{1,3},{2,0},{3,1},{4,6},{5,7},{6,4},{7,5},{8,10},{9,11},{10,... | collective-permute-start | bytes 196616 | tf_op jit(solution)/shard_map/ppermute | solution.py:680
  61.2 5.7 %collective-permute-start.12 = (bf16[128,768]{1,0:T(8,128)(2,1)S(1)}, bf16[128,768]{1,0:T(8,128)(2,1)S(1)}, u32[]{:S(2)}, u32[]{:S(2)}) collective-permute-start(bf16[128,768]{1,0:T(8,128)(2,1)S(1)} %get-tuple-element.119), channel_id=1, source_target_pairs={{0,1},{1,0},{2,3},{3,2},{4,5},{5,4},{6,7},{7,6},{8,9},{9,8},{10,11... | collective-permute-start | bytes 589832 | tf_op jit(solution)/shard_map/ppermute | solution.py:680
  61.4 5.4 %collective-permute-start.13 = (bf16[128,768]{1,0:T(8,128)(2,1)S(1)}, bf16[128,768]{1,0:T(8,128)(2,1)S(1)}, u32[]{:S(2)}, u32[]{:S(2)}) collective-permute-start(bf16[128,768]{1,0:T(8,128)(2,1)S(1)} %get-tuple-element.121), channel_id=1, source_target_pairs={{0,4},{1,5},{2,6},{3,7},{4,0},{5,1},{6,2},{7,3},{8,12},{9,13},{10,... | collective-permute-start | bytes 589832 | tf_op jit(solution)/shard_map/ppermute | solution.py:680
  62.4 4.5 %collective-permute-start.14 = (bf16[80,1024]{1,0:T(8,128)(2,1)S(1)}, bf16[80,1024]{1,0:T(8,128)(2,1)S(1)}, u32[]{:S(2)}, u32[]{:S(2)}) collective-permute-start(bf16[80,1024]{1,0:T(8,128)(2,1)S(1)} %get-tuple-element.123), channel_id=1, source_target_pairs={{0,32},{1,33},{2,34},{3,35},{4,36},{5,37},{6,38},{7,39},{8,40},{9,... | collective-permute-start | bytes 491528 | tf_op jit(solution)/shard_map/ppermute | solution.py:680
  67.6 4.8 %collective-permute-start.15 = (bf16[96,768]{1,0:T(8,128)(2,1)S(1)}, bf16[96,768]{1,0:T(8,128)(2,1)S(1)}, u32[]{:S(2)}, u32[]{:S(2)}) collective-permute-start(bf16[96,768]{1,0:T(8,128)(2,1)S(1)} %get-tuple-element.126), channel_id=1, source_target_pairs={{0,4},{1,5},{2,6},{3,7},{4,0},{5,1},{6,2},{7,3},{8,12},{9,13},{10,... | collective-permute-start | bytes 442376 | tf_op jit(solution)/shard_map/ppermute | solution.py:680
  68.2 4.2 %collective-permute-start.16 = (bf16[64,768]{1,0:T(8,128)(2,1)S(1)}, bf16[64,768]{1,0:T(8,128)(2,1)S(1)}, u32[]{:S(2)}, u32[]{:S(2)}) collective-permute-start(bf16[64,768]{1,0:T(8,128)(2,1)S(1)} %get-tuple-element.128), channel_id=1, source_target_pairs={{0,32},{1,33},{2,34},{3,35},{4,36},{5,37},{6,38},{7,39},{8,40},{9,... | collective-permute-start | bytes 294920 | tf_op jit(solution)/shard_map/ppermute | solution.py:680
  69.2 3.1 %collective-permute-start.17 = (bf16[64,512]{1,0:T(8,128)(2,1)S(1)}, bf16[64,512]{1,0:T(8,128)(2,1)S(1)}, u32[]{:S(2)}, u32[]{:S(2)}) collective-permute-start(bf16[64,512]{1,0:T(8,128)(2,1)S(1)} %get-tuple-element.130), channel_id=1, source_target_pairs={{0,1},{1,0},{2,3},{3,2},{4,5},{5,4},{6,7},{7,6},{8,9},{9,8},{10,11... | collective-permute-start | bytes 196616 | tf_op jit(solution)/shard_map/ppermute | solution.py:680
  73.0 5.2 %collective-permute-start.18 = (bf16[24,2048]{1,0:T(8,128)(2,1)S(1)}, bf16[24,2048]{1,0:T(8,128)(2,1)S(1)}, u32[]{:S(2)}, u32[]{:S(2)}) collective-permute-start(bf16[24,2048]{1,0:T(8,128)(2,1)S(1)} %get-tuple-element.133), channel_id=1, source_target_pairs={{0,28},{1,29},{2,30},{3,31},{4,8},{5,9},{6,10},{7,11},{8,4},{9,5},... | collective-permute-start | bytes 294920 | tf_op jit(solution)/shard_map/ppermute | solution.py:685
  73.1 5.1 %collective-permute-start.19 = (bf16[24,2048]{1,0:T(8,128)(2,1)S(1)}, bf16[24,2048]{1,0:T(8,128)(2,1)S(1)}, u32[]{:S(2)}, u32[]{:S(2)}) collective-permute-start(bf16[24,2048]{1,0:T(8,128)(2,1)S(1)} %get-tuple-element.134), channel_id=1, source_target_pairs={{0,96},{1,97},{2,98},{3,99},{4,100},{5,101},{6,102},{7,103},{8,104... | collective-permute-start | bytes 294920 | tf_op jit(solution)/shard_map/ppermute | solution.py:680
  73.7 7.4 %collective-permute-start.20 = (bf16[24,2048]{1,0:T(8,128)(2,1)S(1)}, bf16[24,2048]{1,0:T(8,128)(2,1)S(1)}, u32[]{:S(2)}, u32[]{:S(2)}) collective-permute-start(bf16[24,2048]{1,0:T(8,128)(2,1)S(1)} %get-tuple-element.135), channel_id=1, source_target_pairs={{0,124},{1,125},{2,126},{3,127},{4,104},{5,105},{6,106},{7,107},{8... | collective-permute-start | bytes 294920 | tf_op jit(solution)/shard_map/ppermute | solution.py:685
  81.7 6.0 %collective-permute-start.21 = (bf16[24,1024]{1,0:T(8,128)(2,1)S(1)}, bf16[24,1024]{1,0:T(8,128)(2,1)S(1)}, u32[]{:S(2)}, u32[]{:S(2)}) collective-permute-start(bf16[24,1024]{1,0:T(8,128)(2,1)S(1)} %get-tuple-element.137), channel_id=1, source_target_pairs={{0,12},{1,13},{2,14},{3,15},{4,24},{5,25},{6,26},{7,27},{8,20},{9,... | collective-permute-start | bytes 147464 | tf_op jit(solution)/shard_map/ppermute | solution.py:685
  81.8 5.9 %collective-permute-start.22 = (bf16[24,1024]{1,0:T(8,128)(2,1)S(1)}, bf16[24,1024]{1,0:T(8,128)(2,1)S(1)}, u32[]{:S(2)}, u32[]{:S(2)}) collective-permute-start(bf16[24,1024]{1,0:T(8,128)(2,1)S(1)} %get-tuple-element.138), channel_id=1, source_target_pairs={{0,128},{1,129},{2,130},{3,131},{4,132},{5,133},{6,134},{7,135},{8... | collective-permute-start | bytes 147464 | tf_op jit(solution)/shard_map/ppermute | solution.py:680
  84.4 7.2 %collective-permute-start.23 = (bf16[24,1024]{1,0:T(8,128)(2,1)S(1)}, bf16[24,1024]{1,0:T(8,128)(2,1)S(1)}, u32[]{:S(2)}, u32[]{:S(2)}) collective-permute-start(bf16[24,1024]{1,0:T(8,128)(2,1)S(1)} %get-tuple-element.139), channel_id=1, source_target_pairs={{0,140},{1,141},{2,142},{3,143},{4,152},{5,153},{6,154},{7,155},{8... | collective-permute-start | bytes 147464 | tf_op jit(solution)/shard_map/ppermute | solution.py:685
  92.2 11.1 %collective-permute-start.24 = (bf16[24,1024]{1,0:T(8,128)(2,1)S(1)}, bf16[24,1024]{1,0:T(8,128)(2,1)S(1)}, u32[]{:S(2)}, u32[]{:S(2)}) collective-permute-start(bf16[24,1024]{1,0:T(8,128)(2,1)S(1)} %get-tuple-element.140.own_ref), channel_id=1, source_target_pairs={{0,1},{1,0},{2,3},{3,2},{4,5},{5,4},{6,7},{7,6},{8,9},{9,8},{10,11... | collective-permute-start | bytes 147464 | tf_op jit(solution)/shard_map/ppermute | solution.py:680
  92.4 10.9 %collective-permute-start.26 = (bf16[16,1024]{1,0:T(8,128)(2,1)S(1)}, bf16[16,1024]{1,0:T(8,128)(2,1)S(1)}, u32[]{:S(2)}, u32[]{:S(2)}) collective-permute-start(bf16[16,1024]{1,0:T(8,128)(2,1)S(1)} %get-tuple-element.141), channel_id=1, source_target_pairs={{0,3},{1,2},{2,1},{3,0},{4,7},{5,6},{6,5},{7,4},{8,11},{9,10},{10,... | collective-permute-start | bytes 98312 | tf_op jit(solution)/shard_map/ppermute | solution.py:680
  100.9 2.4 %collective-permute-start.25 = (bf16[16,1024]{1,0:T(8,128)(2,1)S(1)}, bf16[16,1024]{1,0:T(8,128)(2,1)S(1)}, u32[]{:S(2)}, u32[]{:S(2)}) collective-permute-start(bf16[16,1024]{1,0:T(8,128)(2,1)S(1)} %get-tuple-element.141), channel_id=1, source_target_pairs={{0,2},{1,3},{2,0},{3,1},{4,6},{5,7},{6,4},{7,5},{8,10},{9,11},{10,... | collective-permute-start | bytes 98312 | tf_op jit(solution)/shard_map/ppermute | solution.py:680

commit v6 on v5

--- a/solution.py
+++ b/solution.py
@@ -242,8 +242,7 @@
     )
 
 
-def weight_terms(idx_ref, h, o, dqkv, g, keep_ref, send_ref):
-    core = idx_ref[0]
+def weight_terms(which, *targets):
     p = lax.broadcasted_iota(jnp.int32, (256, 512), 0)
     row = lax.broadcasted_iota(jnp.int32, (256, 512), 1)
     bit = lambda k: (p >> k) & 1
@@ -260,8 +259,8 @@
     base = p & 3
     for to, value in place:
         base = base + (value << to)
-    for which, ref in ((core, keep_ref), (1 - core, send_ref)):
-        pick = jnp.where(row == base + which * 4, 1.0, 0.0).astype(BF16)
+    pick = jnp.where(row == base + which * 4, 1.0, 0.0).astype(BF16)
+    for h, o, dqkv, g, ref in targets:
         ht = dot_nt(pick, h).astype(BF16)
         ot = dot_nt(pick, o).astype(BF16)
         ref[:, 0:1536] = dot(ht, dqkv).astype(BF16)
@@ -403,14 +402,15 @@
     store_pieces(dot(const_ref[1, :, 0:144], back[...]), oown_ref, olon_ref, olat_ref, odia_ref)
 
 
-def weights_kernel(idx_ref, h_ref, o_ref, dqkv_ref, g_ref, keep_ref, send_ref):
-    weight_terms(idx_ref, h_ref[...], o_ref[...], dqkv_ref[...], g_ref[...], keep_ref, send_ref)
+def send_kernel(idx_ref, h_ref, o_ref, dqkv_ref, g_ref, send_ref):
+    target = h_ref[...], o_ref[...], dqkv_ref[...], g_ref[...], send_ref
+    weight_terms(1 - idx_ref[0], target)
 
 
 def third_kernel(
     idx_ref, own_ref, lon_ref, lat_ref, dia_ref, gain_ref, wproj_ref,
     n_ref, qkv_ref, p_ref, o_ref, const_ref, after_ref,
-    g_ref, dqkv_ref, ds0_ref, ds1_ref, keep_ref, send_ref,
+    g_ref, h_ref, dqkv_ref, ds0_ref, ds1_ref, send_ref,
 ):
     masks = lane_masks()
     pieces = load_pieces(slice(512, 1024), own_ref, lon_ref, lat_ref, dia_ref)
@@ -424,7 +424,13 @@
         p4b = p_ref[576 * g : 576 * (g + 1), :]
         group_back(g, qkv_ref[:, 128 * g : 128 * (g + 1)], q4, kg, vg, p4b.astype(F32), p4b, do, masks, dqkv_ref, ds0_ref, ds1_ref)
     h = (n_ref[...] * gain_ref[0:1, :]).astype(BF16)
-    weight_terms(idx_ref, h, o_ref[...], dqkv_ref[...], gb, keep_ref, send_ref)
+    h_ref[...] = h
+    weight_terms(1 - idx_ref[0], (h, o_ref[...], dqkv_ref[...], gb, send_ref))
+
+
+def keep_kernel(idx_ref, *refs):
+    blocks = [[r[...] for r in refs[4 * b : 4 * b + 4]] + [refs[8 + b]] for b in range(2)]
+    weight_terms(idx_ref[0], *blocks)
 
 
 def finish_kernel(
@@ -788,32 +794,24 @@
     )
     pieces = halo((own, lon, lat, dia), 1)
     wshape = ((256, 4 * D), BF16)
-    keep1, send1 = call(weights_kernel, 2, [wshape] * 2, idx, h1, o1, dqkv1, g1)
+    (send1,) = call(send_kernel, 1, [wshape], idx, h1, o1, dqkv1, g1)
     recv1 = flip(send1, "c")
 
     def pairs(*shapes):
         return [(s, BF16) for shape in shapes for s in shape]
 
     cells = ((72, 2, D), BF16)
-    g0, dqkv0, ds00, ds01, keep0, send0 = call(
+    g0, h0, dqkv0, ds00, ds01, send0 = call(
         third_kernel,
         4,
-        [((144, D), BF16), ((144, 3 * D), BF16)] + ds_shapes + [wshape, wshape],
-        idx, *pieces, gains, proj_weight, n0, qkv0, p0, o0, third_const, keep1,
+        [((144, D), BF16)] * 2 + [((144, 3 * D), BF16)] + ds_shapes + [wshape],
+        idx, *pieces, gains, proj_weight, n0, qkv0, p0, o0, third_const, send1,
         specs={6: block(0, (D, D)), 12: ANY},
     )
     recv0 = flip(send0, "c")
-    outputs, grad_inputs, dgain0 = call(
-        finish_kernel,
-        2,
-        [cells, cells, ((1, D), F32)],
-        *pieces, gains, qkv_weight, n0, rstd0, g0, dqkv0, finish_const, keep0,
-        specs={5: block(0, (D, 3 * D)), 11: ANY},
-        scratch=[((144, 2 * D), F32)],
-    )
-    outputs, grad_inputs = [
-        v.reshape(1, 6, 12, 2, D).transpose(0, 3, 1, 2, 4) for v in (outputs, grad_inputs)
-    ]
+    keep0, keep1 = call(
+        keep_kernel, 2, [wshape] * 2, idx, h0, o0, dqkv0, g0, h1, o1, dqkv1, g1
+    )
     ka, sa, kb, sb, kc, sc = call(
         core_kernel,
         1,
@@ -821,6 +819,17 @@
         idx, keep0, recv0, keep1, recv1,
     )
     ra, rb, rc = flip(sa, "x0"), flip(sb, "yl"), flip(sc, "z0")
+    outputs, grad_inputs, dgain0 = call(
+        finish_kernel,
+        2,
+        [cells, cells, ((1, D), F32)],
+        *pieces, gains, qkv_weight, n0, rstd0, g0, dqkv0, finish_const, ka,
+        specs={5: block(0, (D, 3 * D)), 11: ANY},
+        scratch=[((144, 2 * D), F32)],
+    )
+    outputs, grad_inputs = [
+        v.reshape(1, 6, 12, 2, D).transpose(0, 3, 1, 2, 4) for v in (outputs, grad_inputs)
+    ]
     tshape = ((16, 1024), F32)
     tkeep, tsend = call(
         scatter_kernel,

time: 105 us -> 105 us (level)
    ppermute x19, waiting for transfers between devices: 13 us -> 11.7 us  [flip(): lax.ppermute(value, AXES, [(s, s ^ mask_of(axes)) for s in range(256)])]
    pallas_call x14 -> x15, Pallas kernels: 35.1 us -> 36.1 us  [call(): pl.pallas_call(body, grid=(1,), in_specs=[specs.get(i, _whole(a.shape)) f...]
  transfers between devices with their start and end apart: 27 -> 27, of which waited for: 11 -> 11; matrix products, arithmetic and copies ran while one was open for 0% -> 0% of each run, Pallas kernels for 15% -> 16%
where the time goes in v6:
time: 105 us
  starting transfers between devices  47.5 us (45%)
  Pallas kernels  36.1 us (34%)
  waiting for transfers between devices  19.9 us (19%)
    pallas_call x15, Pallas kernels, call(): pl.pallas_call(body, grid=(1,), in_specs=[specs.get(i, _whole(a.shape)) f...  36.1 us
    ppermute x19, starting transfers between devices, flip(): lax.ppermute(value, AXES, [(s, s ^ mask_of(axes)) for s in range(256)])  26.2 us
    ppermute x4, starting transfers between devices, lon_step(): return lax.ppermute(value, AXES, pairs)  13.4 us
    ppermute x19, waiting for transfers between devices, flip(): lax.ppermute(value, AXES, [(s, s ^ mask_of(axes)) for s in range(256)])  11.7 us
    ppermute x4, starting transfers between devices, z_step(): return lax.ppermute(value, AXES, pairs)  7.92 us
    ppermute x4, waiting for transfers between devices, z_step(): return lax.ppermute(value, AXES, pairs)  6.76 us
  transfers between devices with their start and end apart: 27, of which 11 were waited for; matrix products, arithmetic and copies ran while one was open for 0% of the time, Pallas kernels for 16%

profile of v6, /device:TPU:1, one launch (start us, length us, event | category | flops | bytes accessed | tf_op | source)
XLA Modules:
  0.0 104.6 jit_solution(2345012007254313405)
XLA Ops:
  0.7 0.0 copy-start.8
  0.7 8.5 %shard_map.172 = (bf16[40,1024]{1,0:T(8,128)(2,1)}, bf16[40,1024]{1,0:T(8,128)(2,1)}, bf16[40,1024]{1,0:T(8,128)(2,1)}, bf16[40,1024]{1,0:T(8,128)(2,1)}, f32[14...) custom-call(bf16[72,2,512]{2,1,0:T(2,128)(2,1)} %bitcast.19, ...), custom_call_target="tpu_custom_call" | custom-call | flops 8000000000 | bytes 28800000 | tf_op jit(solution)/shard_map/pallas_call | solution.py:667
  9.2 3.3 %collective-permute-start = (bf16[40,1024]{1,0:T(8,128)(2,1)}, bf16[40,1024]{1,0:T(8,128)(2,1)S(1)}, u32[]{:S(2)}, u32[]{:S(2)}) collective-permute-start(bf16[40,1024]{1,0:T(8,128)(2,1)} %get-tuple-element.77), channel_id=1, source_target_pairs={{0,254},{1,255},{2,0},{3,1},{4,2},{5,3},{6,4},{7,5},{8,6},{9,7},{1... | collective-permute-start | bytes 245768 | tf_op jit(solution)/shard_map/ppermute | solution.py:696
  12.5 0.0 collective-permute-start.1
  12.5 10.0 %collective-permute-start.2 = (bf16[40,1024]{1,0:T(8,128)(2,1)}, bf16[40,1024]{1,0:T(8,128)(2,1)S(1)}, u32[]{:S(2)}, u32[]{:S(2)}) collective-permute-start(bf16[40,1024]{1,0:T(8,128)(2,1)} %get-tuple-element.79), channel_id=1, source_target_pairs={{0,255},{1,254},{2,1},{3,0},{4,3},{5,2},{6,5},{7,4},{8,7},{9,6},{1... | collective-permute-start | bytes 245768 | tf_op jit(solution)/shard_map/ppermute | solution.py:696
  22.5 0.1 stack.27.idx_ref
  22.6 0.0 copy-start
  22.6 0.0 copy-start.1
  22.6 0.0 copy-start.4
  22.7 0.0 copy-start.5
  22.7 0.0 copy-start.14
  22.7 3.9 %shard_map.173 = (f32[2304,256]{1,0:T(8,128)S(1)}, s32[144,128]{1,0:T(8,128)S(1)}, s32[24,128]{1,0:T(8,128)S(1)}) custom-call(s32[6]{0:T(128)S(1)} %stack.27.idx_ref, f32[2,2,16,759]{3,2,1,0:T(8,128)S(1)} %copy-done.2, s32[144,144]{1,0:T(8,128)S(1)} %copy-done.3, bf16[160,256]{1,0:T(8,128)(2,1)S(1)} %copy-done.8), custom_call_target="tpu_custom_call" | custom-call | flops 4000000000 | bytes 14400000 | tf_op jit(solution)/shard_map/pallas_call | solution.py:667
  26.6 0.0 collective-permute-done.1.lat_ref
  26.7 5.3 %shard_map.174 = (bf16[40,1024]{1,0:T(8,128)(2,1)S(1)}, bf16[40,1024]{1,0:T(8,128)(2,1)S(1)}, bf16[40,1024]{1,0:T(8,128)(2,1)S(1)}, bf16[40,1024]{1,0:T(8,128)(2...) custom-call(s32[6]{0:T(128)S(1)} %stack.27.idx_ref, ...), custom_call_target="tpu_custom_call" | custom-call | flops 6000000000 | bytes 21600000 | tf_op jit(solution)/shard_map/pallas_call | solution.py:667
  32.0 0.1 collective-permute-start.3
  32.1 0.5 collective-permute-start.4
  32.6 0.0 collective-permute-start.5
  32.6 0.0 copy-start.12
  32.6 1.3 %shard_map.175.after_ref = bf16[256,2048]{1,0:T(8,128)(2,1)S(1)} custom-call(s32[6]{0:T(128)S(1)} %stack.27.idx_ref, bf16[144,512]{1,0:T(8,128)(2,1)S(1)} %get-tuple-element.90.h_ref.refs_4_, bf16[144,512]{1,0:T(8,128)(2,1)S(1)} %get-tuple-element.91.o_ref.refs_5_, bf16[144,1536]{1,0:T(8,128)(2,1)S(1)} %get-tuple-element.92.dqkv_ref.refs_6_, ...), custom_call_target="tpu_custom_call" | custom-call | flops 1000000000 | bytes 3600000 | tf_op jit(solution)/shard_map/pallas_call | solution.py:667
  33.9 1.5 %collective-permute-start.7 = (bf16[256,2048]{1,0:T(8,128)(2,1)S(1)}, bf16[256,2048]{1,0:T(8,128)(2,1)S(1)}, u32[]{:S(2)}, u32[]{:S(2)}) collective-permute-start(bf16[256,2048]{1,0:T(8,128)(2,1)S(1)} %shard_map.175.after_ref), channel_id=1, source_target_pairs={{0,2},{1,3},{2,0},{3,1},{4,6},{5,7},{6,4},{7,5},{8,10},{9,11},{10,... | collective-permute-start | bytes 3145736 | tf_op jit(solution)/shard_map/ppermute | solution.py:686
  35.4 0.0 collective-permute-done.3.lon_ref
  35.4 0.4 collective-permute-done.4.lat_ref
  35.8 1.4 %collective-permute-done.5.dia_ref = bf16[40,1024]{1,0:T(8,128)(2,1)S(1)} collective-permute-done((bf16[40,1024]{1,0:T(8,128)(2,1)S(1)}, bf16[40,1024]{1,0:T(8,128)(2,1)S(1)}, u32[]{:S(2)}, u32[]{:S(2)}) %collective-permute-start.5) | collective-permute-done | bytes 81952 | tf_op jit(solution)/shard_map/ppermute | solution.py:696
  37.2 3.1 %shard_map.176 = (bf16[144,512]{1,0:T(8,128)(2,1)S(1)}, bf16[144,512]{1,0:T(8,128)(2,1)S(1)}, bf16[144,1536]{1,0:T(8,128)(2,1)S(1)}, f32[2304,128]{1,0:T(8,128)S...) custom-call(s32[6]{0:T(128)S(1)} %stack.27.idx_ref, bf16[40,1024]{1,0:T(8,128)(2,1)S(1)} %get-tuple-element.81.own_ref, ...), custom_call_target="tpu_custom_call" | custom-call | flops 4000000000 | bytes 14400000 | tf_op jit(solution)/shard_map/pallas_call | solution.py:667
  40.4 5.7 %collective-permute-start.6 = (bf16[256,2048]{1,0:T(8,128)(2,1)S(1)}, bf16[256,2048]{1,0:T(8,128)(2,1)S(1)}, u32[]{:S(2)}, u32[]{:S(2)}) collective-permute-start(bf16[256,2048]{1,0:T(8,128)(2,1)S(1)} %get-tuple-element.98), channel_id=1, source_target_pairs={{0,2},{1,3},{2,0},{3,1},{4,6},{5,7},{6,4},{7,5},{8,10},{9,11},{10,... | collective-permute-start | bytes 3145736 | tf_op jit(solution)/shard_map/ppermute | solution.py:686
  46.0 1.8 %shard_map.177 = (bf16[256,2048]{1,0:T(8,128)(2,1)S(1)}, bf16[256,2048]{1,0:T(8,128)(2,1)S(1)}) custom-call(s32[6]{0:T(128)S(1)} %stack.27.idx_ref, bf16[144,512]{1,0:T(8,128)(2,1)S(1)} %get-tuple-element.96.refs_0_, bf16[144,512]{1,0:T(8,128)(2,1)S(1)} %copy-done.12, bf16[144,1536]{1,0:T(8,128)(2,1)S(1)} %get-tuple-element.95.refs_2_.dqkv_ref, ...), custom_call_target="tpu_custom_call" | custom-call | flops 2000000000 | bytes 7200000 | tf_op jit(solution)/shard_map/pallas_call | solution.py:667
  47.8 0.5 collective-permute-done.6.r0_ref
  48.3 1.2 %shard_map.178 = (bf16[128,1536]{1,0:T(8,128)(2,1)S(1)}, bf16[128,1536]{1,0:T(8,128)(2,1)S(1)}, bf16[256,768]{1,0:T(8,128)(2,1)S(1)}, bf16[256,768]{1,0:T(8,128)...) custom-call(s32[6]{0:T(128)S(1)} %stack.27.idx_ref, ...), custom_call_target="tpu_custom_call" | custom-call | flops 1000000000 | bytes 3600000 | tf_op jit(solution)/shard_map/pallas_call | solution.py:667
  49.5 0.1 collective-permute-start.10
  49.6 0.1 collective-permute-start.8
  49.7 0.2 collective-permute-start.9
  50.0 1.7 %shard_map.179 = (bf16[72,2,512]{2,1,0:T(2,128)(2,1)}, bf16[72,2,512]{2,1,0:T(2,128)(2,1)}, f32[1,512]{1,0:T(1,128)S(1)}) custom-call(bf16[40,1024]{1,0:T(8,128)(2,1)S(1)} %get-tuple-element.81.own_ref, bf16[40,1024]{1,0:T(8,128)(2,1)S(1)} %collective-permute-done.3.lon_ref, bf16[40,1024]{1,0:T(8,128)(2,1)S(1)} %collective-permute-done.4.lat_ref, ...), custom_call_target="tpu_custom_call" | custom-call | flops 2000000000 | bytes 7200000 | tf_op jit(solution)/shard_map/pallas_call | solution.py:667
  51.7 4.5 %shard_map.180 = (f32[16,1024]{1,0:T(8,128)S(1)}, f32[16,1024]{1,0:T(8,128)S(1)}) custom-call(s32[6]{0:T(128)S(1)} %stack.27.idx_ref, s32[144,128]{1,0:T(8,128)S(1)} %get-tuple-element.108.main_ref, s32[24,128]{1,0:T(8,128)S(1)} %get-tuple-element.109.tail_ref, f32[2304,128]{1,0:T(8,128)S(1)} %get-tuple-element.110.m0_ref, ...), custom_call_target="tpu_custom_call" | custom-call | flops 6000000000 | bytes 21600000 | tf_op jit(solution)/shard_map/pallas_call | solution.py:667
  56.2 0.7 collective-permute-start.11
  57.0 0.9 collective-permute-done.11.u_ref
  57.9 0.0 collective-permute-done.10.rc_ref
  57.9 2.2 %collective-permute-done.8.ra_ref = bf16[128,1536]{1,0:T(8,128)(2,1)S(1)} collective-permute-done((bf16[128,1536]{1,0:T(8,128)(2,1)S(1)}, bf16[128,1536]{1,0:T(8,128)(2,1)S(1)}, u32[]{:S(2)}, u32[]{:S(2)}) %collective-permute-start.8) | collective-permute-done | bytes 393248 | tf_op jit(solution)/shard_map/ppermute | solution.py:686
  60.1 0.1 collective-permute-done.9.rb_ref
  60.2 0.9 shard_map.181
  61.0 0.2 collective-permute-start.12
  61.3 0.9 collective-permute-start.13
  62.2 1.2 %collective-permute-start.14 = (bf16[80,1024]{1,0:T(8,128)(2,1)S(1)}, bf16[80,1024]{1,0:T(8,128)(2,1)S(1)}, u32[]{:S(2)}, u32[]{:S(2)}) collective-permute-start(bf16[80,1024]{1,0:T(8,128)(2,1)S(1)} %get-tuple-element.123), channel_id=1, source_target_pairs={{0,32},{1,33},{2,34},{3,35},{4,36},{5,37},{6,38},{7,39},{8,40},{9,... | collective-permute-start | bytes 491528 | tf_op jit(solution)/shard_map/ppermute | solution.py:686
  63.5 3.2 %collective-permute-done.14.rc_ref = bf16[80,1024]{1,0:T(8,128)(2,1)S(1)} collective-permute-done((bf16[80,1024]{1,0:T(8,128)(2,1)S(1)}, bf16[80,1024]{1,0:T(8,128)(2,1)S(1)}, u32[]{:S(2)}, u32[]{:S(2)}) %collective-permute-start.14) | collective-permute-done | bytes 163872 | tf_op jit(solution)/shard_map/ppermute | solution.py:686
  66.7 0.7 shard_map.182
  67.4 0.6 collective-permute-start.15
  68.0 1.1 %collective-permute-start.16 = (bf16[64,768]{1,0:T(8,128)(2,1)S(1)}, bf16[64,768]{1,0:T(8,128)(2,1)S(1)}, u32[]{:S(2)}, u32[]{:S(2)}) collective-permute-start(bf16[64,768]{1,0:T(8,128)(2,1)S(1)} %get-tuple-element.128), channel_id=1, source_target_pairs={{0,32},{1,33},{2,34},{3,35},{4,36},{5,37},{6,38},{7,39},{8,40},{9,... | collective-permute-start | bytes 294920 | tf_op jit(solution)/shard_map/ppermute | solution.py:686
  69.1 1.3 %collective-permute-start.17 = (bf16[64,512]{1,0:T(8,128)(2,1)S(1)}, bf16[64,512]{1,0:T(8,128)(2,1)S(1)}, u32[]{:S(2)}, u32[]{:S(2)}) collective-permute-start(bf16[64,512]{1,0:T(8,128)(2,1)S(1)} %get-tuple-element.130), channel_id=1, source_target_pairs={{0,1},{1,0},{2,3},{3,2},{4,5},{5,4},{6,7},{7,6},{8,9},{9,8},{10,11... | collective-permute-start | bytes 196616 | tf_op jit(solution)/shard_map/ppermute | solution.py:686
  70.4 1.8 %collective-permute-done.17.rc_ref = bf16[64,512]{1,0:T(8,128)(2,1)S(1)} collective-permute-done((bf16[64,512]{1,0:T(8,128)(2,1)S(1)}, bf16[64,512]{1,0:T(8,128)(2,1)S(1)}, u32[]{:S(2)}, u32[]{:S(2)}) %collective-permute-start.17) | collective-permute-done | bytes 65568 | tf_op jit(solution)/shard_map/ppermute | solution.py:686
  72.2 0.0 collective-permute-done.16.rb_ref
  72.2 0.7 shard_map.183
  72.9 0.1 collective-permute-start.18
  73.0 0.6 collective-permute-start.19
  73.5 4.5 %collective-permute-start.20 = (bf16[24,2048]{1,0:T(8,128)(2,1)S(1)}, bf16[24,2048]{1,0:T(8,128)(2,1)S(1)}, u32[]{:S(2)}, u32[]{:S(2)}) collective-permute-start(bf16[24,2048]{1,0:T(8,128)(2,1)S(1)} %get-tuple-element.135), channel_id=1, source_target_pairs={{0,124},{1,125},{2,126},{3,127},{4,104},{5,105},{6,106},{7,107},{8... | collective-permute-start | bytes 294920 | tf_op jit(solution)/shard_map/ppermute | solution.py:691
  78.0 2.9 %collective-permute-done.20.g3_ref = bf16[24,2048]{1,0:T(8,128)(2,1)S(1)} collective-permute-done((bf16[24,2048]{1,0:T(8,128)(2,1)S(1)}, bf16[24,2048]{1,0:T(8,128)(2,1)S(1)}, u32[]{:S(2)}, u32[]{:S(2)}) %collective-permute-start.20) | collective-permute-done | bytes 98336 | tf_op jit(solution)/shard_map/ppermute | solution.py:691
  80.9 0.6 shard_map.184
  81.5 0.1 collective-permute-start.21
  81.6 2.7 %collective-permute-start.22 = (bf16[24,1024]{1,0:T(8,128)(2,1)S(1)}, bf16[24,1024]{1,0:T(8,128)(2,1)S(1)}, u32[]{:S(2)}, u32[]{:S(2)}) collective-permute-start(bf16[24,1024]{1,0:T(8,128)(2,1)S(1)} %get-tuple-element.138), channel_id=1, source_target_pairs={{0,128},{1,129},{2,130},{3,131},{4,132},{5,133},{6,134},{7,135},{8... | collective-permute-start | bytes 147464 | tf_op jit(solution)/shard_map/ppermute | solution.py:686
  84.3 3.2 %collective-permute-start.23 = (bf16[24,1024]{1,0:T(8,128)(2,1)S(1)}, bf16[24,1024]{1,0:T(8,128)(2,1)S(1)}, u32[]{:S(2)}, u32[]{:S(2)}) collective-permute-start(bf16[24,1024]{1,0:T(8,128)(2,1)S(1)} %get-tuple-element.139), channel_id=1, source_target_pairs={{0,140},{1,141},{2,142},{3,143},{4,152},{5,153},{6,154},{7,155},{8... | collective-permute-start | bytes 147464 | tf_op jit(solution)/shard_map/ppermute | solution.py:691
  87.6 3.9 %collective-permute-done.23.g3_ref = bf16[24,1024]{1,0:T(8,128)(2,1)S(1)} collective-permute-done((bf16[24,1024]{1,0:T(8,128)(2,1)S(1)}, bf16[24,1024]{1,0:T(8,128)(2,1)S(1)}, u32[]{:S(2)}, u32[]{:S(2)}) %collective-permute-start.23) | collective-permute-done | bytes 49184 | tf_op jit(solution)/shard_map/ppermute | solution.py:691
  91.5 0.6 shard_map.185
  92.1 0.3 collective-permute-start.24
  92.4 8.4 %collective-permute-start.26 = (bf16[16,1024]{1,0:T(8,128)(2,1)S(1)}, bf16[16,1024]{1,0:T(8,128)(2,1)S(1)}, u32[]{:S(2)}, u32[]{:S(2)}) collective-permute-start(bf16[16,1024]{1,0:T(8,128)(2,1)S(1)} %get-tuple-element.141), channel_id=1, source_target_pairs={{0,3},{1,2},{2,1},{3,0},{4,7},{5,6},{6,5},{7,4},{8,11},{9,10},{10,... | collective-permute-start | bytes 98312 | tf_op jit(solution)/shard_map/ppermute | solution.py:686
  100.8 2.6 %collective-permute-done.26.dia_ref = bf16[16,1024]{1,0:T(8,128)(2,1)S(1)} collective-permute-done((bf16[16,1024]{1,0:T(8,128)(2,1)S(1)}, bf16[16,1024]{1,0:T(8,128)(2,1)S(1)}, u32[]{:S(2)}, u32[]{:S(2)}) %collective-permute-start.26) | collective-permute-done | bytes 32800 | tf_op jit(solution)/shard_map/ppermute | solution.py:686
  103.3 1.3 %shard_map.186 = (f32[2,512]{1,0:T(2,128)}, f32[2,4,1536]{2,1,0:T(4,128)}, f32[2,4,512]{2,1,0:T(4,128)}, f32[2,2,16,759]{3,2,1,0:T(8,128)}) custom-call(s32[6]{0:T(128)S(1)} %stack.27.idx_ref, bf16[24,1024]{1,0:T(8,128)(2,1)S(1)} %get-tuple-element.140.own_ref, bf16[24,1024]{1,0:T(8,128)(2,1)S(1)} %collective-permute-done.24.lat_ref, ...), custom_call_target="tpu_custom_call" | custom-call | flops 1000000000 | bytes 3600000 | tf_op jit(solution)/shard_map/pallas_call | solution.py:667
  (36 shorter events, 0.1 us)
Async XLA Ops:
  0.6 22.0 %copy-start.2 = (f32[2,2,16,759]{3,2,1,0:T(8,128)S(1)}, f32[2,2,16,759]{3,2,1,0:T(8,128)}, u32[]{:S(2)}) copy-start(f32[2,2,16,759]{3,2,1,0:T(8,128)} %tab_ref.1) | copy-start | bytes 582916
  0.6 22.0 %copy-start.3 = (s32[144,144]{1,0:T(8,128)S(1)}, s32[144,144]{1,0:T(8,128)}, u32[]{:S(2)}) copy-start(s32[144,144]{1,0:T(8,128)} %rel_ref.1) | copy-start | bytes 248836
  0.7 22.0 %copy-start.8 = (bf16[160,256]{1,0:T(8,128)(2,1)S(1)}, bf16[160,256]{1,0:T(8,128)(2,1)}, u32[]{:S(2)}) copy-start(bf16[160,256]{1,0:T(8,128)(2,1)} %constant.46.clone.pm_ref) | copy-start | bytes 245764
  9.2 17.4 %collective-permute-start = (bf16[40,1024]{1,0:T(8,128)(2,1)}, bf16[40,1024]{1,0:T(8,128)(2,1)S(1)}, u32[]{:S(2)}, u32[]{:S(2)}) collective-permute-start(bf16[40,1024]{1,0:T(8,128)(2,1)} %get-tuple-element.77), channel_id=1, source_target_pairs={{0,254},{1,255},{2,0},{3,1},{4,2},{5,3},{6,4},{7,5},{8,6},{9,7},{1... | collective-permute-start | bytes 245768 | tf_op jit(solution)/shard_map/ppermute | solution.py:696
  12.5 14.1 %collective-permute-start.1 = (bf16[40,1024]{1,0:T(8,128)(2,1)}, bf16[40,1024]{1,0:T(8,128)(2,1)S(1)}, u32[]{:S(2)}, u32[]{:S(2)}) collective-permute-start(bf16[40,1024]{1,0:T(8,128)(2,1)} %get-tuple-element.78), channel_id=1, source_target_pairs={{0,1},{1,0},{2,3},{3,2},{4,5},{5,4},{6,7},{7,6},{8,9},{9,8},{10,11... | collective-permute-start | bytes 245768 | tf_op jit(solution)/shard_map/ppermute | solution.py:686
  12.5 14.1 %collective-permute-start.2 = (bf16[40,1024]{1,0:T(8,128)(2,1)}, bf16[40,1024]{1,0:T(8,128)(2,1)S(1)}, u32[]{:S(2)}, u32[]{:S(2)}) collective-permute-start(bf16[40,1024]{1,0:T(8,128)(2,1)} %get-tuple-element.79), channel_id=1, source_target_pairs={{0,255},{1,254},{2,1},{3,0},{4,3},{5,2},{6,5},{7,4},{8,7},{9,6},{1... | collective-permute-start | bytes 245768 | tf_op jit(solution)/shard_map/ppermute | solution.py:696
  22.6 4.0 %copy-start = (bf16[2,512,1536]{2,1,0:T(8,128)(2,1)S(1)}, bf16[2,512,1536]{2,1,0:T(8,128)(2,1)}, u32[]{:S(2)}) copy-start(bf16[2,512,1536]{2,1,0:T(8,128)(2,1)} %wqkv_ref.3) | copy-start | bytes 9437188
  22.6 4.0 %copy-start.1 = (bf16[2,512,512]{2,1,0:T(8,128)(2,1)S(1)}, bf16[2,512,512]{2,1,0:T(8,128)(2,1)}, u32[]{:S(2)}) copy-start(bf16[2,512,512]{2,1,0:T(8,128)(2,1)} %wproj_ref.3) | copy-start | bytes 3145732
  22.6 4.0 %copy-start.4 = (f32[2,512]{1,0:T(2,128)S(1)}, f32[2,512]{1,0:T(2,128)}, u32[]{:S(2)}) copy-start(f32[2,512]{1,0:T(2,128)} %gain_ref.5) | copy-start | bytes 12292
  22.7 4.0 %copy-start.5 = (bf16[5,160,256]{2,1,0:T(8,128)(2,1)S(1)}, bf16[5,160,256]{2,1,0:T(8,128)(2,1)}, u32[]{:S(2)}) copy-start(bf16[5,160,256]{2,1,0:T(8,128)(2,1)} %constant.43.clone.const_ref) | copy-start | bytes 1228804
  22.7 4.0 %copy-start.14 = (bf16[40,1024]{1,0:T(8,128)(2,1)S(1)}, bf16[40,1024]{1,0:T(8,128)(2,1)}, u32[]{:S(2)}) copy-start(bf16[40,1024]{1,0:T(8,128)(2,1)} %get-tuple-element.76.own_ref) | copy-start | bytes 245764
  32.0 3.4 %collective-permute-start.3 = (bf16[40,1024]{1,0:T(8,128)(2,1)S(1)}, bf16[40,1024]{1,0:T(8,128)(2,1)S(1)}, u32[]{:S(2)}, u32[]{:S(2)}) collective-permute-start(bf16[40,1024]{1,0:T(8,128)(2,1)S(1)} %get-tuple-element.82), channel_id=1, source_target_pairs={{0,2},{1,3},{2,4},{3,5},{4,6},{5,7},{6,8},{7,9},{8,10},{9,11},{10,... | collective-permute-start | bytes 245768 | tf_op jit(solution)/shard_map/ppermute | solution.py:696
  32.1 3.7 %collective-permute-start.4 = (bf16[40,1024]{1,0:T(8,128)(2,1)S(1)}, bf16[40,1024]{1,0:T(8,128)(2,1)S(1)}, u32[]{:S(2)}, u32[]{:S(2)}) collective-permute-start(bf16[40,1024]{1,0:T(8,128)(2,1)S(1)} %get-tuple-element.83), channel_id=1, source_target_pairs={{0,1},{1,0},{2,3},{3,2},{4,5},{5,4},{6,7},{7,6},{8,9},{9,8},{10,11... | collective-permute-start | bytes 245768 | tf_op jit(solution)/shard_map/ppermute | solution.py:686
  32.6 4.6 %collective-permute-start.5 = (bf16[40,1024]{1,0:T(8,128)(2,1)S(1)}, bf16[40,1024]{1,0:T(8,128)(2,1)S(1)}, u32[]{:S(2)}, u32[]{:S(2)}) collective-permute-start(bf16[40,1024]{1,0:T(8,128)(2,1)S(1)} %get-tuple-element.84), channel_id=1, source_target_pairs={{0,3},{1,2},{2,5},{3,4},{4,7},{5,6},{6,9},{7,8},{8,11},{9,10},{10,... | collective-permute-start | bytes 245768 | tf_op jit(solution)/shard_map/ppermute | solution.py:696
  32.6 4.6 %copy-start.7 = (bf16[1,160,256]{2,1,0:T(8,128)(2,1)S(1)}, bf16[1,160,256]{2,1,0:T(8,128)(2,1)}, u32[]{:S(2)}) copy-start(bf16[1,160,256]{2,1,0:T(8,128)(2,1)} %constant.44.clone.const_ref) | copy-start | bytes 245764
  32.6 4.6 %copy-start.9 = (f32[144,512]{1,0:T(8,128)S(1)}, f32[144,512]{1,0:T(8,128)}, u32[]{:S(2)}) copy-start(f32[144,512]{1,0:T(8,128)} %get-tuple-element.85.n_ref) | copy-start | bytes 884740
  32.6 4.6 %copy-start.11 = (bf16[2304,256]{1,0:T(8,128)(2,1)S(1)}, bf16[2304,256]{1,0:T(8,128)(2,1)}, u32[]{:S(2)}) copy-start(bf16[2304,256]{1,0:T(8,128)(2,1)} %get-tuple-element.88.p_ref) | copy-start | bytes 3538948
  32.6 4.6 %copy-start.12 = (bf16[144,512]{1,0:T(8,128)(2,1)S(1)}, bf16[144,512]{1,0:T(8,128)(2,1)}, u32[]{:S(2)}) copy-start(bf16[144,512]{1,0:T(8,128)(2,1)} %get-tuple-element.89.o_ref.refs_1_) | copy-start | bytes 442372
  32.6 4.6 %copy-start.13 = (bf16[144,1536]{1,0:T(8,128)(2,1)S(1)}, bf16[144,1536]{1,0:T(8,128)(2,1)}, u32[]{:S(2)}) copy-start(bf16[144,1536]{1,0:T(8,128)(2,1)} %get-tuple-element.87.qkv_ref) | copy-start | bytes 1327108
  33.9 13.9 %collective-permute-start.7 = (bf16[256,2048]{1,0:T(8,128)(2,1)S(1)}, bf16[256,2048]{1,0:T(8,128)(2,1)S(1)}, u32[]{:S(2)}, u32[]{:S(2)}) collective-permute-start(bf16[256,2048]{1,0:T(8,128)(2,1)S(1)} %shard_map.175.after_ref), channel_id=1, source_target_pairs={{0,2},{1,3},{2,0},{3,1},{4,6},{5,7},{6,4},{7,5},{8,10},{9,11},{10,... | collective-permute-start | bytes 3145736 | tf_op jit(solution)/shard_map/ppermute | solution.py:686
  40.4 7.9 %collective-permute-start.6 = (bf16[256,2048]{1,0:T(8,128)(2,1)S(1)}, bf16[256,2048]{1,0:T(8,128)(2,1)S(1)}, u32[]{:S(2)}, u32[]{:S(2)}) collective-permute-start(bf16[256,2048]{1,0:T(8,128)(2,1)S(1)} %get-tuple-element.98), channel_id=1, source_target_pairs={{0,2},{1,3},{2,0},{3,1},{4,6},{5,7},{6,4},{7,5},{8,10},{9,11},{10,... | collective-permute-start | bytes 3145736 | tf_op jit(solution)/shard_map/ppermute | solution.py:686
  48.3 1.7 %copy-start.6 = (bf16[2,160,256]{2,1,0:T(8,128)(2,1)S(1)}, bf16[2,160,256]{2,1,0:T(8,128)(2,1)}, u32[]{:S(2)}) copy-start(bf16[2,160,256]{2,1,0:T(8,128)(2,1)} %constant.45.clone.const_ref) | copy-start | bytes 491524
  48.3 1.7 %copy-start.10 = (f32[144,1]{1,0:T(8,128)S(1)}, f32[144,1]{1,0:T(8,128)}, u32[]{:S(2)}) copy-start(f32[144,1]{1,0:T(8,128)} %get-tuple-element.86.rstd_ref) | copy-start | bytes 1732
  49.5 8.3 %collective-permute-start.10 = (bf16[128,1024]{1,0:T(8,128)(2,1)S(1)}, bf16[128,1024]{1,0:T(8,128)(2,1)S(1)}, u32[]{:S(2)}, u32[]{:S(2)}) collective-permute-start(bf16[128,1024]{1,0:T(8,128)(2,1)S(1)} %get-tuple-element.107), channel_id=1, source_target_pairs={{0,4},{1,5},{2,6},{3,7},{4,0},{5,1},{6,2},{7,3},{8,12},{9,13},{10,... | collective-permute-start | bytes 786440 | tf_op jit(solution)/shard_map/ppermute | solution.py:686
  49.6 10.4 %collective-permute-start.8 = (bf16[128,1536]{1,0:T(8,128)(2,1)S(1)}, bf16[128,1536]{1,0:T(8,128)(2,1)S(1)}, u32[]{:S(2)}, u32[]{:S(2)}) collective-permute-start(bf16[128,1536]{1,0:T(8,128)(2,1)S(1)} %get-tuple-element.103), channel_id=1, source_target_pairs={{0,32},{1,33},{2,34},{3,35},{4,36},{5,37},{6,38},{7,39},{8,40},{9,... | collective-permute-start | bytes 1179656 | tf_op jit(solution)/shard_map/ppermute | solution.py:686
  49.7 10.4 %collective-permute-start.9 = (bf16[256,768]{1,0:T(8,128)(2,1)S(1)}, bf16[256,768]{1,0:T(8,128)(2,1)S(1)}, u32[]{:S(2)}, u32[]{:S(2)}) collective-permute-start(bf16[256,768]{1,0:T(8,128)(2,1)S(1)} %get-tuple-element.105), channel_id=1, source_target_pairs={{0,1},{1,0},{2,3},{3,2},{4,5},{5,4},{6,7},{7,6},{8,9},{9,8},{10,11... | collective-permute-start | bytes 1179656 | tf_op jit(solution)/shard_map/ppermute | solution.py:686
  56.2 1.6 %collective-permute-start.11 = (f32[16,1024]{1,0:T(8,128)S(1)}, f32[16,1024]{1,0:T(8,128)S(1)}, u32[]{:S(2)}, u32[]{:S(2)}) collective-permute-start(f32[16,1024]{1,0:T(8,128)S(1)} %get-tuple-element.117), channel_id=1, source_target_pairs={{0,2},{1,3},{2,0},{3,1},{4,6},{5,7},{6,4},{7,5},{8,10},{9,11},{10,... | collective-permute-start | bytes 196616 | tf_op jit(solution)/shard_map/ppermute | solution.py:686
  61.0 5.7 %collective-permute-start.12 = (bf16[128,768]{1,0:T(8,128)(2,1)S(1)}, bf16[128,768]{1,0:T(8,128)(2,1)S(1)}, u32[]{:S(2)}, u32[]{:S(2)}) collective-permute-start(bf16[128,768]{1,0:T(8,128)(2,1)S(1)} %get-tuple-element.119), channel_id=1, source_target_pairs={{0,1},{1,0},{2,3},{3,2},{4,5},{5,4},{6,7},{7,6},{8,9},{9,8},{10,11... | collective-permute-start | bytes 589832 | tf_op jit(solution)/shard_map/ppermute | solution.py:686
  61.3 5.4 %collective-permute-start.13 = (bf16[128,768]{1,0:T(8,128)(2,1)S(1)}, bf16[128,768]{1,0:T(8,128)(2,1)S(1)}, u32[]{:S(2)}, u32[]{:S(2)}) collective-permute-start(bf16[128,768]{1,0:T(8,128)(2,1)S(1)} %get-tuple-element.121), channel_id=1, source_target_pairs={{0,4},{1,5},{2,6},{3,7},{4,0},{5,1},{6,2},{7,3},{8,12},{9,13},{10,... | collective-permute-start | bytes 589832 | tf_op jit(solution)/shard_map/ppermute | solution.py:686
  62.2 4.5 %collective-permute-start.14 = (bf16[80,1024]{1,0:T(8,128)(2,1)S(1)}, bf16[80,1024]{1,0:T(8,128)(2,1)S(1)}, u32[]{:S(2)}, u32[]{:S(2)}) collective-permute-start(bf16[80,1024]{1,0:T(8,128)(2,1)S(1)} %get-tuple-element.123), channel_id=1, source_target_pairs={{0,32},{1,33},{2,34},{3,35},{4,36},{5,37},{6,38},{7,39},{8,40},{9,... | collective-permute-start | bytes 491528 | tf_op jit(solution)/shard_map/ppermute | solution.py:686
  67.4 4.8 %collective-permute-start.15 = (bf16[96,768]{1,0:T(8,128)(2,1)S(1)}, bf16[96,768]{1,0:T(8,128)(2,1)S(1)}, u32[]{:S(2)}, u32[]{:S(2)}) collective-permute-start(bf16[96,768]{1,0:T(8,128)(2,1)S(1)} %get-tuple-element.126), channel_id=1, source_target_pairs={{0,4},{1,5},{2,6},{3,7},{4,0},{5,1},{6,2},{7,3},{8,12},{9,13},{10,... | collective-permute-start | bytes 442376 | tf_op jit(solution)/shard_map/ppermute | solution.py:686
  68.0 4.2 %collective-permute-start.16 = (bf16[64,768]{1,0:T(8,128)(2,1)S(1)}, bf16[64,768]{1,0:T(8,128)(2,1)S(1)}, u32[]{:S(2)}, u32[]{:S(2)}) collective-permute-start(bf16[64,768]{1,0:T(8,128)(2,1)S(1)} %get-tuple-element.128), channel_id=1, source_target_pairs={{0,32},{1,33},{2,34},{3,35},{4,36},{5,37},{6,38},{7,39},{8,40},{9,... | collective-permute-start | bytes 294920 | tf_op jit(solution)/shard_map/ppermute | solution.py:686
  69.1 3.1 %collective-permute-start.17 = (bf16[64,512]{1,0:T(8,128)(2,1)S(1)}, bf16[64,512]{1,0:T(8,128)(2,1)S(1)}, u32[]{:S(2)}, u32[]{:S(2)}) collective-permute-start(bf16[64,512]{1,0:T(8,128)(2,1)S(1)} %get-tuple-element.130), channel_id=1, source_target_pairs={{0,1},{1,0},{2,3},{3,2},{4,5},{5,4},{6,7},{7,6},{8,9},{9,8},{10,11... | collective-permute-start | bytes 196616 | tf_op jit(solution)/shard_map/ppermute | solution.py:686
  72.9 5.2 %collective-permute-start.18 = (bf16[24,2048]{1,0:T(8,128)(2,1)S(1)}, bf16[24,2048]{1,0:T(8,128)(2,1)S(1)}, u32[]{:S(2)}, u32[]{:S(2)}) collective-permute-start(bf16[24,2048]{1,0:T(8,128)(2,1)S(1)} %get-tuple-element.133), channel_id=1, source_target_pairs={{0,28},{1,29},{2,30},{3,31},{4,8},{5,9},{6,10},{7,11},{8,4},{9,5},... | collective-permute-start | bytes 294920 | tf_op jit(solution)/shard_map/ppermute | solution.py:691
  73.0 5.1 %collective-permute-start.19 = (bf16[24,2048]{1,0:T(8,128)(2,1)S(1)}, bf16[24,2048]{1,0:T(8,128)(2,1)S(1)}, u32[]{:S(2)}, u32[]{:S(2)}) collective-permute-start(bf16[24,2048]{1,0:T(8,128)(2,1)S(1)} %get-tuple-element.134), channel_id=1, source_target_pairs={{0,96},{1,97},{2,98},{3,99},{4,100},{5,101},{6,102},{7,103},{8,104... | collective-permute-start | bytes 294920 | tf_op jit(solution)/shard_map/ppermute | solution.py:686
  73.5 7.4 %collective-permute-start.20 = (bf16[24,2048]{1,0:T(8,128)(2,1)S(1)}, bf16[24,2048]{1,0:T(8,128)(2,1)S(1)}, u32[]{:S(2)}, u32[]{:S(2)}) collective-permute-start(bf16[24,2048]{1,0:T(8,128)(2,1)S(1)} %get-tuple-element.135), channel_id=1, source_target_pairs={{0,124},{1,125},{2,126},{3,127},{4,104},{5,105},{6,106},{7,107},{8... | collective-permute-start | bytes 294920 | tf_op jit(solution)/shard_map/ppermute | solution.py:691
  81.5 6.0 %collective-permute-start.21 = (bf16[24,1024]{1,0:T(8,128)(2,1)S(1)}, bf16[24,1024]{1,0:T(8,128)(2,1)S(1)}, u32[]{:S(2)}, u32[]{:S(2)}) collective-permute-start(bf16[24,1024]{1,0:T(8,128)(2,1)S(1)} %get-tuple-element.137), channel_id=1, source_target_pairs={{0,12},{1,13},{2,14},{3,15},{4,24},{5,25},{6,26},{7,27},{8,20},{9,... | collective-permute-start | bytes 147464 | tf_op jit(solution)/shard_map/ppermute | solution.py:691
  81.6 5.9 %collective-permute-start.22 = (bf16[24,1024]{1,0:T(8,128)(2,1)S(1)}, bf16[24,1024]{1,0:T(8,128)(2,1)S(1)}, u32[]{:S(2)}, u32[]{:S(2)}) collective-permute-start(bf16[24,1024]{1,0:T(8,128)(2,1)S(1)} %get-tuple-element.138), channel_id=1, source_target_pairs={{0,128},{1,129},{2,130},{3,131},{4,132},{5,133},{6,134},{7,135},{8... | collective-permute-start | bytes 147464 | tf_op jit(solution)/shard_map/ppermute | solution.py:686
  84.3 7.1 %collective-permute-start.23 = (bf16[24,1024]{1,0:T(8,128)(2,1)S(1)}, bf16[24,1024]{1,0:T(8,128)(2,1)S(1)}, u32[]{:S(2)}, u32[]{:S(2)}) collective-permute-start(bf16[24,1024]{1,0:T(8,128)(2,1)S(1)} %get-tuple-element.139), channel_id=1, source_target_pairs={{0,140},{1,141},{2,142},{3,143},{4,152},{5,153},{6,154},{7,155},{8... | collective-permute-start | bytes 147464 | tf_op jit(solution)/shard_map/ppermute | solution.py:691
  92.1 11.3 %collective-permute-start.24 = (bf16[24,1024]{1,0:T(8,128)(2,1)S(1)}, bf16[24,1024]{1,0:T(8,128)(2,1)S(1)}, u32[]{:S(2)}, u32[]{:S(2)}) collective-permute-start(bf16[24,1024]{1,0:T(8,128)(2,1)S(1)} %get-tuple-element.140.own_ref), channel_id=1, source_target_pairs={{0,1},{1,0},{2,3},{3,2},{4,5},{5,4},{6,7},{7,6},{8,9},{9,8},{10,11... | collective-permute-start | bytes 147464 | tf_op jit(solution)/shard_map/ppermute | solution.py:686
  92.4 11.0 %collective-permute-start.26 = (bf16[16,1024]{1,0:T(8,128)(2,1)S(1)}, bf16[16,1024]{1,0:T(8,128)(2,1)S(1)}, u32[]{:S(2)}, u32[]{:S(2)}) collective-permute-start(bf16[16,1024]{1,0:T(8,128)(2,1)S(1)} %get-tuple-element.141), channel_id=1, source_target_pairs={{0,3},{1,2},{2,1},{3,0},{4,7},{5,6},{6,5},{7,4},{8,11},{9,10},{10,... | collective-permute-start | bytes 98312 | tf_op jit(solution)/shard_map/ppermute | solution.py:686
  100.8 2.6 %collective-permute-start.25 = (bf16[16,1024]{1,0:T(8,128)(2,1)S(1)}, bf16[16,1024]{1,0:T(8,128)(2,1)S(1)}, u32[]{:S(2)}, u32[]{:S(2)}) collective-permute-start(bf16[16,1024]{1,0:T(8,128)(2,1)S(1)} %get-tuple-element.141), channel_id=1, source_target_pairs={{0,2},{1,3},{2,0},{3,1},{4,6},{5,7},{6,4},{7,5},{8,10},{9,11},{10,... | collective-permute-start | bytes 98312 | tf_op jit(solution)/shard_map/ppermute | solution.py:686

commit v7 on v6

--- a/solution.py
+++ b/solution.py
@@ -242,7 +242,7 @@
     )
 
 
-def weight_terms(which, *targets):
+def weight_terms(h, o, dqkv, g, *targets):
     p = lax.broadcasted_iota(jnp.int32, (256, 512), 0)
     row = lax.broadcasted_iota(jnp.int32, (256, 512), 1)
     bit = lambda k: (p >> k) & 1
@@ -259,8 +259,8 @@
     base = p & 3
     for to, value in place:
         base = base + (value << to)
-    pick = jnp.where(row == base + which * 4, 1.0, 0.0).astype(BF16)
-    for h, o, dqkv, g, ref in targets:
+    for which, ref in targets:
+        pick = jnp.where(row == base + which * 4, 1.0, 0.0).astype(BF16)
         ht = dot_nt(pick, h).astype(BF16)
         ot = dot_nt(pick, o).astype(BF16)
         ref[:, 0:1536] = dot(ht, dqkv).astype(BF16)
@@ -402,9 +402,10 @@
     store_pieces(dot(const_ref[1, :, 0:144], back[...]), oown_ref, olon_ref, olat_ref, odia_ref)
 
 
-def send_kernel(idx_ref, h_ref, o_ref, dqkv_ref, g_ref, send_ref):
-    target = h_ref[...], o_ref[...], dqkv_ref[...], g_ref[...], send_ref
-    weight_terms(1 - idx_ref[0], target)
+def weights_kernel(idx_ref, h_ref, o_ref, dqkv_ref, g_ref, keep_ref, send_ref):
+    core = idx_ref[0]
+    targets = (core, keep_ref), (1 - core, send_ref)
+    weight_terms(h_ref[...], o_ref[...], dqkv_ref[...], g_ref[...], *targets)
 
 
 def third_kernel(
@@ -425,12 +426,11 @@
         group_back(g, qkv_ref[:, 128 * g : 128 * (g + 1)], q4, kg, vg, p4b.astype(F32), p4b, do, masks, dqkv_ref, ds0_ref, ds1_ref)
     h = (n_ref[...] * gain_ref[0:1, :]).astype(BF16)
     h_ref[...] = h
-    weight_terms(1 - idx_ref[0], (h, o_ref[...], dqkv_ref[...], gb, send_ref))
-
-
-def keep_kernel(idx_ref, *refs):
-    blocks = [[r[...] for r in refs[4 * b : 4 * b + 4]] + [refs[8 + b]] for b in range(2)]
-    weight_terms(idx_ref[0], *blocks)
+    weight_terms(h, o_ref[...], dqkv_ref[...], gb, (1 - idx_ref[0], send_ref))
+
+
+def keep_kernel(idx_ref, h_ref, o_ref, dqkv_ref, g_ref, keep_ref):
+    weight_terms(h_ref[...], o_ref[...], dqkv_ref[...], g_ref[...], (idx_ref[0], keep_ref))
 
 
 def finish_kernel(
@@ -794,7 +794,7 @@
     )
     pieces = halo((own, lon, lat, dia), 1)
     wshape = ((256, 4 * D), BF16)
-    (send1,) = call(send_kernel, 1, [wshape], idx, h1, o1, dqkv1, g1)
+    keep1, send1 = call(weights_kernel, 2, [wshape] * 2, idx, h1, o1, dqkv1, g1)
     recv1 = flip(send1, "c")
 
     def pairs(*shapes):
@@ -805,13 +805,11 @@
         third_kernel,
         4,
         [((144, D), BF16)] * 2 + [((144, 3 * D), BF16)] + ds_shapes + [wshape],
-        idx, *pieces, gains, proj_weight, n0, qkv0, p0, o0, third_const, send1,
+        idx, *pieces, gains, proj_weight, n0, qkv0, p0, o0, third_const, keep1,
         specs={6: block(0, (D, D)), 12: ANY},
     )
     recv0 = flip(send0, "c")
-    keep0, keep1 = call(
-        keep_kernel, 2, [wshape] * 2, idx, h0, o0, dqkv0, g0, h1, o1, dqkv1, g1
-    )
+    (keep0,) = call(keep_kernel, 1, [wshape], idx, h0, o0, dqkv0, g0)
     ka, sa, kb, sb, kc, sc = call(
         core_kernel,
         1,

time: 105 us -> 104 us (level)
  transfers between devices with their start and end apart: 27 -> 27, of which waited for: 11 -> 10; matrix products, arithmetic and copies ran while one was open for 0% -> 0% of each run, Pallas kernels for 16% -> 16%
where the time goes in v7:
time: 104 us
  starting transfers between devices  47.5 us (46%)
  Pallas kernels  36.1 us (35%)
  waiting for transfers between devices  19.5 us (19%)
    pallas_call x15, Pallas kernels, call(): pl.pallas_call(body, grid=(1,), in_specs=[specs.get(i, _whole(a.shape)) f...  36.1 us
    ppermute x19, starting transfers between devices, flip(): lax.ppermute(value, AXES, [(s, s ^ mask_of(axes)) for s in range(256)])  26.2 us
    ppermute x4, starting transfers between devices, lon_step(): return lax.ppermute(value, AXES, pairs)  13.4 us
    ppermute x19, waiting for transfers between devices, flip(): lax.ppermute(value, AXES, [(s, s ^ mask_of(axes)) for s in range(256)])  11.6 us
    ppermute x4, starting transfers between devices, z_step(): return lax.ppermute(value, AXES, pairs)  7.93 us
    ppermute x4, waiting for transfers between devices, z_step(): return lax.ppermute(value, AXES, pairs)  6.77 us
  transfers between devices with their start and end apart: 27, of which 10 were waited for; matrix products, arithmetic and copies ran while one was open for 0% of the time, Pallas kernels for 16%

profile of v7, /device:TPU:1, one launch (start us, length us, event | category | flops | bytes accessed | tf_op | source)
XLA Modules:
  0.0 104.2 jit_solution(13895405281074551766)
XLA Ops:
  0.7 0.0 copy-start.8
  0.7 8.5 %shard_map.172 = (bf16[40,1024]{1,0:T(8,128)(2,1)}, bf16[40,1024]{1,0:T(8,128)(2,1)}, bf16[40,1024]{1,0:T(8,128)(2,1)}, bf16[40,1024]{1,0:T(8,128)(2,1)}, f32[14...) custom-call(bf16[72,2,512]{2,1,0:T(2,128)(2,1)} %bitcast.19, ...), custom_call_target="tpu_custom_call" | custom-call | flops 8000000000 | bytes 28800000 | tf_op jit(solution)/shard_map/pallas_call | solution.py:667
  9.2 3.3 %collective-permute-start = (bf16[40,1024]{1,0:T(8,128)(2,1)}, bf16[40,1024]{1,0:T(8,128)(2,1)S(1)}, u32[]{:S(2)}, u32[]{:S(2)}) collective-permute-start(bf16[40,1024]{1,0:T(8,128)(2,1)} %get-tuple-element.77), channel_id=1, source_target_pairs={{0,254},{1,255},{2,0},{3,1},{4,2},{5,3},{6,4},{7,5},{8,6},{9,7},{1... | collective-permute-start | bytes 245768 | tf_op jit(solution)/shard_map/ppermute | solution.py:696
  12.5 10.0 %collective-permute-start.2 = (bf16[40,1024]{1,0:T(8,128)(2,1)}, bf16[40,1024]{1,0:T(8,128)(2,1)S(1)}, u32[]{:S(2)}, u32[]{:S(2)}) collective-permute-start(bf16[40,1024]{1,0:T(8,128)(2,1)} %get-tuple-element.79), channel_id=1, source_target_pairs={{0,255},{1,254},{2,1},{3,0},{4,3},{5,2},{6,5},{7,4},{8,7},{9,6},{1... | collective-permute-start | bytes 245768 | tf_op jit(solution)/shard_map/ppermute | solution.py:696
  22.5 0.1 stack.27.idx_ref
  22.6 0.0 copy-start
  22.6 0.0 copy-start.1
  22.6 0.0 copy-start.4
  22.7 0.0 copy-start.5
  22.7 0.0 copy-start.14
  22.7 3.9 %shard_map.173 = (f32[2304,256]{1,0:T(8,128)S(1)}, s32[144,128]{1,0:T(8,128)S(1)}, s32[24,128]{1,0:T(8,128)S(1)}) custom-call(s32[6]{0:T(128)S(1)} %stack.27.idx_ref, f32[2,2,16,759]{3,2,1,0:T(8,128)S(1)} %copy-done.2, s32[144,144]{1,0:T(8,128)S(1)} %copy-done.3, bf16[160,256]{1,0:T(8,128)(2,1)S(1)} %copy-done.8), custom_call_target="tpu_custom_call" | custom-call | flops 4000000000 | bytes 14400000 | tf_op jit(solution)/shard_map/pallas_call | solution.py:667
  26.6 0.0 collective-permute-done.lon_ref
  26.7 5.3 %shard_map.174 = (bf16[40,1024]{1,0:T(8,128)(2,1)S(1)}, bf16[40,1024]{1,0:T(8,128)(2,1)S(1)}, bf16[40,1024]{1,0:T(8,128)(2,1)S(1)}, bf16[40,1024]{1,0:T(8,128)(2...) custom-call(s32[6]{0:T(128)S(1)} %stack.27.idx_ref, ...), custom_call_target="tpu_custom_call" | custom-call | flops 6000000000 | bytes 21600000 | tf_op jit(solution)/shard_map/pallas_call | solution.py:667
  32.0 0.1 collective-permute-start.3
  32.1 0.5 collective-permute-start.4
  32.6 0.0 collective-permute-start.5
  32.6 1.8 %shard_map.175 = (bf16[256,2048]{1,0:T(8,128)(2,1)S(1)}, bf16[256,2048]{1,0:T(8,128)(2,1)S(1)}) custom-call(s32[6]{0:T(128)S(1)} %stack.27.idx_ref, bf16[144,512]{1,0:T(8,128)(2,1)S(1)} %get-tuple-element.90.h_ref, bf16[144,512]{1,0:T(8,128)(2,1)S(1)} %get-tuple-element.91.o_ref, bf16[144,1536]{1,0:T(8,128)(2,1)S(1)} %get-tuple-element.92.dqkv_ref, ...), custom_call_target="tpu_custom_call" | custom-call | flops 2000000000 | bytes 7200000 | tf_op jit(solution)/shard_map/pallas_call | solution.py:667
  34.4 1.8 %collective-permute-start.7 = (bf16[256,2048]{1,0:T(8,128)(2,1)S(1)}, bf16[256,2048]{1,0:T(8,128)(2,1)S(1)}, u32[]{:S(2)}, u32[]{:S(2)}) collective-permute-start(bf16[256,2048]{1,0:T(8,128)(2,1)S(1)} %get-tuple-element.99), channel_id=1, source_target_pairs={{0,2},{1,3},{2,0},{3,1},{4,6},{5,7},{6,4},{7,5},{8,10},{9,11},{10,... | collective-permute-start | bytes 3145736 | tf_op jit(solution)/shard_map/ppermute | solution.py:686
  36.1 0.0 collective-permute-done.3.lon_ref
  36.1 0.0 collective-permute-done.4.lat_ref
  36.1 1.1 %collective-permute-done.5.dia_ref = bf16[40,1024]{1,0:T(8,128)(2,1)S(1)} collective-permute-done((bf16[40,1024]{1,0:T(8,128)(2,1)S(1)}, bf16[40,1024]{1,0:T(8,128)(2,1)S(1)}, u32[]{:S(2)}, u32[]{:S(2)}) %collective-permute-start.5) | collective-permute-done | bytes 81952 | tf_op jit(solution)/shard_map/ppermute | solution.py:696
  37.2 3.1 %shard_map.176 = (bf16[144,512]{1,0:T(8,128)(2,1)S(1)}, bf16[144,512]{1,0:T(8,128)(2,1)S(1)}, bf16[144,1536]{1,0:T(8,128)(2,1)S(1)}, f32[2304,128]{1,0:T(8,128)S...) custom-call(s32[6]{0:T(128)S(1)} %stack.27.idx_ref, bf16[40,1024]{1,0:T(8,128)(2,1)S(1)} %get-tuple-element.81.own_ref, ...), custom_call_target="tpu_custom_call" | custom-call | flops 4000000000 | bytes 14400000 | tf_op jit(solution)/shard_map/pallas_call | solution.py:667
  40.4 5.4 %collective-permute-start.6 = (bf16[256,2048]{1,0:T(8,128)(2,1)S(1)}, bf16[256,2048]{1,0:T(8,128)(2,1)S(1)}, u32[]{:S(2)}, u32[]{:S(2)}) collective-permute-start(bf16[256,2048]{1,0:T(8,128)(2,1)S(1)} %get-tuple-element.98), channel_id=1, source_target_pairs={{0,2},{1,3},{2,0},{3,1},{4,6},{5,7},{6,4},{7,5},{8,10},{9,11},{10,... | collective-permute-start | bytes 3145736 | tf_op jit(solution)/shard_map/ppermute | solution.py:686
  45.8 1.3 %shard_map.177.k0_ref = bf16[256,2048]{1,0:T(8,128)(2,1)S(1)} custom-call(s32[6]{0:T(128)S(1)} %stack.27.idx_ref, bf16[144,512]{1,0:T(8,128)(2,1)S(1)} %get-tuple-element.97.h_ref, bf16[144,512]{1,0:T(8,128)(2,1)S(1)} %copy-done.10, bf16[144,1536]{1,0:T(8,128)(2,1)S(1)} %get-tuple-element.96.dqkv_ref, bf16[144,512]{1,0:T(8,128)(2,1)S(1)} %get-tuple-element.95.g_ref), custom_call_target="tpu_custom_call" | custom-call | flops 1000000000 | bytes 3600000 | tf_op jit(solution)/shard_map/pallas_call | solution.py:667
  47.0 0.0 copy-start.6
  47.1 1.0 collective-permute-done.6.r0_ref
  48.1 1.2 %shard_map.178 = (bf16[128,1536]{1,0:T(8,128)(2,1)S(1)}, bf16[128,1536]{1,0:T(8,128)(2,1)S(1)}, bf16[256,768]{1,0:T(8,128)(2,1)S(1)}, bf16[256,768]{1,0:T(8,128)...) custom-call(s32[6]{0:T(128)S(1)} %stack.27.idx_ref, bf16[256,2048]{1,0:T(8,128)(2,1)S(1)} %shard_map.177.k0_ref, ...), custom_call_target="tpu_custom_call" | custom-call | flops 1000000000 | bytes 3600000 | tf_op jit(solution)/shard_map/pallas_call | solution.py:667
  49.3 0.1 collective-permute-start.10
  49.4 0.1 collective-permute-start.8
  49.5 0.3 collective-permute-start.9
  49.7 1.7 %shard_map.179 = (bf16[72,2,512]{2,1,0:T(2,128)(2,1)}, bf16[72,2,512]{2,1,0:T(2,128)(2,1)}, f32[1,512]{1,0:T(1,128)S(1)}) custom-call(bf16[40,1024]{1,0:T(8,128)(2,1)S(1)} %get-tuple-element.81.own_ref, bf16[40,1024]{1,0:T(8,128)(2,1)S(1)} %collective-permute-done.3.lon_ref, bf16[40,1024]{1,0:T(8,128)(2,1)S(1)} %collective-permute-done.4.lat_ref, ...), custom_call_target="tpu_custom_call" | custom-call | flops 2000000000 | bytes 7200000 | tf_op jit(solution)/shard_map/pallas_call | solution.py:667
  51.5 4.5 %shard_map.180 = (f32[16,1024]{1,0:T(8,128)S(1)}, f32[16,1024]{1,0:T(8,128)S(1)}) custom-call(s32[6]{0:T(128)S(1)} %stack.27.idx_ref, s32[144,128]{1,0:T(8,128)S(1)} %get-tuple-element.108.main_ref, s32[24,128]{1,0:T(8,128)S(1)} %get-tuple-element.109.tail_ref, f32[2304,128]{1,0:T(8,128)S(1)} %get-tuple-element.110.m0_ref, ...), custom_call_target="tpu_custom_call" | custom-call | flops 6000000000 | bytes 21600000 | tf_op jit(solution)/shard_map/pallas_call | solution.py:667
  56.0 0.7 collective-permute-start.11
  56.7 0.9 collective-permute-done.11.u_ref
  57.6 2.1 %collective-permute-done.8.ra_ref = bf16[128,1536]{1,0:T(8,128)(2,1)S(1)} collective-permute-done((bf16[128,1536]{1,0:T(8,128)(2,1)S(1)}, bf16[128,1536]{1,0:T(8,128)(2,1)S(1)}, u32[]{:S(2)}, u32[]{:S(2)}) %collective-permute-start.8) | collective-permute-done | bytes 393248 | tf_op jit(solution)/shard_map/ppermute | solution.py:686
  59.8 0.1 collective-permute-done.9.rb_ref
  59.9 0.9 shard_map.181
  60.8 0.3 collective-permute-start.12
  61.0 0.9 collective-permute-start.13
  62.0 1.2 %collective-permute-start.14 = (bf16[80,1024]{1,0:T(8,128)(2,1)S(1)}, bf16[80,1024]{1,0:T(8,128)(2,1)S(1)}, u32[]{:S(2)}, u32[]{:S(2)}) collective-permute-start(bf16[80,1024]{1,0:T(8,128)(2,1)S(1)} %get-tuple-element.123), channel_id=1, source_target_pairs={{0,32},{1,33},{2,34},{3,35},{4,36},{5,37},{6,38},{7,39},{8,40},{9,... | collective-permute-start | bytes 491528 | tf_op jit(solution)/shard_map/ppermute | solution.py:686
  63.2 3.2 %collective-permute-done.14.rc_ref = bf16[80,1024]{1,0:T(8,128)(2,1)S(1)} collective-permute-done((bf16[80,1024]{1,0:T(8,128)(2,1)S(1)}, bf16[80,1024]{1,0:T(8,128)(2,1)S(1)}, u32[]{:S(2)}, u32[]{:S(2)}) %collective-permute-start.14) | collective-permute-done | bytes 163872 | tf_op jit(solution)/shard_map/ppermute | solution.py:686
  66.5 0.0 collective-permute-done.12.ra_ref
  66.5 0.0 collective-permute-done.13.rb_ref
  66.5 0.7 shard_map.182
  67.2 0.6 collective-permute-start.15
  67.8 1.0 %collective-permute-start.16 = (bf16[64,768]{1,0:T(8,128)(2,1)S(1)}, bf16[64,768]{1,0:T(8,128)(2,1)S(1)}, u32[]{:S(2)}, u32[]{:S(2)}) collective-permute-start(bf16[64,768]{1,0:T(8,128)(2,1)S(1)} %get-tuple-element.128), channel_id=1, source_target_pairs={{0,32},{1,33},{2,34},{3,35},{4,36},{5,37},{6,38},{7,39},{8,40},{9,... | collective-permute-start | bytes 294920 | tf_op jit(solution)/shard_map/ppermute | solution.py:686
  68.8 1.3 %collective-permute-start.17 = (bf16[64,512]{1,0:T(8,128)(2,1)S(1)}, bf16[64,512]{1,0:T(8,128)(2,1)S(1)}, u32[]{:S(2)}, u32[]{:S(2)}) collective-permute-start(bf16[64,512]{1,0:T(8,128)(2,1)S(1)} %get-tuple-element.130), channel_id=1, source_target_pairs={{0,1},{1,0},{2,3},{3,2},{4,5},{5,4},{6,7},{7,6},{8,9},{9,8},{10,11... | collective-permute-start | bytes 196616 | tf_op jit(solution)/shard_map/ppermute | solution.py:686
  70.1 1.8 %collective-permute-done.17.rc_ref = bf16[64,512]{1,0:T(8,128)(2,1)S(1)} collective-permute-done((bf16[64,512]{1,0:T(8,128)(2,1)S(1)}, bf16[64,512]{1,0:T(8,128)(2,1)S(1)}, u32[]{:S(2)}, u32[]{:S(2)}) %collective-permute-start.17) | collective-permute-done | bytes 65568 | tf_op jit(solution)/shard_map/ppermute | solution.py:686
  71.9 0.0 collective-permute-done.16.rb_ref
  72.0 0.7 shard_map.183
  72.6 0.1 collective-permute-start.18
  72.7 0.6 collective-permute-start.19
  73.3 4.5 %collective-permute-start.20 = (bf16[24,2048]{1,0:T(8,128)(2,1)S(1)}, bf16[24,2048]{1,0:T(8,128)(2,1)S(1)}, u32[]{:S(2)}, u32[]{:S(2)}) collective-permute-start(bf16[24,2048]{1,0:T(8,128)(2,1)S(1)} %get-tuple-element.135), channel_id=1, source_target_pairs={{0,124},{1,125},{2,126},{3,127},{4,104},{5,105},{6,106},{7,107},{8... | collective-permute-start | bytes 294920 | tf_op jit(solution)/shard_map/ppermute | solution.py:691
  77.8 2.9 %collective-permute-done.20.g3_ref = bf16[24,2048]{1,0:T(8,128)(2,1)S(1)} collective-permute-done((bf16[24,2048]{1,0:T(8,128)(2,1)S(1)}, bf16[24,2048]{1,0:T(8,128)(2,1)S(1)}, u32[]{:S(2)}, u32[]{:S(2)}) %collective-permute-start.20) | collective-permute-done | bytes 98336 | tf_op jit(solution)/shard_map/ppermute | solution.py:691
  80.6 0.6 shard_map.184
  81.3 0.1 collective-permute-start.21
  81.4 2.7 %collective-permute-start.22 = (bf16[24,1024]{1,0:T(8,128)(2,1)S(1)}, bf16[24,1024]{1,0:T(8,128)(2,1)S(1)}, u32[]{:S(2)}, u32[]{:S(2)}) collective-permute-start(bf16[24,1024]{1,0:T(8,128)(2,1)S(1)} %get-tuple-element.138), channel_id=1, source_target_pairs={{0,128},{1,129},{2,130},{3,131},{4,132},{5,133},{6,134},{7,135},{8... | collective-permute-start | bytes 147464 | tf_op jit(solution)/shard_map/ppermute | solution.py:686
  84.1 3.3 %collective-permute-start.23 = (bf16[24,1024]{1,0:T(8,128)(2,1)S(1)}, bf16[24,1024]{1,0:T(8,128)(2,1)S(1)}, u32[]{:S(2)}, u32[]{:S(2)}) collective-permute-start(bf16[24,1024]{1,0:T(8,128)(2,1)S(1)} %get-tuple-element.139), channel_id=1, source_target_pairs={{0,140},{1,141},{2,142},{3,143},{4,152},{5,153},{6,154},{7,155},{8... | collective-permute-start | bytes 147464 | tf_op jit(solution)/shard_map/ppermute | solution.py:691
  87.3 3.9 %collective-permute-done.23.g3_ref = bf16[24,1024]{1,0:T(8,128)(2,1)S(1)} collective-permute-done((bf16[24,1024]{1,0:T(8,128)(2,1)S(1)}, bf16[24,1024]{1,0:T(8,128)(2,1)S(1)}, u32[]{:S(2)}, u32[]{:S(2)}) %collective-permute-start.23) | collective-permute-done | bytes 49184 | tf_op jit(solution)/shard_map/ppermute | solution.py:691
  91.2 0.6 shard_map.185
  91.8 0.2 collective-permute-start.24
  92.0 8.5 %collective-permute-start.26 = (bf16[16,1024]{1,0:T(8,128)(2,1)S(1)}, bf16[16,1024]{1,0:T(8,128)(2,1)S(1)}, u32[]{:S(2)}, u32[]{:S(2)}) collective-permute-start(bf16[16,1024]{1,0:T(8,128)(2,1)S(1)} %get-tuple-element.141), channel_id=1, source_target_pairs={{0,3},{1,2},{2,1},{3,0},{4,7},{5,6},{6,5},{7,4},{8,11},{9,10},{10,... | collective-permute-start | bytes 98312 | tf_op jit(solution)/shard_map/ppermute | solution.py:686
  100.5 2.3 %collective-permute-done.26.dia_ref = bf16[16,1024]{1,0:T(8,128)(2,1)S(1)} collective-permute-done((bf16[16,1024]{1,0:T(8,128)(2,1)S(1)}, bf16[16,1024]{1,0:T(8,128)(2,1)S(1)}, u32[]{:S(2)}, u32[]{:S(2)}) %collective-permute-start.26) | collective-permute-done | bytes 32800 | tf_op jit(solution)/shard_map/ppermute | solution.py:686
  102.9 1.3 %shard_map.186 = (f32[2,512]{1,0:T(2,128)}, f32[2,4,1536]{2,1,0:T(4,128)}, f32[2,4,512]{2,1,0:T(4,128)}, f32[2,2,16,759]{3,2,1,0:T(8,128)}) custom-call(s32[6]{0:T(128)S(1)} %stack.27.idx_ref, bf16[24,1024]{1,0:T(8,128)(2,1)S(1)} %get-tuple-element.140.own_ref, bf16[24,1024]{1,0:T(8,128)(2,1)S(1)} %collective-permute-done.24.lat_ref, ...), custom_call_target="tpu_custom_call" | custom-call | flops 1000000000 | bytes 3600000 | tf_op jit(solution)/shard_map/pallas_call | solution.py:667
  (36 shorter events, 0.1 us)
Async XLA Ops:
  0.6 22.0 %copy-start.2 = (f32[2,2,16,759]{3,2,1,0:T(8,128)S(1)}, f32[2,2,16,759]{3,2,1,0:T(8,128)}, u32[]{:S(2)}) copy-start(f32[2,2,16,759]{3,2,1,0:T(8,128)} %tab_ref.1) | copy-start | bytes 582916
  0.6 22.0 %copy-start.3 = (s32[144,144]{1,0:T(8,128)S(1)}, s32[144,144]{1,0:T(8,128)}, u32[]{:S(2)}) copy-start(s32[144,144]{1,0:T(8,128)} %rel_ref.1) | copy-start | bytes 248836
  0.7 22.0 %copy-start.8 = (bf16[160,256]{1,0:T(8,128)(2,1)S(1)}, bf16[160,256]{1,0:T(8,128)(2,1)}, u32[]{:S(2)}) copy-start(bf16[160,256]{1,0:T(8,128)(2,1)} %constant.46.clone.pm_ref) | copy-start | bytes 245764
  9.2 17.4 %collective-permute-start = (bf16[40,1024]{1,0:T(8,128)(2,1)}, bf16[40,1024]{1,0:T(8,128)(2,1)S(1)}, u32[]{:S(2)}, u32[]{:S(2)}) collective-permute-start(bf16[40,1024]{1,0:T(8,128)(2,1)} %get-tuple-element.77), channel_id=1, source_target_pairs={{0,254},{1,255},{2,0},{3,1},{4,2},{5,3},{6,4},{7,5},{8,6},{9,7},{1... | collective-permute-start | bytes 245768 | tf_op jit(solution)/shard_map/ppermute | solution.py:696
  12.5 14.1 %collective-permute-start.1 = (bf16[40,1024]{1,0:T(8,128)(2,1)}, bf16[40,1024]{1,0:T(8,128)(2,1)S(1)}, u32[]{:S(2)}, u32[]{:S(2)}) collective-permute-start(bf16[40,1024]{1,0:T(8,128)(2,1)} %get-tuple-element.78), channel_id=1, source_target_pairs={{0,1},{1,0},{2,3},{3,2},{4,5},{5,4},{6,7},{7,6},{8,9},{9,8},{10,11... | collective-permute-start | bytes 245768 | tf_op jit(solution)/shard_map/ppermute | solution.py:686
  12.5 14.1 %collective-permute-start.2 = (bf16[40,1024]{1,0:T(8,128)(2,1)}, bf16[40,1024]{1,0:T(8,128)(2,1)S(1)}, u32[]{:S(2)}, u32[]{:S(2)}) collective-permute-start(bf16[40,1024]{1,0:T(8,128)(2,1)} %get-tuple-element.79), channel_id=1, source_target_pairs={{0,255},{1,254},{2,1},{3,0},{4,3},{5,2},{6,5},{7,4},{8,7},{9,6},{1... | collective-permute-start | bytes 245768 | tf_op jit(solution)/shard_map/ppermute | solution.py:696
  22.6 4.0 %copy-start = (bf16[2,512,1536]{2,1,0:T(8,128)(2,1)S(1)}, bf16[2,512,1536]{2,1,0:T(8,128)(2,1)}, u32[]{:S(2)}) copy-start(bf16[2,512,1536]{2,1,0:T(8,128)(2,1)} %wqkv_ref.3) | copy-start | bytes 9437188
  22.6 4.0 %copy-start.1 = (bf16[2,512,512]{2,1,0:T(8,128)(2,1)S(1)}, bf16[2,512,512]{2,1,0:T(8,128)(2,1)}, u32[]{:S(2)}) copy-start(bf16[2,512,512]{2,1,0:T(8,128)(2,1)} %wproj_ref.3) | copy-start | bytes 3145732
  22.6 4.0 %copy-start.4 = (f32[2,512]{1,0:T(2,128)S(1)}, f32[2,512]{1,0:T(2,128)}, u32[]{:S(2)}) copy-start(f32[2,512]{1,0:T(2,128)} %gain_ref.5) | copy-start | bytes 12292
  22.7 4.0 %copy-start.5 = (bf16[5,160,256]{2,1,0:T(8,128)(2,1)S(1)}, bf16[5,160,256]{2,1,0:T(8,128)(2,1)}, u32[]{:S(2)}) copy-start(bf16[5,160,256]{2,1,0:T(8,128)(2,1)} %constant.43.clone.const_ref) | copy-start | bytes 1228804
  22.7 4.0 %copy-start.14 = (bf16[40,1024]{1,0:T(8,128)(2,1)S(1)}, bf16[40,1024]{1,0:T(8,128)(2,1)}, u32[]{:S(2)}) copy-start(bf16[40,1024]{1,0:T(8,128)(2,1)} %get-tuple-element.76.own_ref) | copy-start | bytes 245764
  32.0 4.1 %collective-permute-start.3 = (bf16[40,1024]{1,0:T(8,128)(2,1)S(1)}, bf16[40,1024]{1,0:T(8,128)(2,1)S(1)}, u32[]{:S(2)}, u32[]{:S(2)}) collective-permute-start(bf16[40,1024]{1,0:T(8,128)(2,1)S(1)} %get-tuple-element.82), channel_id=1, source_target_pairs={{0,2},{1,3},{2,4},{3,5},{4,6},{5,7},{6,8},{7,9},{8,10},{9,11},{10,... | collective-permute-start | bytes 245768 | tf_op jit(solution)/shard_map/ppermute | solution.py:696
  32.1 4.0 %collective-permute-start.4 = (bf16[40,1024]{1,0:T(8,128)(2,1)S(1)}, bf16[40,1024]{1,0:T(8,128)(2,1)S(1)}, u32[]{:S(2)}, u32[]{:S(2)}) collective-permute-start(bf16[40,1024]{1,0:T(8,128)(2,1)S(1)} %get-tuple-element.83), channel_id=1, source_target_pairs={{0,1},{1,0},{2,3},{3,2},{4,5},{5,4},{6,7},{7,6},{8,9},{9,8},{10,11... | collective-permute-start | bytes 245768 | tf_op jit(solution)/shard_map/ppermute | solution.py:686
  32.6 4.7 %collective-permute-start.5 = (bf16[40,1024]{1,0:T(8,128)(2,1)S(1)}, bf16[40,1024]{1,0:T(8,128)(2,1)S(1)}, u32[]{:S(2)}, u32[]{:S(2)}) collective-permute-start(bf16[40,1024]{1,0:T(8,128)(2,1)S(1)} %get-tuple-element.84), channel_id=1, source_target_pairs={{0,3},{1,2},{2,5},{3,4},{4,7},{5,6},{6,9},{7,8},{8,11},{9,10},{10,... | collective-permute-start | bytes 245768 | tf_op jit(solution)/shard_map/ppermute | solution.py:696
  32.6 4.7 %copy-start.7 = (bf16[1,160,256]{2,1,0:T(8,128)(2,1)S(1)}, bf16[1,160,256]{2,1,0:T(8,128)(2,1)}, u32[]{:S(2)}) copy-start(bf16[1,160,256]{2,1,0:T(8,128)(2,1)} %constant.44.clone.const_ref) | copy-start | bytes 245764
  32.6 4.7 %copy-start.9 = (f32[144,512]{1,0:T(8,128)S(1)}, f32[144,512]{1,0:T(8,128)}, u32[]{:S(2)}) copy-start(f32[144,512]{1,0:T(8,128)} %get-tuple-element.85.n_ref) | copy-start | bytes 884740
  32.6 4.7 %copy-start.10 = (bf16[144,512]{1,0:T(8,128)(2,1)S(1)}, bf16[144,512]{1,0:T(8,128)(2,1)}, u32[]{:S(2)}) copy-start(bf16[144,512]{1,0:T(8,128)(2,1)} %get-tuple-element.89.o_ref) | copy-start | bytes 442372
  32.6 4.7 %copy-start.12 = (bf16[2304,256]{1,0:T(8,128)(2,1)S(1)}, bf16[2304,256]{1,0:T(8,128)(2,1)}, u32[]{:S(2)}) copy-start(bf16[2304,256]{1,0:T(8,128)(2,1)} %get-tuple-element.88.p_ref) | copy-start | bytes 3538948
  32.6 4.7 %copy-start.13 = (bf16[144,1536]{1,0:T(8,128)(2,1)S(1)}, bf16[144,1536]{1,0:T(8,128)(2,1)}, u32[]{:S(2)}) copy-start(bf16[144,1536]{1,0:T(8,128)(2,1)} %get-tuple-element.87.qkv_ref) | copy-start | bytes 1327108
  34.4 12.7 %collective-permute-start.7 = (bf16[256,2048]{1,0:T(8,128)(2,1)S(1)}, bf16[256,2048]{1,0:T(8,128)(2,1)S(1)}, u32[]{:S(2)}, u32[]{:S(2)}) collective-permute-start(bf16[256,2048]{1,0:T(8,128)(2,1)S(1)} %get-tuple-element.99), channel_id=1, source_target_pairs={{0,2},{1,3},{2,0},{3,1},{4,6},{5,7},{6,4},{7,5},{8,10},{9,11},{10,... | collective-permute-start | bytes 3145736 | tf_op jit(solution)/shard_map/ppermute | solution.py:686
  40.4 7.7 %collective-permute-start.6 = (bf16[256,2048]{1,0:T(8,128)(2,1)S(1)}, bf16[256,2048]{1,0:T(8,128)(2,1)S(1)}, u32[]{:S(2)}, u32[]{:S(2)}) collective-permute-start(bf16[256,2048]{1,0:T(8,128)(2,1)S(1)} %get-tuple-element.98), channel_id=1, source_target_pairs={{0,2},{1,3},{2,0},{3,1},{4,6},{5,7},{6,4},{7,5},{8,10},{9,11},{10,... | collective-permute-start | bytes 3145736 | tf_op jit(solution)/shard_map/ppermute | solution.py:686
  47.0 2.7 %copy-start.6 = (bf16[2,160,256]{2,1,0:T(8,128)(2,1)S(1)}, bf16[2,160,256]{2,1,0:T(8,128)(2,1)}, u32[]{:S(2)}) copy-start(bf16[2,160,256]{2,1,0:T(8,128)(2,1)} %constant.45.clone.const_ref) | copy-start | bytes 491524
  47.1 2.7 %copy-start.11 = (f32[144,1]{1,0:T(8,128)S(1)}, f32[144,1]{1,0:T(8,128)}, u32[]{:S(2)}) copy-start(f32[144,1]{1,0:T(8,128)} %get-tuple-element.86.rstd_ref) | copy-start | bytes 1732
  49.3 8.4 %collective-permute-start.10 = (bf16[128,1024]{1,0:T(8,128)(2,1)S(1)}, bf16[128,1024]{1,0:T(8,128)(2,1)S(1)}, u32[]{:S(2)}, u32[]{:S(2)}) collective-permute-start(bf16[128,1024]{1,0:T(8,128)(2,1)S(1)} %get-tuple-element.107), channel_id=1, source_target_pairs={{0,4},{1,5},{2,6},{3,7},{4,0},{5,1},{6,2},{7,3},{8,12},{9,13},{10,... | collective-permute-start | bytes 786440 | tf_op jit(solution)/shard_map/ppermute | solution.py:686
  49.4 10.4 %collective-permute-start.8 = (bf16[128,1536]{1,0:T(8,128)(2,1)S(1)}, bf16[128,1536]{1,0:T(8,128)(2,1)S(1)}, u32[]{:S(2)}, u32[]{:S(2)}) collective-permute-start(bf16[128,1536]{1,0:T(8,128)(2,1)S(1)} %get-tuple-element.103), channel_id=1, source_target_pairs={{0,32},{1,33},{2,34},{3,35},{4,36},{5,37},{6,38},{7,39},{8,40},{9,... | collective-permute-start | bytes 1179656 | tf_op jit(solution)/shard_map/ppermute | solution.py:686
  49.5 10.4 %collective-permute-start.9 = (bf16[256,768]{1,0:T(8,128)(2,1)S(1)}, bf16[256,768]{1,0:T(8,128)(2,1)S(1)}, u32[]{:S(2)}, u32[]{:S(2)}) collective-permute-start(bf16[256,768]{1,0:T(8,128)(2,1)S(1)} %get-tuple-element.105), channel_id=1, source_target_pairs={{0,1},{1,0},{2,3},{3,2},{4,5},{5,4},{6,7},{7,6},{8,9},{9,8},{10,11... | collective-permute-start | bytes 1179656 | tf_op jit(solution)/shard_map/ppermute | solution.py:686
  56.0 1.6 %collective-permute-start.11 = (f32[16,1024]{1,0:T(8,128)S(1)}, f32[16,1024]{1,0:T(8,128)S(1)}, u32[]{:S(2)}, u32[]{:S(2)}) collective-permute-start(f32[16,1024]{1,0:T(8,128)S(1)} %get-tuple-element.117), channel_id=1, source_target_pairs={{0,2},{1,3},{2,0},{3,1},{4,6},{5,7},{6,4},{7,5},{8,10},{9,11},{10,... | collective-permute-start | bytes 196616 | tf_op jit(solution)/shard_map/ppermute | solution.py:686
  60.8 5.7 %collective-permute-start.12 = (bf16[128,768]{1,0:T(8,128)(2,1)S(1)}, bf16[128,768]{1,0:T(8,128)(2,1)S(1)}, u32[]{:S(2)}, u32[]{:S(2)}) collective-permute-start(bf16[128,768]{1,0:T(8,128)(2,1)S(1)} %get-tuple-element.119), channel_id=1, source_target_pairs={{0,1},{1,0},{2,3},{3,2},{4,5},{5,4},{6,7},{7,6},{8,9},{9,8},{10,11... | collective-permute-start | bytes 589832 | tf_op jit(solution)/shard_map/ppermute | solution.py:686
  61.0 5.4 %collective-permute-start.13 = (bf16[128,768]{1,0:T(8,128)(2,1)S(1)}, bf16[128,768]{1,0:T(8,128)(2,1)S(1)}, u32[]{:S(2)}, u32[]{:S(2)}) collective-permute-start(bf16[128,768]{1,0:T(8,128)(2,1)S(1)} %get-tuple-element.121), channel_id=1, source_target_pairs={{0,4},{1,5},{2,6},{3,7},{4,0},{5,1},{6,2},{7,3},{8,12},{9,13},{10,... | collective-permute-start | bytes 589832 | tf_op jit(solution)/shard_map/ppermute | solution.py:686
  62.0 4.5 %collective-permute-start.14 = (bf16[80,1024]{1,0:T(8,128)(2,1)S(1)}, bf16[80,1024]{1,0:T(8,128)(2,1)S(1)}, u32[]{:S(2)}, u32[]{:S(2)}) collective-permute-start(bf16[80,1024]{1,0:T(8,128)(2,1)S(1)} %get-tuple-element.123), channel_id=1, source_target_pairs={{0,32},{1,33},{2,34},{3,35},{4,36},{5,37},{6,38},{7,39},{8,40},{9,... | collective-permute-start | bytes 491528 | tf_op jit(solution)/shard_map/ppermute | solution.py:686
  67.2 4.8 %collective-permute-start.15 = (bf16[96,768]{1,0:T(8,128)(2,1)S(1)}, bf16[96,768]{1,0:T(8,128)(2,1)S(1)}, u32[]{:S(2)}, u32[]{:S(2)}) collective-permute-start(bf16[96,768]{1,0:T(8,128)(2,1)S(1)} %get-tuple-element.126), channel_id=1, source_target_pairs={{0,4},{1,5},{2,6},{3,7},{4,0},{5,1},{6,2},{7,3},{8,12},{9,13},{10,... | collective-permute-start | bytes 442376 | tf_op jit(solution)/shard_map/ppermute | solution.py:686
  67.8 4.2 %collective-permute-start.16 = (bf16[64,768]{1,0:T(8,128)(2,1)S(1)}, bf16[64,768]{1,0:T(8,128)(2,1)S(1)}, u32[]{:S(2)}, u32[]{:S(2)}) collective-permute-start(bf16[64,768]{1,0:T(8,128)(2,1)S(1)} %get-tuple-element.128), channel_id=1, source_target_pairs={{0,32},{1,33},{2,34},{3,35},{4,36},{5,37},{6,38},{7,39},{8,40},{9,... | collective-permute-start | bytes 294920 | tf_op jit(solution)/shard_map/ppermute | solution.py:686
  68.8 3.1 %collective-permute-start.17 = (bf16[64,512]{1,0:T(8,128)(2,1)S(1)}, bf16[64,512]{1,0:T(8,128)(2,1)S(1)}, u32[]{:S(2)}, u32[]{:S(2)}) collective-permute-start(bf16[64,512]{1,0:T(8,128)(2,1)S(1)} %get-tuple-element.130), channel_id=1, source_target_pairs={{0,1},{1,0},{2,3},{3,2},{4,5},{5,4},{6,7},{7,6},{8,9},{9,8},{10,11... | collective-permute-start | bytes 196616 | tf_op jit(solution)/shard_map/ppermute | solution.py:686
  72.6 5.2 %collective-permute-start.18 = (bf16[24,2048]{1,0:T(8,128)(2,1)S(1)}, bf16[24,2048]{1,0:T(8,128)(2,1)S(1)}, u32[]{:S(2)}, u32[]{:S(2)}) collective-permute-start(bf16[24,2048]{1,0:T(8,128)(2,1)S(1)} %get-tuple-element.133), channel_id=1, source_target_pairs={{0,28},{1,29},{2,30},{3,31},{4,8},{5,9},{6,10},{7,11},{8,4},{9,5},... | collective-permute-start | bytes 294920 | tf_op jit(solution)/shard_map/ppermute | solution.py:691
  72.7 5.1 %collective-permute-start.19 = (bf16[24,2048]{1,0:T(8,128)(2,1)S(1)}, bf16[24,2048]{1,0:T(8,128)(2,1)S(1)}, u32[]{:S(2)}, u32[]{:S(2)}) collective-permute-start(bf16[24,2048]{1,0:T(8,128)(2,1)S(1)} %get-tuple-element.134), channel_id=1, source_target_pairs={{0,96},{1,97},{2,98},{3,99},{4,100},{5,101},{6,102},{7,103},{8,104... | collective-permute-start | bytes 294920 | tf_op jit(solution)/shard_map/ppermute | solution.py:686
  73.3 7.4 %collective-permute-start.20 = (bf16[24,2048]{1,0:T(8,128)(2,1)S(1)}, bf16[24,2048]{1,0:T(8,128)(2,1)S(1)}, u32[]{:S(2)}, u32[]{:S(2)}) collective-permute-start(bf16[24,2048]{1,0:T(8,128)(2,1)S(1)} %get-tuple-element.135), channel_id=1, source_target_pairs={{0,124},{1,125},{2,126},{3,127},{4,104},{5,105},{6,106},{7,107},{8... | collective-permute-start | bytes 294920 | tf_op jit(solution)/shard_map/ppermute | solution.py:691
  81.3 6.0 %collective-permute-start.21 = (bf16[24,1024]{1,0:T(8,128)(2,1)S(1)}, bf16[24,1024]{1,0:T(8,128)(2,1)S(1)}, u32[]{:S(2)}, u32[]{:S(2)}) collective-permute-start(bf16[24,1024]{1,0:T(8,128)(2,1)S(1)} %get-tuple-element.137), channel_id=1, source_target_pairs={{0,12},{1,13},{2,14},{3,15},{4,24},{5,25},{6,26},{7,27},{8,20},{9,... | collective-permute-start | bytes 147464 | tf_op jit(solution)/shard_map/ppermute | solution.py:691
  81.4 5.9 %collective-permute-start.22 = (bf16[24,1024]{1,0:T(8,128)(2,1)S(1)}, bf16[24,1024]{1,0:T(8,128)(2,1)S(1)}, u32[]{:S(2)}, u32[]{:S(2)}) collective-permute-start(bf16[24,1024]{1,0:T(8,128)(2,1)S(1)} %get-tuple-element.138), channel_id=1, source_target_pairs={{0,128},{1,129},{2,130},{3,131},{4,132},{5,133},{6,134},{7,135},{8... | collective-permute-start | bytes 147464 | tf_op jit(solution)/shard_map/ppermute | solution.py:686
  84.1 7.2 %collective-permute-start.23 = (bf16[24,1024]{1,0:T(8,128)(2,1)S(1)}, bf16[24,1024]{1,0:T(8,128)(2,1)S(1)}, u32[]{:S(2)}, u32[]{:S(2)}) collective-permute-start(bf16[24,1024]{1,0:T(8,128)(2,1)S(1)} %get-tuple-element.139), channel_id=1, source_target_pairs={{0,140},{1,141},{2,142},{3,143},{4,152},{5,153},{6,154},{7,155},{8... | collective-permute-start | bytes 147464 | tf_op jit(solution)/shard_map/ppermute | solution.py:691
  91.8 11.1 %collective-permute-start.24 = (bf16[24,1024]{1,0:T(8,128)(2,1)S(1)}, bf16[24,1024]{1,0:T(8,128)(2,1)S(1)}, u32[]{:S(2)}, u32[]{:S(2)}) collective-permute-start(bf16[24,1024]{1,0:T(8,128)(2,1)S(1)} %get-tuple-element.140.own_ref), channel_id=1, source_target_pairs={{0,1},{1,0},{2,3},{3,2},{4,5},{5,4},{6,7},{7,6},{8,9},{9,8},{10,11... | collective-permute-start | bytes 147464 | tf_op jit(solution)/shard_map/ppermute | solution.py:686
  92.0 10.9 %collective-permute-start.26 = (bf16[16,1024]{1,0:T(8,128)(2,1)S(1)}, bf16[16,1024]{1,0:T(8,128)(2,1)S(1)}, u32[]{:S(2)}, u32[]{:S(2)}) collective-permute-start(bf16[16,1024]{1,0:T(8,128)(2,1)S(1)} %get-tuple-element.141), channel_id=1, source_target_pairs={{0,3},{1,2},{2,1},{3,0},{4,7},{5,6},{6,5},{7,4},{8,11},{9,10},{10,... | collective-permute-start | bytes 98312 | tf_op jit(solution)/shard_map/ppermute | solution.py:686
  100.5 2.4 %collective-permute-start.25 = (bf16[16,1024]{1,0:T(8,128)(2,1)S(1)}, bf16[16,1024]{1,0:T(8,128)(2,1)S(1)}, u32[]{:S(2)}, u32[]{:S(2)}) collective-permute-start(bf16[16,1024]{1,0:T(8,128)(2,1)S(1)} %get-tuple-element.141), channel_id=1, source_target_pairs={{0,2},{1,3},{2,0},{3,1},{4,6},{5,7},{6,4},{7,5},{8,10},{9,11},{10,... | collective-permute-start | bytes 98312 | tf_op jit(solution)/shard_map/ppermute | solution.py:686
